TPU v7x, 32 devices: a whole 2x2x4 slice. The times are simulated.
32 devices in a mesh: dp: 8 (over z, core), tensor: 4 (over y, x).
Axes of the slice: x: 2, y: 2, z: 4, core: 2. Of those that a mesh axis runs over, the one named last changes fastest.
Arguments:
- layer_input: bfloat16 [8, 2048, 2048], P('dp', 'tensor'), may hold values from -6 to 6
- ln_gain: bfloat16 [2048], P(('dp', 'tensor')), may hold values from 0.5 to 1.5
- ln_bias: bfloat16 [2048], P(('dp', 'tensor')), may hold values from -1.1953125 to 1.1953125
- out_bias: bfloat16 [2048], P(('dp', 'tensor')), may hold values from -1.796875 to 1.796875
- w_qkv: bfloat16 [2048, 3, 2048], P('dp', None, 'tensor'), may hold values from -0.125 to 0.125
- b_qkv: bfloat16 [3, 32, 64], P(None, 'tensor', 'dp'), may hold values from -1.796875 to 1.796875
- w_out: bfloat16 [2048, 2048], P('tensor', 'dp'), may hold values from -1 to 1
- w_fc1: bfloat16 [2048, 8192], P('dp', 'tensor'), may hold values from -0.125 to 0.125
- b_fc1: bfloat16 [128, 64], P('tensor', 'dp'), may hold values from -1.796875 to 1.796875
- w_fc2: bfloat16 [8192, 2048], P('tensor', 'dp'), may hold values from -0.0625 to 0.0625
- out_grad: bfloat16 [8, 2048, 2048], P('dp', 'tensor'), may hold values from -6 to 6
Outputs:
- layer_output: bfloat16 [8, 2048, 2048], P('dp', 'tensor')
- input_grad: float32 [8, 2048, 2048], P('dp', 'tensor')
- ln_gain_grad: float32 [2048], P(('dp', 'tensor'))
- ln_bias_grad: float32 [2048], P(('dp', 'tensor'))
- out_bias_grad: float32 [2048], P(('dp', 'tensor'))
- w_qkv_grad: float32 [2048, 3, 2048], P('dp', None, 'tensor')
- b_qkv_grad: float32 [3, 32, 64], P(None, 'tensor', 'dp')
- w_out_grad: float32 [2048, 2048], P('tensor', 'dp')
- w_fc1_grad: float32 [2048, 8192], P('dp', 'tensor')
- b_fc1_grad: float32 [128, 64], P('tensor', 'dp')
- w_fc2_grad: float32 [8192, 2048], P('tensor', 'dp')
All inputs are finite; a program needn't handle non-finite values.
Results may differ from a plain program's by a relative error of at most 0.014.
Values may be sent and summed in bfloat16 or wider, within the bound.
No kernel may reach another device: no remote copies, remote signals or barrier semaphores. Data moves between devices by JAX's collectives and lax.ppermute only.
A program may use at most 192 MiB of HBM per device.

v0:
```python
from functools import partial
import math

import jax
import jax.numpy as jnp
from jax import lax
from jax.sharding import PartitionSpec as P

D = 2048
HD = 64
ROT = 32


EPSILON = 1e-05


def rotary_tables(length):
    half_rot = ROT // 2
    frequency = 10000.0 ** (-2.0 * jnp.arange(half_rot, dtype=jnp.float32) / ROT)
    angles = jnp.arange(length, dtype=jnp.float32)[:, None] * frequency[None, :]
    return (jnp.cos(angles), jnp.sin(angles))


def rotate(tensor, cosine, sine_table):
    half_rot = ROT // 2
    first_half = tensor[..., :half_rot]
    second_half = tensor[..., half_rot:ROT]
    cos_rows = cosine[:, None, :]
    sin_rows = sine_table[:, None, :]
    return jnp.concatenate(
        [
            first_half * cos_rows - second_half * sin_rows,
            second_half * cos_rows + first_half * sin_rows,
            tensor[..., ROT:],
        ],
        axis=-1,
    )


def by_head(tensor):
    return jnp.transpose(tensor, (0, 2, 1, 3)).reshape(-1, tensor.shape[1], tensor.shape[3])


def to_tokens(tensor, seq_count):
    heads_total, length, head_width = tensor.shape
    return jnp.transpose(
        tensor.reshape(seq_count, heads_total // seq_count, length, head_width), (0, 2, 1, 3)
    )


def block_setup(length):
    block_rows = 512
    offsets = jnp.arange(length // block_rows, dtype=jnp.int32) * block_rows
    return (block_rows, offsets)


def masked_scores(q_rows, keys, offset, block_rows, scale):
    positions = jnp.arange(keys.shape[0], dtype=jnp.int32)
    scores = (
        lax.dot_general(q_rows, keys, (((1,), (1,)), ((), ())), preferred_element_type=jnp.float32)
        * scale
    )
    allowed = positions[None, :] <= (offset + positions[:block_rows])[:, None]
    return jnp.where(allowed, scores, -1e30)


def attend_head(triple):
    queries, keys, values = triple
    length = queries.shape[0]
    block_rows, offsets = block_setup(length)
    scale = 1.0 / math.sqrt(queries.shape[1])

    def one_block(offset):
        q_rows = lax.dynamic_slice_in_dim(queries, offset, block_rows, 0)
        scores = masked_scores(q_rows, keys, offset, block_rows, scale)
        row_max = jnp.max(scores, axis=1, keepdims=True)
        exp_scores = jnp.exp(scores - row_max)
        row_total = jnp.sum(exp_scores, axis=1, keepdims=True)
        probs_low = (exp_scores / row_total).astype(jnp.bfloat16)
        context = jnp.dot(probs_low, values, preferred_element_type=jnp.float32).astype(
            jnp.bfloat16
        )
        return (context, (row_max + jnp.log(row_total))[:, 0])

    context, log_total = lax.map(one_block, offsets)
    return (context.reshape(length, -1), log_total.reshape(length))


def attend_back(group):
    queries, keys, values, context_grad, log_total = group
    length = queries.shape[0]
    block_rows, offsets = block_setup(length)
    scale = 1.0 / math.sqrt(queries.shape[1])
    first_dims = (((0,), (0,)), ((), ()))

    def one_block(totals, offset):
        key_grad, value_grad = totals
        q_rows = lax.dynamic_slice_in_dim(queries, offset, block_rows, 0)
        grad_rows = lax.dynamic_slice_in_dim(context_grad, offset, block_rows, 0)
        lse_rows = lax.dynamic_slice_in_dim(log_total, offset, block_rows, 0)
        scores = masked_scores(q_rows, keys, offset, block_rows, scale)
        probs = jnp.exp(scores - lse_rows[:, None])
        probs_grad = lax.dot_general(
            grad_rows, values, (((1,), (1,)), ((), ())), preferred_element_type=jnp.float32
        )
        row_delta = jnp.sum(probs * probs_grad, axis=1, keepdims=True)
        score_grad = (probs * (probs_grad - row_delta)).astype(jnp.bfloat16)
        query_grad = jnp.dot(score_grad, keys, preferred_element_type=jnp.float32) * scale
        key_grad = (
            key_grad
            + lax.dot_general(score_grad, q_rows, first_dims, preferred_element_type=jnp.float32)
            * scale
        )
        value_grad = value_grad + lax.dot_general(
            probs.astype(jnp.bfloat16), grad_rows, first_dims, preferred_element_type=jnp.float32
        )
        return ((key_grad, value_grad), query_grad)

    zero_grad = jnp.zeros(keys.shape, jnp.float32)
    (key_grad, value_grad), query_grad = lax.scan(one_block, (zero_grad, zero_grad), offsets)
    return (query_grad.reshape(length, -1), key_grad, value_grad)


def per_device(
    layer_input, ln_gain, ln_bias, out_bias, w_qkv, b_qkv, w_out, w_fc1, b_fc1, w_fc2, out_grad
):
    gain_full, shift_full, bias_full = (
        lax.all_gather(ln_gain, ("dp", "tensor"), axis=0, tiled=True),
        lax.all_gather(ln_bias, ("dp", "tensor"), axis=0, tiled=True),
        lax.all_gather(out_bias, ("dp", "tensor"), axis=0, tiled=True),
    )
    gain_full = gain_full.astype(jnp.float32)
    shift_full = shift_full.astype(jnp.float32)
    bias_full = bias_full.astype(jnp.float32)
    inputs = layer_input.astype(jnp.float32)
    center = jnp.mean(inputs, axis=-1, keepdims=True)
    centered = inputs - center
    variance = jnp.mean(centered * centered, axis=-1, keepdims=True)
    inv_std = lax.rsqrt(variance + EPSILON)
    unit_rows = centered * inv_std
    normed = (unit_rows * gain_full + shift_full).astype(jnp.bfloat16)
    normed_all = lax.all_gather(normed, "tensor", axis=1, tiled=True)
    seq_count, length = (normed_all.shape[0], normed_all.shape[1])
    token_count = seq_count * length
    flat_rows = normed_all.reshape(token_count, D)
    full_qkv, full_bqkv, full_out, full_fc1, full_bfc1, full_fc2 = (
        lax.all_gather(w_qkv, "dp", axis=0, tiled=True),
        lax.all_gather(b_qkv, "dp", axis=2, tiled=True),
        lax.all_gather(w_out, "dp", axis=1, tiled=True),
        lax.all_gather(w_fc1, "dp", axis=0, tiled=True),
        lax.all_gather(b_fc1, "dp", axis=1, tiled=True),
        lax.all_gather(w_fc2, "dp", axis=1, tiled=True),
    )
    inner_width = full_out.shape[0]
    head_count = inner_width // HD
    merged = jnp.dot(
        flat_rows, full_qkv.reshape(D, 3 * inner_width), preferred_element_type=jnp.float32
    )
    merged = (merged + full_bqkv.reshape(3 * inner_width).astype(jnp.float32)).reshape(
        seq_count, length, 3, head_count, HD
    )
    cosine, sine_table = rotary_tables(length)
    head_q = by_head(rotate(merged[:, :, 0], cosine, sine_table).astype(jnp.bfloat16))
    head_k = by_head(rotate(merged[:, :, 1], cosine, sine_table).astype(jnp.bfloat16))
    head_v = by_head(merged[:, :, 2].astype(jnp.bfloat16))
    context_heads, log_total = lax.map(attend_head, (head_q, head_k, head_v))
    context = to_tokens(context_heads, seq_count).reshape(token_count, inner_width)
    hidden = jnp.dot(flat_rows, full_fc1, preferred_element_type=jnp.float32) + full_bfc1.reshape(
        -1
    ).astype(jnp.float32)
    activation = jax.nn.gelu(hidden, approximate=True).astype(jnp.bfloat16)
    partial_sum = jnp.dot(context, full_out, preferred_element_type=jnp.float32) + jnp.dot(
        activation, full_fc2, preferred_element_type=jnp.float32
    )
    branch = lax.psum_scatter(
        partial_sum.reshape(seq_count, length, D).astype(jnp.bfloat16),
        "tensor",
        scatter_dimension=1,
        tiled=True,
    ).astype(jnp.float32)
    layer_output = (inputs + branch + bias_full).astype(jnp.bfloat16)
    grad_local = out_grad.astype(jnp.float32)
    grad_all = lax.all_gather(out_grad, "tensor", axis=1, tiled=True).reshape(token_count, D)
    back_qkv, back_out, back_fc1, back_fc2 = (
        lax.all_gather(w_qkv, "dp", axis=0, tiled=True),
        lax.all_gather(w_out, "dp", axis=1, tiled=True),
        lax.all_gather(w_fc1, "dp", axis=0, tiled=True),
        lax.all_gather(w_fc2, "dp", axis=1, tiled=True),
    )
    first_dims = (((0,), (0,)), ((), ()))
    last_dims = (((1,), (1,)), ((), ()))
    w_fc2_part = lax.dot_general(
        activation, grad_all, first_dims, preferred_element_type=jnp.float32
    )
    w_out_part = lax.dot_general(context, grad_all, first_dims, preferred_element_type=jnp.float32)
    act_grad = lax.dot_general(grad_all, back_fc2, last_dims, preferred_element_type=jnp.float32)
    gelu_back = jax.vjp(partial(jax.nn.gelu, approximate=True), hidden)[1]
    hidden_grad = gelu_back(act_grad)[0].astype(jnp.bfloat16)
    context_grad = lax.dot_general(
        grad_all, back_out, last_dims, preferred_element_type=jnp.float32
    ).astype(jnp.bfloat16)
    grad_heads = by_head(context_grad.reshape(seq_count, length, head_count, HD))
    query_grad, key_grad, value_grad = lax.map(
        attend_back, (head_q, head_k, head_v, grad_heads, log_total)
    )
    query_grad = rotate(to_tokens(query_grad, seq_count), cosine, -sine_table)
    key_grad = rotate(to_tokens(key_grad, seq_count), cosine, -sine_table)
    value_grad = to_tokens(value_grad, seq_count)
    merged_grad = (
        jnp.stack([query_grad, key_grad, value_grad], axis=2)
        .astype(jnp.bfloat16)
        .reshape(token_count, 3 * inner_width)
    )
    w_qkv_part = lax.dot_general(
        flat_rows, merged_grad, first_dims, preferred_element_type=jnp.float32
    ).reshape(D, 3, inner_width)
    b_qkv_part = jnp.sum(merged_grad, axis=0, dtype=jnp.float32).reshape(3, head_count, HD)
    w_fc1_part = lax.dot_general(
        flat_rows, hidden_grad, first_dims, preferred_element_type=jnp.float32
    )
    b_fc1_part = jnp.sum(hidden_grad, axis=0, dtype=jnp.float32).reshape(-1, HD)
    normed_grad = lax.dot_general(
        merged_grad,
        back_qkv.reshape(D, 3 * inner_width),
        last_dims,
        preferred_element_type=jnp.float32,
    )
    normed_grad = normed_grad + lax.dot_general(
        hidden_grad, back_fc1, last_dims, preferred_element_type=jnp.float32
    )
    normed_sum = lax.psum_scatter(
        normed_grad.reshape(seq_count, length, D).astype(jnp.bfloat16),
        "tensor",
        scatter_dimension=1,
        tiled=True,
    ).astype(jnp.float32)
    scaled_grad = normed_sum * gain_full
    input_grad = grad_local + inv_std * (
        scaled_grad
        - jnp.mean(scaled_grad, axis=-1, keepdims=True)
        - unit_rows * jnp.mean(scaled_grad * unit_rows, axis=-1, keepdims=True)
    )
    gain_part = jnp.sum(normed_sum * unit_rows, axis=(0, 1))
    shift_part = jnp.sum(normed_sum, axis=(0, 1))
    bias_part = jnp.sum(grad_local, axis=(0, 1))
    w_qkv_grad, b_qkv_grad, w_out_grad, w_fc1_grad, b_fc1_grad, w_fc2_grad = (
        lax.psum_scatter(
            w_qkv_part.astype(jnp.bfloat16), "dp", scatter_dimension=0, tiled=True
        ).astype(jnp.float32),
        lax.psum_scatter(
            b_qkv_part.astype(jnp.bfloat16), "dp", scatter_dimension=2, tiled=True
        ).astype(jnp.float32),
        lax.psum_scatter(
            w_out_part.astype(jnp.bfloat16), "dp", scatter_dimension=1, tiled=True
        ).astype(jnp.float32),
        lax.psum_scatter(
            w_fc1_part.astype(jnp.bfloat16), "dp", scatter_dimension=0, tiled=True
        ).astype(jnp.float32),
        lax.psum_scatter(
            b_fc1_part.astype(jnp.bfloat16), "dp", scatter_dimension=1, tiled=True
        ).astype(jnp.float32),
        lax.psum_scatter(
            w_fc2_part.astype(jnp.bfloat16), "dp", scatter_dimension=1, tiled=True
        ).astype(jnp.float32),
    )
    ln_gain_grad, ln_bias_grad, out_bias_grad = (
        lax.psum_scatter(gain_part, ("dp", "tensor"), scatter_dimension=0, tiled=True),
        lax.psum_scatter(shift_part, ("dp", "tensor"), scatter_dimension=0, tiled=True),
        lax.psum_scatter(bias_part, ("dp", "tensor"), scatter_dimension=0, tiled=True),
    )
    return (
        layer_output,
        input_grad,
        ln_gain_grad,
        ln_bias_grad,
        out_bias_grad,
        w_qkv_grad,
        b_qkv_grad,
        w_out_grad,
        w_fc1_grad,
        b_fc1_grad,
        w_fc2_grad,
    )


def solution(mesh):
    in_specs = (
        P("dp", "tensor", None),
        P(("dp", "tensor")),
        P(("dp", "tensor")),
        P(("dp", "tensor")),
        P("dp", None, "tensor"),
        P(None, "tensor", "dp"),
        P("tensor", "dp"),
        P("dp", "tensor"),
        P("tensor", "dp"),
        P("tensor", "dp"),
        P("dp", "tensor", None),
    )
    out_specs = (
        P("dp", "tensor", None),
        P("dp", "tensor", None),
        P(("dp", "tensor")),
        P(("dp", "tensor")),
        P(("dp", "tensor")),
        P("dp", None, "tensor"),
        P(None, "tensor", "dp"),
        P("tensor", "dp"),
        P("dp", "tensor"),
        P("tensor", "dp"),
        P("tensor", "dp"),
    )
    return jax.shard_map(
        per_device, mesh=mesh, in_specs=in_specs, out_specs=out_specs, check_vma=False
    )
```

profile of v0, /device:TPU:0, one launch (start us, length us, event | category | flops | bytes accessed | tf_op | source)
XLA Modules:
  0.0 1668.1 jit_solution(11400459536492059489)
XLA Ops:
  12.3 50.8 %all-reduce.9 = (bf16[2048]{0:T(1024)(128)(2,1)S(1)}, bf16[2048]{0:T(1024)(128)(2,1)S(1)}, bf16[2048]{0:T(1024)(128)(2,1)}) all-reduce(bf16[2048]{0:T(1024)(128)(2,1)S(1)} %dynamic-update-slice.1, bf16[2048]{0:T(1024)(128)(2,1)S(1)} %dynamic-update-slice, ...), channel_id=1, replica_groups=mesh['dp'=8,'tensor'=4] {'dp','tensor'}, use_global_device_ids=true, to_apply=%add.1 | all-reduce | flops 6144 | bytes 24576
  71.4 17.7 %all_gather.41 = bf16[3,8,64]{1,0,2:T(4,128)(2,1)S(1)} all-gather(bf16[3,8,8]{1,0,2:T(4,128)(2,1)S(1)} %copy.111), channel_id=1, replica_groups=mesh['dp'=8,'tensor'=4] {'dp'}, dimensions={2}, use_global_device_ids=true | all-gather | bytes 3456 | tf_op jit(solution)/shard_map/all_gather | solution.py:148
  90.5 12.9 all_gather.44
  104.2 64.0 %all-gather.7.cloned.1.call-done = bf16[1,2048,2048]{2,1,0:T(8,128)(2,1)} async-done(((bf16[1,512,2048]{2,1,0:T(8,128)(2,1)}), bf16[1,2048,2048]{2,1,0:T(8,128)(2,1)}) %all-gather.7.cloned.1.call-update) | async-done | bytes 8388624 | tf_op jit(solution)/shard_map/all_gather | solution.py:142
  168.2 17.8 %convolution_add_fusion.1 = f32[2048,1536]{0,1:T(8,128)S(1)} fusion(bf16[2048,1536]{0,1:T(8,128)(2,1)} %bitcast.215, bf16[1,2048,2048]{2,1,0:T(8,128)(2,1)} %all-gather.7.cloned.1.call-done, f32[1536]{0:T(1024)S(1)} %reshape.413), kind=kOutput, calls=%fused_computation.61 | convolution fusion | flops 12888047616 | bytes 27269120 | tf_op jit(solution)/shard_map/dot_general | solution.py:156
  191.2 3.2 copy.113
  194.4 4.9 copy.114
  202.5 356.9 %while.54 = (s32[]{:T(128)}, bf16[8,2048,64]{1,2,0:T(8,128)(2,1)}, f32[8,2048]{1,0:T(8,128)S(1)}, bf16[8,2048,64]{2,1,0:T(8,128)(2,1)}, bf16[8,2048,64]{2,1,0:T(...) while((s32[]{:T(128)}, bf16[8,2048,64]{1,2,0:T(8,128)(2,1)}, ...), condition=%wide.region_7.8_spmd, body=%wide.region_2.7_spmd.sunk | while | flops 277905920 | bytes 33809312 | solution.py:166
  204.9 41.5 %while.57 = (s32[]{:T(128)}, bf16[4,512,64]{1,2,0:T(8,128)(2,1)S(1)}, f32[4,512]{1,0:T(4,128)S(1)}, s32[4]{0:T(128)S(1)}, bf16[2048,64]{1,0:T(8,128)(2,1)S(1)}, ...) while((s32[]{:T(128)}, ...), condition=%wide.region_6.6_spmd, body=%wide.region_3.5_spmd.sunk | while | flops 277905920 | bytes 30630080 | solution.py:85
  211.9 3.6 fusion.140
  222.4 3.2 fusion.140
  232.6 3.2 fusion.140
  242.7 3.7 fusion.140
  250.2 40.5 %while.57 = (s32[]{:T(128)}, bf16[4,512,64]{1,2,0:T(8,128)(2,1)S(1)}, f32[4,512]{1,0:T(4,128)S(1)}, s32[4]{0:T(128)S(1)}, bf16[2048,64]{1,0:T(8,128)(2,1)S(1)}, ...) while((s32[]{:T(128)}, ...), condition=%wide.region_6.6_spmd, body=%wide.region_3.5_spmd.sunk | while | flops 277905920 | bytes 30630080 | solution.py:85
  294.6 40.8 %while.57 = (s32[]{:T(128)}, bf16[4,512,64]{1,2,0:T(8,128)(2,1)S(1)}, f32[4,512]{1,0:T(4,128)S(1)}, s32[4]{0:T(128)S(1)}, bf16[2048,64]{1,0:T(8,128)(2,1)S(1)}, ...) while((s32[]{:T(128)}, ...), condition=%wide.region_6.6_spmd, body=%wide.region_3.5_spmd.sunk | while | flops 277905920 | bytes 30630080 | solution.py:85
  301.6 3.2 fusion.140
  311.8 3.2 fusion.140
  321.9 3.2 fusion.140
  332.1 3.3 fusion.140
  339.2 40.5 %while.57 = (s32[]{:T(128)}, bf16[4,512,64]{1,2,0:T(8,128)(2,1)S(1)}, f32[4,512]{1,0:T(4,128)S(1)}, s32[4]{0:T(128)S(1)}, bf16[2048,64]{1,0:T(8,128)(2,1)S(1)}, ...) while((s32[]{:T(128)}, ...), condition=%wide.region_6.6_spmd, body=%wide.region_3.5_spmd.sunk | while | flops 277905920 | bytes 30630080 | solution.py:85
  346.2 3.2 fusion.140
  356.3 3.2 fusion.140
  366.4 3.2 fusion.140
  376.6 3.2 fusion.140
  383.9 40.8 %while.57 = (s32[]{:T(128)}, bf16[4,512,64]{1,2,0:T(8,128)(2,1)S(1)}, f32[4,512]{1,0:T(4,128)S(1)}, s32[4]{0:T(128)S(1)}, bf16[2048,64]{1,0:T(8,128)(2,1)S(1)}, ...) while((s32[]{:T(128)}, ...), condition=%wide.region_6.6_spmd, body=%wide.region_3.5_spmd.sunk | while | flops 277905920 | bytes 30630080 | solution.py:85
  390.8 3.2 fusion.140
  401.0 3.2 fusion.140
  411.1 3.2 fusion.140
  421.3 3.4 fusion.140
  428.5 40.5 %while.57 = (s32[]{:T(128)}, bf16[4,512,64]{1,2,0:T(8,128)(2,1)S(1)}, f32[4,512]{1,0:T(4,128)S(1)}, s32[4]{0:T(128)S(1)}, bf16[2048,64]{1,0:T(8,128)(2,1)S(1)}, ...) while((s32[]{:T(128)}, ...), condition=%wide.region_6.6_spmd, body=%wide.region_3.5_spmd.sunk | while | flops 277905920 | bytes 30630080 | solution.py:85
  435.5 3.2 fusion.140
  445.6 3.2 fusion.140
  455.7 3.2 fusion.140
  472.9 40.5 %while.57 = (s32[]{:T(128)}, bf16[4,512,64]{1,2,0:T(8,128)(2,1)S(1)}, f32[4,512]{1,0:T(4,128)S(1)}, s32[4]{0:T(128)S(1)}, bf16[2048,64]{1,0:T(8,128)(2,1)S(1)}, ...) while((s32[]{:T(128)}, ...), condition=%wide.region_6.6_spmd, body=%wide.region_3.5_spmd.sunk | while | flops 277905920 | bytes 30630080 | solution.py:85
  517.2 40.5 %while.57 = (s32[]{:T(128)}, bf16[4,512,64]{1,2,0:T(8,128)(2,1)S(1)}, f32[4,512]{1,0:T(4,128)S(1)}, s32[4]{0:T(128)S(1)}, bf16[2048,64]{1,0:T(8,128)(2,1)S(1)}, ...) while((s32[]{:T(128)}, ...), condition=%wide.region_6.6_spmd, body=%wide.region_3.5_spmd.sunk | while | flops 277905920 | bytes 30630080 | solution.py:85
  559.4 8.5 fusion.71
  567.9 3.2 copy.118
  571.1 589.2 %while.56 = (s32[]{:T(128)}, f32[8,2048,64]{1,2,0:T(8,128)}, f32[8,2048,64]{1,2,0:T(8,128)}, bf16[8,2048,64]{1,2,0:T(8,128)(2,1)}, bf16[8,2048,64]{2,1,0:T(8,128...) while((s32[]{:T(128)}, f32[8,2048,64]{1,2,0:T(8,128)}, ...), condition=%wide.region_13.14_spmd, body=%wide.region_9.13_spmd.sunk | while | flops 682263040 | bytes 76185624 | solution.py:203
  577.9 62.3 %while.58 = (s32[]{:T(128)}, f32[2048,64]{0,1:T(8,128)}, f32[2048,64]{0,1:T(8,128)S(1)}, f32[4,512,64]{1,2,0:T(8,128)}, s32[4]{0:T(128)S(1)}, /*index=5*/bf16[20...) while((s32[]{:T(128)}, f32[2048,64]{0,1:T(8,128)}, ...), condition=%wide.region_12.12_spmd.clone, body=%wide.region_10.11_spmd.clone.sunk | while | flops 682263040 | bytes 68827904 | solution.py:120
  651.5 62.4 %while.58 = (s32[]{:T(128)}, f32[2048,64]{0,1:T(8,128)}, f32[2048,64]{0,1:T(8,128)S(1)}, f32[4,512,64]{1,2,0:T(8,128)}, s32[4]{0:T(128)S(1)}, /*index=5*/bf16[20...) while((s32[]{:T(128)}, f32[2048,64]{0,1:T(8,128)}, ...), condition=%wide.region_12.12_spmd.clone, body=%wide.region_10.11_spmd.clone.sunk | while | flops 682263040 | bytes 68827904 | solution.py:120
  725.2 62.4 %while.58 = (s32[]{:T(128)}, f32[2048,64]{0,1:T(8,128)}, f32[2048,64]{0,1:T(8,128)S(1)}, f32[4,512,64]{1,2,0:T(8,128)}, s32[4]{0:T(128)S(1)}, /*index=5*/bf16[20...) while((s32[]{:T(128)}, f32[2048,64]{0,1:T(8,128)}, ...), condition=%wide.region_12.12_spmd.clone, body=%wide.region_10.11_spmd.clone.sunk | while | flops 682263040 | bytes 68827904 | solution.py:120
  798.8 62.4 %while.58 = (s32[]{:T(128)}, f32[2048,64]{0,1:T(8,128)}, f32[2048,64]{0,1:T(8,128)S(1)}, f32[4,512,64]{1,2,0:T(8,128)}, s32[4]{0:T(128)S(1)}, /*index=5*/bf16[20...) while((s32[]{:T(128)}, f32[2048,64]{0,1:T(8,128)}, ...), condition=%wide.region_12.12_spmd.clone, body=%wide.region_10.11_spmd.clone.sunk | while | flops 682263040 | bytes 68827904 | solution.py:120
  872.5 62.4 %while.58 = (s32[]{:T(128)}, f32[2048,64]{0,1:T(8,128)}, f32[2048,64]{0,1:T(8,128)S(1)}, f32[4,512,64]{1,2,0:T(8,128)}, s32[4]{0:T(128)S(1)}, /*index=5*/bf16[20...) while((s32[]{:T(128)}, f32[2048,64]{0,1:T(8,128)}, ...), condition=%wide.region_12.12_spmd.clone, body=%wide.region_10.11_spmd.clone.sunk | while | flops 682263040 | bytes 68827904 | solution.py:120
  946.1 62.4 %while.58 = (s32[]{:T(128)}, f32[2048,64]{0,1:T(8,128)}, f32[2048,64]{0,1:T(8,128)S(1)}, f32[4,512,64]{1,2,0:T(8,128)}, s32[4]{0:T(128)S(1)}, /*index=5*/bf16[20...) while((s32[]{:T(128)}, f32[2048,64]{0,1:T(8,128)}, ...), condition=%wide.region_12.12_spmd.clone, body=%wide.region_10.11_spmd.clone.sunk | while | flops 682263040 | bytes 68827904 | solution.py:120
  1019.8 62.4 %while.58 = (s32[]{:T(128)}, f32[2048,64]{0,1:T(8,128)}, f32[2048,64]{0,1:T(8,128)S(1)}, f32[4,512,64]{1,2,0:T(8,128)}, s32[4]{0:T(128)S(1)}, /*index=5*/bf16[20...) while((s32[]{:T(128)}, f32[2048,64]{0,1:T(8,128)}, ...), condition=%wide.region_12.12_spmd.clone, body=%wide.region_10.11_spmd.clone.sunk | while | flops 682263040 | bytes 68827904 | solution.py:120
  1093.4 62.4 %while.58 = (s32[]{:T(128)}, f32[2048,64]{0,1:T(8,128)}, f32[2048,64]{0,1:T(8,128)S(1)}, f32[4,512,64]{1,2,0:T(8,128)}, s32[4]{0:T(128)S(1)}, /*index=5*/bf16[20...) while((s32[]{:T(128)}, f32[2048,64]{0,1:T(8,128)}, ...), condition=%wide.region_12.12_spmd.clone, body=%wide.region_10.11_spmd.clone.sunk | while | flops 682263040 | bytes 68827904 | solution.py:120
  1164.1 3.3 multiply_subtract_fusion.1
  1167.4 9.1 fusion.74
  1181.0 15.9 fusion.85
  1196.9 15.1 fusion.59
  1212.1 24.4 %fusion.41 = f32[2048,2048]{1,0:T(8,128)} fusion(bf16[2048,2048]{1,0:T(8,128)(2,1)} %all-gather.13.cloned.1.call-done, bf16[1,2048,2048]{2,1,0:T(8,128)(2,1)} %all-gather.7.cloned.1.call-done), kind=kOutput, calls=%fused_computation.74 | convolution fusion | flops 17179869184 | bytes 33554432 | tf_op jit(solution)/shard_map/dot_general | solution.py:168
  1236.5 36.1 %fusion.83 = (bf16[2048]{0:T(1024)(128)(2,1)}, bf16[2048,2048]{1,0:T(8,128)(2,1)}) fusion(f32[2048,2048]{1,0:T(8,128)} %fusion.41, f32[2048]{0:T(1024)S(1)} %copy-done.16, bf16[2048,2048]{1,0:T(8,128)(2,1)} %all-gather.15.cloned.1.call-done, bf16[1,2048,2048]{2,1,0:T(8,128)(2,1)} %all-gather.17.cloned.1.call-done), kind=kOutput, calls=%fused_computation.139 | convolution fusion | flops 17272141824 | bytes 41955328 | tf_op jit(solution)/shard_map/dot_general | solution.py:196
  1272.6 25.8 %fusion.51 = bf16[1,2048,2048]{2,1,0:T(8,128)(2,1)} fusion(f32[2048,2048]{1,0:T(8,128)} %fusion.85, bf16[2048,2048]{1,0:T(8,128)(2,1)} %get-tuple-element.475, bf16[2048,2048]{1,0:T(8,128)(2,1)} %all-gather.13.cloned.1.call-done), kind=kOutput, calls=%fused_computation.80 | convolution fusion | flops 17188257792 | bytes 41943040 | tf_op jit(solution)/shard_map/dot_general | solution.py:228
  1300.0 10.0 fusion.84
  1310.0 28.7 %fusion.50 = bf16[1,2048,2048]{2,1,0:T(8,128)(2,1)} fusion(f32[2048,2048]{1,0:T(8,128)} %fusion.84, bf16[2048,2048]{1,0:T(8,128)(2,1)} %all-gather.15.cloned.1.call-done, f32[2048,2048]{1,0:T(8,128)} %fusion.41, f32[2048]{0:T(1024)S(1)} %copy-done.16), kind=kOutput, calls=%fused_computation.79 | convolution fusion | flops 17230200832 | bytes 50339840 | tf_op jit(solution)/shard_map/dot_general | solution.py:172
  1338.8 24.6 %fusion.44 = bf16[2048,2048]{1,0:T(8,128)(2,1)} fusion(bf16[2048,2048]{1,0:T(8,128)(2,1)} %get-tuple-element.475, bf16[1,2048,2048]{2,1,0:T(8,128)(2,1)} %all-gather.7.cloned.1.call-done), kind=kOutput, calls=%fused_computation.77 | convolution fusion | flops 17184063488 | bytes 25165824 | tf_op jit(solution)/shard_map/dot_general | solution.py:218
  1363.4 27.3 %fusion.47 = bf16[2048,2048]{1,0:T(8,128)(2,1)} fusion(bf16[1,2048,2048]{2,1,0:T(8,128)(2,1)} %all-gather.17.cloned.1.call-done, f32[2048,2048]{1,0:T(8,128)} %fusion.41, f32[2048]{0:T(1024)S(1)} %copy-done.16), kind=kOutput, calls=%fused_computation.78 | convolution fusion | flops 17226006528 | bytes 33562624 | tf_op jit(solution)/shard_map/dot_general | solution.py:192
  1392.8 29.2 %all-reduce.10 = (bf16[3,8,64]{2,1,0:T(8,128)(2,1)S(1)}, bf16[32,64]{1,0:T(8,128)(2,1)S(1)}) all-reduce(bf16[3,8,64]{2,1,0:T(8,128)(2,1)S(1)} %copy-done.15, bf16[32,64]{1,0:T(8,128)(2,1)S(1)} %convert_element_type.201), channel_id=8, replica_groups=mesh['dp'=8,'tensor'=4] {'dp'}, use_global_device_ids=true, to_apply=%region_25.26.clone | all-reduce | flops 3584 | bytes 14336
  1427.7 3.5 fusion.70
  1431.2 44.0 %reduce-scatter.9.cloned.1.call-done = bf16[1,512,2048]{2,1,0:T(8,128)(2,1)} async-done(((bf16[1,2048,2048]{2,1,0:T(8,128)(2,1)}), bf16[1,512,2048]{2,1,0:T(8,128)(2,1)}) %reduce-scatter.9.cloned.1.call-update) | async-done | bytes 2097168 | tf_op jit(solution)/shard_map/reduce_scatter | solution.py:175
  1475.2 6.5 convert_reduce_fusion.2
  1481.6 41.4 %all-reduce.8 = (f32[2048]{0:T(1024)S(1)}, f32[2048]{0:T(1024)S(1)}, f32[2048]{0:T(1024)S(1)}) all-reduce(f32[2048]{0:T(1024)S(1)} %get-tuple-element.368, f32[2048]{0:T(1024)S(1)} %get-tuple-element.371, f32[2048]{0:T(1024)S(1)} %get-tuple-element.464), channel_id=4, replica_groups=mesh['dp'=8,'tensor'=4] {'dp','tensor'}, use_global_device_ids=true, to_apply=%region_18.19.clone | all-reduce | flops 6144 | bytes 49152
  1524.8 43.4 %reduce-scatter.17.cloned.1.call-done = bf16[256,2048]{1,0:T(8,128)(2,1)} async-done(((bf16[2048,2048]{1,0:T(8,128)(2,1)}), bf16[256,2048]{1,0:T(8,128)(2,1)}) %reduce-scatter.17.cloned.1.call-update) | async-done | bytes 1048592 | tf_op jit(solution)/shard_map/reduce_scatter | solution.py:256
  1571.0 87.3 %reduce-scatter.19.cloned.1.call-done = bf16[2048,256]{1,0:T(8,128)(2,1)} async-done(((bf16[2048,2048]{1,0:T(8,128)(2,1)}), bf16[2048,256]{1,0:T(8,128)(2,1)}) %reduce-scatter.19.cloned.1.call-update) | async-done | bytes 1048592 | tf_op jit(solution)/shard_map/reduce_scatter | solution.py:262
  (1006 shorter events, 803.4 us)
Async XLA Ops:
  7.2 58.0 %copy-start.3 = (bf16[1,512,2048]{2,1,0:T(8,128)(2,1)S(1)}, bf16[1,512,2048]{2,1,0:T(8,128)(2,1)}, u32[]{:S(2)}) copy-start(bf16[1,512,2048]{2,1,0:T(8,128)(2,1)} %param.19) | copy-start | bytes 6291460
  7.2 97.0 %all-gather.9.cloned.1.call-start = ((), (), s32[]{:S(2)}) async-start(), calls=%async_computation.7 | async-start | bytes 7077888 | tf_op jit(solution)/shard_map/all_gather | solution.py:147
  9.7 158.5 %all-gather.7.cloned.1.call-start = ((), (), s32[]{:S(2)}) async-start(), calls=%async_computation.6 | async-start | bytes 10485760 | tf_op jit(solution)/shard_map/all_gather | solution.py:142
  63.1 2.8 copy-start.9
  68.7 2.6 copy-start.17
  68.7 21.8 %copy-start.20 = (bf16[32,8]{0,1:T(8,128)(2,1)S(1)}, bf16[32,8]{0,1:T(8,128)(2,1)}, u32[]{:S(2)}) copy-start(bf16[32,8]{0,1:T(8,128)(2,1)} %param.27) | copy-start | bytes 1540
  68.7 490.7 %all-gather.11.cloned.1.call-start = ((), (), s32[]{:S(2)}) async-start(), calls=%async_computation.8 | async-start | bytes 2359296 | tf_op jit(solution)/shard_map/all_gather | solution.py:149
  69.5 490.0 %all-gather.17.cloned.1.call-start = ((), (), s32[]{:S(2)}) async-start(), calls=%async_computation.12 | async-start | bytes 10485760 | tf_op jit(solution)/shard_map/all_gather | solution.py:183
  70.0 1142.1 %all-gather.13.cloned.1.call-start = ((), (), s32[]{:S(2)}) async-start(), calls=%async_computation.9 | async-start | bytes 9437184 | tf_op jit(solution)/shard_map/all_gather | solution.py:150
  70.6 1165.9 %all-gather.15.cloned.1.call-start = ((), (), s32[]{:S(2)}) async-start(), calls=%async_computation.10 | async-start | bytes 9437184 | tf_op jit(solution)/shard_map/all_gather | solution.py:152
  71.2 1352.2 %reduce-scatter.15.cloned.1.call-start = ((), (), s32[]{:S(2)}) async-start(), calls=%async_computation.15 | async-start | bytes 2359296 | tf_op jit(solution)/shard_map/reduce_scatter | solution.py:253
  90.5 98.5 %copy-start.8 = (f32[2048,16]{0,1:T(8,128)}, f32[2048,16]{0,1:T(8,128)S(1)}, u32[]{:S(2)}) copy-start(f32[2048,16]{0,1:T(8,128)S(1)} %get-tuple-element.473) | copy-start | bytes 393220
  194.4 4.9 copy-start.5
  298.7 2.1 copy-start.2
  588.0 3.8 copy-start.1
  603.4 4.0 copy-start.1
  619.1 4.0 copy-start.1
  634.7 4.0 copy-start.1
  661.7 3.8 copy-start.1
  677.1 4.0 copy-start.1
  690.2 2.1 copy-start
  692.7 4.0 copy-start.1
  705.9 2.1 copy-start
  708.4 4.0 copy-start.1
  735.3 3.8 copy-start.1
  750.7 4.0 copy-start.1
  766.4 4.0 copy-start.1
  782.0 4.0 copy-start.1
  809.0 3.8 copy-start.1
  824.4 4.0 copy-start.1
  840.0 4.0 copy-start.1
  855.7 4.0 copy-start.1
  882.6 3.8 copy-start.1
  898.0 4.0 copy-start.1
  913.7 4.0 copy-start.1
  929.3 4.0 copy-start.1
  956.3 3.8 copy-start.1
  971.7 4.0 copy-start.1
  987.3 4.0 copy-start.1
  1003.0 4.0 copy-start.1
  1029.9 3.8 copy-start.1
  1045.3 4.0 copy-start.1
  1061.0 4.0 copy-start.1
  1076.6 4.0 copy-start.1
  1103.6 3.8 copy-start.1
  1119.0 4.0 copy-start.1
  1134.6 4.0 copy-start.1
  1150.3 4.0 copy-start.1
  1160.3 3.8 copy-start.6
  1162.2 5.2 copy-start.22
  1176.5 248.7 %reduce-scatter.13.cloned.1.call-start = ((), (), s32[]{:S(2)}) async-start(), calls=%async_computation.14 | async-start | bytes 7077888 | tf_op jit(solution)/shard_map/reduce_scatter | solution.py:247
  1178.1 2.6 slice-start.2
  1178.5 2.5 slice-start.3
  1178.5 18.4 %slice-start = ((s8[8388608]{0:T(1024)(128)(4,1)}), s8[4194304]{0:T(1024)(128)(4,1)S(1)}, s32[]{:S(2)}) async-start(s8[8388608]{0:T(1024)(128)(4,1)} %bitcast.213), calls=%async_computation.18 | async-start | bytes 8388608
  1181.0 15.9 slice-start.1
  1212.0 24.5 %copy-start.16 = (f32[2048]{0:T(1024)S(1)}, f32[2048]{0:T(1024)}, u32[]{:S(2)}) copy-start(f32[2048]{0:T(1024)} %reshape.414) | copy-start | bytes 24580
  1212.1 215.6 %reduce-scatter.11.cloned.1.call-start = ((), (), s32[]{:S(2)}) async-start(), calls=%async_computation.13 | async-start | bytes 10485760 | tf_op jit(solution)/shard_map/reduce_scatter | solution.py:231
  1298.4 176.7 %reduce-scatter.9.cloned.1.call-start = ((), (), s32[]{:S(2)}) async-start(), calls=%async_computation.11 | async-start | bytes 10485760 | tf_op jit(solution)/shard_map/reduce_scatter | solution.py:175
  1338.7 229.5 %reduce-scatter.17.cloned.1.call-start = ((), (), s32[]{:S(2)}) async-start(), calls=%async_computation.16 | async-start | bytes 9437184 | tf_op jit(solution)/shard_map/reduce_scatter | solution.py:256
  1363.3 295.0 %reduce-scatter.19.cloned.1.call-start = ((), (), s32[]{:S(2)}) async-start(), calls=%async_computation.17 | async-start | bytes 9437184 | tf_op jit(solution)/shard_map/reduce_scatter | solution.py:262
  1390.8 36.9 %copy-start.4 = (bf16[1,512,2048]{2,1,0:T(8,128)(2,1)S(1)}, bf16[1,512,2048]{2,1,0:T(8,128)(2,1)}, u32[]{:S(2)}) copy-start(bf16[1,512,2048]{2,1,0:T(8,128)(2,1)} %param.19) | copy-start | bytes 6291460
  1390.8 36.9 %copy-start.10 = (f32[2048]{0:T(1024)S(1)}, f32[2048]{0:T(1024)}, u32[]{:S(2)}) copy-start(f32[2048]{0:T(1024)} %copy-done.9) | copy-start | bytes 24580
  1390.8 36.9 %copy-start.12 = (f32[512]{0:T(512)S(1)}, f32[512]{0:T(512)}, u32[]{:S(2)}) copy-start(f32[512]{0:T(512)} %copy-done.11) | copy-start | bytes 6148
  1390.8 36.9 %copy-start.14 = (f32[512]{0:T(512)S(1)}, f32[512]{0:T(512)}, u32[]{:S(2)}) copy-start(f32[512]{0:T(512)} %copy-done.13) | copy-start | bytes 6148
  (69 other events, 135.7 us)
Sparse Core Ops, SparseCore 0:
  10.2 68.9 all-gather.8
  81.6 86.5 all-gather.6
  169.8 30.8 all-gather.10
  202.3 86.6 all-gather.16
  290.5 82.0 all-gather.12
  374.1 81.0 all-gather.14
  1176.6 36.4 reduce-scatter.14
  1215.4 68.2 reduce-scatter.12
  1298.6 86.9 reduce-scatter.10
  1388.7 86.4 reduce-scatter.8
  1477.5 90.6 reduce-scatter.16
  1570.3 87.9 reduce-scatter.18
where the time goes:
time: 1680 us; the launch traced here: 1670 us
  matrix products  689 us (41%)
  local copies, waits for them, and re-layouts  327 us (19%)
  waiting for transfers between devices  241 us (14%)
  blocking collectives  152 us (9%)
  loops' own time  129 us (8%)
  other arithmetic  114 us (7%)
    while x200, local copies, waits for them, and re-layouts  132 us
    unnamed x3, blocking collectives  121 us
    dot_general x64, matrix products, masked_scores(): lax.dot_general(q_rows, keys, (((1,), (1,)), ((), ())), preferred_element...  111 us
    dot_general x32, matrix products, one_block(): jnp.dot(probs_low, values, preferred_element_type=jnp.float32)  103 us
    reduce_scatter x1, waiting for transfers between devices, per_device(): lax.psum_scatter(w_fc2_part.astype(jnp.bfloat16), 'dp', scatter_dimension...  87.3 us
    dot_general x32, matrix products, one_block(): lax.dot_general(score_grad, q_rows, first_dims, preferred_element_type=jn...  81.1 us
    squeeze x48, local copies, waits for them, and re-layouts, per_device(): context_heads, log_total = lax.map(attend_head, (head_q, head_k, head_v))  72.7 us
    another operation x8, loops' own time, attend_back(): lax.scan(one_block, (zero_grad, zero_grad), offsets)  64.3 us
  transfers between devices with their start and end apart: 12, of which 4 were waited for; matrix products, arithmetic and copies ran while one was open for 59% of the time, Pallas kernels for 0%

commit v1 on v0

v1 whole, which is shorter than its diff:
```python
import functools
import math

import jax
import jax.numpy as jnp
from jax import lax
from jax.experimental import pallas as pl
from jax.experimental.pallas import tpu as pltpu
from jax.sharding import PartitionSpec as P

HD = 64
ROT = 32
EPSILON = 1e-05
NEG = -1e30
LOG2E = math.log2(math.e)
BF = jnp.bfloat16
F32 = jnp.float32
VMEM_BYTES = 56 << 20

NN = (((1,), (0,)), ((), ()))
NT = (((1,), (1,)), ((), ()))
TN = (((0,), (0,)), ((), ()))


def dot(a, b, dims):
    return lax.dot_general(a, b, dims, preferred_element_type=F32)


def call(kernel, name, flops, moved, **kwargs):
    return pl.pallas_call(
        kernel,
        name=name,
        compiler_params=pltpu.CompilerParams(vmem_limit_bytes=VMEM_BYTES),
        cost_estimate=pl.CostEstimate(flops=int(flops), bytes_accessed=int(moved), transcendentals=0),
        **kwargs,
    )


def struct(shape, dtype=BF):
    return jax.ShapeDtypeStruct(shape, dtype)


def order_columns(blocks, x, g):
    rows, width = x.shape
    count = blocks.shape[0]
    cols = width // count

    def kernel(blk, x_ref, g_ref, xo_ref, go_ref, sum_ref):
        xo_ref[...] = x_ref[...]
        go_ref[...] = g_ref[...]
        total = jnp.sum(g_ref[...].astype(F32), axis=0, keepdims=True)
        sum_ref[...] = jnp.broadcast_to(total, (8, cols))

    source = pl.BlockSpec((rows, cols), lambda p, blk: (0, blk[p]))
    target = pl.BlockSpec((rows, cols), lambda p, blk: (0, p))
    return call(
        kernel,
        "order_columns",
        0,
        8 * rows * width,
        grid_spec=pltpu.PrefetchScalarGridSpec(
            num_scalar_prefetch=1,
            grid=(count,),
            in_specs=[source, source],
            out_specs=[target, target, pl.BlockSpec((8, cols), lambda p, blk: (0, blk[p]))],
        ),
        out_shape=[struct(x.shape), struct(x.shape), struct((8, width), F32)],
    )(blocks, x, g)


def rotary_rows(length):
    half = ROT // 2
    frequency = 10000.0 ** (-2.0 * jnp.arange(half, dtype=F32) / ROT)
    angles = jnp.arange(length, dtype=F32)[:, None] * frequency[None, :]
    cosine, sine = jnp.cos(angles), jnp.sin(angles)
    ones, zeros = jnp.ones((length, HD - ROT), F32), jnp.zeros((length, HD - ROT), F32)
    blank = jnp.zeros_like(sine)
    keep = jnp.concatenate([cosine, cosine, ones], axis=1)
    ahead = jnp.concatenate([-sine, blank, zeros], axis=1)
    behind = jnp.concatenate([blank, sine, zeros], axis=1)
    return tuple(jnp.concatenate([t, t], axis=1) for t in (keep, ahead, behind))


def turn(u, keep, ahead, behind):
    return u * keep + pltpu.roll(u, 128 - ROT // 2, 1) * ahead + pltpu.roll(u, ROT // 2, 1) * behind


def norm_project(out_blocks, pieces, rows, gain, shift, bias, tables, w_own, w_sib):
    width = pieces[0].shape[1]
    half = w_own.shape[0]
    inner = bias.shape[1] // 3
    starts, total = [], 0
    for piece in pieces:
        starts.append(total)
        total += piece.shape[0] // rows
    length = total * rows
    n = len(pieces)

    def kernel(blk, *refs):
        piece_refs = refs[:n]
        gain_ref, shift_ref, bias_ref, keep_ref, ahead_ref, behind_ref, wo_ref, ws_ref = refs[n : n + 8]
        normed_ref, unit_ref, qkv_ref, rows_ref = refs[n + 8 :]
        step = pl.program_id(0)
        for i in range(n):
            last = starts[i + 1] if i + 1 < n else total

            @pl.when((step >= starts[i]) & (step < last))
            def _(i=i):
                rows_ref[...] = piece_refs[i][...]

        x = rows_ref[...].astype(F32)
        centered = x - jnp.mean(x, axis=1, keepdims=True)
        variance = jnp.mean(centered * centered, axis=1, keepdims=True)
        unit = centered * lax.rsqrt(variance + EPSILON)
        unit_ref[...] = unit.astype(BF)
        normed = (unit * gain_ref[...] + shift_ref[...]).astype(BF)
        normed_ref[...] = normed
        for part in range(3):
            cols = slice(part * inner, (part + 1) * inner)
            merged = (
                dot(normed[:, :half], wo_ref[:, cols], NN)
                + dot(normed[:, half:], ws_ref[:, cols], NN)
                + bias_ref[:, cols]
            )
            for pair in range(inner // 128):
                u = merged[:, pair * 128 : (pair + 1) * 128]
                if part < 2:
                    u = turn(u, keep_ref[...], ahead_ref[...], behind_ref[...])
                start = part * inner + pair * 128
                qkv_ref[:, start : start + 128] = u.astype(BF)

    def piece_spec(i):
        count = pieces[i].shape[0] // rows
        return pl.BlockSpec((rows, width), lambda j, blk: (jnp.clip(j - starts[i], 0, count - 1), 0))

    def whole(shape):
        return pl.BlockSpec(shape, lambda j, blk: (0, 0))

    def placed(cols):
        return pl.BlockSpec((rows, cols), lambda j, blk: (blk[j], 0))

    return call(
        kernel,
        "norm_project",
        2 * length * width * 3 * inner,
        6 * length * width + 12 * width * inner,
        grid_spec=pltpu.PrefetchScalarGridSpec(
            num_scalar_prefetch=1,
            grid=(total,),
            in_specs=[piece_spec(i) for i in range(n)]
            + [whole((1, width)), whole((1, width)), whole((1, 3 * inner))]
            + [placed(128)] * 3
            + [whole((half, 3 * inner))] * 2,
            out_specs=[placed(width), placed(width), placed(3 * inner)],
            scratch_shapes=[pltpu.VMEM((rows, width), BF)],
        ),
        out_shape=[struct((length, width)), struct((length, width)), struct((length, 3 * inner))],
    )(out_blocks, *pieces, gain, shift, bias, *tables, w_own, w_sib)


def attend(qkv):
    length = qkv.shape[0]
    inner = qkv.shape[1] // 3
    pairs = inner // 128
    block = min(512, length)
    count = length // block
    scale = LOG2E / math.sqrt(HD)

    def kernel(q_ref, k_ref, v_ref, o_ref, lse_ref):
        lane = lax.broadcasted_iota(jnp.int32, (1, 128), 1)
        for index in range(count):

            @pl.when(pl.program_id(1) == index)
            def _(index=index):
                queries = q_ref[...]
                blank = jnp.zeros_like(queries)
                end = (index + 1) * block
                keys, values = k_ref[:end, :], v_ref[:end, :]
                found = []
                for head in range(2):
                    mine = (lane < HD) if head == 0 else (lane >= HD)
                    scores = dot(jnp.where(mine, queries, blank), keys, NT)
                    row = lax.broadcasted_iota(jnp.int32, (block, block), 0)
                    col = lax.broadcasted_iota(jnp.int32, (block, block), 1)
                    last = jnp.where(col <= row, scores[:, end - block :], NEG)
                    if index:
                        scores = jnp.concatenate([scores[:, : end - block], last], axis=1)
                    else:
                        scores = last
                    top = jnp.max(scores, axis=1, keepdims=True)
                    weights = jnp.exp2((scores - top) * scale)
                    total = jnp.sum(weights, axis=1, keepdims=True)
                    found.append((top, total, dot(weights.astype(BF), values, NN)))
                (top0, total0, out0), (top1, total1, out1) = found
                o_ref[...] = jnp.where(lane < HD, out0 / total0, out1 / total1).astype(BF)
                log_total = jnp.where(
                    lane < HD, top0 * scale + jnp.log2(total0), top1 * scale + jnp.log2(total1)
                ).T
                lse_ref[0, 0:1, :] = log_total[0:1, :]
                lse_ref[0, 1:2, :] = log_total[HD : HD + 1, :]

    return call(
        kernel,
        "attend",
        4 * length * length * inner,
        8 * length * inner,
        grid=(pairs, count),
        in_specs=[
            pl.BlockSpec((block, 128), lambda h, i: (i, h)),
            pl.BlockSpec((length, 128), lambda h, i: (0, pairs + h)),
            pl.BlockSpec((length, 128), lambda h, i: (0, 2 * pairs + h)),
        ],
        out_specs=[
            pl.BlockSpec((block, 128), lambda h, i: (i, h)),
            pl.BlockSpec((1, 2, block), lambda h, i: (h, 0, i)),
        ],
        out_shape=[struct((length, inner)), struct((pairs, 2, length), F32)],
    )(qkv, qkv, qkv)


def attend_back(qkv, context, context_grad, log_total, tables):
    length = qkv.shape[0]
    inner = qkv.shape[1] // 3
    pairs = inner // 128
    block = min(512, length)
    count = length // block
    scale = LOG2E / math.sqrt(HD)
    shrink = 1.0 / math.sqrt(HD)

    def kernel(q_ref, k_ref, v_ref, o_ref, do_ref, lse_ref, keep_ref, ahead_ref, behind_ref, *rest):
        dq_ref, dk_ref, dv_ref, sum_ref, k_total, v_total = rest
        step = pl.program_id(1)
        lane = lax.broadcasted_iota(jnp.int32, (1, 128), 1)
        rows_here = pl.ds(pl.multiple_of(step * block, block), block)

        @pl.when(step == 0)
        def _():
            k_total[...] = jnp.zeros_like(k_total)
            v_total[...] = jnp.zeros_like(v_total)
            sum_ref[...] = jnp.zeros_like(sum_ref)

        def turn_back(u, rows):
            return turn(u, keep_ref[rows, :], -ahead_ref[rows, :], -behind_ref[rows, :])

        for index in range(count):

            @pl.when(step == index)
            def _(index=index):
                queries, grads = q_ref[...], do_ref[...]
                blank = jnp.zeros_like(queries)
                products = (grads.astype(F32) * o_ref[...].astype(F32)).T
                q_total = [None, None]
                for other in range(index + 1):
                    rows = slice(other * block, (other + 1) * block)
                    keys, values = k_ref[rows, :], v_ref[rows, :]
                    dk, dv = k_total[rows, :], v_total[rows, :]
                    for head in range(2):
                        mine = (lane < HD) if head == 0 else (lane >= HD)
                        q_head = jnp.where(mine, queries, blank)
                        do_head = jnp.where(mine, grads, blank)
                        delta = jnp.sum(
                            products[head * HD : (head + 1) * HD], axis=0, keepdims=True
                        )
                        scores = dot(keys, q_head, NT)
                        if other == index:
                            row = lax.broadcasted_iota(jnp.int32, (block, block), 0)
                            col = lax.broadcasted_iota(jnp.int32, (block, block), 1)
                            scores = jnp.where(row <= col, scores, NEG)
                        probs = jnp.exp2(scores * scale - lse_ref[0, head : head + 1, :])
                        probs_grad = dot(values, do_head, NT)
                        score_grad = (probs * (probs_grad - delta)).astype(BF)
                        dv = dv + dot(probs.astype(BF), do_head, NN)
                        dk = dk + dot(score_grad, q_head, NN)
                        term = dot(score_grad, keys, TN)
                        q_total[head] = term if other == 0 else q_total[head] + term
                    k_total[rows, :] = dk
                    v_total[rows, :] = dv
                dq = jnp.where(lane < HD, q_total[0], q_total[1]) * shrink
                rows = slice(index * block, (index + 1) * block)
                dq = turn_back(dq, rows).astype(BF)
                dq_ref[...] = dq
                sum_ref[0, 0:1, :] += jnp.sum(dq.astype(F32), axis=0, keepdims=True)

        @pl.when(step == count - 1)
        def _():
            for index in range(count):
                rows = slice(index * block, (index + 1) * block)
                dk = turn_back(k_total[rows, :] * shrink, rows).astype(BF)
                dk_ref[rows, :] = dk
                sum_ref[0, 1:2, :] += jnp.sum(dk.astype(F32), axis=0, keepdims=True)
                dv = v_total[rows, :].astype(BF)
                dv_ref[rows, :] = dv
                sum_ref[0, 2:3, :] += jnp.sum(dv.astype(F32), axis=0, keepdims=True)

    def column(offset):
        return pl.BlockSpec((length, 128), lambda h, i: (0, offset + h))

    def rows_of(offset):
        return pl.BlockSpec((block, 128), lambda h, i: (i, offset + h))

    table = pl.BlockSpec((length, 128), lambda h, i: (0, 0))
    return call(
        kernel,
        "attend_back",
        10 * length * length * inner,
        16 * length * inner,
        grid=(pairs, count),
        in_specs=[
            rows_of(0),
            column(pairs),
            column(2 * pairs),
            rows_of(0),
            rows_of(0),
            pl.BlockSpec((1, 2, block), lambda h, i: (h, 0, i)),
            table,
            table,
            table,
        ],
        out_specs=[
            rows_of(0),
            column(0),
            column(0),
            pl.BlockSpec((1, 8, 128), lambda h, i: (h, 0, 0)),
        ],
        out_shape=[struct((length, inner))] * 3 + [struct((pairs, 8, 128), F32)],
        scratch_shapes=[pltpu.VMEM((length, 128), F32)] * 2,
    )(qkv, qkv, qkv, context, context_grad, log_total, *tables)


def expand(normed, w_own, w_sib, bias):
    length, width = normed.shape
    half, units = w_own.shape
    rows, cols = min(512, length), min(1024, units)

    def kernel(a_ref, wo_ref, ws_ref, b_ref, act_ref, slope_ref):
        hidden = (
            dot(a_ref[:, :half], wo_ref[...], NN)
            + dot(a_ref[:, half:], ws_ref[...], NN)
            + b_ref[...]
        )
        c = math.sqrt(2.0 / math.pi)
        square = hidden * hidden
        inner = hidden * (c + (c * 0.044715) * square)
        gate = 0.5 + 0.5 * jnp.tanh(inner)
        act = hidden * gate
        act_ref[...] = act.astype(BF)
        slope_ref[...] = (
            gate + act * (1.0 - gate) * (2.0 * c + (6.0 * c * 0.044715) * square)
        ).astype(BF)

    out = pl.BlockSpec((rows, cols), lambda n, m: (m, n))
    weight = pl.BlockSpec((half, cols), lambda n, m: (0, n))
    return call(
        kernel,
        "expand",
        2 * length * width * units,
        2 * length * width + 2 * width * units + 4 * length * units,
        grid=(units // cols, length // rows),
        in_specs=[
            pl.BlockSpec((rows, width), lambda n, m: (m, 0)),
            weight,
            weight,
            pl.BlockSpec((1, cols), lambda n, m: (0, n)),
        ],
        out_specs=[out, out],
        out_shape=[struct((length, units))] * 2,
    )(normed, w_own, w_sib, bias)


def hidden_back(g_all, w_own, w_sib, slope):
    length, width = g_all.shape
    half, units = w_own.shape
    rows, cols = min(512, length), min(1024, units)

    def kernel(g_ref, wo_ref, ws_ref, slope_ref, out_ref, sum_ref):
        grad = dot(g_ref[:, :half], wo_ref[...], NN) + dot(g_ref[:, half:], ws_ref[...], NN)
        low = (grad * slope_ref[...].astype(F32)).astype(BF)
        out_ref[...] = low

        @pl.when(pl.program_id(1) == 0)
        def _():
            sum_ref[...] = jnp.zeros_like(sum_ref)

        sum_ref[0:1, :] += jnp.sum(low.astype(F32), axis=0, keepdims=True)

    out = pl.BlockSpec((rows, cols), lambda n, m: (m, n))
    weight = pl.BlockSpec((half, cols), lambda n, m: (0, n))
    return call(
        kernel,
        "hidden_back",
        2 * length * width * units,
        2 * length * width + 2 * width * units + 4 * length * units,
        grid=(units // cols, length // rows),
        in_specs=[pl.BlockSpec((rows, width), lambda n, m: (m, 0)), weight, weight, out],
        out_specs=[out, pl.BlockSpec((8, cols), lambda n, m: (0, n))],
        out_shape=[struct((length, units)), struct((8, units), F32)],
    )(g_all, w_own, w_sib, slope)


def context_back(g_all, w_own, w_sib):
    length, width = g_all.shape
    half, cols = w_own.shape
    inner = cols // 4
    rows = min(512, length)

    def kernel(g_ref, wo_ref, ws_ref, out_ref):
        out_ref[...] = (
            dot(g_ref[:, :half], wo_ref[...], NN) + dot(g_ref[:, half:], ws_ref[...], NN)
        ).astype(BF)

    weight = pl.BlockSpec((half, inner), lambda m: (0, 3))
    return call(
        kernel,
        "context_back",
        2 * length * width * inner,
        2 * length * width + 2 * width * inner + 2 * length * inner,
        grid=(length // rows,),
        in_specs=[pl.BlockSpec((rows, width), lambda m: (m, 0)), weight, weight],
        out_specs=pl.BlockSpec((rows, inner), lambda m: (m, 0)),
        out_shape=struct((length, inner)),
    )(g_all, w_own, w_sib)


def weight_grad(rows_in, side, right, name):
    length, width = rows_in.shape
    half = width // 2
    units = right.shape[1]
    rows, cols = min(1024, half), min(1024, units)
    per_side = half // rows

    def kernel(a_ref, b_ref, out_ref):
        out_ref[...] = dot(a_ref[...], b_ref[...], TN).astype(BF)

    return call(
        kernel,
        name,
        2 * length * half * units,
        2 * length * half + 2 * length * units + 2 * half * units,
        grid=(units // cols, per_side),
        in_specs=[
            pl.BlockSpec((length, rows), lambda n, m: (0, side * per_side + m)),
            pl.BlockSpec((length, cols), lambda n, m: (0, n)),
        ],
        out_specs=pl.BlockSpec((rows, cols), lambda n, m: (m, n)),
        out_shape=struct((half, units)),
    )(rows_in, right)


def weight_grad_heads(normed, g_all, side, dq, dk, dv, context):
    length, width = normed.shape
    half = width // 2
    inner = dq.shape[1]

    def kernel(a_ref, g_ref, q_ref, k_ref, v_ref, c_ref, out_ref):
        for part, right in enumerate((q_ref, k_ref, v_ref, c_ref)):

            @pl.when(pl.program_id(0) == part)
            def _(part=part, right=right):
                left = a_ref if part < 3 else g_ref
                out_ref[...] = dot(left[...], right[...], TN).astype(BF)

    left = pl.BlockSpec((length, half), lambda n: (0, side))
    right = pl.BlockSpec((length, inner), lambda n: (0, 0))
    return call(
        kernel,
        "weight_grad_heads",
        8 * length * half * inner,
        4 * length * half + 8 * length * inner + 8 * half * inner,
        grid=(4,),
        in_specs=[left, left, right, right, right, right],
        out_specs=pl.BlockSpec((half, inner), lambda n: (0, n)),
        out_shape=struct((half, 4 * inner)),
    )(normed, g_all, dq, dk, dv, context)


def branch_half(act, context, w_fc2, w_heads):
    length, units = act.shape
    half = w_fc2.shape[0]
    inner = context.shape[1]
    rows = min(512, length)

    def kernel(a_ref, c_ref, w_ref, o_ref, out_ref):
        out_ref[...] = (dot(a_ref[...], w_ref[...], NT) + dot(c_ref[...], o_ref[...], NT)).astype(BF)

    return call(
        kernel,
        "branch_half",
        2 * length * half * (units + inner),
        2 * length * (units + inner) + 2 * half * (units + inner) + 2 * length * half,
        grid=(length // rows,),
        in_specs=[
            pl.BlockSpec((rows, units), lambda m: (m, 0)),
            pl.BlockSpec((rows, inner), lambda m: (m, 0)),
            pl.BlockSpec((half, units), lambda m: (0, 0)),
            pl.BlockSpec((half, inner), lambda m: (0, 3)),
        ],
        out_specs=pl.BlockSpec((rows, half), lambda m: (m, 0)),
        out_shape=struct((length, half)),
    )(act, context, w_fc2, w_heads)


def normed_back_half(dq, dk, dv, hidden_grad, unit, side, w_heads, w_fc1):
    length, inner = dq.shape
    half, units = w_fc1.shape
    rows = min(512, length)

    def kernel(q_ref, k_ref, v_ref, h_ref, u_ref, w_ref, f_ref, out_ref, sum_ref):
        total = dot(h_ref[...], f_ref[...], NT)
        for part, ref in enumerate((q_ref, k_ref, v_ref)):
            total = total + dot(ref[...], w_ref[:, part * inner : (part + 1) * inner], NT)
        low = total.astype(BF)
        out_ref[...] = low

        @pl.when(pl.program_id(0) == 0)
        def _():
            sum_ref[...] = jnp.zeros_like(sum_ref)

        wide = low.astype(F32)
        sum_ref[0:1, :] += jnp.sum(wide * u_ref[...].astype(F32), axis=0, keepdims=True)
        sum_ref[1:2, :] += jnp.sum(wide, axis=0, keepdims=True)

    head = pl.BlockSpec((rows, inner), lambda m: (m, 0))
    return call(
        kernel,
        "normed_back_half",
        2 * length * half * (units + 3 * inner),
        2 * length * (units + 3 * inner) + 2 * half * (units + 3 * inner) + 4 * length * half,
        grid=(length // rows,),
        in_specs=[
            head,
            head,
            head,
            pl.BlockSpec((rows, units), lambda m: (m, 0)),
            pl.BlockSpec((rows, half), lambda m: (m, side)),
            pl.BlockSpec((half, 3 * inner), lambda m: (0, 0)),
            pl.BlockSpec((half, units), lambda m: (0, 0)),
        ],
        out_specs=[
            pl.BlockSpec((rows, half), lambda m: (m, 0)),
            pl.BlockSpec((8, half), lambda m: (0, 0)),
        ],
        out_shape=[struct((length, half)), struct((8, half), F32)],
    )(dq, dk, dv, hidden_grad, unit, w_heads, w_fc1)


def add_branch(blocks, x, own, sib, out_bias):
    rows, width = x.shape
    count = blocks.shape[0]
    cols = width // count
    per_half = count // 2

    def kernel(blk, x_ref, own_ref, sib_ref, bias_ref, out_ref):
        step = pl.program_id(0)
        base = x_ref[...].astype(F32)

        @pl.when(step < per_half)
        def _():
            out_ref[...] = (base + own_ref[...].astype(F32) + bias_ref[...]).astype(BF)

        @pl.when(step >= per_half)
        def _():
            out_ref[...] = (base + sib_ref[...].astype(F32) + bias_ref[...]).astype(BF)

    return call(
        kernel,
        "add_branch",
        0,
        6 * rows * width,
        grid_spec=pltpu.PrefetchScalarGridSpec(
            num_scalar_prefetch=1,
            grid=(count,),
            in_specs=[
                pl.BlockSpec((rows, cols), lambda p, blk: (0, p)),
                pl.BlockSpec((rows, cols), lambda p, blk: (0, jnp.minimum(p, per_half - 1))),
                pl.BlockSpec((rows, cols), lambda p, blk: (0, jnp.maximum(p - per_half, 0))),
                pl.BlockSpec((1, cols), lambda p, blk: (0, p)),
            ],
            out_specs=pl.BlockSpec((rows, cols), lambda p, blk: (0, blk[p])),
        ),
        out_shape=struct((rows, width)),
    )(blocks, x, own, sib, out_bias)


def norm_back(blocks, x, g, own, sib, gain):
    length, width = x.shape
    half = width // 2
    count = blocks.shape[0]
    cols = width // count
    rows = min(128, length)

    def kernel(blk, x_ref, g_ref, own_ref, sib_ref, gain_ref, out_ref):
        x = x_ref[...].astype(F32)
        centered = x - jnp.mean(x, axis=1, keepdims=True)
        variance = jnp.mean(centered * centered, axis=1, keepdims=True)
        inv_std = lax.rsqrt(variance + EPSILON)
        unit = centered * inv_std
        grads = jnp.concatenate([own_ref[...].astype(F32), sib_ref[...].astype(F32)], axis=1)
        scaled = grads * gain_ref[...]
        mean = jnp.mean(scaled, axis=1, keepdims=True)
        along = jnp.mean(scaled * unit, axis=1, keepdims=True)
        result = g_ref[...].astype(F32) + inv_std * (scaled - mean - unit * along)
        for p in range(count):
            place = pl.ds(pl.multiple_of(blk[p] * cols, cols), cols)
            out_ref[:, place] = result[:, p * cols : (p + 1) * cols]

    full = pl.BlockSpec((rows, width), lambda m, blk: (m, 0))
    part = pl.BlockSpec((rows, half), lambda m, blk: (m, 0))
    return call(
        kernel,
        "norm_back",
        0,
        10 * length * width,
        grid_spec=pltpu.PrefetchScalarGridSpec(
            num_scalar_prefetch=1,
            grid=(length // rows,),
            in_specs=[full, full, part, part, pl.BlockSpec((1, width), lambda m, blk: (0, 0))],
            out_specs=full,
        ),
        out_shape=struct((length, width), F32),
    )(blocks, x, g, own, sib, gain)


def flip_sum(value, axis, size, first=1):
    bit = first
    while bit < size:
        value = value + lax.ppermute(value, axis, [(i, i ^ bit) for i in range(size)])
        bit *= 2
    return value


def per_device(
    sizes, layer_input, ln_gain, ln_bias, out_bias, w_qkv, b_qkv, w_out, w_fc1, b_fc1, w_fc2, out_grad
):
    n_dp, n_tensor = sizes
    chips = n_dp // 2
    ring = [(z * 2 + c, ((z + 1) % chips) * 2 + c) for z in range(chips) for c in range(2)]
    swap = [(i, i ^ 1) for i in range(n_dp)]
    d_index, t_index = lax.axis_index("dp"), lax.axis_index("tensor")
    place, core = d_index // 2, d_index % 2
    steps = jnp.arange(chips, dtype=jnp.int32)
    behind = ((place - steps) % chips) * 2
    blocks = jnp.concatenate([behind + core, behind + (1 - core)]).astype(jnp.int32)

    local, width = layer_input.shape[1:]
    depth = w_qkv.shape[0]
    inner = w_qkv.shape[2]
    units = w_fc1.shape[1]
    heads = inner // HD
    length = local * n_tensor

    group_heads = jnp.concatenate([w_qkv.reshape(depth, 3 * inner), w_out.T], axis=1)
    groups = [group_heads, w_fc1, w_fc2.T]

    def gather(piece):
        pieces = [piece]
        for _ in range(chips - 1):
            pieces.append(lax.ppermute(pieces[-1], "dp", ring))
        own = jnp.concatenate(pieces, axis=0)
        return own, lax.ppermute(own, "dp", swap)

    third = ln_gain.shape[0]
    vectors = jnp.stack([ln_gain, ln_bias, out_bias]).astype(F32).reshape(1, 3 * third)
    table = jnp.where(jnp.arange(n_tensor)[:, None] == t_index, vectors, 0.0)
    table = flip_sum(table, "tensor", n_tensor)
    packed = jnp.concatenate(
        [table.reshape(-1), b_qkv.astype(F32).reshape(-1), b_fc1.astype(F32).reshape(-1)]
    )[None, :]
    packed = jnp.where(jnp.arange(n_dp)[:, None] == d_index, packed, 0.0)
    packed = flip_sum(packed, "dp", n_dp)
    cut = n_tensor * 3 * third
    vectors = packed[:, :cut].reshape(n_dp, n_tensor, 3, third)
    vectors = jnp.transpose(vectors, (2, 0, 1, 3)).reshape(3, n_dp, n_tensor * third)
    chosen = (blocks[:, None] == jnp.arange(n_dp)[None, :]).astype(F32)
    vectors = jnp.einsum("pd,kdj->kpj", chosen, vectors, precision=lax.Precision.HIGHEST)
    gain, shift, bias_out = (vectors[i].reshape(1, width) for i in range(3))
    tail = cut + b_qkv.size
    bias_qkv = jnp.transpose(packed[:, cut:tail].reshape(n_dp, 3, heads, -1), (1, 2, 0, 3))
    bias_qkv = bias_qkv.reshape(1, 3 * inner)
    bias_fc1 = jnp.transpose(packed[:, tail:].reshape(n_dp, units // HD, -1), (1, 0, 2))
    bias_fc1 = bias_fc1.reshape(1, units)

    x, g, bias_part = order_columns(blocks, layer_input[0], out_grad[0])
    rows = min(256, local)
    x_all = lax.all_gather(x, "tensor", axis=0, tiled=True)
    pieces, out_blocks = [x_all], jnp.arange(length // rows, dtype=jnp.int32)
    g_all = lax.all_gather(g, "tensor", axis=0, tiled=True)

    heads_own, heads_sib = gather(groups[0])
    tables = rotary_rows(length)
    normed, unit, qkv = norm_project(
        out_blocks, pieces, rows, gain, shift, bias_qkv, tables, heads_own, heads_sib
    )
    context, log_total = attend(qkv)

    fc1_own, fc1_sib = gather(groups[1])
    act, slope = expand(normed, fc1_own, fc1_sib, bias_fc1)

    def scatter(sib_part, own_part):
        other = lax.ppermute(sib_part, "dp", swap)

        def step(k):
            cut = slice(k * depth, (k + 1) * depth)
            return own_part[cut].astype(F32) + other[cut].astype(F32)

        moving = None
        for k in list(range(1, chips)) + [0]:
            total = step(k) if moving is None else step(k) + moving.astype(F32)
            if k:
                moving = lax.ppermute(total.astype(BF), "dp", ring)
        return total.astype(BF).astype(F32) if chips == 1 else total

    fc2_sib_grad = weight_grad(g_all, 1, act, "fc2_grad")
    fc2_own_grad = weight_grad(g_all, 0, act, "fc2_grad")
    w_fc2_grad = scatter(fc2_sib_grad, fc2_own_grad).T

    context_grad = context_back(g_all, heads_own, heads_sib)
    fc2_own, fc2_sib = gather(groups[2])
    hidden_grad, b_fc1_part = hidden_back(g_all, fc2_own, fc2_sib, slope)
    fc1_sib_grad = weight_grad(normed, 1, hidden_grad, "fc1_grad")
    fc1_own_grad = weight_grad(normed, 0, hidden_grad, "fc1_grad")
    w_fc1_grad = scatter(fc1_sib_grad, fc1_own_grad)

    branch = [
        lax.psum_scatter(
            branch_half(act, context, w2, wh), "tensor", scatter_dimension=0, tiled=True
        )
        for w2, wh in ((fc2_own, heads_own), (fc2_sib, heads_sib))
    ]
    layer_output = add_branch(blocks, x, branch[0], branch[1], bias_out)

    dq, dk, dv, b_qkv_part = attend_back(qkv, context, context_grad, log_total, tables)
    back = [
        normed_back_half(dq, dk, dv, hidden_grad, unit, side, wh, w1)
        for side, wh, w1 in ((0, heads_own, fc1_own), (1, heads_sib, fc1_sib))
    ]
    normed_sum = [
        lax.psum_scatter(part, "tensor", scatter_dimension=0, tiled=True) for part, _ in back
    ]
    heads_sib_grad = weight_grad_heads(normed, g_all, 1, dq, dk, dv, context)
    heads_own_grad = weight_grad_heads(normed, g_all, 0, dq, dk, dv, context)
    heads_grad = scatter(heads_sib_grad, heads_own_grad)
    w_qkv_grad = heads_grad[:, : 3 * inner].reshape(depth, 3, inner)
    w_out_grad = heads_grad[:, 3 * inner :].T

    input_grad = norm_back(blocks, x, g, normed_sum[0], normed_sum[1], gain)

    norm_sums = jnp.concatenate([back[0][1][:2], back[1][1][:2]], axis=1).reshape(2, n_dp, depth)
    norm_sums = jnp.einsum("pd,kpj->kdj", chosen, norm_sums, precision=lax.Precision.HIGHEST)
    vector_sums = jnp.concatenate([norm_sums.reshape(2, width), bias_part[:1]], axis=0)
    vector_sums = flip_sum(vector_sums, "tensor", n_tensor)
    unit_sums = jnp.concatenate(
        [
            vector_sums.reshape(-1),
            jnp.transpose(b_qkv_part[:, :3, :], (1, 0, 2)).reshape(-1),
            b_fc1_part[0],
        ]
    )
    unit_sums = flip_sum(unit_sums, "dp", n_dp)
    mine = unit_sums[: 3 * width].reshape(3, n_dp * n_tensor, third)
    mine = lax.dynamic_index_in_dim(mine, d_index * n_tensor + t_index, 1, keepdims=False)
    b_width = HD // n_dp
    b_qkv_grad = lax.dynamic_slice_in_dim(
        unit_sums[3 * width : 3 * width + 3 * inner].reshape(3, heads, HD), d_index * b_width, b_width, 2
    )
    b_fc1_grad = lax.dynamic_slice_in_dim(
        unit_sums[3 * width + 3 * inner :].reshape(units // HD, HD), d_index * b_width, b_width, 1
    )
    return (
        layer_output[None],
        input_grad[None],
        mine[0],
        mine[1],
        mine[2],
        w_qkv_grad,
        b_qkv_grad,
        w_out_grad,
        w_fc1_grad,
        b_fc1_grad,
        w_fc2_grad,
    )


def solution(mesh):
    in_specs = (
        P("dp", "tensor", None),
        P(("dp", "tensor")),
        P(("dp", "tensor")),
        P(("dp", "tensor")),
        P("dp", None, "tensor"),
        P(None, "tensor", "dp"),
        P("tensor", "dp"),
        P("dp", "tensor"),
        P("tensor", "dp"),
        P("tensor", "dp"),
        P("dp", "tensor", None),
    )
    out_specs = (
        P("dp", "tensor", None),
        P("dp", "tensor", None),
        P(("dp", "tensor")),
        P(("dp", "tensor")),
        P(("dp", "tensor")),
        P("dp", None, "tensor"),
        P(None, "tensor", "dp"),
        P("tensor", "dp"),
        P("dp", "tensor"),
        P("tensor", "dp"),
        P("tensor", "dp"),
    )
    sizes = (mesh.shape["dp"], mesh.shape["tensor"])
    return jax.shard_map(
        functools.partial(per_device, sizes),
        mesh=mesh,
        in_specs=in_specs,
        out_specs=out_specs,
        check_vma=False,
    )
```

time: 1680 us -> 878 us (0.52)
  matrix products: 689 us -> 0.32 us
  Pallas kernels: 0 us -> 403 us
  local copies, waits for them, and re-layouts: 327 us -> 40.6 us
  blocking collectives: 152 us -> 0 us
  loops' own time: 129 us -> 0 us
  waiting for transfers between devices: 241 us -> 349 us
  other arithmetic: 114 us -> 41.6 us
  starting transfers between devices: 0.48 us -> 18.3 us
    dot_general x236 -> x2, matrix products: 689 us -> 0.32 us  [the longest x1 0.2 us: per_device(): jnp.einsum('pd,kdj->kpj', chosen, vectors, precision=lax.Precision.HIGHEST)]
    pallas_call x0 -> x19, Pallas kernels: none -> 403 us  [the longest x1 77.7 us: attend_back(): call(kernel, 'attend_back', 10 * length * length * inner, 16 * length * i...]
    ppermute x0 -> x34, waiting for transfers between devices: none -> 348 us  [the longest x9 171 us: scatter(): moving = lax.ppermute(total.astype(BF), 'dp', ring)]
    reduce_scatter x6 -> x4, waiting for transfers between devices: 175 us -> 0.01 us  [the longest x2 0.01 us: per_device(): lax.psum_scatter(part, 'tensor', scatter_dimension=0, tiled=True)]
    while x219 -> x0, local copies, waits for them, and re-layouts: 156 us -> none
    another operation x18 -> x0, loops' own time: 129 us -> none  [the longest x8 64.3 us: attend_back(): lax.scan(one_block, (zero_grad, zero_grad), offsets)]
    unnamed x3 -> x0, blocking collectives: 121 us -> none
    squeeze x49 -> x1, local copies, waits for them, and re-layouts: 73.8 us -> 0.53 us  [per_device(): mine[2]]
  transfers between devices with their start and end apart: 12 -> 40, of which waited for: 4 -> 20; matrix products, arithmetic and copies ran while one was open for 59% -> 9% of each run, Pallas kernels for 0% -> 39%
where the time goes in v1:
time: 878 us; the launch traced here: 868 us
  Pallas kernels  403 us (46%)
  waiting for transfers between devices  349 us (40%)
  other arithmetic  41.6 us (5%)
  local copies, waits for them, and re-layouts  40.6 us (5%)
  starting transfers between devices  18.3 us (2%)
  between operations  15.2 us (2%)
    ppermute x9, waiting for transfers between devices, scatter(): moving = lax.ppermute(total.astype(BF), 'dp', ring)  171 us
    ppermute x9, waiting for transfers between devices, gather(): pieces.append(lax.ppermute(pieces[-1], 'dp', ring))  170 us
    pallas_call x1, Pallas kernels, attend_back(): call(kernel, 'attend_back', 10 * length * length * inner, 16 * length * i...  77.7 us
    pallas_call x4, Pallas kernels, weight_grad(): call(kernel, name, 2 * length * half * units, 2 * length * half + 2 * len...  56 us
    pallas_call x2, Pallas kernels, normed_back_half(): call(kernel, 'normed_back_half', 2 * length * half * (units + 3 * inner),...  49.1 us
    pallas_call x1, Pallas kernels, attend(): call(kernel, 'attend', 4 * length * length * inner, 8 * length * inner, g...  42.5 us
    pallas_call x2, Pallas kernels, weight_grad_heads(): call(kernel, 'weight_grad_heads', 8 * length * half * inner, 4 * length *...  34.3 us
    pallas_call x2, Pallas kernels, branch_half(): call(kernel, 'branch_half', 2 * length * half * (units + inner), 2 * leng...  32.5 us
  transfers between devices with their start and end apart: 40, of which 20 were waited for; matrix products, arithmetic and copies ran while one was open for 9% of the time, Pallas kernels for 39%

profile of v1, /device:TPU:0, one launch (start us, length us, event | category | flops | bytes accessed | tf_op | source)
XLA Modules:
  0.0 868.5 jit_solution(3304529669839967)
XLA Ops:
  7.9 7.5 order_columns.1
  17.1 3.1 collective-permute-start.5
  20.2 25.2 %collective-permute-done.5 = bf16[256,2048]{1,0:T(8,128)(2,1)S(1)} collective-permute-done((bf16[256,2048]{1,0:T(8,128)(2,1)S(1)}, bf16[256,2048]{1,0:T(8,128)(2,1)S(1)}, u32[]{:S(2)}, u32[]{:S(2)}) %collective-permute-start.5) | collective-permute-done | bytes 1048608 | tf_op jit(solution)/shard_map/ppermute | solution.py:657
  47.6 26.7 %collective-permute-done.6 = bf16[256,2048]{1,0:T(8,128)(2,1)} collective-permute-done((bf16[256,2048]{1,0:T(8,128)(2,1)S(1)}, bf16[256,2048]{1,0:T(8,128)(2,1)}, u32[]{:S(2)}, u32[]{:S(2)}) %collective-permute-start.6) | collective-permute-done | bytes 1048608 | tf_op jit(solution)/shard_map/ppermute | solution.py:657
  76.8 20.0 %collective-permute-done.9 = bf16[256,2048]{1,0:T(8,128)(2,1)} collective-permute-done((bf16[256,2048]{1,0:T(8,128)(2,1)}, bf16[256,2048]{1,0:T(8,128)(2,1)}, u32[]{:S(2)}, u32[]{:S(2)}) %collective-permute-start.9) | collective-permute-done | bytes 1048608 | tf_op jit(solution)/shard_map/ppermute | solution.py:657
  96.8 22.5 %collective-permute-done.7 = bf16[256,2048]{1,0:T(8,128)(2,1)} collective-permute-done((bf16[256,2048]{1,0:T(8,128)(2,1)}, bf16[256,2048]{1,0:T(8,128)(2,1)}, u32[]{:S(2)}, u32[]{:S(2)}) %collective-permute-start.7) | collective-permute-done | bytes 1048608 | tf_op jit(solution)/shard_map/ppermute | solution.py:657
  119.3 5.9 pad_maximum_fusion.refs_7_.o_ref.wo_ref.w_ref
  128.2 1.8 collective-permute-done.1
  130.2 11.5 %collective-permute-done.13 = bf16[256,2048]{1,0:T(8,128)(2,1)} collective-permute-done((bf16[256,2048]{1,0:T(8,128)(2,1)S(1)}, bf16[256,2048]{1,0:T(8,128)(2,1)}, u32[]{:S(2)}, u32[]{:S(2)}) %collective-permute-start.13) | collective-permute-done | bytes 1048608 | tf_op jit(solution)/shard_map/ppermute | solution.py:657
  141.8 22.3 %collective-permute-done.10 = bf16[256,2048]{1,0:T(8,128)(2,1)S(1)} collective-permute-done((bf16[256,2048]{1,0:T(8,128)(2,1)}, bf16[256,2048]{1,0:T(8,128)(2,1)S(1)}, u32[]{:S(2)}, u32[]{:S(2)}) %collective-permute-start.10) | collective-permute-done | bytes 1048608 | tf_op jit(solution)/shard_map/ppermute | solution.py:657
  164.3 2.3 constant_dynamic-update-slice_fusion.2
  166.6 20.2 %collective-permute-done.14 = bf16[256,2048]{1,0:T(8,128)(2,1)} collective-permute-done((bf16[256,2048]{1,0:T(8,128)(2,1)}, bf16[256,2048]{1,0:T(8,128)(2,1)}, u32[]{:S(2)}, u32[]{:S(2)}) %collective-permute-start.14) | collective-permute-done | bytes 1048608 | tf_op jit(solution)/shard_map/ppermute | solution.py:657
  187.8 21.3 %collective-permute-done.11 = bf16[256,2048]{1,0:T(8,128)(2,1)S(1)} collective-permute-done((bf16[256,2048]{1,0:T(8,128)(2,1)S(1)}, bf16[256,2048]{1,0:T(8,128)(2,1)S(1)}, u32[]{:S(2)}, u32[]{:S(2)}) %collective-permute-start.11) | collective-permute-done | bytes 1048608 | tf_op jit(solution)/shard_map/ppermute | solution.py:657
  210.6 4.8 fusion
  215.5 4.6 concatenate.46.refs_6_.behind_ref
  220.1 4.6 concatenate.45.refs_5_.ahead_ref
  224.7 3.0 concatenate.44.refs_4_.keep_ref
  227.7 4.7 collective-permute-done.4
  235.9 3.6 pad_maximum_fusion.1.w_ref.wo_ref
  240.1 25.2 %norm_project.1 = (bf16[2048,2048]{1,0:T(8,128)(2,1)}, bf16[2048,2048]{1,0:T(8,128)(2,1)}, bf16[2048,1536]{1,0:T(8,128)(2,1)}) custom-call(s32[8]{0:T(128)} %iota.44.blk, bf16[2048,2048]{1,0:T(8,128)(2,1)} %all-gather.3.cloned.1.call-done.refs_0_, f32[1,2048]{1,0:T(1,128)} %bitcast.74, f32[1,2048]{1,0:T(1,128)} %bitcast.77, f32[1,1536]{1,0:T(1,128)} %reshape.133.refs_3_, ...), custom_call_target="tpu_custom_call" | custom-call | flops 12884901888 | bytes 37748736 | tf_op jit(solution)/shard_map/norm_project/pallas_call | solution.py:142
  265.3 42.5 %attend.1 = (bf16[2048,512]{1,0:T(8,128)(2,1)}, f32[4,2,2048]{2,1,0:T(2,128)}) custom-call(bf16[2048,1536]{1,0:T(8,128)(2,1)} %get-tuple-element.34.q_ref.k_ref.v_ref, bf16[2048,1536]{1,0:T(8,128)(2,1)} %get-tuple-element.34.q_ref.k_ref.v_ref, bf16[2048,1536]{1,0:T(8,128)(2,1)} %get-tuple-element.34.q_ref.k_ref.v_ref), custom_call_target="tpu_custom_call" | custom-call | flops 8589934592 | bytes 8388608 | tf_op jit(solution)/shard_map/attend/pallas_call | solution.py:202
  307.8 8.7 context_back.1.do_ref
  316.5 30.3 %expand.1 = (bf16[2048,2048]{1,0:T(8,128)(2,1)}, bf16[2048,2048]{1,0:T(8,128)(2,1)}) custom-call(bf16[2048,2048]{1,0:T(8,128)(2,1)} %get-tuple-element.32.a_ref, bf16[1024,2048]{1,0:T(8,128)(2,1)} %constant_dynamic-update-slice_fusion.wo_ref.f_ref, bf16[1024,2048]{1,0:T(8,128)(2,1)} %collective-permute-done.12.ws_ref.f_ref, f32[1,2048]{1,0:T(1,128)} %reshape.136.b_ref), custom_call_target="tpu_custom_call" | custom-call | flops 17179869184 | bytes 33554432 | tf_op jit(solution)/shard_map/expand/pallas_call | solution.py:353
  346.8 77.7 %attend_back.1 = (bf16[2048,512]{1,0:T(8,128)(2,1)}, bf16[2048,512]{1,0:T(8,128)(2,1)}, bf16[2048,512]{1,0:T(8,128)(2,1)}, f32[4,8,128]{2,1,0:T(8,128)}) custom-call(bf16[2048,1536]{1,0:T(8,128)(2,1)} %get-tuple-element.34.q_ref.k_ref.v_ref, bf16[2048,1536]{1,0:T(8,128)(2,1)} %get-tuple-element.34.q_ref.k_ref.v_ref, ...), custom_call_target="tpu_custom_call" | custom-call | flops 21474836480 | bytes 16777216 | tf_op jit(solution)/shard_map/attend_back/pallas_call | solution.py:302
  424.5 25.0 %hidden_back.1 = (bf16[2048,2048]{1,0:T(8,128)(2,1)}, f32[8,2048]{1,0:T(8,128)}) custom-call(bf16[2048,2048]{1,0:T(8,128)(2,1)} %all-gather.5.cloned.1.call-done.g_ref.a_ref, bf16[1024,2048]{1,0:T(8,128)(2,1)} %pad_maximum_fusion.1.w_ref.wo_ref, bf16[1024,2048]{1,0:T(8,128)(2,1)} %collective-permute-done.16.w_ref.ws_ref, ...), custom_call_target="tpu_custom_call" | custom-call | flops 17179869184 | bytes 33554432 | tf_op jit(solution)/shard_map/hidden_back/pallas_call | solution.py:388
  449.6 24.3 %normed_back_half.3 = (bf16[2048,1024]{1,0:T(8,128)(2,1)}, f32[8,1024]{1,0:T(8,128)}) custom-call(bf16[2048,512]{1,0:T(8,128)(2,1)} %get-tuple-element.38.q_ref, bf16[2048,512]{1,0:T(8,128)(2,1)} %get-tuple-element.39.k_ref, bf16[2048,512]{1,0:T(8,128)(2,1)} %get-tuple-element.40.v_ref, bf16[2048,2048]{1,0:T(8,128)(2,1)} %get-tuple-element.42.h_ref.b_ref, ...), custom_call_target="tpu_custom_call" | custom-call | flops 15032385536 | bytes 30408704 | tf_op jit(solution)/shard_map/normed_back_half/pallas_call | solution.py:523
  473.9 24.8 %normed_back_half.2 = (bf16[2048,1024]{1,0:T(8,128)(2,1)}, f32[8,1024]{1,0:T(8,128)}) custom-call(bf16[2048,512]{1,0:T(8,128)(2,1)} %get-tuple-element.38.q_ref, bf16[2048,512]{1,0:T(8,128)(2,1)} %get-tuple-element.39.k_ref, bf16[2048,512]{1,0:T(8,128)(2,1)} %get-tuple-element.40.v_ref, bf16[2048,2048]{1,0:T(8,128)(2,1)} %get-tuple-element.42.h_ref.b_ref, ...), custom_call_target="tpu_custom_call" | custom-call | flops 15032385536 | bytes 30408704 | tf_op jit(solution)/shard_map/normed_back_half/pallas_call | solution.py:523
  498.8 16.0 %branch_half.2 = bf16[2048,1024]{1,0:T(8,128)(2,1)} custom-call(bf16[2048,2048]{1,0:T(8,128)(2,1)} %get-tuple-element.33.a_ref.b_ref, bf16[2048,512]{1,0:T(8,128)(2,1)} %get-tuple-element.35.c_ref.o_ref, bf16[1024,2048]{1,0:T(8,128)(2,1)} %pad_maximum_fusion.1.w_ref.wo_ref, bf16[1024,2048]{1,0:T(8,128)(2,1)} %pad_maximum_fusion.refs_7_.o_ref.wo_ref.w_ref), custom_call_target="tpu_custom_call" | custom-call | flops 10737418240 | bytes 19922944 | tf_op jit(solution)/shard_map/branch_half/pallas_call | solution.py:485
  516.4 17.0 %weight_grad_heads.3 = bf16[1024,2048]{1,0:T(8,128)(2,1)} custom-call(bf16[2048,2048]{1,0:T(8,128)(2,1)} %get-tuple-element.32.a_ref, bf16[2048,2048]{1,0:T(8,128)(2,1)} %all-gather.5.cloned.1.call-done.g_ref.a_ref, bf16[2048,512]{1,0:T(8,128)(2,1)} %get-tuple-element.38.q_ref, bf16[2048,512]{1,0:T(8,128)(2,1)} %get-tuple-element.39.k_ref, ...), custom_call_target="tpu_custom_call" | custom-call | flops 8589934592 | bytes 20971520 | tf_op jit(solution)/shard_map/weight_grad_heads/pallas_call | solution.py:464
  536.6 14.0 %fc2_grad.3 = bf16[1024,2048]{1,0:T(8,128)(2,1)} custom-call(bf16[2048,2048]{1,0:T(8,128)(2,1)} %all-gather.5.cloned.1.call-done.g_ref.a_ref, bf16[2048,2048]{1,0:T(8,128)(2,1)} %get-tuple-element.33.a_ref.b_ref), custom_call_target="tpu_custom_call" | custom-call | flops 8589934592 | bytes 16777216 | tf_op jit(solution)/shard_map/fc2_grad/pallas_call | solution.py:434
  550.5 14.2 %fc1_grad.3 = bf16[1024,2048]{1,0:T(8,128)(2,1)} custom-call(bf16[2048,2048]{1,0:T(8,128)(2,1)} %get-tuple-element.32.a_ref, bf16[2048,2048]{1,0:T(8,128)(2,1)} %get-tuple-element.42.h_ref.b_ref), custom_call_target="tpu_custom_call" | custom-call | flops 8589934592 | bytes 16777216 | tf_op jit(solution)/shard_map/fc1_grad/pallas_call | solution.py:434
  565.2 16.4 %branch_half.3 = bf16[2048,1024]{1,0:T(8,128)(2,1)} custom-call(bf16[2048,2048]{1,0:T(8,128)(2,1)} %get-tuple-element.33.a_ref.b_ref, bf16[2048,512]{1,0:T(8,128)(2,1)} %get-tuple-element.35.c_ref.o_ref, bf16[1024,2048]{1,0:T(8,128)(2,1)} %collective-permute-done.16.w_ref.ws_ref, bf16[1024,2048]{1,0:T(8,128)(2,1)} %collective-permute-done.8.refs_8_.o_ref.ws_ref.w_ref), custom_call_target="tpu_custom_call" | custom-call | flops 10737418240 | bytes 19922944 | tf_op jit(solution)/shard_map/branch_half/pallas_call | solution.py:485
  581.7 1.8 collective-permute-start.18
  585.8 13.9 %fc1_grad.2 = bf16[1024,2048]{1,0:T(8,128)(2,1)} custom-call(bf16[2048,2048]{1,0:T(8,128)(2,1)} %get-tuple-element.32.a_ref, bf16[2048,2048]{1,0:T(8,128)(2,1)} %get-tuple-element.42.h_ref.b_ref), custom_call_target="tpu_custom_call" | custom-call | flops 8589934592 | bytes 16777216 | tf_op jit(solution)/shard_map/fc1_grad/pallas_call | solution.py:434
  599.9 17.3 %weight_grad_heads.2 = bf16[1024,2048]{1,0:T(8,128)(2,1)} custom-call(bf16[2048,2048]{1,0:T(8,128)(2,1)} %get-tuple-element.32.a_ref, bf16[2048,2048]{1,0:T(8,128)(2,1)} %all-gather.5.cloned.1.call-done.g_ref.a_ref, bf16[2048,512]{1,0:T(8,128)(2,1)} %get-tuple-element.38.q_ref, bf16[2048,512]{1,0:T(8,128)(2,1)} %get-tuple-element.39.k_ref, ...), custom_call_target="tpu_custom_call" | custom-call | flops 8589934592 | bytes 20971520 | tf_op jit(solution)/shard_map/weight_grad_heads/pallas_call | solution.py:464
  617.2 13.9 %fc2_grad.2 = bf16[1024,2048]{1,0:T(8,128)(2,1)} custom-call(bf16[2048,2048]{1,0:T(8,128)(2,1)} %all-gather.5.cloned.1.call-done.g_ref.a_ref, bf16[2048,2048]{1,0:T(8,128)(2,1)} %get-tuple-element.33.a_ref.b_ref), custom_call_target="tpu_custom_call" | custom-call | flops 8589934592 | bytes 16777216 | tf_op jit(solution)/shard_map/fc2_grad/pallas_call | solution.py:434
  633.4 2.1 add_convert_fusion.8
  635.5 2.0 collective-permute-start.23
  637.5 1.9 add_convert_fusion.2
  641.0 1.6 add_convert_fusion.5
  642.6 2.0 collective-permute-start.27
  644.6 19.2 %collective-permute-done.23 = bf16[256,2048]{1,0:T(8,128)(2,1)S(1)} collective-permute-done((bf16[256,2048]{1,0:T(8,128)(2,1)S(1)}, bf16[256,2048]{1,0:T(8,128)(2,1)S(1)}, u32[]{:S(2)}, u32[]{:S(2)}) %collective-permute-start.23) | collective-permute-done | bytes 1048608 | tf_op jit(solution)/shard_map/ppermute | solution.py:709
  663.8 1.8 add_convert_fusion.7
  665.9 20.4 %collective-permute-done.31 = bf16[256,2048]{1,0:T(8,128)(2,1)S(1)} collective-permute-done((bf16[256,2048]{1,0:T(8,128)(2,1)S(1)}, bf16[256,2048]{1,0:T(8,128)(2,1)S(1)}, u32[]{:S(2)}, u32[]{:S(2)}) %collective-permute-start.31) | collective-permute-done | bytes 1048608 | tf_op jit(solution)/shard_map/ppermute | solution.py:709
  686.3 1.8 add_convert_fusion.1
  688.1 20.6 %collective-permute-done.27 = bf16[256,2048]{1,0:T(8,128)(2,1)S(1)} collective-permute-done((bf16[256,2048]{1,0:T(8,128)(2,1)S(1)}, bf16[256,2048]{1,0:T(8,128)(2,1)S(1)}, u32[]{:S(2)}, u32[]{:S(2)}) %collective-permute-start.27) | collective-permute-done | bytes 1048608 | tf_op jit(solution)/shard_map/ppermute | solution.py:709
  708.7 1.8 add_convert_fusion.4
  710.6 20.6 %collective-permute-done.24 = bf16[256,2048]{1,0:T(8,128)(2,1)S(1)} collective-permute-done((bf16[256,2048]{1,0:T(8,128)(2,1)S(1)}, bf16[256,2048]{1,0:T(8,128)(2,1)S(1)}, u32[]{:S(2)}, u32[]{:S(2)}) %collective-permute-start.24) | collective-permute-done | bytes 1048608 | tf_op jit(solution)/shard_map/ppermute | solution.py:709
  731.2 1.8 add_convert_fusion.6
  733.0 20.6 %collective-permute-done.32 = bf16[256,2048]{1,0:T(8,128)(2,1)S(1)} collective-permute-done((bf16[256,2048]{1,0:T(8,128)(2,1)S(1)}, bf16[256,2048]{1,0:T(8,128)(2,1)S(1)}, u32[]{:S(2)}, u32[]{:S(2)}) %collective-permute-start.32) | collective-permute-done | bytes 1048608 | tf_op jit(solution)/shard_map/ppermute | solution.py:709
  753.7 2.7 add_convert_fusion
  756.4 19.7 %collective-permute-done.28 = bf16[256,2048]{1,0:T(8,128)(2,1)S(1)} collective-permute-done((bf16[256,2048]{1,0:T(8,128)(2,1)S(1)}, bf16[256,2048]{1,0:T(8,128)(2,1)S(1)}, u32[]{:S(2)}, u32[]{:S(2)}) %collective-permute-start.28) | collective-permute-done | bytes 1048608 | tf_op jit(solution)/shard_map/ppermute | solution.py:709
  776.2 2.7 add_convert_fusion.3
  778.9 19.7 %collective-permute-done.25 = bf16[256,2048]{1,0:T(8,128)(2,1)S(1)} collective-permute-done((bf16[256,2048]{1,0:T(8,128)(2,1)S(1)}, bf16[256,2048]{1,0:T(8,128)(2,1)S(1)}, u32[]{:S(2)}, u32[]{:S(2)}) %collective-permute-start.25) | collective-permute-done | bytes 1048608 | tf_op jit(solution)/shard_map/ppermute | solution.py:709
  798.6 1.7 convert_add_fusion.1
  801.7 3.0 copy.39
  804.7 3.0 copy.40
  808.7 12.5 %collective-permute-done.33 = bf16[256,2048]{1,0:T(8,128)(2,1)} collective-permute-done((bf16[256,2048]{1,0:T(8,128)(2,1)}, bf16[256,2048]{1,0:T(8,128)(2,1)}, u32[]{:S(2)}, u32[]{:S(2)}) %collective-permute-start.33) | collective-permute-done | bytes 1048608 | tf_op jit(solution)/shard_map/ppermute | solution.py:709
  821.2 2.4 add_bitcast_fusion
  823.6 1.8 copy.43
  825.4 17.5 %collective-permute-done.29 = bf16[256,2048]{1,0:T(8,128)(2,1)} collective-permute-done((bf16[256,2048]{1,0:T(8,128)(2,1)}, bf16[256,2048]{1,0:T(8,128)(2,1)}, u32[]{:S(2)}, u32[]{:S(2)}) %collective-permute-start.29) | collective-permute-done | bytes 1048608 | tf_op jit(solution)/shard_map/ppermute | solution.py:709
  842.9 3.7 convert_add_fusion
  846.7 7.4 norm_back.1
  854.1 7.1 add_branch.1
  (176 shorter events, 31.4 us)
Async XLA Ops:
  7.2 232.4 %all-gather.3.cloned.1.call-start = ((), (), s32[]{:S(2)}) async-start(), calls=%async_computation.4 | async-start | bytes 10485760 | tf_op jit(solution)/shard_map/all_gather | solution.py:684
  7.9 8.4 copy-start.9
  7.9 8.5 copy-start.8
  15.4 58.9 %copy-start.14 = (bf16[64]{0:T(256)(128)(2,1)S(1)}, bf16[64]{0:T(256)(128)(2,1)}, u32[]{:S(2)}) copy-start(bf16[64]{0:T(256)(128)(2,1)} %param.14) | copy-start | bytes 388
  15.4 58.9 %copy-start.15 = (bf16[64]{0:T(256)(128)(2,1)S(1)}, bf16[64]{0:T(256)(128)(2,1)}, u32[]{:S(2)}) copy-start(bf16[64]{0:T(256)(128)(2,1)} %param.13) | copy-start | bytes 388
  15.4 58.9 %copy-start.16 = (bf16[64]{0:T(256)(128)(2,1)S(1)}, bf16[64]{0:T(256)(128)(2,1)}, u32[]{:S(2)}) copy-start(bf16[64]{0:T(256)(128)(2,1)} %param.12) | copy-start | bytes 388
  15.4 60.6 %copy-start.5 = (bf16[2048,256]{1,0:T(8,128)(2,1)S(1)}, bf16[2048,256]{1,0:T(8,128)(2,1)}, u32[]{:S(2)}) copy-start(bf16[2048,256]{1,0:T(8,128)(2,1)} %param.20) | copy-start | bytes 3145732
  15.4 292.3 %all-gather.5.cloned.1.call-start = ((), (), s32[]{:S(2)}) async-start(), calls=%async_computation.7 | async-start | bytes 10485760 | tf_op jit(solution)/shard_map/all_gather | solution.py:686
  16.2 830.5 %reduce-scatter.11.cloned.1.call-start = ((), (), s32[]{:S(2)}) async-start(), calls=%async_computation.9 | async-start | bytes 5242880 | tf_op jit(solution)/shard_map/reduce_scatter | solution.py:737
  17.1 28.3 %collective-permute-start.5 = (bf16[256,2048]{1,0:T(8,128)(2,1)S(1)}, bf16[256,2048]{1,0:T(8,128)(2,1)S(1)}, u32[]{:S(2)}, u32[]{:S(2)}) collective-permute-start(bf16[256,2048]{1,0:T(8,128)(2,1)S(1)} %pad_maximum_fusion.2), channel_id=1, source_target_pairs={{0,8},{4,12},{8,16},{12,20},{16,24},{20,28},{24,0},{28,4},{1,9},{5... | collective-permute-start | bytes 3145736 | tf_op jit(solution)/shard_map/ppermute | solution.py:657
  45.4 1.0 copy-start.7
  46.3 28.0 %collective-permute-start.6 = (bf16[256,2048]{1,0:T(8,128)(2,1)S(1)}, bf16[256,2048]{1,0:T(8,128)(2,1)}, u32[]{:S(2)}, u32[]{:S(2)}) collective-permute-start(bf16[256,2048]{1,0:T(8,128)(2,1)S(1)} %collective-permute-done.5), channel_id=1, source_target_pairs={{0,8},{4,12},{8,16},{12,20},{16,24},{20,28},{24,0},{28,4},{1,9},{5... | collective-permute-start | bytes 3145736 | tf_op jit(solution)/shard_map/ppermute | solution.py:657
  46.3 50.5 %collective-permute-start.9 = (bf16[256,2048]{1,0:T(8,128)(2,1)}, bf16[256,2048]{1,0:T(8,128)(2,1)}, u32[]{:S(2)}, u32[]{:S(2)}) collective-permute-start(bf16[256,2048]{1,0:T(8,128)(2,1)} %param.18), channel_id=1, source_target_pairs={{0,8},{4,12},{8,16},{12,20},{16,24},{20,28},{24,0},{28,4},{1,9},{5... | collective-permute-start | bytes 3145736 | tf_op jit(solution)/shard_map/ppermute | solution.py:657
  74.3 44.9 %collective-permute-start.7 = (bf16[256,2048]{1,0:T(8,128)(2,1)}, bf16[256,2048]{1,0:T(8,128)(2,1)}, u32[]{:S(2)}, u32[]{:S(2)}) collective-permute-start(bf16[256,2048]{1,0:T(8,128)(2,1)} %collective-permute-done.6), channel_id=1, source_target_pairs={{0,8},{4,12},{8,16},{12,20},{16,24},{20,28},{24,0},{28,4},{1,9},{5... | collective-permute-start | bytes 3145736 | tf_op jit(solution)/shard_map/ppermute | solution.py:657
  74.5 51.7 %collective-permute-start = (f32[4,192]{1,0:T(4,128)S(1)}, f32[4,192]{1,0:T(4,128)S(1)}, u32[]{:S(2)}, u32[]{:S(2)}) collective-permute-start(f32[4,192]{1,0:T(4,128)S(1)} %broadcast_select_fusion.1), channel_id=1, source_target_pairs={{0,1},{1,0},{2,3},{3,2},{4,5},{5,4},{6,7},{7,6},{8,9},{9,8},{10,11... | collective-permute-start | bytes 9224 | tf_op jit(solution)/shard_map/ppermute | solution.py:626
  76.7 48.5 %copy-start.3 = (bf16[2048,256]{0,1:T(8,128)(2,1)}, bf16[2048,256]{0,1:T(8,128)(2,1)S(1)}, u32[]{:S(2)}) copy-start(bf16[2048,256]{0,1:T(8,128)(2,1)S(1)} %copy.37) | copy-start | bytes 3145732
  76.7 48.5 %copy-start.6 = (bf16[256,2048]{1,0:T(8,128)(2,1)S(1)}, bf16[256,2048]{1,0:T(8,128)(2,1)}, u32[]{:S(2)}) copy-start(bf16[256,2048]{1,0:T(8,128)(2,1)} %param.18) | copy-start | bytes 3145732
  76.7 51.3 %copy-start.11 = (bf16[3,8,8]{2,1,0:T(8,128)(2,1)S(1)}, bf16[3,8,8]{2,1,0:T(8,128)(2,1)}, u32[]{:S(2)}) copy-start(bf16[3,8,8]{2,1,0:T(8,128)(2,1)} %param.16) | copy-start | bytes 1156
  76.7 51.3 %copy-start.13 = (bf16[32,8]{0,1:T(8,128)(2,1)S(1)}, bf16[32,8]{0,1:T(8,128)(2,1)}, u32[]{:S(2)}) copy-start(bf16[32,8]{0,1:T(8,128)(2,1)} %param.19) | copy-start | bytes 1540
  76.7 65.0 %collective-permute-start.13 = (bf16[256,2048]{1,0:T(8,128)(2,1)S(1)}, bf16[256,2048]{1,0:T(8,128)(2,1)}, u32[]{:S(2)}, u32[]{:S(2)}) collective-permute-start(bf16[256,2048]{1,0:T(8,128)(2,1)S(1)} %bitcast.58), channel_id=1, source_target_pairs={{0,8},{4,12},{8,16},{12,20},{16,24},{20,28},{24,0},{28,4},{1,9},{5... | collective-permute-start | bytes 3145736 | tf_op jit(solution)/shard_map/ppermute | solution.py:657
  96.8 67.4 %collective-permute-start.10 = (bf16[256,2048]{1,0:T(8,128)(2,1)}, bf16[256,2048]{1,0:T(8,128)(2,1)S(1)}, u32[]{:S(2)}, u32[]{:S(2)}) collective-permute-start(bf16[256,2048]{1,0:T(8,128)(2,1)} %collective-permute-done.9), channel_id=1, source_target_pairs={{0,8},{4,12},{8,16},{12,20},{16,24},{20,28},{24,0},{28,4},{1,9},{5... | collective-permute-start | bytes 3145736 | tf_op jit(solution)/shard_map/ppermute | solution.py:657
  125.2 114.4 %collective-permute-start.8 = (bf16[1024,2048]{1,0:T(8,128)(2,1)}, bf16[1024,2048]{1,0:T(8,128)(2,1)}, u32[]{:S(2)}, u32[]{:S(2)}) collective-permute-start(bf16[1024,2048]{1,0:T(8,128)(2,1)} %pad_maximum_fusion.refs_7_.o_ref.wo_ref.w_ref), channel_id=1, source_target_pairs={{0,4},{4,0},{8,12},{12,8},{16,20},{20,16},{24,28},{28,24},{1,5},{5... | collective-permute-start | bytes 12582920 | tf_op jit(solution)/shard_map/ppermute | solution.py:659
  126.3 3.7 collective-permute-start.1
  141.7 45.0 %collective-permute-start.14 = (bf16[256,2048]{1,0:T(8,128)(2,1)}, bf16[256,2048]{1,0:T(8,128)(2,1)}, u32[]{:S(2)}, u32[]{:S(2)}) collective-permute-start(bf16[256,2048]{1,0:T(8,128)(2,1)} %collective-permute-done.13), channel_id=1, source_target_pairs={{0,8},{4,12},{8,16},{12,20},{16,24},{20,28},{24,0},{28,4},{1,9},{5... | collective-permute-start | bytes 3145736 | tf_op jit(solution)/shard_map/ppermute | solution.py:657
  141.8 22.4 %collective-permute-start.2 = (f32[8,1216]{1,0:T(8,128)S(1)}, f32[8,1216]{1,0:T(8,128)S(1)}, u32[]{:S(2)}, u32[]{:S(2)}) collective-permute-start(f32[8,1216]{1,0:T(8,128)S(1)} %broadcast_select_fusion), channel_id=1, source_target_pairs={{0,4},{4,0},{8,12},{12,8},{16,20},{20,16},{24,28},{28,24},{1,5},{5... | collective-permute-start | bytes 116744 | tf_op jit(solution)/shard_map/ppermute | solution.py:626
  164.2 44.9 %collective-permute-start.11 = (bf16[256,2048]{1,0:T(8,128)(2,1)S(1)}, bf16[256,2048]{1,0:T(8,128)(2,1)S(1)}, u32[]{:S(2)}, u32[]{:S(2)}) collective-permute-start(bf16[256,2048]{1,0:T(8,128)(2,1)S(1)} %collective-permute-done.10), channel_id=1, source_target_pairs={{0,8},{4,12},{8,16},{12,20},{16,24},{20,28},{24,0},{28,4},{1,9},{5... | collective-permute-start | bytes 3145736 | tf_op jit(solution)/shard_map/ppermute | solution.py:657
  164.3 45.9 %collective-permute-start.3 = (f32[8,1216]{1,0:T(8,128)S(1)}, f32[8,1216]{1,0:T(8,128)S(1)}, u32[]{:S(2)}, u32[]{:S(2)}) collective-permute-start(f32[8,1216]{1,0:T(8,128)S(1)} %fusion.5), channel_id=1, source_target_pairs={{0,8},{4,12},{8,0},{12,4},{16,24},{20,28},{24,16},{28,20},{1,9},{5... | collective-permute-start | bytes 116744 | tf_op jit(solution)/shard_map/ppermute | solution.py:626
  186.8 49.1 %collective-permute-start.15 = (bf16[256,2048]{1,0:T(8,128)(2,1)}, bf16[256,2048]{1,0:T(8,128)(2,1)}, u32[]{:S(2)}, u32[]{:S(2)}) collective-permute-start(bf16[256,2048]{1,0:T(8,128)(2,1)} %collective-permute-done.14), channel_id=1, source_target_pairs={{0,8},{4,12},{8,16},{12,20},{16,24},{20,28},{24,0},{28,4},{1,9},{5... | collective-permute-start | bytes 3145736 | tf_op jit(solution)/shard_map/ppermute | solution.py:657
  210.2 106.3 %collective-permute-start.12 = (bf16[1024,2048]{1,0:T(8,128)(2,1)}, bf16[1024,2048]{1,0:T(8,128)(2,1)}, u32[]{:S(2)}, u32[]{:S(2)}) collective-permute-start(bf16[1024,2048]{1,0:T(8,128)(2,1)} %constant_dynamic-update-slice_fusion.wo_ref.f_ref), channel_id=1, source_target_pairs={{0,4},{4,0},{8,12},{12,8},{16,20},{20,16},{24,28},{28,24},{1,5},{5... | collective-permute-start | bytes 12582920 | tf_op jit(solution)/shard_map/ppermute | solution.py:659
  210.2 22.2 %collective-permute-start.4 = (f32[8,1216]{1,0:T(8,128)S(1)}, f32[8,1216]{1,0:T(8,128)S(1)}, u32[]{:S(2)}, u32[]{:S(2)}) collective-permute-start(f32[8,1216]{1,0:T(8,128)S(1)} %fusion.20), channel_id=1, source_target_pairs={{0,16},{4,20},{8,24},{12,28},{16,0},{20,4},{24,8},{28,12},{1,17},{... | collective-permute-start | bytes 116744 | tf_op jit(solution)/shard_map/ppermute | solution.py:626
  224.6 8.1 copy-start.10
  224.7 11.2 %copy-start.4 = (bf16[2048,256]{0,1:T(8,128)(2,1)S(1)}, bf16[2048,256]{0,1:T(8,128)(2,1)}, u32[]{:S(2)}) copy-start(bf16[2048,256]{0,1:T(8,128)(2,1)} %copy-done.3) | copy-start | bytes 3145732
  239.5 185.1 %collective-permute-start.16 = (bf16[1024,2048]{1,0:T(8,128)(2,1)}, bf16[1024,2048]{1,0:T(8,128)(2,1)}, u32[]{:S(2)}, u32[]{:S(2)}) collective-permute-start(bf16[1024,2048]{1,0:T(8,128)(2,1)} %pad_maximum_fusion.1.w_ref.wo_ref), channel_id=1, source_target_pairs={{0,4},{4,0},{8,12},{12,8},{16,20},{20,16},{24,28},{28,24},{1,5},{5... | collective-permute-start | bytes 12582920 | tf_op jit(solution)/shard_map/ppermute | solution.py:659
  473.9 372.8 %reduce-scatter.9.cloned.1.call-start = ((), (), s32[]{:S(2)}) async-start(), calls=%async_computation.8 | async-start | bytes 5242880 | tf_op jit(solution)/shard_map/reduce_scatter | solution.py:737
  498.8 355.3 %reduce-scatter.5.cloned.1.call-start = ((), (), s32[]{:S(2)}) async-start(), calls=%async_computation.5 | async-start | bytes 5242880 | tf_op jit(solution)/shard_map/reduce_scatter | solution.py:724
  514.9 339.2 %reduce-scatter.7.cloned.1.call-start = ((), (), s32[]{:S(2)}) async-start(), calls=%async_computation.6 | async-start | bytes 5242880 | tf_op jit(solution)/shard_map/reduce_scatter | solution.py:724
  533.4 100.0 %collective-permute-start.22 = (bf16[1024,2048]{1,0:T(8,128)(2,1)}, bf16[1024,2048]{1,0:T(8,128)(2,1)}, u32[]{:S(2)}, u32[]{:S(2)}) collective-permute-start(bf16[1024,2048]{1,0:T(8,128)(2,1)} %weight_grad_heads.3), channel_id=1, source_target_pairs={{0,4},{4,0},{8,12},{12,8},{16,20},{20,16},{24,28},{28,24},{1,5},{5... | collective-permute-start | bytes 12582920 | tf_op jit(solution)/shard_map/ppermute | solution.py:699
  535.8 45.9 %collective-permute-start.17 = (f32[3,2048]{1,0:T(4,128)S(1)}, f32[3,2048]{1,0:T(4,128)S(1)}, u32[]{:S(2)}, u32[]{:S(2)}) collective-permute-start(f32[3,2048]{1,0:T(4,128)S(1)} %pad_maximum_fusion.4), channel_id=1, source_target_pairs={{0,1},{1,0},{2,3},{3,2},{4,5},{5,4},{6,7},{7,6},{8,9},{9,8},{10,11... | collective-permute-start | bytes 73736 | tf_op jit(solution)/shard_map/ppermute | solution.py:626
  550.5 87.0 %collective-permute-start.30 = (bf16[1024,2048]{1,0:T(8,128)(2,1)}, bf16[1024,2048]{1,0:T(8,128)(2,1)}, u32[]{:S(2)}, u32[]{:S(2)}) collective-permute-start(bf16[1024,2048]{1,0:T(8,128)(2,1)} %fc2_grad.3), channel_id=1, source_target_pairs={{0,4},{4,0},{8,12},{12,8},{16,20},{20,16},{24,28},{28,24},{1,5},{5... | collective-permute-start | bytes 12582920 | tf_op jit(solution)/shard_map/ppermute | solution.py:699
  564.7 18.8 %copy-start.12 = (f32[4,8,128]{2,1,0:T(8,128)S(1)}, f32[4,8,128]{2,1,0:T(8,128)}, u32[]{:S(2)}) copy-start(f32[4,8,128]{2,1,0:T(8,128)} %get-tuple-element.49) | copy-start | bytes 49156
  564.7 76.3 %collective-permute-start.26 = (bf16[1024,2048]{1,0:T(8,128)(2,1)}, bf16[1024,2048]{1,0:T(8,128)(2,1)}, u32[]{:S(2)}, u32[]{:S(2)}) collective-permute-start(bf16[1024,2048]{1,0:T(8,128)(2,1)} %fc1_grad.3), channel_id=1, source_target_pairs={{0,4},{4,0},{8,12},{12,8},{16,20},{20,16},{24,28},{28,24},{1,5},{5... | collective-permute-start | bytes 12582920 | tf_op jit(solution)/shard_map/ppermute | solution.py:699
  581.7 4.0 collective-permute-start.18
  585.7 14.0 %collective-permute-start.19 = (f32[9728]{0:T(1024)S(1)}, f32[9728]{0:T(1024)S(1)}, u32[]{:S(2)}, u32[]{:S(2)}) collective-permute-start(f32[9728]{0:T(1024)S(1)} %pad_maximum_fusion.3), channel_id=1, source_target_pairs={{0,4},{4,0},{8,12},{12,8},{16,20},{20,16},{24,28},{28,24},{1,5},{5... | collective-permute-start | bytes 116744 | tf_op jit(solution)/shard_map/ppermute | solution.py:626
  599.8 17.3 %collective-permute-start.20 = (f32[9728]{0:T(1024)S(1)}, f32[9728]{0:T(1024)S(1)}, u32[]{:S(2)}, u32[]{:S(2)}) collective-permute-start(f32[9728]{0:T(1024)S(1)} %fusion.18), channel_id=1, source_target_pairs={{0,8},{4,12},{8,0},{12,4},{16,24},{20,28},{24,16},{28,20},{1,9},{5... | collective-permute-start | bytes 116744 | tf_op jit(solution)/shard_map/ppermute | solution.py:626
  617.1 14.0 %collective-permute-start.21 = (f32[9728]{0:T(1024)S(1)}, f32[9728]{0:T(1024)S(1)}, u32[]{:S(2)}, u32[]{:S(2)}) collective-permute-start(f32[9728]{0:T(1024)S(1)} %add.149), channel_id=1, source_target_pairs={{0,16},{4,20},{8,24},{12,28},{16,0},{20,4},{24,8},{28,12},{1,17},{... | collective-permute-start | bytes 116744 | tf_op jit(solution)/shard_map/ppermute | solution.py:626
  632.2 8.8 %copy-start = (bf16[1024,2048]{1,0:T(8,128)(2,1)S(1)}, bf16[1024,2048]{1,0:T(8,128)(2,1)}, u32[]{:S(2)}) copy-start(bf16[1024,2048]{1,0:T(8,128)(2,1)} %fc1_grad.2) | copy-start | bytes 12582916
  633.4 30.4 %copy-start.2 = (bf16[1024,2048]{1,0:T(8,128)(2,1)S(1)}, bf16[1024,2048]{1,0:T(8,128)(2,1)}, u32[]{:S(2)}) copy-start(bf16[1024,2048]{1,0:T(8,128)(2,1)} %weight_grad_heads.2) | copy-start | bytes 12582916
  635.5 28.3 %collective-permute-start.23 = (bf16[256,2048]{1,0:T(8,128)(2,1)S(1)}, bf16[256,2048]{1,0:T(8,128)(2,1)S(1)}, u32[]{:S(2)}, u32[]{:S(2)}) collective-permute-start(bf16[256,2048]{1,0:T(8,128)(2,1)S(1)} %add_convert_fusion.8), channel_id=1, source_target_pairs={{0,8},{4,12},{8,16},{12,20},{16,24},{20,28},{24,0},{28,4},{1,9},{5... | collective-permute-start | bytes 3145736 | tf_op jit(solution)/shard_map/ppermute | solution.py:709
  639.4 46.8 %copy-start.1 = (bf16[1024,2048]{1,0:T(8,128)(2,1)S(1)}, bf16[1024,2048]{1,0:T(8,128)(2,1)}, u32[]{:S(2)}) copy-start(bf16[1024,2048]{1,0:T(8,128)(2,1)} %fc2_grad.2) | copy-start | bytes 12582916
  639.5 46.8 %collective-permute-start.31 = (bf16[256,2048]{1,0:T(8,128)(2,1)S(1)}, bf16[256,2048]{1,0:T(8,128)(2,1)S(1)}, u32[]{:S(2)}, u32[]{:S(2)}) collective-permute-start(bf16[256,2048]{1,0:T(8,128)(2,1)S(1)} %add_convert_fusion.2), channel_id=1, source_target_pairs={{0,8},{4,12},{8,16},{12,20},{16,24},{20,28},{24,0},{28,4},{1,9},{5... | collective-permute-start | bytes 3145736 | tf_op jit(solution)/shard_map/ppermute | solution.py:709
  642.6 66.1 %collective-permute-start.27 = (bf16[256,2048]{1,0:T(8,128)(2,1)S(1)}, bf16[256,2048]{1,0:T(8,128)(2,1)S(1)}, u32[]{:S(2)}, u32[]{:S(2)}) collective-permute-start(bf16[256,2048]{1,0:T(8,128)(2,1)S(1)} %add_convert_fusion.5), channel_id=1, source_target_pairs={{0,8},{4,12},{8,16},{12,20},{16,24},{20,28},{24,0},{28,4},{1,9},{5... | collective-permute-start | bytes 3145736 | tf_op jit(solution)/shard_map/ppermute | solution.py:709
  665.6 65.6 %collective-permute-start.24 = (bf16[256,2048]{1,0:T(8,128)(2,1)S(1)}, bf16[256,2048]{1,0:T(8,128)(2,1)S(1)}, u32[]{:S(2)}, u32[]{:S(2)}) collective-permute-start(bf16[256,2048]{1,0:T(8,128)(2,1)S(1)} %add_convert_fusion.7), channel_id=1, source_target_pairs={{0,8},{4,12},{8,16},{12,20},{16,24},{20,28},{24,0},{28,4},{1,9},{5... | collective-permute-start | bytes 3145736 | tf_op jit(solution)/shard_map/ppermute | solution.py:709
  688.1 65.6 %collective-permute-start.32 = (bf16[256,2048]{1,0:T(8,128)(2,1)S(1)}, bf16[256,2048]{1,0:T(8,128)(2,1)S(1)}, u32[]{:S(2)}, u32[]{:S(2)}) collective-permute-start(bf16[256,2048]{1,0:T(8,128)(2,1)S(1)} %add_convert_fusion.1), channel_id=1, source_target_pairs={{0,8},{4,12},{8,16},{12,20},{16,24},{20,28},{24,0},{28,4},{1,9},{5... | collective-permute-start | bytes 3145736 | tf_op jit(solution)/shard_map/ppermute | solution.py:709
  710.5 65.6 %collective-permute-start.28 = (bf16[256,2048]{1,0:T(8,128)(2,1)S(1)}, bf16[256,2048]{1,0:T(8,128)(2,1)S(1)}, u32[]{:S(2)}, u32[]{:S(2)}) collective-permute-start(bf16[256,2048]{1,0:T(8,128)(2,1)S(1)} %add_convert_fusion.4), channel_id=1, source_target_pairs={{0,8},{4,12},{8,16},{12,20},{16,24},{20,28},{24,0},{28,4},{1,9},{5... | collective-permute-start | bytes 3145736 | tf_op jit(solution)/shard_map/ppermute | solution.py:709
  733.0 65.6 %collective-permute-start.25 = (bf16[256,2048]{1,0:T(8,128)(2,1)S(1)}, bf16[256,2048]{1,0:T(8,128)(2,1)S(1)}, u32[]{:S(2)}, u32[]{:S(2)}) collective-permute-start(bf16[256,2048]{1,0:T(8,128)(2,1)S(1)} %add_convert_fusion.6), channel_id=1, source_target_pairs={{0,8},{4,12},{8,16},{12,20},{16,24},{20,28},{24,0},{28,4},{1,9},{5... | collective-permute-start | bytes 3145736 | tf_op jit(solution)/shard_map/ppermute | solution.py:709
  756.4 64.8 %collective-permute-start.33 = (bf16[256,2048]{1,0:T(8,128)(2,1)}, bf16[256,2048]{1,0:T(8,128)(2,1)}, u32[]{:S(2)}, u32[]{:S(2)}) collective-permute-start(bf16[256,2048]{1,0:T(8,128)(2,1)} %add_convert_fusion), channel_id=1, source_target_pairs={{0,8},{4,12},{8,16},{12,20},{16,24},{20,28},{24,0},{28,4},{1,9},{5... | collective-permute-start | bytes 3145736 | tf_op jit(solution)/shard_map/ppermute | solution.py:709
  778.9 64.1 %collective-permute-start.29 = (bf16[256,2048]{1,0:T(8,128)(2,1)}, bf16[256,2048]{1,0:T(8,128)(2,1)}, u32[]{:S(2)}, u32[]{:S(2)}) collective-permute-start(bf16[256,2048]{1,0:T(8,128)(2,1)} %add_convert_fusion.3), channel_id=1, source_target_pairs={{0,8},{4,12},{8,16},{12,20},{16,24},{20,28},{24,0},{28,4},{1,9},{5... | collective-permute-start | bytes 3145736 | tf_op jit(solution)/shard_map/ppermute | solution.py:709
Sparse Core Ops, SparseCore 0:
  15.5 90.3 all-gather.2
  108.4 87.6 all-gather.4
  474.0 50.7 reduce-scatter.10
  527.9 52.6 reduce-scatter.8
  583.4 52.8 reduce-scatter.4
  639.5 52.6 reduce-scatter.6

commit v2 on v1

v2 whole, which is shorter than its diff:
```python
import functools
import math

import jax
import jax.numpy as jnp
from jax import lax
from jax.experimental import pallas as pl
from jax.experimental.pallas import tpu as pltpu
from jax.sharding import PartitionSpec as P

HD = 64
ROT = 32
EPSILON = 1e-05
NEG = -1e30
LOG2E = math.log2(math.e)
BF = jnp.bfloat16
F32 = jnp.float32
VMEM_BYTES = 56 << 20

NN = (((1,), (0,)), ((), ()))
NT = (((1,), (1,)), ((), ()))
TN = (((0,), (0,)), ((), ()))


def dot(a, b, dims):
    return lax.dot_general(a, b, dims, preferred_element_type=F32)


def call(kernel, name, flops, moved, operands, grid, in_specs, out_specs, out_shape, scratch=(), prefetch=(), aliases=None, after=()):
    front = len(prefetch) + len(in_specs)

    def body(*refs):
        kernel(*refs[:front], *refs[front + len(after) :])

    return pl.pallas_call(
        body,
        name=name,
        grid_spec=pltpu.PrefetchScalarGridSpec(
            num_scalar_prefetch=len(prefetch),
            grid=grid,
            in_specs=list(in_specs) + [pl.BlockSpec(memory_space=pl.ANY)] * len(after),
            out_specs=out_specs,
            scratch_shapes=list(scratch),
        ),
        out_shape=out_shape,
        input_output_aliases=aliases or {},
        compiler_params=pltpu.CompilerParams(vmem_limit_bytes=VMEM_BYTES),
        cost_estimate=pl.CostEstimate(flops=int(flops), bytes_accessed=int(moved), transcendentals=0),
    )(*prefetch, *operands, *after)


class Weights:
    def __init__(self, arrays, placed=False):
        self.arrays = list(arrays)
        self.placed = placed
        self.cols = self.arrays[0].shape[1]
        self.rows = sum(a.shape[0] for a in self.arrays)

    def copies(self, refs, blk, count, side, col, cols, target, sems):
        found = []

        def add(source, start, size, place):
            found.append(
                pltpu.make_async_copy(
                    source.at[pl.ds(start, size), pl.ds(col, cols)],
                    target.at[pl.ds(place, size), :],
                    sems.at[len(found)],
                )
            )

        half = self.rows // 2
        if self.placed:
            size = self.rows // count
            first, last = (0, count) if side is None else (side * count // 2, (side + 1) * count // 2)
            for p in range(first, last):
                add(refs[0], pl.multiple_of(blk[p] * size, size), size, (p - first) * size)
            return found
        place = 0
        for ref, array in zip(refs, self.arrays):
            size = array.shape[0]
            if side is None or place // half == side:
                add(ref, 0, size, place - (side or 0) * half)
            place += size
        return found

    def number(self, count, side=None):
        total = count if self.placed else len(self.arrays)
        return total if side is None else total // 2


def struct(shape, dtype=BF):
    return jax.ShapeDtypeStruct(shape, dtype)


def tie(values, after):
    n = len(values)
    anywhere = pl.BlockSpec(memory_space=pl.ANY)

    def kernel(*refs):
        del refs

    return pl.pallas_call(
        kernel,
        name="tie",
        in_specs=[anywhere] * (n + len(after)),
        out_specs=[anywhere] * n,
        out_shape=[struct(v.shape, v.dtype) for v in values],
        input_output_aliases={i: i for i in range(n)},
    )(*values, *after)


def order_columns(blocks, x, after=()):
    rows, width = x.shape
    count = blocks.shape[0]
    cols = width // count
    step_rows = min(256, rows)

    def kernel(blk, x_ref, out_ref, sum_ref):
        for p in range(count):
            place = pl.ds(pl.multiple_of(blk[p] * cols, cols), cols)
            out_ref[:, p * cols : (p + 1) * cols] = x_ref[:, place]

        @pl.when(pl.program_id(0) == 0)
        def _():
            sum_ref[...] = jnp.zeros_like(sum_ref)

        sum_ref[0:1, :] += jnp.sum(x_ref[...].astype(F32), axis=0, keepdims=True)

    block = pl.BlockSpec((step_rows, width), lambda m, blk: (m, 0))
    return call(
        kernel,
        "order_columns",
        0,
        4 * rows * width,
        (x,),
        (rows // step_rows,),
        [block],
        [block, pl.BlockSpec((8, width), lambda m, blk: (0, 0))],
        [struct(x.shape), struct((8, width), F32)],
        prefetch=(blocks,),
        after=after,
    )


def heads_shard(w_qkv, w_out, after):
    depth, wide = w_qkv.shape
    inner = w_out.shape[0]

    def kernel(q_ref, o_ref, out_ref):
        out_ref[:, :wide] = q_ref[...]
        out_ref[:, wide:] = o_ref[...].T

    return call(
        kernel,
        "heads_shard",
        0,
        4 * depth * (wide + inner),
        (w_qkv, w_out),
        (1,),
        [pl.BlockSpec(w_qkv.shape, lambda i: (0, 0)), pl.BlockSpec(w_out.shape, lambda i: (0, 0))],
        pl.BlockSpec((depth, wide + inner), lambda i: (0, 0)),
        struct((depth, wide + inner)),
        after=after,
    )


def stage(weight, flip, after, rows=None):
    start, count = rows or (0, weight.shape[0])
    taken = (count, weight.shape[1])
    shape = taken[::-1] if flip else taken

    def kernel(w_ref, out_ref):
        out_ref[...] = w_ref[...].T if flip else w_ref[...]

    return call(
        kernel,
        "stage_weight",
        0,
        4 * taken[0] * taken[1],
        (weight,),
        (1,),
        [pl.BlockSpec(taken, lambda i: (start // count, 0))],
        pl.BlockSpec(shape, lambda i: (0, 0)),
        struct(shape),
        after=after,
    )


def rotary_rows(length):
    lane = jnp.arange(128, dtype=jnp.int32)[None, :] % HD
    half = ROT // 2
    frequency = 10000.0 ** (-2.0 * (lane % half).astype(F32) / ROT)
    angles = jnp.arange(length, dtype=F32)[:, None] * frequency
    cosine, sine = jnp.cos(angles), jnp.sin(angles)
    keep = jnp.where(lane < ROT, cosine, 1.0)
    ahead = jnp.where(lane < half, -sine, 0.0)
    behind = jnp.where((lane >= half) & (lane < ROT), sine, 0.0)
    return keep, ahead, behind


def turn(u, keep, ahead, behind):
    return u * keep + pltpu.roll(u, 128 - ROT // 2, 1) * ahead + pltpu.roll(u, ROT // 2, 1) * behind


def norm_project(blocks, out_blocks, pieces, rows, gain, shift, bias, tables, weights, after=()):
    width = pieces[0].shape[1]
    wide = bias.shape[1]
    inner = wide // 3
    starts, total = [], 0
    for piece in pieces:
        starts.append(total)
        total += piece.shape[0] // rows
    length = total * rows
    n, k, count = len(pieces), len(weights.arrays), blocks.shape[0]

    def kernel(blk, places, *refs):
        piece_refs = refs[:n]
        gain_ref, shift_ref, bias_ref, keep_ref, ahead_ref, behind_ref = refs[n : n + 6]
        w_refs = refs[n + 6 : n + 6 + k]
        normed_ref, unit_ref, qkv_ref, rows_ref, w_ref, sems = refs[n + 6 + k :]
        step = pl.program_id(0)
        copies = weights.copies(w_refs, blk, count, None, 0, wide, w_ref, sems)

        @pl.when(step == 0)
        def _():
            for copy in copies:
                copy.start()

        for i in range(n):
            last = starts[i + 1] if i + 1 < n else total

            @pl.when((step >= starts[i]) & (step < last))
            def _(i=i):
                rows_ref[...] = piece_refs[i][...]

        x = rows_ref[...].astype(F32)
        centered = x - jnp.mean(x, axis=1, keepdims=True)
        variance = jnp.mean(centered * centered, axis=1, keepdims=True)
        unit = centered * lax.rsqrt(variance + EPSILON)
        unit_ref[...] = unit.astype(BF)
        normed = (unit * gain_ref[...] + shift_ref[...]).astype(BF)
        normed_ref[...] = normed

        @pl.when(step == 0)
        def _():
            for copy in copies:
                copy.wait()

        for part in range(3):
            cols = slice(part * inner, (part + 1) * inner)
            merged = dot(normed_ref[...], w_ref[:, cols], NN) + bias_ref[:, cols]
            for pair in range(inner // 128):
                u = merged[:, pair * 128 : (pair + 1) * 128]
                if part < 2:
                    u = turn(u, keep_ref[...], ahead_ref[...], behind_ref[...])
                start = part * inner + pair * 128
                qkv_ref[:, start : start + 128] = u.astype(BF)

    def piece_spec(i):
        number = pieces[i].shape[0] // rows
        return pl.BlockSpec((rows, width), lambda j, b, o: (jnp.clip(j - starts[i], 0, number - 1), 0))

    def whole(shape):
        return pl.BlockSpec(shape, lambda j, b, o: (0, 0))

    def placed(cols):
        return pl.BlockSpec((rows, cols), lambda j, b, o: (o[j], 0))

    return call(
        kernel,
        "norm_project",
        3 * length * width * wide,
        6 * length * width + 4 * width * wide,
        (*pieces, gain, shift, bias, *tables, *weights.arrays),
        (total,),
        [piece_spec(i) for i in range(n)]
        + [whole((1, width)), whole((1, width)), whole((1, wide))]
        + [placed(128)] * 3
        + [pl.BlockSpec(memory_space=pl.ANY)] * k,
        [placed(width), placed(width), placed(wide)],
        [struct((length, width)), struct((length, width)), struct((length, wide))],
        scratch=[
            pltpu.VMEM((rows, width), BF),
            pltpu.VMEM((width, wide), BF),
            pltpu.SemaphoreType.DMA((weights.number(count),)),
        ],
        prefetch=(blocks, out_blocks),
        after=after,
    )


def attend(qkv, first, number, before=None, after=()):
    length = qkv.shape[0]
    inner = qkv.shape[1] // 3
    pairs = inner // 128
    block = min(512, length)
    count = length // block
    scale = LOG2E / math.sqrt(HD)
    n = 0 if before is None else 1

    def kernel(q_ref, k_ref, v_ref, *refs):
        o_ref, lse_ref, turned_ref = refs[n:]
        lane = lax.broadcasted_iota(jnp.int32, (1, 128), 1)

        @pl.when(pl.program_id(1) == 0)
        def _():
            turned_ref[...] = v_ref[...].T

        for index in range(count):

            @pl.when(pl.program_id(1) == index)
            def _(index=index):
                queries = q_ref[...]
                blank = jnp.zeros_like(queries)
                end = (index + 1) * block
                found = []
                for head in range(2):
                    mine = (lane < HD) if head == 0 else (lane >= HD)
                    scores = dot(k_ref[:end, :], jnp.where(mine, queries, blank), NT)
                    row = lax.broadcasted_iota(jnp.int32, (block, block), 0)
                    col = lax.broadcasted_iota(jnp.int32, (block, block), 1)
                    last = jnp.where(row <= col, scores[end - block :], NEG)
                    if index:
                        scores = jnp.concatenate([scores[: end - block], last], axis=0)
                    else:
                        scores = last
                    top = jnp.max(scores, axis=0, keepdims=True)
                    weights = jnp.exp2((scores - top) * scale)
                    total = jnp.sum(weights, axis=0, keepdims=True)
                    out = dot(turned_ref[head * HD : (head + 1) * HD, :end], weights.astype(BF), NN)
                    found.append(out / total)
                    lse_ref[0, head : head + 1, :] = top * scale + jnp.log2(total)
                o_ref[...] = jnp.concatenate(found, axis=0).T.astype(BF)

    return call(
        kernel,
        "attend",
        40 * length * length * 128 * number,
        8 * length * 128 * number,
        (qkv, qkv, qkv) + ((before,) if n else ()),
        (number, count),
        [
            pl.BlockSpec((block, 128), lambda h, i: (i, first + h)),
            pl.BlockSpec((length, 128), lambda h, i: (0, pairs + first + h)),
            pl.BlockSpec((length, 128), lambda h, i: (0, 2 * pairs + first + h)),
        ]
        + [pl.BlockSpec(memory_space=pl.ANY)] * n,
        [
            pl.BlockSpec((block, 128), lambda h, i: (i, first + h)),
            pl.BlockSpec((1, 2, block), lambda h, i: (h, 0, i)),
        ],
        [struct((length, inner)), struct((number, 2, length), F32)],
        scratch=[pltpu.VMEM((128, length), BF)],
        aliases={3: 0} if n else {},
        after=after,
    )


def attend_back(qkv, context, context_grad, log_total, tables, after=()):
    length = qkv.shape[0]
    inner = qkv.shape[1] // 3
    pairs = inner // 128
    block = min(512, length)
    count = length // block
    scale = LOG2E / math.sqrt(HD)
    shrink = 1.0 / math.sqrt(HD)

    def kernel(q_ref, k_ref, v_ref, o_ref, do_ref, lse_ref, keep_ref, ahead_ref, behind_ref, *rest):
        dq_ref, dk_ref, dv_ref, sum_ref, k_total, v_total = rest
        step = pl.program_id(1)
        lane = lax.broadcasted_iota(jnp.int32, (1, 128), 1)

        @pl.when(step == 0)
        def _():
            k_total[...] = jnp.zeros_like(k_total)
            v_total[...] = jnp.zeros_like(v_total)
            sum_ref[...] = jnp.zeros_like(sum_ref)

        def turn_back(u, rows):
            return turn(u, keep_ref[rows, :], -ahead_ref[rows, :], -behind_ref[rows, :])

        for index in range(count):

            @pl.when(step == index)
            def _(index=index):
                queries, grads = q_ref[...], do_ref[...]
                blank = jnp.zeros_like(queries)
                queries_turned, grads_turned = queries.T, grads.T
                products = grads.astype(F32) * o_ref[...].astype(F32)
                log_totals = lse_ref[0].T
                q_total = [None, None]
                for other in range(index + 1):
                    rows = slice(other * block, (other + 1) * block)
                    keys, values = k_ref[rows, :], v_ref[rows, :]
                    for head in range(2):
                        mine = (lane < HD) if head == 0 else (lane >= HD)
                        here = slice(head * HD, (head + 1) * HD)
                        delta = jnp.sum(products[:, here], axis=1, keepdims=True)
                        scores = dot(jnp.where(mine, queries, blank), keys, NT)
                        if other == index:
                            row = lax.broadcasted_iota(jnp.int32, (block, block), 0)
                            col = lax.broadcasted_iota(jnp.int32, (block, block), 1)
                            scores = jnp.where(col <= row, scores, NEG)
                        probs = jnp.exp2(scores * scale - log_totals[:, head : head + 1])
                        probs_grad = dot(jnp.where(mine, grads, blank), values, NT)
                        score_grad = (probs * (probs_grad - delta)).astype(BF)
                        v_total[here, rows] += dot(grads_turned[here, :], probs.astype(BF), NN)
                        k_total[here, rows] += dot(queries_turned[here, :], score_grad, NN)
                        term = dot(score_grad, keys, NN)
                        q_total[head] = term if other == 0 else q_total[head] + term
                dq = jnp.where(lane < HD, q_total[0], q_total[1]) * shrink
                rows = slice(index * block, (index + 1) * block)
                dq = turn_back(dq, rows).astype(BF)
                dq_ref[...] = dq
                sum_ref[0, 0:1, :] += jnp.sum(dq.astype(F32), axis=0, keepdims=True)

        @pl.when(step == count - 1)
        def _():
            for index in range(count):
                rows = slice(index * block, (index + 1) * block)
                dk = turn_back(k_total[:, rows].T * shrink, rows).astype(BF)
                dk_ref[rows, :] = dk
                sum_ref[0, 1:2, :] += jnp.sum(dk.astype(F32), axis=0, keepdims=True)
                dv = v_total[:, rows].T.astype(BF)
                dv_ref[rows, :] = dv
                sum_ref[0, 2:3, :] += jnp.sum(dv.astype(F32), axis=0, keepdims=True)

    def column(offset):
        return pl.BlockSpec((length, 128), lambda h, i: (0, offset + h))

    def rows_of(offset):
        return pl.BlockSpec((block, 128), lambda h, i: (i, offset + h))

    table = pl.BlockSpec((length, 128), lambda h, i: (0, 0))
    return call(
        kernel,
        "attend_back",
        60 * length * length * inner,
        16 * length * inner,
        (qkv, qkv, qkv, context, context_grad, log_total, *tables),
        (pairs, count),
        [
            rows_of(0),
            column(pairs),
            column(2 * pairs),
            rows_of(0),
            rows_of(0),
            pl.BlockSpec((1, 2, block), lambda h, i: (h, 0, i)),
            table,
            table,
            table,
        ],
        [rows_of(0), column(0), column(0), pl.BlockSpec((1, 8, 128), lambda h, i: (h, 0, 0))],
        [struct((length, inner))] * 3 + [struct((pairs, 8, 128), F32)],
        scratch=[pltpu.VMEM((128, length), F32)] * 2,
        after=after,
    )


def times_weights(blocks, rows_in, weights, col, total_cols, name, extra, outs, finish, after=()):
    length, width = rows_in.shape
    rows, cols = min(512, length), min(1024, total_cols)
    chunks = total_cols // cols
    k, count, e = len(weights.arrays), blocks.shape[0], len(extra)
    number = weights.number(count)

    def kernel(blk, a_ref, *refs):
        w_refs, extra_refs, out_refs = refs[:k], refs[k : k + e], refs[k + e : -2]
        w_ref, sems = refs[-2:]
        copies = [
            weights.copies(w_refs, blk, count, None, col + c * cols, cols, w_ref.at[c], sems.at[c])
            for c in range(chunks)
        ]

        @pl.when((pl.program_id(0) == 0) & (pl.program_id(1) == 0))
        def _():
            for chunk in copies:
                for copy in chunk:
                    copy.start()

        for c in range(chunks):

            @pl.when((pl.program_id(0) == c) & (pl.program_id(1) == 0))
            def _(c=c):
                for copy in copies[c]:
                    copy.wait()

        finish(dot(a_ref[...], w_ref[pl.program_id(0)], NN), extra_refs, out_refs)

    specs = {
        "block": pl.BlockSpec((rows, cols), lambda n, m, blk: (m, n)),
        "row": pl.BlockSpec((1, cols), lambda n, m, blk: (0, n)),
        "sum": pl.BlockSpec((8, cols), lambda n, m, blk: (0, n)),
    }
    shapes = {"block": struct((length, total_cols)), "sum": struct((8, total_cols), F32)}
    return call(
        kernel,
        name,
        2 * length * width * total_cols,
        2 * length * width + 2 * width * total_cols + 4 * length * total_cols,
        (rows_in, *weights.arrays, *(value for _, value in extra)),
        (chunks, length // rows),
        [pl.BlockSpec((rows, width), lambda n, m, blk: (m, 0))]
        + [pl.BlockSpec(memory_space=pl.ANY)] * k
        + [specs[kind] for kind, _ in extra],
        [specs[kind] for kind in outs],
        [shapes[kind] for kind in outs],
        scratch=[
            pltpu.VMEM((chunks, width, cols), BF),
            pltpu.SemaphoreType.DMA((chunks, number)),
        ],
        prefetch=(blocks,),
        after=after,
    )


def expand(blocks, normed, weights, bias, after=()):
    def finish(product, extra_refs, out_refs):
        hidden = product + extra_refs[0][...]
        c = math.sqrt(2.0 / math.pi)
        square = hidden * hidden
        inner = hidden * (c + (c * 0.044715) * square)
        gate = 0.5 + 0.5 * jnp.tanh(inner)
        act = hidden * gate
        out_refs[0][...] = act.astype(BF)
        out_refs[1][...] = (
            gate + act * (1.0 - gate) * (2.0 * c + (6.0 * c * 0.044715) * square)
        ).astype(BF)

    return times_weights(
        blocks, normed, weights, 0, weights.cols, "expand", [("row", bias)], ["block", "block"], finish, after
    )


def hidden_back(blocks, g_all, weights, slope, after=()):
    def finish(product, extra_refs, out_refs):
        low = (product * extra_refs[0][...].astype(F32)).astype(BF)
        out_refs[0][...] = low

        @pl.when(pl.program_id(1) == 0)
        def _():
            out_refs[1][...] = jnp.zeros_like(out_refs[1])

        out_refs[1][0:1, :] += jnp.sum(low.astype(F32), axis=0, keepdims=True)

    return times_weights(
        blocks, g_all, weights, 0, weights.cols, "hidden_back", [("block", slope)], ["block", "sum"], finish, after
    )


def context_back(blocks, g_all, weights, after=()):
    inner = weights.cols // 4

    def finish(product, extra_refs, out_refs):
        out_refs[0][...] = product.astype(BF)

    return times_weights(
        blocks, g_all, weights, 3 * inner, inner, "context_back", [], ["block"], finish, after
    )[0]


def weight_grad(blocks, rows_in, rights, cols, name, after=()):
    length, width = rows_in.shape
    half = width // 2
    count = blocks.shape[0]
    depth = width // count
    starts, total = [], 0
    for right in rights:
        starts.append(total)
        total += right.shape[1] // cols
    n = len(rights)

    def kernel(blk, a_ref, *refs):
        out_ref = refs[n]
        chunk, side = pl.program_id(0), pl.program_id(1)
        for i in range(n):
            last = starts[i + 1] if i + 1 < n else total

            @pl.when((chunk >= starts[i]) & (chunk < last))
            def _(i=i):
                product = dot(a_ref[...], refs[i][...], TN).astype(BF)
                for p in range(count // 2):
                    place = pl.multiple_of(blk[side * (count // 2) + p] * depth, depth)
                    out_ref[pl.ds(place, depth), :] = product[p * depth : (p + 1) * depth]

    def right_spec(i):
        number = rights[i].shape[1] // cols
        return pl.BlockSpec(
            (length, cols), lambda n, s, blk: (0, jnp.clip(n - starts[i], 0, number - 1))
        )

    return call(
        kernel,
        name,
        2 * length * width * total * cols,
        2 * length * width + 4 * length * total * cols + 2 * width * total * cols,
        (rows_in, *rights),
        (total, 2),
        [pl.BlockSpec((length, half), lambda n, s, blk: (0, s))] + [right_spec(i) for i in range(n)],
        pl.BlockSpec((width, cols), lambda n, s, blk: (0, n)),
        struct((width, total * cols)),
        prefetch=(blocks,),
        after=after,
    )


def weight_grad_halves(rows_in, rights, cols, name, after=()):
    length, width = rows_in.shape
    half = width // 2
    starts, total = [], 0
    for right in rights:
        starts.append(total)
        total += right.shape[1] // cols
    n = len(rights)

    def kernel(a_ref, *refs):
        sib_ref, own_ref = refs[n:]
        side, chunk = pl.program_id(0), pl.program_id(1)
        for i in range(n):
            last = starts[i + 1] if i + 1 < n else total

            @pl.when((chunk >= starts[i]) & (chunk < last))
            def _(i=i):
                product = dot(a_ref[...], refs[i][...], TN).astype(BF)

                @pl.when(side == 0)
                def _():
                    sib_ref[...] = product

                @pl.when(side == 1)
                def _():
                    own_ref[...] = product

    def right_spec(i):
        number = rights[i].shape[1] // cols
        return pl.BlockSpec((length, cols), lambda s, n: (0, jnp.clip(n - starts[i], 0, number - 1)))

    return call(
        kernel,
        name,
        2 * length * width * total * cols,
        2 * length * width + 4 * length * total * cols + 2 * width * total * cols,
        (rows_in, *rights),
        (2, total),
        [pl.BlockSpec((length, half), lambda s, n: (0, 1 - s))] + [right_spec(i) for i in range(n)],
        [
            pl.BlockSpec((half, cols), lambda s, n: (0, jnp.where(s == 0, n, total - 1))),
            pl.BlockSpec((half, cols), lambda s, n: (0, jnp.where(s == 0, 0, n))),
        ],
        [struct((half, total * cols))] * 2,
        after=after,
    )


def split_outputs(split, rows, half, count):
    if split is None:
        return [(0, half, {m: m for m in range(count)}, lambda m, blk: (m, 0))]
    send_first = (({0: 1, 1: 0}), lambda m, blk: (jnp.where(m < 1, 1, 0), 0))
    keep_first = (({2: 1, 3: 0}), lambda m, blk: (jnp.where(m < 3, 1, 0), 0))
    send_second = (({0: 1, 2: 0}), lambda m, blk: (jnp.where(m < 2, 1, 0), 0))
    keep_second = (({1: 1, 3: 0}), lambda m, blk: (jnp.where(m < 3, 1, 0), 0))
    if split == "first":
        return [(0, half, *send_first), (0, half, *keep_first)]
    if split == "second":
        return [(0, half, *send_second), (0, half, *keep_second)]
    part = half // 2
    return [
        (0, part, *send_first),
        (0, part, *keep_first),
        (part, part, *send_second),
        (part, part, *keep_second),
    ]


def store_outputs(plan, out_refs, low):
    step = pl.program_id(0)
    for (col, cols, steps, _), ref in zip(plan, out_refs):
        if len(steps) > 2:
            ref[...] = low[:, col : col + cols]
            continue
        first, second = steps

        @pl.when((step == first) | (step == second))
        def _(ref=ref, col=col, cols=cols):
            ref[...] = low[:, col : col + cols]


def rows_back(blocks, order, split, lefts, groups, side, name, unit=None, after=()):
    length = lefts[0].shape[0]
    count, places = blocks.shape[0], order.shape[0]
    half = groups[0][0].rows // 2
    rows = length // places
    widths = [left.shape[1] for left in lefts]
    depth = sum(widths)
    n = len(lefts)
    arrays = [array for weights, _, _ in groups for array in weights.arrays]
    k = len(arrays)
    number = sum(weights.number(count, side) for weights, _, _ in groups)
    plan = split_outputs(split, rows, half, places)
    u = 0 if unit is None else 1

    def kernel(blk, places_ref, *refs):
        left_refs, unit_refs, w_refs = refs[:n], refs[n : n + u], refs[n + u : n + u + k]
        out_refs = refs[n + u + k : n + u + k + len(plan)]
        sum_refs = refs[n + u + k + len(plan) : n + 2 * u + k + len(plan)]
        joined_ref, w_ref, sems = refs[-3:]

        copies, at, col, used = [], 0, 0, 0
        for weights, start, cols in groups:
            more = len(weights.arrays)
            found = weights.copies(
                w_refs[at : at + more],
                blk,
                count,
                side,
                start,
                cols,
                w_ref.at[:, pl.ds(col, cols)],
                sems.at[pl.ds(used, weights.number(count, side))],
            )
            copies += found
            at, col, used = at + more, col + cols, used + len(found)

        @pl.when(pl.program_id(0) == 0)
        def _():
            for copy in copies:
                copy.start()

        col = 0
        for ref, cols in zip(left_refs, widths):
            joined_ref[:, col : col + cols] = ref[...]
            col += cols

        @pl.when(pl.program_id(0) == 0)
        def _():
            for copy in copies:
                copy.wait()

        low = dot(joined_ref[...], w_ref[...], NT).astype(BF)
        store_outputs(plan, out_refs, low)
        if u:

            @pl.when(pl.program_id(0) == 0)
            def _():
                sum_refs[0][...] = jnp.zeros_like(sum_refs[0])

            wide = low.astype(F32)
            sum_refs[0][0:1, :] += jnp.sum(wide * unit_refs[0][...].astype(F32), axis=0, keepdims=True)
            sum_refs[0][1:2, :] += jnp.sum(wide, axis=0, keepdims=True)

    def left_spec(cols, column=0):
        return pl.BlockSpec((rows, cols), lambda m, blk, o: (o[m], column))

    def out_spec(cols, where):
        return pl.BlockSpec((rows, cols), lambda m, blk, o: where(m, blk))

    return call(
        kernel,
        name,
        2 * length * half * depth,
        2 * length * depth + 2 * half * depth + 2 * length * half,
        (*lefts, *([unit] if u else []), *arrays),
        (places,),
        [left_spec(cols) for cols in widths]
        + [left_spec(half, side)] * u
        + [pl.BlockSpec(memory_space=pl.ANY)] * k,
        [out_spec(cols, where) for _, cols, _, where in plan]
        + [pl.BlockSpec((8, half), lambda m, blk, o: (0, 0))] * u,
        [struct((len(steps) * rows, cols)) for _, cols, steps, _ in plan] + [struct((8, half), F32)] * u,
        scratch=[
            pltpu.VMEM((rows, depth), BF),
            pltpu.VMEM((half, depth), BF),
            pltpu.SemaphoreType.DMA((number,)),
        ],
        prefetch=(blocks, order),
        after=after,
    )


def end_call(kernel, name, blocks, fulls, terms, vector, dtype, after):
    length, width = fulls[0].shape
    rows = min(128, length)
    n = len(fulls)
    counts = [len(part) for part in terms]

    def body(blk, *refs):
        at, parts = n, []
        for number in counts:
            total = refs[at][...].astype(F32)
            for ref in refs[at + 1 : at + number]:
                total = total + ref[...].astype(F32)
            parts.append(total)
            at += number
        result = kernel([ref[...].astype(F32) for ref in refs[:n]], jnp.concatenate(parts, axis=1), refs[at][...])
        out_ref = refs[at + 1]
        cols = width // blocks.shape[0]
        for p in range(blocks.shape[0]):
            place = pl.ds(pl.multiple_of(blk[p] * cols, cols), cols)
            out_ref[:, place] = result[:, p * cols : (p + 1) * cols].astype(dtype)

    full = pl.BlockSpec((rows, width), lambda m, blk: (m, 0))
    flat = [array for part in terms for array in part]
    return call(
        body,
        name,
        0,
        10 * length * width,
        (*fulls, *flat, vector),
        (length // rows,),
        [full] * n
        + [pl.BlockSpec((rows, array.shape[1]), lambda m, blk: (m, 0)) for array in flat]
        + [pl.BlockSpec((1, width), lambda m, blk: (0, 0))],
        full,
        struct((length, width), dtype),
        prefetch=(blocks,),
        after=after,
    )


def add_branch(blocks, x, terms, out_bias, after=()):
    return end_call(
        lambda fulls, branch, bias: fulls[0] + branch + bias, "add_branch", blocks, (x,), terms, out_bias, BF, after
    )


def norm_back(blocks, x, g, terms, gain, after=()):
    def kernel(fulls, grads, scale):
        x, g = fulls
        centered = x - jnp.mean(x, axis=1, keepdims=True)
        variance = jnp.mean(centered * centered, axis=1, keepdims=True)
        inv_std = lax.rsqrt(variance + EPSILON)
        unit = centered * inv_std
        scaled = grads * scale
        mean = jnp.mean(scaled, axis=1, keepdims=True)
        along = jnp.mean(scaled * unit, axis=1, keepdims=True)
        return g + inv_std * (scaled - mean - unit * along)

    return end_call(kernel, "norm_back", blocks, (x, g), terms, gain, F32, after)


def flip(value, axis, size, bit):
    return lax.ppermute(value, axis, [(i, i ^ bit) for i in range(size)])


def flip_sums(value, axis, size):
    found, bit = [value], 1
    while bit < size:
        found.append(found[-1] + flip(found[-1], axis, size, bit))
        bit *= 2
    return found


def pick(steps, k):
    return steps[min(k, len(steps) - 1)]


class Ring:
    def __init__(self, n_dp):
        self.size = n_dp
        self.chips = n_dp // 2

    def send(self, value):
        pairs = [
            (z * 2 + c, ((z + 1) % self.chips) * 2 + c) for z in range(self.chips) for c in range(2)
        ]
        return lax.ppermute(value, "dp", pairs)

    def swap(self, value):
        return flip(value, "dp", self.size, 1)

    def extend(self, pieces, steps, after):
        while len(pieces) <= min(steps, self.chips - 1):
            pieces.append(self.send(pieces[-1]))
        pieces[-1:] = tie(pieces[-1:], after)


def per_device(
    sizes, layer_input, ln_gain, ln_bias, out_bias, w_qkv, b_qkv, w_out, w_fc1, b_fc1, w_fc2, out_grad
):
    n_dp, n_tensor = sizes
    ring = Ring(n_dp)
    chips = ring.chips
    d_index, t_index = lax.axis_index("dp"), lax.axis_index("tensor")
    place, core = d_index // 2, d_index % 2
    steps = jnp.arange(chips, dtype=jnp.int32)
    behind = ((place - steps) % chips) * 2
    blocks = jnp.concatenate([behind + core, behind + (1 - core)]).astype(jnp.int32)
    square = n_tensor == 4

    local, width = layer_input.shape[1:]
    depth = w_qkv.shape[0]
    inner = w_qkv.shape[2]
    units = w_fc1.shape[1]
    heads = inner // HD
    length = local * n_tensor
    pairs = inner // 128

    third = ln_gain.shape[0]
    vectors = jnp.stack([ln_gain, ln_bias, out_bias]).astype(F32).reshape(1, 3 * third)
    table = jnp.where(jnp.arange(n_tensor)[:, None] == t_index, vectors, 0.0)
    tables_small = flip_sums(table, "tensor", n_tensor)
    packed = jnp.concatenate(
        [tables_small[-1].reshape(-1), b_qkv.astype(F32).reshape(-1), b_fc1.astype(F32).reshape(-1)]
    )[None, :]
    packed = jnp.where(jnp.arange(n_dp)[:, None] == d_index, packed, 0.0)
    packed_steps = flip_sums(packed, "dp", n_dp)
    packed = packed_steps[-1]
    cut = n_tensor * 3 * third
    vectors = packed[:, :cut].reshape(n_dp, n_tensor, 3, third)
    vectors = jnp.transpose(vectors, (2, 0, 1, 3)).reshape(3, n_dp, n_tensor * third)
    chosen = (blocks[:, None] == jnp.arange(n_dp)[None, :]).astype(F32)
    vectors = jnp.einsum("pd,kdj->kpj", chosen, vectors, precision=lax.Precision.HIGHEST)
    gain, shift, bias_out = (vectors[i].reshape(1, width) for i in range(3))
    tail = cut + b_qkv.size
    bias_qkv = jnp.transpose(packed[:, cut:tail].reshape(n_dp, 3, heads, -1), (1, 2, 0, 3))
    bias_qkv = bias_qkv.reshape(1, 3 * inner)
    bias_fc1 = jnp.transpose(packed[:, tail:].reshape(n_dp, units // HD, -1), (1, 0, 2))
    bias_fc1 = bias_fc1.reshape(1, units)
    tables = rotary_rows(length)

    x, _ = order_columns(blocks, layer_input[0])
    shard = heads_shard(w_qkv.reshape(depth, 3 * inner), w_out, [x])
    rows = min(256, local)
    heads_own, heads_sib = [shard], []
    if square:
        cut = local // 2
        lower = x[cut:]
        beside, below = [flip(x[:cut], "tensor", 4, 1)], [flip(x[:cut], "tensor", 4, 2)]
        heads_own.append(ring.send(shard))
        heads_sib.append(ring.swap(shard))
        lower, heads_own[1], beside[0], below[0] = tie(
            [lower, heads_own[1], beside[0], below[0]], [tables_small[-1], heads_sib[0]]
        )
        beside.append(flip(lower, "tensor", 4, 1))
        below.append(flip(lower, "tensor", 4, 2))
        heads_own.append(ring.send(heads_own[1]))
        heads_sib.append(ring.swap(heads_own[1]))
        heads_own[2], beside[1], below[1] = tie(
            [heads_own[2], beside[1], below[1]], [pick(packed_steps, 2), heads_sib[1], tables[0]]
        )
        across = [flip(beside[0], "tensor", 4, 2), flip(below[1], "tensor", 4, 1)]
        for _ in range(chips - 3):
            heads_own.append(ring.send(heads_own[-1]))
            heads_sib.append(ring.swap(heads_own[-2]))
        heads_own[-1], *across = tie([heads_own[-1], *across], [gain, heads_sib[-1]])
        heads_sib.append(ring.swap(heads_own[-1]))
        pieces = [x, *beside, *below, *across]
        rows = min(rows, cut)
        each = local // rows
        relative = [r * each + i for r in (0, 1, 2, 3) for i in range(each)]
        relative = jnp.array(relative, jnp.int32)
        out_blocks = ((relative // each) ^ t_index) * each + relative % each
        g, bias_part = order_columns(blocks, out_grad[0], after=across)
        order = (jnp.array([3, 1, 2, 0], jnp.int32) ^ t_index).astype(jnp.int32)
    else:
        for _ in range(chips - 1):
            heads_own.append(ring.send(heads_own[-1]))
        heads_sib = [ring.swap(piece) for piece in heads_own]
        pieces = [lax.all_gather(x, "tensor", axis=0, tiled=True)]
        out_blocks = jnp.arange(length // rows, dtype=jnp.int32)
        g, bias_part = order_columns(blocks, out_grad[0])
        order = jnp.arange(n_tensor, dtype=jnp.int32)
    heads_weights = Weights(heads_own + heads_sib)
    g_all = lax.all_gather(g, "tensor", axis=0, tiled=True)

    def split(kind):
        return kind if square else None

    bits = {"first": [1], "second": [2], "both": [1, 2]}

    def cross_once(kind, parts):
        if not square:
            return [lax.psum_scatter(parts[0], "tensor", scatter_dimension=0, tiled=True)]
        return [flip(parts[2 * i], "tensor", 4, bit) for i, bit in enumerate(bits[kind])]

    def cross_add(parts, got):
        if not square:
            return []
        kept = parts[1::2]
        return [(k[local:].astype(F32) + r[local:].astype(F32)).astype(BF) for k, r in zip(kept, got)]

    def cross_twice(kind, sums):
        return [flip(value, "tensor", 4, 3 - bit) for value, bit in zip(sums, bits[kind])] if square else []

    def cross_terms(parts, got, last):
        if not square:
            return [got]
        return [list(terms) for terms in zip(parts[1::2], got, last)]

    fc1_pieces = [stage(w_fc1, False, [heads_own[-1]])]
    normed, unit, qkv = norm_project(
        blocks, out_blocks, pieces, rows, gain, shift, bias_qkv, tables, heads_weights, after=[fc1_pieces[0]]
    )
    ring.extend(fc1_pieces, 1, [qkv])
    first = pairs // 2
    context, log_first = attend(qkv, 0, first, after=[fc1_pieces[-1]])
    ring.extend(fc1_pieces, 2, [log_first])
    context, log_second = attend(qkv, first, pairs - first, before=context, after=[fc1_pieces[-1]])
    log_total = jnp.concatenate([log_first, log_second], axis=0)
    ring.extend(fc1_pieces, chips - 1, [log_second])
    fc1_own = jnp.concatenate(fc1_pieces, axis=0)
    fc1_weights = Weights([fc1_own, ring.swap(fc1_own)])
    fc2_shard = stage(w_fc2, True, [fc1_own])
    fc2_weights = Weights([lax.all_gather(fc2_shard, "dp", axis=0, tiled=True)], placed=True)
    context_grad = context_back(blocks, g_all, heads_weights, after=[fc2_shard, log_second])
    act, slope = expand(blocks, normed, fc1_weights, bias_fc1, after=[context_grad])

    def scatter(parts):
        return lax.psum_scatter(parts, "dp", scatter_dimension=0, tiled=True)

    fc2_sums = scatter(weight_grad(blocks, g_all, [act, context], min(512, inner), "fc2_grad"))
    backs = attend_back(qkv, context, context_grad, log_total, tables, after=[act])
    heads_cols, fc2_cols = (heads_weights, 0, 3 * inner), (fc2_weights, 0, units)
    out_cols, fc1_cols = (heads_weights, 3 * inner, inner), (fc1_weights, 0, units)
    branch = []
    for side, kind in enumerate(("first", "second")):
        parts = rows_back(
            blocks, order, split(kind), [act, context], [fc2_cols, out_cols], side, "branch_half",
            after=[backs[0]] if side == 0 else branch[0],
        )
        branch.append(parts)
    branch_got = [cross_once("first", branch[0]), cross_once("second", branch[1])]
    hidden_grad, b_fc1_part = hidden_back(blocks, g_all, fc2_weights, slope, after=branch[1])
    fc1_grad = weight_grad(blocks, normed, [hidden_grad], min(512, units), "fc1_grad")
    fc1_grad, branch_got[0][0], branch_got[1][0] = tie([fc1_grad, branch_got[0][0], branch_got[1][0]], [])
    fc1_sums = scatter(fc1_grad)
    branch_sums = [cross_add(parts, got) for parts, got in zip(branch, branch_got)]
    branch_last = [cross_twice(kind, sums) for kind, sums in zip(("first", "second"), branch_sums)]
    heads_grads = weight_grad_halves(
        normed, backs[:3], inner, "heads_grad", after=[fc1_grad, *branch_sums[0], *branch_sums[1]]
    )
    if square:
        heads_sib_grad, heads_own_grad, branch_last[0][0], branch_last[1][0] = tie(
            [*heads_grads, branch_last[0][0], branch_last[1][0]], []
        )
    else:
        heads_sib_grad, heads_own_grad = heads_grads
    branch_terms = [
        part for parts in zip(branch, branch_got, branch_last) for part in cross_terms(*parts)
    ]
    heads_other = ring.swap(heads_sib_grad)
    lefts = [*backs[:3], hidden_grad]
    back_own = rows_back(
        blocks, order, split("both"), lefts, [heads_cols, fc1_cols], 0, "normed_back_half", unit=unit,
        after=[heads_own_grad],
    )
    *back_own, heads_other = tie([*back_own, heads_other], [])

    def ring_add(k, moving):
        cut = slice(k * depth, (k + 1) * depth)
        total = heads_own_grad[cut].astype(F32) + heads_other[cut].astype(F32)
        return total if moving is None else total + moving.astype(F32)

    own_got = cross_once("both", back_own[:-1])
    message = ring_add(1, None).astype(BF)
    moving = ring.send(message)
    back_sib = rows_back(
        blocks, order, split("both"), lefts, [heads_cols, fc1_cols], 1, "normed_back_half", unit=unit,
        after=[message],
    )
    n = len(back_sib)
    *joined, moving = tie([*back_sib, *own_got, moving], [])
    back_sib, own_got = joined[:n], joined[n:]
    sib_got = cross_once("both", back_sib[:-1])
    own_sums = cross_add(back_own[:-1], own_got)
    own_last = cross_twice("both", own_sums)
    message = ring_add(2, moving).astype(BF) if chips > 2 else None
    for k in range(2, chips):
        moving = ring.send(message if k == 2 else ring_add(k, moving).astype(BF))
    layer_output = add_branch(blocks, x, branch_terms, bias_out, after=[back_sib[0], *own_sums])
    layer_output, *sib_got = tie([layer_output, *sib_got], [])
    sib_last = cross_twice("both", cross_add(back_sib[:-1], sib_got))
    heads_sums = ring_add(0, moving)
    back_terms = cross_terms(back_own[:-1], own_got, own_last) + cross_terms(back_sib[:-1], sib_got, sib_last)
    input_grad = norm_back(blocks, x, g, back_terms, gain)

    w_qkv_grad = heads_sums.reshape(depth, 3, inner)
    w_out_grad = fc2_sums[:, units:].T.astype(F32)
    w_fc1_grad = fc1_sums.astype(F32)
    w_fc2_grad = fc2_sums[:, :units].T.astype(F32)

    norm_sums = jnp.concatenate([back_own[-1][:2], back_sib[-1][:2]], axis=1).reshape(2, n_dp, depth)
    norm_sums = jnp.einsum("pd,kpj->kdj", chosen, norm_sums, precision=lax.Precision.HIGHEST)
    vector_sums = jnp.concatenate([norm_sums.reshape(2, width), bias_part[:1]], axis=0)
    vector_sums = flip_sums(vector_sums, "tensor", n_tensor)[-1]
    unit_sums = jnp.concatenate(
        [
            vector_sums.reshape(-1),
            jnp.transpose(backs[3][:, :3, :], (1, 0, 2)).reshape(-1),
            b_fc1_part[0],
        ]
    )
    unit_sums = flip_sums(unit_sums, "dp", n_dp)[-1]
    mine = unit_sums[: 3 * width].reshape(3, n_dp * n_tensor, third)
    mine = lax.dynamic_index_in_dim(mine, d_index * n_tensor + t_index, 1, keepdims=False)
    b_width = HD // n_dp
    b_qkv_grad = lax.dynamic_slice_in_dim(
        unit_sums[3 * width : 3 * width + 3 * inner].reshape(3, heads, HD), d_index * b_width, b_width, 2
    )
    b_fc1_grad = lax.dynamic_slice_in_dim(
        unit_sums[3 * width + 3 * inner :].reshape(units // HD, HD), d_index * b_width, b_width, 1
    )
    return (
        layer_output[None],
        input_grad[None],
        mine[0],
        mine[1],
        mine[2],
        w_qkv_grad,
        b_qkv_grad,
        w_out_grad,
        w_fc1_grad,
        b_fc1_grad,
        w_fc2_grad,
    )


def solution(mesh):
    in_specs = (
        P("dp", "tensor", None),
        P(("dp", "tensor")),
        P(("dp", "tensor")),
        P(("dp", "tensor")),
        P("dp", None, "tensor"),
        P(None, "tensor", "dp"),
        P("tensor", "dp"),
        P("dp", "tensor"),
        P("tensor", "dp"),
        P("tensor", "dp"),
        P("dp", "tensor", None),
    )
    out_specs = (
        P("dp", "tensor", None),
        P("dp", "tensor", None),
        P(("dp", "tensor")),
        P(("dp", "tensor")),
        P(("dp", "tensor")),
        P("dp", None, "tensor"),
        P(None, "tensor", "dp"),
        P("tensor", "dp"),
        P("dp", "tensor"),
        P("tensor", "dp"),
        P("tensor", "dp"),
    )
    sizes = (mesh.shape["dp"], mesh.shape["tensor"])
    return jax.shard_map(
        functools.partial(per_device, sizes),
        mesh=mesh,
        in_specs=in_specs,
        out_specs=out_specs,
        check_vma=False,
    )
```

time: 878 us -> 666 us (0.76)
  waiting for transfers between devices: 349 us -> 126 us
  starting transfers between devices: 18.3 us -> 36.7 us
    ppermute x34 -> x43, waiting for transfers between devices: 348 us -> 126 us  [the longest x34 92.1 us: flip(): return lax.ppermute(value, axis, [(i, i ^ bit) for i in range(size)])]
    ppermute x34 -> x43, starting transfers between devices: 18 us -> 36.3 us  [the longest x34 30.5 us: flip(): return lax.ppermute(value, axis, [(i, i ^ bit) for i in range(size)])]
    concatenate x5 -> x1, local copies, waits for them, and re-layouts: 13.2 us -> 0.08 us  [per_device(): jnp.concatenate([tables_small[-1].reshape(-1), b_qkv.astype(F32).reshape(...]
    unnamed x49 -> x110, local copies, waits for them, and re-layouts: 14.9 us -> 25.3 us
    pallas_call x19 -> x32, Pallas kernels: 403 us -> 407 us  [the longest x21 407 us: call(): pl.pallas_call(body, name=name, grid_spec=pltpu.PrefetchScalarGridSpec(nu...]
    convert_element_type x9 -> x12, other arithmetic: 18.2 us -> 20.8 us  [the longest x6 8.65 us: cross_add(): (k[local:].astype(F32) + r[local:].astype(F32)).astype(BF)]
  transfers between devices with their start and end apart: 40 -> 47, of which waited for: 20 -> 13; matrix products, arithmetic and copies ran while one was open for 9% -> 8% of each run, Pallas kernels for 39% -> 60%
where the time goes in v2:
time: 666 us; the launch traced here: 658 us
  Pallas kernels  407 us (61%)
  waiting for transfers between devices  126 us (19%)
  local copies, waits for them, and re-layouts  37.3 us (6%)
  starting transfers between devices  36.7 us (6%)
  other arithmetic  35.6 us (5%)
  between operations  15 us (2%)
    pallas_call x21, Pallas kernels, call(): pl.pallas_call(body, name=name, grid_spec=pltpu.PrefetchScalarGridSpec(nu...  407 us
    ppermute x34, waiting for transfers between devices, flip(): return lax.ppermute(value, axis, [(i, i ^ bit) for i in range(size)])  92.1 us
    ppermute x9, waiting for transfers between devices, send(): return lax.ppermute(value, 'dp', pairs)  34.3 us
    ppermute x34, starting transfers between devices, flip(): return lax.ppermute(value, axis, [(i, i ^ bit) for i in range(size)])  30.5 us
    unnamed x110, local copies, waits for them, and re-layouts  25.3 us
  transfers between devices with their start and end apart: 47, of which 13 were waited for; matrix products, arithmetic and copies ran while one was open for 8% of the time, Pallas kernels for 60%

profile of v2, /device:TPU:0, one launch (start us, length us, event | category | flops | bytes accessed | tf_op | source)
XLA Modules:
  0.0 657.9 jit_solution(13136624205519729029)
XLA Ops:
  7.2 1.4 copy.70
  10.5 3.4 order_columns.2
  13.9 2.5 heads_shard.1.refs_15_.refs_2_.refs_5_.refs_7_
  16.4 3.1 collective-permute-start
  19.5 1.6 fusion.25
  21.0 1.5 collective-permute-start.1
  22.5 1.5 collective-permute-start.2
  24.8 22.2 %collective-permute-done.3 = f32[4,192]{1,0:T(4,128)S(1)} collective-permute-done((f32[4,192]{1,0:T(4,128)S(1)}, f32[4,192]{1,0:T(4,128)S(1)}, u32[]{:S(2)}, u32[]{:S(2)}) %collective-permute-start.3) | collective-permute-done | bytes 3104 | tf_op jit(solution)/shard_map/ppermute | solution.py:842
  47.0 1.5 collective-permute-start.4
  48.8 1.8 collective-permute-done.4
  53.1 1.6 collective-permute-start.6
  54.7 1.5 collective-permute-start.7
  56.2 1.5 collective-permute-start.8
  57.8 1.6 collective-permute-start.10
  59.4 5.0 fusion.1
  64.5 16.6 %collective-permute-done.10 = f32[8,1216]{1,0:T(8,128)S(1)} collective-permute-done((f32[8,1216]{1,0:T(8,128)S(1)}, f32[8,1216]{1,0:T(8,128)S(1)}, u32[]{:S(2)}, u32[]{:S(2)}) %collective-permute-start.10) | collective-permute-done | bytes 38944 | tf_op jit(solution)/shard_map/ppermute | solution.py:842
  81.8 1.5 collective-permute-start.13
  85.0 1.4 collective-permute-start.14
  87.6 26.0 %collective-permute-done.15 = f32[8,1216]{1,0:T(8,128)S(1)} collective-permute-done((f32[8,1216]{1,0:T(8,128)S(1)}, f32[8,1216]{1,0:T(8,128)S(1)}, u32[]{:S(2)}, u32[]{:S(2)}) %collective-permute-start.15) | collective-permute-done | bytes 38944 | tf_op jit(solution)/shard_map/ppermute | solution.py:842
  116.9 3.4 order_columns.3
  123.6 2.4 stage_weight.2.refs_23_
  127.1 29.8 %norm_project.1 = (bf16[2048,2048]{1,0:T(8,128)(2,1)}, bf16[2048,2048]{1,0:T(8,128)(2,1)}, bf16[2048,1536]{1,0:T(8,128)(2,1)}) custom-call(s32[8]{0:T(128)} %pad_add_fusion.refs_0_, s32[8]{0:T(128)} %fusion.10.refs_1_, bf16[512,2048]{1,0:T(8,128)(2,1)} %get-tuple-element.79.refs_2_.refs_1_, bf16[256,2048]{1,0:T(8,128)(2,1)} %get-tuple-element.80.refs_3_, ...), custom_call_target="tpu_custom_call" | custom-call | flops 19327352832 | bytes 37748736 | tf_op jit(solution)/shard_map/norm_project/pallas_call | solution.py:35
  158.8 20.1 %attend.2 = (bf16[2048,512]{1,0:T(8,128)(2,1)}, f32[2,2,2048]{2,1,0:T(2,128)}) custom-call(bf16[2048,1536]{1,0:T(8,128)(2,1)} %get-tuple-element.91.refs_1_.refs_0_.refs_2_, bf16[2048,1536]{1,0:T(8,128)(2,1)} %get-tuple-element.91.refs_1_.refs_0_.refs_2_, bf16[2048,1536]{1,0:T(8,128)(2,1)} %get-tuple-element.91.refs_1_.refs_0_.refs_2_, ...), custom_call_target="tpu_custom_call" | custom-call | flops 42949672960 | bytes 4194304 | tf_op jit(solution)/shard_map/attend/pallas_call | solution.py:35
  178.9 7.0 %collective-permute-done.19.refs_0_ = bf16[256,2048]{1,0:T(8,128)(2,1)S(1)} collective-permute-done((bf16[256,2048]{1,0:T(8,128)(2,1)}, bf16[256,2048]{1,0:T(8,128)(2,1)S(1)}, u32[]{:S(2)}, u32[]{:S(2)}) %collective-permute-start.19) | collective-permute-done | bytes 1048608 | tf_op jit(solution)/shard_map/ppermute | solution.py:866
  187.0 19.8 %attend.3 = (bf16[2048,512]{1,0:T(8,128)(2,1)}, f32[2,2,2048]{2,1,0:T(2,128)}) custom-call(bf16[2048,1536]{1,0:T(8,128)(2,1)} %get-tuple-element.91.refs_1_.refs_0_.refs_2_, bf16[2048,1536]{1,0:T(8,128)(2,1)} %get-tuple-element.91.refs_1_.refs_0_.refs_2_, ...), custom_call_target="tpu_custom_call", output_to_operand_aliasing={{0}: (3, {})} | custom-call | flops 42949672960 | bytes 4194304 | tf_op jit(solution)/shard_map/attend/pallas_call | solution.py:35
  206.9 6.9 %collective-permute-done.20.refs_0_ = bf16[256,2048]{1,0:T(8,128)(2,1)S(1)} collective-permute-done((bf16[256,2048]{1,0:T(8,128)(2,1)}, bf16[256,2048]{1,0:T(8,128)(2,1)S(1)}, u32[]{:S(2)}, u32[]{:S(2)}) %collective-permute-start.20) | collective-permute-done | bytes 1048608 | tf_op jit(solution)/shard_map/ppermute | solution.py:866
  214.7 3.4 pad_maximum_fusion.refs_1_.refs_2_.refs_15_
  218.1 2.5 stage_weight.3.refs_10_
  222.0 10.7 %context_back.1.refs_5_.refs_4_ = bf16[2048,512]{1,0:T(8,128)(2,1)} custom-call(s32[8]{0:T(128)} %pad_add_fusion.refs_0_, bf16[2048,2048]{1,0:T(8,128)(2,1)} %all-gather.3.cloned.1.call-done.refs_1_, bf16[256,2048]{1,0:T(8,128)(2,1)} %heads_shard.1.refs_15_.refs_2_.refs_5_.refs_7_, bf16[256,2048]{1,0:T(8,128)(2,1)} %get-tuple-element.81.refs_16_.refs_3_.refs_6_.refs_8_, ...), custom_call_target="tpu_custom_call" | custom-call | flops 4294967296 | bytes 14680064 | tf_op jit(solution)/shard_map/context_back/pallas_call | solution.py:35
  232.8 31.8 %expand.1 = (bf16[2048,2048]{1,0:T(8,128)(2,1)}, bf16[2048,2048]{1,0:T(8,128)(2,1)}) custom-call(s32[8]{0:T(128)} %pad_add_fusion.refs_0_, bf16[2048,2048]{1,0:T(8,128)(2,1)} %get-tuple-element.90.refs_1_.refs_0_, bf16[1024,2048]{1,0:T(8,128)(2,1)} %pad_maximum_fusion.refs_1_.refs_2_.refs_15_, bf16[1024,2048]{1,0:T(8,128)(2,1)} %collective-permute-done.21.refs_3_.refs_16_, ...), custom_call_target="tpu_custom_call" | custom-call | flops 17179869184 | bytes 33554432 | tf_op jit(solution)/shard_map/expand/pallas_call | solution.py:35
  264.6 32.2 %fc2_grad.1 = bf16[2048,2560]{1,0:T(8,128)(2,1)} custom-call(s32[8]{0:T(128)} %pad_add_fusion.refs_0_, bf16[2048,2048]{1,0:T(8,128)(2,1)} %all-gather.3.cloned.1.call-done.refs_1_, bf16[2048,2048]{1,0:T(8,128)(2,1)} %get-tuple-element.96.refs_9_.refs_2_, bf16[2048,512]{1,0:T(8,128)(2,1)} %get-tuple-element.97.refs_3_), custom_call_target="tpu_custom_call" | custom-call | flops 21474836480 | bytes 39845888 | tf_op jit(solution)/shard_map/fc2_grad/pallas_call | solution.py:35
  298.6 65.5 %attend_back.1 = (bf16[2048,512]{1,0:T(8,128)(2,1)}, bf16[2048,512]{1,0:T(8,128)(2,1)}, bf16[2048,512]{1,0:T(8,128)(2,1)}, f32[4,8,128]{2,1,0:T(8,128)}) custom-call(bf16[2048,1536]{1,0:T(8,128)(2,1)} %get-tuple-element.91.refs_1_.refs_0_.refs_2_, bf16[2048,1536]{1,0:T(8,128)(2,1)} %get-tuple-element.91.refs_1_.refs_0_.refs_2_, ...), custom_call_target="tpu_custom_call" | custom-call | flops 128849018880 | bytes 16777216 | tf_op jit(solution)/shard_map/attend_back/pallas_call | solution.py:35
  364.2 19.2 %branch_half.2 = (bf16[1024,1024]{1,0:T(8,128)(2,1)}, bf16[1024,1024]{1,0:T(8,128)(2,1)}) custom-call(s32[8]{0:T(128)} %pad_add_fusion.refs_0_, s32[4]{0:T(128)} %broadcast_xor_fusion.refs_1_, bf16[2048,2048]{1,0:T(8,128)(2,1)} %get-tuple-element.96.refs_9_.refs_2_, bf16[2048,512]{1,0:T(8,128)(2,1)} %get-tuple-element.97.refs_3_, ...), custom_call_target="tpu_custom_call" | custom-call | flops 10737418240 | bytes 19922944 | tf_op jit(solution)/shard_map/branch_half/pallas_call | solution.py:35
  383.3 1.6 collective-permute-start.22
  385.0 19.2 %branch_half.3 = (bf16[1024,1024]{1,0:T(8,128)(2,1)}, bf16[1024,1024]{1,0:T(8,128)(2,1)}) custom-call(s32[8]{0:T(128)} %pad_add_fusion.refs_0_, s32[4]{0:T(128)} %broadcast_xor_fusion.refs_1_, bf16[2048,2048]{1,0:T(8,128)(2,1)} %get-tuple-element.96.refs_9_.refs_2_, bf16[2048,512]{1,0:T(8,128)(2,1)} %get-tuple-element.97.refs_3_, ...), custom_call_target="tpu_custom_call" | custom-call | flops 10737418240 | bytes 19922944 | tf_op jit(solution)/shard_map/branch_half/pallas_call | solution.py:35
  404.8 26.6 %hidden_back.1 = (bf16[2048,2048]{1,0:T(8,128)(2,1)}, f32[8,2048]{1,0:T(8,128)}) custom-call(s32[8]{0:T(128)} %pad_add_fusion.refs_0_, bf16[2048,2048]{1,0:T(8,128)(2,1)} %all-gather.3.cloned.1.call-done.refs_1_, bf16[2048,2048]{1,0:T(8,128)(2,1)} %all-gather.5.cloned.1.call-done.refs_4_.refs_2_, bf16[2048,2048]{1,0:T(8,128)(2,1)} %get-tuple-element.100.refs_3_, ...), custom_call_target="tpu_custom_call" | custom-call | flops 17179869184 | bytes 33554432 | tf_op jit(solution)/shard_map/hidden_back/pallas_call | solution.py:35
  431.4 25.9 %fc1_grad.1.refs_0_ = bf16[2048,2048]{1,0:T(8,128)(2,1)} custom-call(s32[8]{0:T(128)} %pad_add_fusion.refs_0_, bf16[2048,2048]{1,0:T(8,128)(2,1)} %get-tuple-element.90.refs_1_.refs_0_, bf16[2048,2048]{1,0:T(8,128)(2,1)} %get-tuple-element.104.refs_2_.refs_5_), custom_call_target="tpu_custom_call" | custom-call | flops 17179869184 | bytes 33554432 | tf_op jit(solution)/shard_map/fc1_grad/pallas_call | solution.py:35
  457.3 1.3 copy-done.1
  458.7 2.1 add_convert_fusion.refs_6_
  461.9 1.5 collective-permute-start.24
  463.4 20.8 %heads_grad.1 = (bf16[1024,1536]{1,0:T(8,128)(2,1)}, bf16[1024,1536]{1,0:T(8,128)(2,1)}) custom-call(bf16[2048,2048]{1,0:T(8,128)(2,1)} %get-tuple-element.90.refs_1_.refs_0_, bf16[2048,512]{1,0:T(8,128)(2,1)} %get-tuple-element.98.refs_13_.refs_1_.refs_2_, bf16[2048,512]{1,0:T(8,128)(2,1)} %get-tuple-element.106.refs_2_.refs_3_, ...), custom_call_target="tpu_custom_call" | custom-call | flops 12884901888 | bytes 27262976 | tf_op jit(solution)/shard_map/heads_grad/pallas_call | solution.py:35
  484.2 1.7 collective-permute-done.25.refs_3_
  488.9 27.6 %normed_back_half.2 = (bf16[1024,512]{1,0:T(8,128)(2,1)}, bf16[1024,512]{1,0:T(8,128)(2,1)}, bf16[1024,512]{1,0:T(8,128)(2,1)}, bf16[1024,512]{1,0:T(8,128)(2,1)}, f32[8,1024]{1,0:T(8,128)}) custom-call(s32[8]{0:T(128)} %pad_add_fusion.refs_0_, s32[4]{0:T(128)} %broadcast_xor_fusion.refs_1_, bf16[2048,512]{1,0:T(8,128)(2,1)} %get-tuple-element.98.refs_13_.refs_1_.refs_2_, ...), custom_call_target="tpu_custom_call" | custom-call | flops 15032385536 | bytes 26214400 | tf_op jit(solution)/shard_map/normed_back_half/pallas_call | solution.py:35
  516.5 1.7 copy-done.3
  518.2 1.7 add_convert_fusion.4.refs_17_
  523.0 27.8 %normed_back_half.3 = (bf16[1024,512]{1,0:T(8,128)(2,1)}, bf16[1024,512]{1,0:T(8,128)(2,1)}, bf16[1024,512]{1,0:T(8,128)(2,1)}, bf16[1024,512]{1,0:T(8,128)(2,1)}, f32[8,1024]{1,0:T(8,128)}) custom-call(s32[8]{0:T(128)} %pad_add_fusion.refs_0_, s32[4]{0:T(128)} %broadcast_xor_fusion.refs_1_, bf16[2048,512]{1,0:T(8,128)(2,1)} %get-tuple-element.98.refs_13_.refs_1_.refs_2_, ...), custom_call_target="tpu_custom_call" | custom-call | flops 15032385536 | bytes 26214400 | tf_op jit(solution)/shard_map/normed_back_half/pallas_call | solution.py:35
  550.8 8.1 %collective-permute-done.29.refs_7_ = bf16[256,1536]{1,0:T(8,128)(2,1)S(1)} collective-permute-done((bf16[256,1536]{1,0:T(8,128)(2,1)S(1)}, bf16[256,1536]{1,0:T(8,128)(2,1)S(1)}, u32[]{:S(2)}, u32[]{:S(2)}) %collective-permute-start.29) | collective-permute-done | bytes 786464 | tf_op jit(solution)/shard_map/ppermute | solution.py:866
  561.7 1.2 collective-permute-start.36
  563.5 2.2 collective-permute-done.36
  567.7 2.1 collective-permute-done.37
  569.9 2.7 add_convert_fusion.3
  576.7 18.4 %collective-permute-done.39 = f32[9728]{0:T(1024)S(1)} collective-permute-done((f32[9728]{0:T(1024)S(1)}, f32[9728]{0:T(1024)S(1)}, u32[]{:S(2)}, u32[]{:S(2)}) %collective-permute-start.39) | collective-permute-done | bytes 38944 | tf_op jit(solution)/shard_map/ppermute | solution.py:842
  596.9 6.6 %add_branch.1.refs_0_ = bf16[512,2048]{1,0:T(8,128)(2,1)} custom-call(s32[8]{0:T(128)} %pad_add_fusion.refs_0_, bf16[512,2048]{1,0:T(8,128)(2,1)} %get-tuple-element.79.refs_2_.refs_1_, bf16[1024,1024]{1,0:T(8,128)(2,1)} %get-tuple-element.99.refs_14_.refs_2_, bf16[1024,1024]{1,0:T(8,128)(2,1)} %get-tuple-element.105.refs_3_, ...), custom_call_target="tpu_custom_call" | custom-call | bytes 10485760 | tf_op jit(solution)/shard_map/add_branch/pallas_call | solution.py:35
  604.7 2.5 add_convert_fusion.2
  609.3 2.1 add_convert_fusion.5
  612.6 2.1 add_convert_fusion.6
  615.7 12.3 %collective-permute-done.42 = bf16[256,1536]{1,0:T(8,128)(2,1)} collective-permute-done((bf16[256,1536]{1,0:T(8,128)(2,1)}, bf16[256,1536]{1,0:T(8,128)(2,1)}, u32[]{:S(2)}, u32[]{:S(2)}) %collective-permute-start.42) | collective-permute-done | bytes 786464 | tf_op jit(solution)/shard_map/ppermute | solution.py:866
  628.0 2.8 convert_add_fusion
  630.8 1.9 copy.78
  632.6 1.6 copy.79
  634.3 8.5 %norm_back.1 = f32[512,2048]{1,0:T(8,128)} custom-call(s32[8]{0:T(128)} %pad_add_fusion.refs_0_, bf16[512,2048]{1,0:T(8,128)(2,1)} %get-tuple-element.79.refs_2_.refs_1_, bf16[512,2048]{1,0:T(8,128)(2,1)} %get-tuple-element.95.refs_2_, bf16[1024,512]{1,0:T(8,128)(2,1)} %get-tuple-element.131.refs_3_, bf16[1024,512]{1,0:T(8,128)(2,1)} %get-tuple-element.132.refs_4_, ...), custom_call_target="tpu_custom_call" | custom-call | bytes 10485760 | tf_op jit(solution)/shard_map/norm_back/pallas_call | solution.py:35
  642.8 1.5 convert_bitcast_fusion
  644.3 1.8 copy.82
  648.1 2.8 convert_element_type.181
  (257 shorter events, 50.1 us)
Async XLA Ops:
  7.2 214.9 %all-gather.3.cloned.1.call-start = ((), (), s32[]{:S(2)}) async-start(), calls=%async_computation.2 | async-start | bytes 10485760 | tf_op jit(solution)/shard_map/all_gather | solution.py:964
  13.9 5.6 copy-start
  16.4 7.7 %copy-start.46 = (bf16[64]{0:T(256)(128)(2,1)S(1)}, bf16[64]{0:T(256)(128)(2,1)}, u32[]{:S(2)}) copy-start(bf16[64]{0:T(256)(128)(2,1)} %param.16) | copy-start | bytes 388
  16.4 7.7 %copy-start.47 = (bf16[64]{0:T(256)(128)(2,1)S(1)}, bf16[64]{0:T(256)(128)(2,1)}, u32[]{:S(2)}) copy-start(bf16[64]{0:T(256)(128)(2,1)} %param.15) | copy-start | bytes 388
  16.4 7.7 %copy-start.48 = (bf16[64]{0:T(256)(128)(2,1)S(1)}, bf16[64]{0:T(256)(128)(2,1)}, u32[]{:S(2)}) copy-start(bf16[64]{0:T(256)(128)(2,1)} %param.14) | copy-start | bytes 388
  16.4 32.2 %copy-start.45 = (bf16[32,8]{0,1:T(8,128)(2,1)S(1)}, bf16[32,8]{0,1:T(8,128)(2,1)}, u32[]{:S(2)}) copy-start(bf16[32,8]{0,1:T(8,128)(2,1)} %param.21) | copy-start | bytes 1540
  16.4 32.3 %copy-start.43 = (bf16[3,8,8]{2,1,0:T(8,128)(2,1)S(1)}, bf16[3,8,8]{2,1,0:T(8,128)(2,1)}, u32[]{:S(2)}) copy-start(bf16[3,8,8]{2,1,0:T(8,128)(2,1)} %param.18) | copy-start | bytes 1156
  16.4 34.6 %collective-permute-start = (bf16[256,2048]{1,0:T(8,128)(2,1)}, bf16[256,2048]{1,0:T(8,128)(2,1)S(1)}, u32[]{:S(2)}, u32[]{:S(2)}) collective-permute-start(bf16[256,2048]{1,0:T(8,128)(2,1)} %heads_shard.1.refs_15_.refs_2_.refs_5_.refs_7_), channel_id=1, source_target_pairs={{0,8},{4,12},{8,16},{12,20},{16,24},{20,28},{24,0},{28,4},{1,9},{5... | collective-permute-start | bytes 3145736 | tf_op jit(solution)/shard_map/ppermute | solution.py:866
  19.5 31.5 %collective-permute-start.5 = (bf16[256,2048]{1,0:T(8,128)(2,1)}, bf16[256,2048]{1,0:T(8,128)(2,1)S(1)}, u32[]{:S(2)}, u32[]{:S(2)}) collective-permute-start(bf16[256,2048]{1,0:T(8,128)(2,1)} %heads_shard.1.refs_15_.refs_2_.refs_5_.refs_7_), channel_id=1, source_target_pairs={{0,4},{4,0},{8,12},{12,8},{16,20},{20,16},{24,28},{28,24},{1,5},{5... | collective-permute-start | bytes 3145736 | tf_op jit(solution)/shard_map/ppermute | solution.py:842
  21.0 30.0 %collective-permute-start.1 = (bf16[256,2048]{1,0:T(8,128)(2,1)}, bf16[256,2048]{1,0:T(8,128)(2,1)}, u32[]{:S(2)}, u32[]{:S(2)}) collective-permute-start(bf16[256,2048]{1,0:T(8,128)(2,1)} %get-tuple-element.169), channel_id=1, source_target_pairs={{0,1},{1,0},{2,3},{3,2},{4,5},{5,4},{6,7},{7,6},{8,9},{9,8},{10,11... | collective-permute-start | bytes 3145736 | tf_op jit(solution)/shard_map/ppermute | solution.py:842
  22.5 28.5 %collective-permute-start.2 = (bf16[256,2048]{1,0:T(8,128)(2,1)}, bf16[256,2048]{1,0:T(8,128)(2,1)S(1)}, u32[]{:S(2)}, u32[]{:S(2)}) collective-permute-start(bf16[256,2048]{1,0:T(8,128)(2,1)} %get-tuple-element.169), channel_id=1, source_target_pairs={{0,2},{1,3},{2,0},{3,1},{4,6},{5,7},{6,4},{7,5},{8,10},{9,11},{10,... | collective-permute-start | bytes 3145736 | tf_op jit(solution)/shard_map/ppermute | solution.py:842
  24.2 22.7 %collective-permute-start.3 = (f32[4,192]{1,0:T(4,128)S(1)}, f32[4,192]{1,0:T(4,128)S(1)}, u32[]{:S(2)}, u32[]{:S(2)}) collective-permute-start(f32[4,192]{1,0:T(4,128)S(1)} %broadcast_select_fusion.1), channel_id=1, source_target_pairs={{0,1},{1,0},{2,3},{3,2},{4,5},{5,4},{6,7},{7,6},{8,9},{9,8},{10,11... | collective-permute-start | bytes 9224 | tf_op jit(solution)/shard_map/ppermute | solution.py:842
  47.0 3.6 collective-permute-start.4
  50.9 6.8 %collective-permute-start.9 = (f32[8,1216]{1,0:T(8,128)S(1)}, f32[8,1216]{1,0:T(8,128)S(1)}, u32[]{:S(2)}, u32[]{:S(2)}) collective-permute-start(f32[8,1216]{1,0:T(8,128)S(1)} %broadcast_select_fusion), channel_id=1, source_target_pairs={{0,4},{4,0},{8,12},{12,8},{16,20},{20,16},{24,28},{28,24},{1,5},{5... | collective-permute-start | bytes 116744 | tf_op jit(solution)/shard_map/ppermute | solution.py:842
  52.6 30.7 %collective-permute-start.11 = (bf16[256,2048]{1,0:T(8,128)(2,1)}, bf16[256,2048]{1,0:T(8,128)(2,1)S(1)}, u32[]{:S(2)}, u32[]{:S(2)}) collective-permute-start(bf16[256,2048]{1,0:T(8,128)(2,1)} %get-tuple-element.81.refs_16_.refs_3_.refs_6_.refs_8_), channel_id=1, source_target_pairs={{0,4},{4,0},{8,12},{12,8},{16,20},{20,16},{24,28},{28,24},{1,5},{5... | collective-permute-start | bytes 3145736 | tf_op jit(solution)/shard_map/ppermute | solution.py:842
  53.1 30.2 %collective-permute-start.6 = (bf16[256,2048]{1,0:T(8,128)(2,1)}, bf16[256,2048]{1,0:T(8,128)(2,1)S(1)}, u32[]{:S(2)}, u32[]{:S(2)}) collective-permute-start(bf16[256,2048]{1,0:T(8,128)(2,1)} %get-tuple-element.81.refs_16_.refs_3_.refs_6_.refs_8_), channel_id=1, source_target_pairs={{0,8},{4,12},{8,16},{12,20},{16,24},{20,28},{24,0},{28,4},{1,9},{5... | collective-permute-start | bytes 3145736 | tf_op jit(solution)/shard_map/ppermute | solution.py:866
  54.7 28.6 %collective-permute-start.7 = (bf16[256,2048]{1,0:T(8,128)(2,1)}, bf16[256,2048]{1,0:T(8,128)(2,1)S(1)}, u32[]{:S(2)}, u32[]{:S(2)}) collective-permute-start(bf16[256,2048]{1,0:T(8,128)(2,1)} %get-tuple-element.82), channel_id=1, source_target_pairs={{0,1},{1,0},{2,3},{3,2},{4,5},{5,4},{6,7},{7,6},{8,9},{9,8},{10,11... | collective-permute-start | bytes 3145736 | tf_op jit(solution)/shard_map/ppermute | solution.py:842
  56.2 27.1 %collective-permute-start.8 = (bf16[256,2048]{1,0:T(8,128)(2,1)}, bf16[256,2048]{1,0:T(8,128)(2,1)}, u32[]{:S(2)}, u32[]{:S(2)}) collective-permute-start(bf16[256,2048]{1,0:T(8,128)(2,1)} %get-tuple-element.82), channel_id=1, source_target_pairs={{0,2},{1,3},{2,0},{3,1},{4,6},{5,7},{6,4},{7,5},{8,10},{9,11},{10,... | collective-permute-start | bytes 3145736 | tf_op jit(solution)/shard_map/ppermute | solution.py:842
  57.8 23.3 %collective-permute-start.10 = (f32[8,1216]{1,0:T(8,128)S(1)}, f32[8,1216]{1,0:T(8,128)S(1)}, u32[]{:S(2)}, u32[]{:S(2)}) collective-permute-start(f32[8,1216]{1,0:T(8,128)S(1)} %fusion.4), channel_id=1, source_target_pairs={{0,8},{4,12},{8,0},{12,4},{16,24},{20,28},{24,16},{28,20},{1,9},{5... | collective-permute-start | bytes 116744 | tf_op jit(solution)/shard_map/ppermute | solution.py:842
  81.8 33.4 %collective-permute-start.13 = (bf16[256,2048]{1,0:T(8,128)(2,1)}, bf16[256,2048]{1,0:T(8,128)(2,1)}, u32[]{:S(2)}, u32[]{:S(2)}) collective-permute-start(bf16[256,2048]{1,0:T(8,128)(2,1)} %get-tuple-element.80.refs_3_), channel_id=1, source_target_pairs={{0,2},{1,3},{2,0},{3,1},{4,6},{5,7},{6,4},{7,5},{8,10},{9,11},{10,... | collective-permute-start | bytes 3145736 | tf_op jit(solution)/shard_map/ppermute | solution.py:842
  85.0 28.9 %copy-start.41 = (s32[8]{0:T(128)S(1)}, s32[8]{0:T(128)}, u32[]{:S(2)}) copy-start(s32[8]{0:T(128)} %pad_add_fusion.refs_0_) | copy-start | bytes 100
  85.0 30.3 %collective-permute-start.12 = (bf16[256,2048]{1,0:T(8,128)(2,1)}, bf16[256,2048]{1,0:T(8,128)(2,1)S(1)}, u32[]{:S(2)}, u32[]{:S(2)}) collective-permute-start(bf16[256,2048]{1,0:T(8,128)(2,1)} %get-tuple-element.86.refs_17_.refs_4_.refs_7_.refs_9_), channel_id=1, source_target_pairs={{0,8},{4,12},{8,16},{12,20},{16,24},{20,28},{24,0},{28,4},{1,9},{5... | collective-permute-start | bytes 3145736 | tf_op jit(solution)/shard_map/ppermute | solution.py:866
  85.0 30.3 %collective-permute-start.14 = (bf16[256,2048]{1,0:T(8,128)(2,1)}, bf16[256,2048]{1,0:T(8,128)(2,1)S(1)}, u32[]{:S(2)}, u32[]{:S(2)}) collective-permute-start(bf16[256,2048]{1,0:T(8,128)(2,1)} %get-tuple-element.85.refs_6_), channel_id=1, source_target_pairs={{0,1},{1,0},{2,3},{3,2},{4,5},{5,4},{6,7},{7,6},{8,9},{9,8},{10,11... | collective-permute-start | bytes 3145736 | tf_op jit(solution)/shard_map/ppermute | solution.py:842
  86.4 28.9 %collective-permute-start.16 = (bf16[256,2048]{1,0:T(8,128)(2,1)}, bf16[256,2048]{1,0:T(8,128)(2,1)S(1)}, u32[]{:S(2)}, u32[]{:S(2)}) collective-permute-start(bf16[256,2048]{1,0:T(8,128)(2,1)} %get-tuple-element.86.refs_17_.refs_4_.refs_7_.refs_9_), channel_id=1, source_target_pairs={{0,4},{4,0},{8,12},{12,8},{16,20},{20,16},{24,28},{28,24},{1,5},{5... | collective-permute-start | bytes 3145736 | tf_op jit(solution)/shard_map/ppermute | solution.py:842
  86.4 27.2 %collective-permute-start.15 = (f32[8,1216]{1,0:T(8,128)S(1)}, f32[8,1216]{1,0:T(8,128)S(1)}, u32[]{:S(2)}, u32[]{:S(2)}) collective-permute-start(f32[8,1216]{1,0:T(8,128)S(1)} %copy-done.36), channel_id=1, source_target_pairs={{0,16},{4,20},{8,24},{12,28},{16,0},{20,4},{24,8},{28,12},{1,17},{... | collective-permute-start | bytes 116744 | tf_op jit(solution)/shard_map/ppermute | solution.py:842
  120.4 243.8 %all-gather.5.cloned.1.call-start = ((), (), s32[]{:S(2)}) async-start(), calls=%async_computation.3 | async-start | bytes 9437184 | tf_op jit(solution)/shard_map/all_gather | solution.py:1004
  121.6 4.5 collective-permute-start.17
  126.0 30.9 %collective-permute-start.18 = (bf16[256,2048]{1,0:T(8,128)(2,1)}, bf16[256,2048]{1,0:T(8,128)(2,1)S(1)}, u32[]{:S(2)}, u32[]{:S(2)}) collective-permute-start(bf16[256,2048]{1,0:T(8,128)(2,1)} %stage_weight.2.refs_23_), channel_id=1, source_target_pairs={{0,8},{4,12},{8,16},{12,20},{16,24},{20,28},{24,0},{28,4},{1,9},{5... | collective-permute-start | bytes 3145736 | tf_op jit(solution)/shard_map/ppermute | solution.py:866
  157.9 28.0 %collective-permute-start.19 = (bf16[256,2048]{1,0:T(8,128)(2,1)}, bf16[256,2048]{1,0:T(8,128)(2,1)S(1)}, u32[]{:S(2)}, u32[]{:S(2)}) collective-permute-start(bf16[256,2048]{1,0:T(8,128)(2,1)} %tie.14.refs_3_), channel_id=1, source_target_pairs={{0,8},{4,12},{8,16},{12,20},{16,24},{20,28},{24,0},{28,4},{1,9},{5... | collective-permute-start | bytes 3145736 | tf_op jit(solution)/shard_map/ppermute | solution.py:866
  186.9 26.9 %collective-permute-start.20 = (bf16[256,2048]{1,0:T(8,128)(2,1)}, bf16[256,2048]{1,0:T(8,128)(2,1)S(1)}, u32[]{:S(2)}, u32[]{:S(2)}) collective-permute-start(bf16[256,2048]{1,0:T(8,128)(2,1)} %tie.15.refs_4_), channel_id=1, source_target_pairs={{0,8},{4,12},{8,16},{12,20},{16,24},{20,28},{24,0},{28,4},{1,9},{5... | collective-permute-start | bytes 3145736 | tf_op jit(solution)/shard_map/ppermute | solution.py:866
  206.8 7.9 %copy-start.20 = (bf16[256,2048]{1,0:T(8,128)(2,1)S(1)}, bf16[256,2048]{1,0:T(8,128)(2,1)}, u32[]{:S(2)}) copy-start(bf16[256,2048]{1,0:T(8,128)(2,1)} %stage_weight.2.refs_23_) | copy-start | bytes 3145732
  206.8 7.9 %copy-start.25 = (bf16[256,2048]{1,0:T(8,128)(2,1)S(1)}, bf16[256,2048]{1,0:T(8,128)(2,1)}, u32[]{:S(2)}) copy-start(bf16[256,2048]{1,0:T(8,128)(2,1)} %tie.15.refs_4_) | copy-start | bytes 3145732
  220.7 422.1 %reduce-scatter.3.cloned.1.call-start = ((), (), s32[]{:S(2)}) async-start(), calls=%async_computation.4 | async-start | bytes 11796480 | tf_op jit(solution)/shard_map/reduce_scatter | solution.py:1009
  221.0 11.8 %collective-permute-start.21 = (bf16[1024,2048]{1,0:T(8,128)(2,1)}, bf16[1024,2048]{1,0:T(8,128)(2,1)}, u32[]{:S(2)}, u32[]{:S(2)}) collective-permute-start(bf16[1024,2048]{1,0:T(8,128)(2,1)} %pad_maximum_fusion.refs_1_.refs_2_.refs_15_), channel_id=1, source_target_pairs={{0,4},{4,0},{8,12},{12,8},{16,20},{20,16},{24,28},{28,24},{1,5},{5... | collective-permute-start | bytes 12582920 | tf_op jit(solution)/shard_map/ppermute | solution.py:842
  296.8 351.3 %reduce-scatter.5.cloned.1.call-start = ((), (), s32[]{:S(2)}) async-start(), calls=%async_computation.5 | async-start | bytes 9437184 | tf_op jit(solution)/shard_map/reduce_scatter | solution.py:1009
  383.3 73.9 %collective-permute-start.22 = (bf16[1024,1024]{1,0:T(8,128)(2,1)}, bf16[1024,1024]{1,0:T(8,128)(2,1)S(1)}, u32[]{:S(2)}, u32[]{:S(2)}) collective-permute-start(bf16[1024,1024]{1,0:T(8,128)(2,1)} %get-tuple-element.101.refs_13_), channel_id=1, source_target_pairs={{0,1},{1,0},{2,3},{3,2},{4,5},{5,4},{6,7},{7,6},{8,9},{9,8},{10,11... | collective-permute-start | bytes 6291464 | tf_op jit(solution)/shard_map/ppermute | solution.py:842
  404.2 53.1 %collective-permute-start.23 = (bf16[1024,1024]{1,0:T(8,128)(2,1)}, bf16[1024,1024]{1,0:T(8,128)(2,1)}, u32[]{:S(2)}, u32[]{:S(2)}) collective-permute-start(bf16[1024,1024]{1,0:T(8,128)(2,1)} %get-tuple-element.102.refs_4_), channel_id=1, source_target_pairs={{0,2},{1,3},{2,0},{3,1},{4,6},{5,7},{6,4},{7,5},{8,10},{9,11},{10,... | collective-permute-start | bytes 6291464 | tf_op jit(solution)/shard_map/ppermute | solution.py:842
  460.8 25.2 %collective-permute-start.25 = (bf16[512,1024]{1,0:T(8,128)(2,1)S(1)}, bf16[512,1024]{1,0:T(8,128)(2,1)S(1)}, u32[]{:S(2)}, u32[]{:S(2)}) collective-permute-start(bf16[512,1024]{1,0:T(8,128)(2,1)S(1)} %add_convert_fusion.refs_6_), channel_id=1, source_target_pairs={{0,1},{1,0},{2,3},{3,2},{4,5},{5,4},{6,7},{7,6},{8,9},{9,8},{10,11... | collective-permute-start | bytes 3145736 | tf_op jit(solution)/shard_map/ppermute | solution.py:842
  461.9 25.2 %collective-permute-start.24 = (bf16[512,1024]{1,0:T(8,128)(2,1)S(1)}, bf16[512,1024]{1,0:T(8,128)(2,1)S(1)}, u32[]{:S(2)}, u32[]{:S(2)}) collective-permute-start(bf16[512,1024]{1,0:T(8,128)(2,1)S(1)} %add_convert_fusion.1.refs_5_), channel_id=1, source_target_pairs={{0,2},{1,3},{2,0},{3,1},{4,6},{5,7},{6,4},{7,5},{8,10},{9,11},{10,... | collective-permute-start | bytes 3145736 | tf_op jit(solution)/shard_map/ppermute | solution.py:842
  488.0 28.5 %collective-permute-start.26 = (bf16[1024,1536]{1,0:T(8,128)(2,1)}, bf16[1024,1536]{1,0:T(8,128)(2,1)S(1)}, u32[]{:S(2)}, u32[]{:S(2)}) collective-permute-start(bf16[1024,1536]{1,0:T(8,128)(2,1)} %get-tuple-element.121), channel_id=1, source_target_pairs={{0,4},{4,0},{8,12},{12,8},{16,20},{20,16},{24,28},{28,24},{1,5},{5... | collective-permute-start | bytes 9437192 | tf_op jit(solution)/shard_map/ppermute | solution.py:842
  518.2 3.0 copy-start.31
  519.9 3.1 copy-start.35
  519.9 39.0 %collective-permute-start.29 = (bf16[256,1536]{1,0:T(8,128)(2,1)S(1)}, bf16[256,1536]{1,0:T(8,128)(2,1)S(1)}, u32[]{:S(2)}, u32[]{:S(2)}) collective-permute-start(bf16[256,1536]{1,0:T(8,128)(2,1)S(1)} %add_convert_fusion.4.refs_17_), channel_id=1, source_target_pairs={{0,8},{4,12},{8,16},{12,20},{16,24},{20,28},{24,0},{28,4},{1,9},{5... | collective-permute-start | bytes 2359304 | tf_op jit(solution)/shard_map/ppermute | solution.py:866
  520.0 39.0 %collective-permute-start.27 = (bf16[1024,512]{1,0:T(8,128)(2,1)S(1)}, bf16[1024,512]{1,0:T(8,128)(2,1)S(1)}, u32[]{:S(2)}, u32[]{:S(2)}) collective-permute-start(bf16[1024,512]{1,0:T(8,128)(2,1)S(1)} %copy-done.30), channel_id=1, source_target_pairs={{0,1},{1,0},{2,3},{3,2},{4,5},{5,4},{6,7},{7,6},{8,9},{9,8},{10,11... | collective-permute-start | bytes 3145736 | tf_op jit(solution)/shard_map/ppermute | solution.py:842
  521.2 37.8 %collective-permute-start.28 = (bf16[1024,512]{1,0:T(8,128)(2,1)S(1)}, bf16[1024,512]{1,0:T(8,128)(2,1)S(1)}, u32[]{:S(2)}, u32[]{:S(2)}) collective-permute-start(bf16[1024,512]{1,0:T(8,128)(2,1)S(1)} %copy-done.31), channel_id=1, source_target_pairs={{0,2},{1,3},{2,0},{3,1},{4,6},{5,7},{6,4},{7,5},{8,10},{9,11},{10,... | collective-permute-start | bytes 3145736 | tf_op jit(solution)/shard_map/ppermute | solution.py:842
  560.6 6.2 copy-start.44
  560.6 9.3 %copy-start.4 = (bf16[1024,1536]{1,0:T(8,128)(2,1)S(1)}, bf16[1024,1536]{1,0:T(8,128)(2,1)}, u32[]{:S(2)}) copy-start(bf16[1024,1536]{1,0:T(8,128)(2,1)} %get-tuple-element.122) | copy-start | bytes 9437188
  561.7 4.0 collective-permute-start.36
  565.7 4.0 collective-permute-start.37
  569.8 5.1 copy-start.10
  569.8 5.1 copy-start.12
  569.8 4.9 collective-permute-start.38
  569.9 26.1 %copy-start.8 = (bf16[1024,512]{1,0:T(8,128)(2,1)S(1)}, bf16[1024,512]{1,0:T(8,128)(2,1)}, u32[]{:S(2)}) copy-start(bf16[1024,512]{1,0:T(8,128)(2,1)} %get-tuple-element.132.refs_4_) | copy-start | bytes 3145732
  569.9 26.1 %copy-start.11 = (bf16[1024,512]{1,0:T(8,128)(2,1)S(1)}, bf16[1024,512]{1,0:T(8,128)(2,1)}, u32[]{:S(2)}) copy-start(bf16[1024,512]{1,0:T(8,128)(2,1)} %get-tuple-element.131.refs_3_) | copy-start | bytes 3145732
  572.6 32.1 %collective-permute-start.41 = (bf16[256,1536]{1,0:T(8,128)(2,1)}, bf16[256,1536]{1,0:T(8,128)(2,1)}, u32[]{:S(2)}, u32[]{:S(2)}) collective-permute-start(bf16[256,1536]{1,0:T(8,128)(2,1)} %add_convert_fusion.3), channel_id=1, source_target_pairs={{0,8},{4,12},{8,16},{12,20},{16,24},{20,28},{24,0},{28,4},{1,9},{5... | collective-permute-start | bytes 2359304 | tf_op jit(solution)/shard_map/ppermute | solution.py:866
  572.6 36.7 %collective-permute-start.30 = (bf16[1024,512]{1,0:T(8,128)(2,1)}, bf16[1024,512]{1,0:T(8,128)(2,1)}, u32[]{:S(2)}, u32[]{:S(2)}) collective-permute-start(bf16[1024,512]{1,0:T(8,128)(2,1)} %get-tuple-element.130.refs_9_), channel_id=1, source_target_pairs={{0,1},{1,0},{2,3},{3,2},{4,5},{5,4},{6,7},{7,6},{8,9},{9,8},{10,11... | collective-permute-start | bytes 3145736 | tf_op jit(solution)/shard_map/ppermute | solution.py:842
  573.7 35.6 %collective-permute-start.31 = (bf16[1024,512]{1,0:T(8,128)(2,1)}, bf16[1024,512]{1,0:T(8,128)(2,1)}, u32[]{:S(2)}, u32[]{:S(2)}) collective-permute-start(bf16[1024,512]{1,0:T(8,128)(2,1)} %get-tuple-element.135), channel_id=1, source_target_pairs={{0,2},{1,3},{2,0},{3,1},{4,6},{5,7},{6,4},{7,5},{8,10},{9,11},{10,... | collective-permute-start | bytes 3145736 | tf_op jit(solution)/shard_map/ppermute | solution.py:842
  574.7 20.3 %collective-permute-start.39 = (f32[9728]{0:T(1024)S(1)}, f32[9728]{0:T(1024)S(1)}, u32[]{:S(2)}, u32[]{:S(2)}) collective-permute-start(f32[9728]{0:T(1024)S(1)} %fusion.24), channel_id=1, source_target_pairs={{0,8},{4,12},{8,0},{12,4},{16,24},{20,28},{24,16},{28,20},{1,9},{5... | collective-permute-start | bytes 116744 | tf_op jit(solution)/shard_map/ppermute | solution.py:842
  575.8 58.4 %collective-permute-start.33 = (bf16[512,512]{1,0:T(8,128)(2,1)}, bf16[512,512]{1,0:T(8,128)(2,1)}, u32[]{:S(2)}, u32[]{:S(2)}) collective-permute-start(bf16[512,512]{1,0:T(8,128)(2,1)} %add_convert_fusion.7.refs_11_), channel_id=1, source_target_pairs={{0,1},{1,0},{2,3},{3,2},{4,5},{5,4},{6,7},{7,6},{8,9},{9,8},{10,11... | collective-permute-start | bytes 1572872 | tf_op jit(solution)/shard_map/ppermute | solution.py:842
  595.1 8.5 %collective-permute-start.40 = (f32[9728]{0:T(1024)S(1)}, f32[9728]{0:T(1024)S(1)}, u32[]{:S(2)}, u32[]{:S(2)}) collective-permute-start(f32[9728]{0:T(1024)S(1)} %add.195), channel_id=1, source_target_pairs={{0,16},{4,20},{8,24},{12,28},{16,0},{20,4},{24,8},{28,12},{1,17},{... | collective-permute-start | bytes 116744 | tf_op jit(solution)/shard_map/ppermute | solution.py:842
  603.5 30.7 %collective-permute-start.32 = (bf16[512,512]{1,0:T(8,128)(2,1)}, bf16[512,512]{1,0:T(8,128)(2,1)}, u32[]{:S(2)}, u32[]{:S(2)}) collective-permute-start(bf16[512,512]{1,0:T(8,128)(2,1)} %add_convert_fusion.8.refs_10_), channel_id=1, source_target_pairs={{0,2},{1,3},{2,0},{3,1},{4,6},{5,7},{6,4},{7,5},{8,10},{9,11},{10,... | collective-permute-start | bytes 1572872 | tf_op jit(solution)/shard_map/ppermute | solution.py:842
  607.2 20.8 %collective-permute-start.42 = (bf16[256,1536]{1,0:T(8,128)(2,1)}, bf16[256,1536]{1,0:T(8,128)(2,1)}, u32[]{:S(2)}, u32[]{:S(2)}) collective-permute-start(bf16[256,1536]{1,0:T(8,128)(2,1)} %add_convert_fusion.2), channel_id=1, source_target_pairs={{0,8},{4,12},{8,16},{12,20},{16,24},{20,28},{24,0},{28,4},{1,9},{5... | collective-permute-start | bytes 2359304 | tf_op jit(solution)/shard_map/ppermute | solution.py:866
  611.4 22.8 %collective-permute-start.35 = (bf16[512,512]{1,0:T(8,128)(2,1)}, bf16[512,512]{1,0:T(8,128)(2,1)}, u32[]{:S(2)}, u32[]{:S(2)}) collective-permute-start(bf16[512,512]{1,0:T(8,128)(2,1)} %add_convert_fusion.5), channel_id=1, source_target_pairs={{0,1},{1,0},{2,3},{3,2},{4,5},{5,4},{6,7},{7,6},{8,9},{9,8},{10,11... | collective-permute-start | bytes 1572872 | tf_op jit(solution)/shard_map/ppermute | solution.py:842
  614.7 19.6 %collective-permute-start.34 = (bf16[512,512]{1,0:T(8,128)(2,1)}, bf16[512,512]{1,0:T(8,128)(2,1)}, u32[]{:S(2)}, u32[]{:S(2)}) collective-permute-start(bf16[512,512]{1,0:T(8,128)(2,1)} %add_convert_fusion.6), channel_id=1, source_target_pairs={{0,2},{1,3},{2,0},{3,1},{4,6},{5,7},{6,4},{7,5},{8,10},{9,11},{10,... | collective-permute-start | bytes 1572872 | tf_op jit(solution)/shard_map/ppermute | solution.py:842
  (33 other events, 45.8 us)
Sparse Core Ops, SparseCore 0:
  120.5 84.7 all-gather.2
  220.8 79.3 all-gather.4
  302.5 107.9 reduce-scatter.2
  458.8 103.6 reduce-scatter.4

commit v3 on v2

--- a/solution.py
+++ b/solution.py
@@ -24,6 +24,11 @@
 
 def dot(a, b, dims):
     return lax.dot_general(a, b, dims, preferred_element_type=F32)
+
+
+def eight_rows(value):
+    rows, cols = value.shape
+    return jnp.sum(value.reshape(rows // 8, 8, cols), axis=0)
 
 
 def call(kernel, name, flops, moved, operands, grid, in_specs, out_specs, out_shape, scratch=(), prefetch=(), aliases=None, after=()):
@@ -50,11 +55,12 @@
 
 
 class Weights:
-    def __init__(self, arrays, placed=False):
+    def __init__(self, arrays, size=None, placed=False):
         self.arrays = list(arrays)
         self.placed = placed
         self.cols = self.arrays[0].shape[1]
-        self.rows = sum(a.shape[0] for a in self.arrays)
+        self.size = size or self.arrays[0].shape[0]
+        self.rows = self.arrays[0].shape[0] if placed else self.size * len(self.arrays)
 
     def copies(self, refs, blk, count, side, col, cols, target, sems):
         found = []
@@ -76,8 +82,8 @@
                 add(refs[0], pl.multiple_of(blk[p] * size, size), size, (p - first) * size)
             return found
         place = 0
-        for ref, array in zip(refs, self.arrays):
-            size = array.shape[0]
+        for ref in refs:
+            size = self.size
             if side is None or place // half == side:
                 add(ref, 0, size, place - (side or 0) * half)
             place += size
@@ -142,7 +148,7 @@
     )
 
 
-def heads_shard(w_qkv, w_out, after):
+def heads_shard(w_qkv, w_out):
     depth, wide = w_qkv.shape
     inner = w_out.shape[0]
 
@@ -157,10 +163,9 @@
         4 * depth * (wide + inner),
         (w_qkv, w_out),
         (1,),
-        [pl.BlockSpec(w_qkv.shape, lambda i: (0, 0)), pl.BlockSpec(w_out.shape, lambda i: (0, 0))],
+        [pl.BlockSpec(w.shape, lambda i: (0, 0)) for w in (w_qkv, w_out)],
         pl.BlockSpec((depth, wide + inner), lambda i: (0, 0)),
         struct((depth, wide + inner)),
-        after=after,
     )
 
 
@@ -202,22 +207,22 @@
     return u * keep + pltpu.roll(u, 128 - ROT // 2, 1) * ahead + pltpu.roll(u, ROT // 2, 1) * behind
 
 
-def norm_project(blocks, out_blocks, pieces, rows, gain, shift, bias, tables, weights, after=()):
-    width = pieces[0].shape[1]
+def ordered(ref, blk, count, cols):
+    return jnp.concatenate(
+        [ref[:, pl.ds(pl.multiple_of(blk[p] * cols, cols), cols)] for p in range(count)], axis=1
+    )
+
+
+def norm_project(blocks, x_all, gain, shift, bias, tables, weights, after=()):
+    length, width = x_all.shape
     wide = bias.shape[1]
     inner = wide // 3
-    starts, total = [], 0
-    for piece in pieces:
-        starts.append(total)
-        total += piece.shape[0] // rows
-    length = total * rows
-    n, k, count = len(pieces), len(weights.arrays), blocks.shape[0]
-
-    def kernel(blk, places, *refs):
-        piece_refs = refs[:n]
-        gain_ref, shift_ref, bias_ref, keep_ref, ahead_ref, behind_ref = refs[n : n + 6]
-        w_refs = refs[n + 6 : n + 6 + k]
-        normed_ref, unit_ref, qkv_ref, rows_ref, w_ref, sems = refs[n + 6 + k :]
+    rows = min(256, length)
+    k, count = len(weights.arrays), blocks.shape[0]
+
+    def kernel(blk, x_ref, gain_ref, shift_ref, bias_ref, keep_ref, ahead_ref, behind_ref, *refs):
+        w_refs = refs[:k]
+        normed_ref, unit_ref, qkv_ref, w_ref, sems = refs[k:]
         step = pl.program_id(0)
         copies = weights.copies(w_refs, blk, count, None, 0, wide, w_ref, sems)
 
@@ -226,20 +231,12 @@
             for copy in copies:
                 copy.start()
 
-        for i in range(n):
-            last = starts[i + 1] if i + 1 < n else total
-
-            @pl.when((step >= starts[i]) & (step < last))
-            def _(i=i):
-                rows_ref[...] = piece_refs[i][...]
-
-        x = rows_ref[...].astype(F32)
+        x = ordered(x_ref, blk, count, width // count).astype(F32)
         centered = x - jnp.mean(x, axis=1, keepdims=True)
         variance = jnp.mean(centered * centered, axis=1, keepdims=True)
         unit = centered * lax.rsqrt(variance + EPSILON)
         unit_ref[...] = unit.astype(BF)
-        normed = (unit * gain_ref[...] + shift_ref[...]).astype(BF)
-        normed_ref[...] = normed
+        normed_ref[...] = (unit * gain_ref[...] + shift_ref[...]).astype(BF)
 
         @pl.when(step == 0)
         def _():
@@ -256,35 +253,26 @@
                 start = part * inner + pair * 128
                 qkv_ref[:, start : start + 128] = u.astype(BF)
 
-    def piece_spec(i):
-        number = pieces[i].shape[0] // rows
-        return pl.BlockSpec((rows, width), lambda j, b, o: (jnp.clip(j - starts[i], 0, number - 1), 0))
-
     def whole(shape):
-        return pl.BlockSpec(shape, lambda j, b, o: (0, 0))
-
-    def placed(cols):
-        return pl.BlockSpec((rows, cols), lambda j, b, o: (o[j], 0))
+        return pl.BlockSpec(shape, lambda j, blk: (0, 0))
+
+    def block(cols):
+        return pl.BlockSpec((rows, cols), lambda j, blk: (j, 0))
 
     return call(
         kernel,
         "norm_project",
         3 * length * width * wide,
         6 * length * width + 4 * width * wide,
-        (*pieces, gain, shift, bias, *tables, *weights.arrays),
-        (total,),
-        [piece_spec(i) for i in range(n)]
-        + [whole((1, width)), whole((1, width)), whole((1, wide))]
-        + [placed(128)] * 3
+        (x_all, gain, shift, bias, *tables, *weights.arrays),
+        (length // rows,),
+        [block(width), whole((1, width)), whole((1, width)), whole((1, wide))]
+        + [block(128)] * 3
         + [pl.BlockSpec(memory_space=pl.ANY)] * k,
-        [placed(width), placed(width), placed(wide)],
+        [block(width), block(width), block(wide)],
         [struct((length, width)), struct((length, width)), struct((length, wide))],
-        scratch=[
-            pltpu.VMEM((rows, width), BF),
-            pltpu.VMEM((width, wide), BF),
-            pltpu.SemaphoreType.DMA((weights.number(count),)),
-        ],
-        prefetch=(blocks, out_blocks),
+        scratch=[pltpu.VMEM((width, wide), BF), pltpu.SemaphoreType.DMA((weights.number(count),))],
+        prefetch=(blocks,),
         after=after,
     )
 
@@ -412,7 +400,7 @@
                 rows = slice(index * block, (index + 1) * block)
                 dq = turn_back(dq, rows).astype(BF)
                 dq_ref[...] = dq
-                sum_ref[0, 0:1, :] += jnp.sum(dq.astype(F32), axis=0, keepdims=True)
+                sum_ref[0, 0:8, :] += eight_rows(dq.astype(F32))
 
         @pl.when(step == count - 1)
         def _():
@@ -420,10 +408,10 @@
                 rows = slice(index * block, (index + 1) * block)
                 dk = turn_back(k_total[:, rows].T * shrink, rows).astype(BF)
                 dk_ref[rows, :] = dk
-                sum_ref[0, 1:2, :] += jnp.sum(dk.astype(F32), axis=0, keepdims=True)
+                sum_ref[0, 8:16, :] += eight_rows(dk.astype(F32))
                 dv = v_total[:, rows].T.astype(BF)
                 dv_ref[rows, :] = dv
-                sum_ref[0, 2:3, :] += jnp.sum(dv.astype(F32), axis=0, keepdims=True)
+                sum_ref[0, 16:24, :] += eight_rows(dv.astype(F32))
 
     def column(offset):
         return pl.BlockSpec((length, 128), lambda h, i: (0, offset + h))
@@ -450,15 +438,16 @@
             table,
             table,
         ],
-        [rows_of(0), column(0), column(0), pl.BlockSpec((1, 8, 128), lambda h, i: (h, 0, 0))],
-        [struct((length, inner))] * 3 + [struct((pairs, 8, 128), F32)],
+        [rows_of(0), column(0), column(0), pl.BlockSpec((1, 24, 128), lambda h, i: (h, 0, 0))],
+        [struct((length, inner))] * 3 + [struct((pairs, 24, 128), F32)],
         scratch=[pltpu.VMEM((128, length), F32)] * 2,
         after=after,
     )
 
 
-def times_weights(blocks, rows_in, weights, col, total_cols, name, extra, outs, finish, after=()):
+def times_weights(blocks, rows_in, weights, name, extra, outs, finish, after=()):
     length, width = rows_in.shape
+    total_cols = weights.cols
     rows, cols = min(512, length), min(1024, total_cols)
     chunks = total_cols // cols
     k, count, e = len(weights.arrays), blocks.shape[0], len(extra)
@@ -467,25 +456,26 @@
     def kernel(blk, a_ref, *refs):
         w_refs, extra_refs, out_refs = refs[:k], refs[k : k + e], refs[k + e : -2]
         w_ref, sems = refs[-2:]
+        chunk, step = pl.program_id(0), pl.program_id(1)
         copies = [
-            weights.copies(w_refs, blk, count, None, col + c * cols, cols, w_ref.at[c], sems.at[c])
+            weights.copies(w_refs, blk, count, None, c * cols, cols, w_ref.at[c], sems.at[c])
             for c in range(chunks)
         ]
 
-        @pl.when((pl.program_id(0) == 0) & (pl.program_id(1) == 0))
+        @pl.when((chunk == 0) & (step == 0))
         def _():
-            for chunk in copies:
-                for copy in chunk:
+            for per_chunk in copies:
+                for copy in per_chunk:
                     copy.start()
 
         for c in range(chunks):
 
-            @pl.when((pl.program_id(0) == c) & (pl.program_id(1) == 0))
+            @pl.when((chunk == c) & (step == 0))
             def _(c=c):
                 for copy in copies[c]:
                     copy.wait()
 
-        finish(dot(a_ref[...], w_ref[pl.program_id(0)], NN), extra_refs, out_refs)
+        finish(dot(a_ref[...], w_ref[chunk], NN), step == 0, extra_refs, out_refs)
 
     specs = {
         "block": pl.BlockSpec((rows, cols), lambda n, m, blk: (m, n)),
@@ -515,7 +505,7 @@
 
 
 def expand(blocks, normed, weights, bias, after=()):
-    def finish(product, extra_refs, out_refs):
+    def finish(product, first, extra_refs, out_refs):
         hidden = product + extra_refs[0][...]
         c = math.sqrt(2.0 / math.pi)
         square = hidden * hidden
@@ -528,55 +518,70 @@
         ).astype(BF)
 
     return times_weights(
-        blocks, normed, weights, 0, weights.cols, "expand", [("row", bias)], ["block", "block"], finish, after
+        blocks, normed, weights, "expand", [("row", bias)], ["block", "block"], finish, after
     )
 
 
 def hidden_back(blocks, g_all, weights, slope, after=()):
-    def finish(product, extra_refs, out_refs):
-        low = (product * extra_refs[0][...].astype(F32)).astype(BF)
-        out_refs[0][...] = low
-
-        @pl.when(pl.program_id(1) == 0)
+    def finish(product, first, extra_refs, out_refs):
+        grad = product * extra_refs[0][...].astype(F32)
+        out_refs[0][...] = grad.astype(BF)
+
+        @pl.when(first)
         def _():
             out_refs[1][...] = jnp.zeros_like(out_refs[1])
 
-        out_refs[1][0:1, :] += jnp.sum(low.astype(F32), axis=0, keepdims=True)
+        out_refs[1][...] += eight_rows(grad)
 
     return times_weights(
-        blocks, g_all, weights, 0, weights.cols, "hidden_back", [("block", slope)], ["block", "sum"], finish, after
-    )
-
-
-def context_back(blocks, g_all, weights, after=()):
-    inner = weights.cols // 4
-
-    def finish(product, extra_refs, out_refs):
-        out_refs[0][...] = product.astype(BF)
-
-    return times_weights(
-        blocks, g_all, weights, 3 * inner, inner, "context_back", [], ["block"], finish, after
-    )[0]
-
-
-def weight_grad(blocks, rows_in, rights, cols, name, after=()):
+        blocks, g_all, weights, "hidden_back", [("block", slope)], ["block", "sum"], finish, after
+    )
+
+
+def columns_of(rights, cols):
+    starts, total = [], 0
+    for right in rights:
+        starts.append(total)
+        total += right.shape[1] // cols
+    return starts + [total]
+
+
+def weight_grad(blocks, rows_in, rights, cols, name, weights=None, after=()):
     length, width = rows_in.shape
     half = width // 2
     count = blocks.shape[0]
     depth = width // count
-    starts, total = [], 0
-    for right in rights:
-        starts.append(total)
-        total += right.shape[1] // cols
-    n = len(rights)
+    starts = columns_of(rights, cols)
+    n, total = len(rights), starts[-1]
+    k = len(weights.arrays) if weights else 0
+    more = 1 if k else 0
 
     def kernel(blk, a_ref, *refs):
-        out_ref = refs[n]
+        w_refs, out_ref = refs[n : n + k], refs[n + k]
         chunk, side = pl.program_id(0), pl.program_id(1)
+        if more:
+            back_ref, w_ref, sum_ref, sems = refs[n + k + 1 :]
+            inner = w_ref.shape[1]
+            copies = weights.copies(w_refs, blk, count, None, 3 * inner, inner, w_ref, sems)
+
+            @pl.when((chunk == 0) & (side == 0))
+            def _():
+                for copy in copies:
+                    copy.start()
+
+            @pl.when((chunk == total) & (side == 0))
+            def _():
+                for copy in copies:
+                    copy.wait()
+                sum_ref[...] = dot(a_ref[...], w_ref[:half, :], NN)
+
+            @pl.when((chunk == total) & (side == 1))
+            def _():
+                back_ref[...] = (sum_ref[...] + dot(a_ref[...], w_ref[half:, :], NN)).astype(BF)
+
         for i in range(n):
-            last = starts[i + 1] if i + 1 < n else total
-
-            @pl.when((chunk >= starts[i]) & (chunk < last))
+
+            @pl.when((chunk >= starts[i]) & (chunk < starts[i + 1]))
             def _(i=i):
                 product = dot(a_ref[...], refs[i][...], TN).astype(BF)
                 for p in range(count // 2):
@@ -584,21 +589,36 @@
                     out_ref[pl.ds(place, depth), :] = product[p * depth : (p + 1) * depth]
 
     def right_spec(i):
-        number = rights[i].shape[1] // cols
+        number = starts[i + 1] - starts[i]
         return pl.BlockSpec(
             (length, cols), lambda n, s, blk: (0, jnp.clip(n - starts[i], 0, number - 1))
         )
 
+    out_specs = [pl.BlockSpec((width, cols), lambda n, s, blk: (0, jnp.minimum(n, total - 1)))]
+    out_shape = [struct((width, total * cols))]
+    scratch = []
+    if more:
+        inner = weights.cols // 4
+        out_specs.append(pl.BlockSpec((length, inner), lambda n, s, blk: (0, 0)))
+        out_shape.append(struct((length, inner)))
+        scratch = [
+            pltpu.VMEM((width, inner), BF),
+            pltpu.VMEM((length, inner), F32),
+            pltpu.SemaphoreType.DMA((weights.number(count),)),
+        ]
     return call(
         kernel,
         name,
         2 * length * width * total * cols,
         2 * length * width + 4 * length * total * cols + 2 * width * total * cols,
-        (rows_in, *rights),
-        (total, 2),
-        [pl.BlockSpec((length, half), lambda n, s, blk: (0, s))] + [right_spec(i) for i in range(n)],
-        pl.BlockSpec((width, cols), lambda n, s, blk: (0, n)),
-        struct((width, total * cols)),
+        (rows_in, *rights, *(weights.arrays if more else ())),
+        (total + more, 2),
+        [pl.BlockSpec((length, half), lambda n, s, blk: (0, s))]
+        + [right_spec(i) for i in range(n)]
+        + [pl.BlockSpec(memory_space=pl.ANY)] * k,
+        out_specs,
+        out_shape,
+        scratch=scratch,
         prefetch=(blocks,),
         after=after,
     )
@@ -607,19 +627,15 @@
 def weight_grad_halves(rows_in, rights, cols, name, after=()):
     length, width = rows_in.shape
     half = width // 2
-    starts, total = [], 0
-    for right in rights:
-        starts.append(total)
-        total += right.shape[1] // cols
-    n = len(rights)
+    starts = columns_of(rights, cols)
+    n, total = len(rights), starts[-1]
 
     def kernel(a_ref, *refs):
         sib_ref, own_ref = refs[n:]
         side, chunk = pl.program_id(0), pl.program_id(1)
         for i in range(n):
-            last = starts[i + 1] if i + 1 < n else total
-
-            @pl.when((chunk >= starts[i]) & (chunk < last))
+
+            @pl.when((chunk >= starts[i]) & (chunk < starts[i + 1]))
             def _(i=i):
                 product = dot(a_ref[...], refs[i][...], TN).astype(BF)
 
@@ -632,7 +648,7 @@
                     own_ref[...] = product
 
     def right_spec(i):
-        number = rights[i].shape[1] // cols
+        number = starts[i + 1] - starts[i]
         return pl.BlockSpec((length, cols), lambda s, n: (0, jnp.clip(n - starts[i], 0, number - 1)))
 
     return call(
@@ -672,20 +688,7 @@
     ]
 
 
-def store_outputs(plan, out_refs, low):
-    step = pl.program_id(0)
-    for (col, cols, steps, _), ref in zip(plan, out_refs):
-        if len(steps) > 2:
-            ref[...] = low[:, col : col + cols]
-            continue
-        first, second = steps
-
-        @pl.when((step == first) | (step == second))
-        def _(ref=ref, col=col, cols=cols):
-            ref[...] = low[:, col : col + cols]
-
-
-def rows_back(blocks, order, split, lefts, groups, side, name, unit=None, after=()):
+def rows_back(blocks, order, split, lefts, groups, side, name, after=()):
     length = lefts[0].shape[0]
     count, places = blocks.shape[0], order.shape[0]
     half = groups[0][0].rows // 2
@@ -695,61 +698,70 @@
     n = len(lefts)
     arrays = [array for weights, _, _ in groups for array in weights.arrays]
     k = len(arrays)
-    number = sum(weights.number(count, side) for weights, _, _ in groups)
+    pieces = count // 2
     plan = split_outputs(split, rows, half, places)
-    u = 0 if unit is None else 1
 
     def kernel(blk, places_ref, *refs):
-        left_refs, unit_refs, w_refs = refs[:n], refs[n : n + u], refs[n + u : n + u + k]
-        out_refs = refs[n + u + k : n + u + k + len(plan)]
-        sum_refs = refs[n + u + k + len(plan) : n + 2 * u + k + len(plan)]
-        joined_ref, w_ref, sems = refs[-3:]
-
-        copies, at, col, used = [], 0, 0, 0
-        for weights, start, cols in groups:
+        left_refs, w_refs = refs[:n], refs[n : n + k]
+        out_refs = refs[n + k : n + k + len(plan)]
+        joined_ref, w_ref, left_sems, sems = refs[-4:]
+        step = pl.program_id(0)
+
+        def left_copies(at):
+            slot, start, col, found = lax.rem(at, 2), pl.multiple_of(places_ref[at] * rows, rows), 0, []
+            for i, (ref, cols) in enumerate(zip(left_refs, widths)):
+                found.append(
+                    pltpu.make_async_copy(
+                        ref.at[pl.ds(start, rows), :],
+                        joined_ref.at[slot, :, pl.ds(col, cols)],
+                        left_sems.at[slot, i],
+                    )
+                )
+                col += cols
+            return found
+
+        per_group, at, col = [], 0, 0
+        for i, (weights, start, cols) in enumerate(groups):
             more = len(weights.arrays)
-            found = weights.copies(
-                w_refs[at : at + more],
-                blk,
-                count,
-                side,
-                start,
-                cols,
-                w_ref.at[:, pl.ds(col, cols)],
-                sems.at[pl.ds(used, weights.number(count, side))],
+            per_group.append(
+                weights.copies(
+                    w_refs[at : at + more], blk, count, side, start, cols, w_ref.at[:, pl.ds(col, cols)], sems.at[i]
+                )
             )
-            copies += found
-            at, col, used = at + more, col + cols, used + len(found)
-
-        @pl.when(pl.program_id(0) == 0)
+            at, col = at + more, col + cols
+
+        @pl.when(step == 0)
         def _():
-            for copy in copies:
+            for copy in left_copies(0):
                 copy.start()
-
-        col = 0
-        for ref, cols in zip(left_refs, widths):
-            joined_ref[:, col : col + cols] = ref[...]
-            col += cols
-
-        @pl.when(pl.program_id(0) == 0)
+            for piece in per_group:
+                for copy in piece:
+                    copy.start()
+
+        @pl.when(step + 1 < places)
         def _():
-            for copy in copies:
-                copy.wait()
-
-        low = dot(joined_ref[...], w_ref[...], NT).astype(BF)
-        store_outputs(plan, out_refs, low)
-        if u:
-
-            @pl.when(pl.program_id(0) == 0)
-            def _():
-                sum_refs[0][...] = jnp.zeros_like(sum_refs[0])
-
-            wide = low.astype(F32)
-            sum_refs[0][0:1, :] += jnp.sum(wide * unit_refs[0][...].astype(F32), axis=0, keepdims=True)
-            sum_refs[0][1:2, :] += jnp.sum(wide, axis=0, keepdims=True)
-
-    def left_spec(cols, column=0):
-        return pl.BlockSpec((rows, cols), lambda m, blk, o: (o[m], column))
+            for copy in left_copies(step + 1):
+                copy.start()
+
+        for copy in left_copies(step):
+            copy.wait()
+
+        @pl.when(step == 0)
+        def _():
+            for piece in per_group:
+                for copy in piece:
+                    copy.wait()
+
+        low = dot(joined_ref[lax.rem(step, 2)], w_ref[...], NT).astype(BF)
+        for (col, cols, steps, _), ref in zip(plan, out_refs):
+
+            def store(ref=ref, col=col, cols=cols):
+                ref[...] = low[:, col : col + cols]
+
+            if len(steps) > 2:
+                store()
+            else:
+                pl.when(functools.reduce(jnp.logical_or, [step == at for at in steps]))(store)
 
     def out_spec(cols, where):
         return pl.BlockSpec((rows, cols), lambda m, blk, o: where(m, blk))
@@ -759,21 +771,91 @@
         name,
         2 * length * half * depth,
         2 * length * depth + 2 * half * depth + 2 * length * half,
-        (*lefts, *([unit] if u else []), *arrays),
+        (*lefts, *arrays),
         (places,),
-        [left_spec(cols) for cols in widths]
-        + [left_spec(half, side)] * u
-        + [pl.BlockSpec(memory_space=pl.ANY)] * k,
-        [out_spec(cols, where) for _, cols, _, where in plan]
-        + [pl.BlockSpec((8, half), lambda m, blk, o: (0, 0))] * u,
-        [struct((len(steps) * rows, cols)) for _, cols, steps, _ in plan] + [struct((8, half), F32)] * u,
+        [pl.BlockSpec(memory_space=pl.ANY)] * (n + k),
+        [out_spec(cols, where) for _, cols, _, where in plan],
+        [struct((len(steps) * rows, cols)) for _, cols, steps, _ in plan],
         scratch=[
-            pltpu.VMEM((rows, depth), BF),
+            pltpu.VMEM((2, rows, depth), BF),
             pltpu.VMEM((half, depth), BF),
-            pltpu.SemaphoreType.DMA((number,)),
+            pltpu.SemaphoreType.DMA((2, n)),
+            pltpu.SemaphoreType.DMA((len(groups), pieces)),
         ],
         prefetch=(blocks, order),
         after=after,
+    )
+
+
+def gain_sums(order, split, parts, unit, after=()):
+    length, width = unit.shape
+    half, places = width // 2, order.shape[0]
+    rows = length // places
+    plan = split_outputs(split, rows, half, places)
+    n = len(plan)
+
+    def kernel(places_ref, unit_ref, *refs):
+        sum_ref = refs[2 * n]
+        step = pl.program_id(0)
+
+        @pl.when(step == 0)
+        def _():
+            sum_ref[...] = jnp.zeros_like(sum_ref)
+
+        for side in range(2):
+            for i, (col, cols, steps, _) in enumerate(plan):
+
+                def add(ref=refs[side * n + i], start=side * half + col, cols=cols):
+                    here = slice(start, start + cols)
+                    wide = ref[...].astype(F32)
+                    sum_ref[0:8, here] += eight_rows(wide * unit_ref[:, here].astype(F32))
+                    sum_ref[8:16, here] += eight_rows(wide)
+
+                if len(steps) > 2:
+                    add()
+                else:
+                    pl.when(functools.reduce(jnp.logical_or, [step == at for at in steps]))(add)
+
+    def spec(cols, where):
+        return pl.BlockSpec((rows, cols), lambda m, o: where(m, o))
+
+    return call(
+        kernel,
+        "gain_sums",
+        0,
+        4 * length * width,
+        (unit, *parts[0], *parts[1]),
+        (places,),
+        [pl.BlockSpec((rows, width), lambda m, o: (o[m], 0))]
+        + [spec(cols, where) for _, cols, _, where in plan] * 2,
+        pl.BlockSpec((16, width), lambda m, o: (0, 0)),
+        struct((16, width), F32),
+        prefetch=(order,),
+        after=after,
+    )
+
+
+def turned_sums(sums, units):
+    depth, cols = sums.shape
+    inner = cols - units
+
+    def kernel(sums_ref, fc2_ref, out_ref):
+        fc2_ref[...] = sums_ref[:, :units].T.astype(F32)
+        out_ref[...] = sums_ref[:, units:].T.astype(F32)
+
+    def whole(shape):
+        return pl.BlockSpec(shape, lambda i: (0, 0))
+
+    return call(
+        kernel,
+        "turned_sums",
+        0,
+        6 * depth * cols,
+        (sums,),
+        (1,),
+        [whole((depth, cols))],
+        [whole((units, depth)), whole((inner, depth))],
+        [struct((units, depth), F32), struct((inner, depth), F32)],
     )
 
 
@@ -791,10 +873,11 @@
                 total = total + ref[...].astype(F32)
             parts.append(total)
             at += number
-        result = kernel([ref[...].astype(F32) for ref in refs[:n]], jnp.concatenate(parts, axis=1), refs[at][...])
-        out_ref = refs[at + 1]
-        cols = width // blocks.shape[0]
-        for p in range(blocks.shape[0]):
+        count, out_ref = blocks.shape[0], refs[at + 1]
+        cols = width // count
+        values = [ordered(ref, blk, count, cols).astype(F32) for ref in refs[:n]]
+        result = kernel(values, jnp.concatenate(parts, axis=1), refs[at][...])
+        for p in range(count):
             place = pl.ds(pl.multiple_of(blk[p] * cols, cols), cols)
             out_ref[:, place] = result[:, p * cols : (p + 1) * cols].astype(dtype)
 
@@ -842,16 +925,12 @@
     return lax.ppermute(value, axis, [(i, i ^ bit) for i in range(size)])
 
 
-def flip_sums(value, axis, size):
-    found, bit = [value], 1
+def flip_sum(value, axis, size):
+    bit = 1
     while bit < size:
-        found.append(found[-1] + flip(found[-1], axis, size, bit))
+        value = value + flip(value, axis, size, bit)
         bit *= 2
-    return found
-
-
-def pick(steps, k):
-    return steps[min(k, len(steps) - 1)]
+    return value
 
 
 class Ring:
@@ -867,11 +946,6 @@
 
     def swap(self, value):
         return flip(value, "dp", self.size, 1)
-
-    def extend(self, pieces, steps, after):
-        while len(pieces) <= min(steps, self.chips - 1):
-            pieces.append(self.send(pieces[-1]))
-        pieces[-1:] = tie(pieces[-1:], after)
 
 
 def per_device(
@@ -896,72 +970,51 @@
     pairs = inner // 128
 
     third = ln_gain.shape[0]
+    x, g = layer_input[0], out_grad[0]
+    x_all = lax.all_gather(x, "tensor", axis=0, tiled=True)
+    heads_own, heads_sib = [heads_shard(w_qkv.reshape(depth, 3 * inner), w_out)], []
+
+    def ring_step(own, sib, after):
+        own.append(ring.send(own[-1]))
+        sib.append(ring.swap(own[-2]))
+        own[-1], sib[-1], *rest = tie([own[-1], sib[-1], *after], [])
+        return rest
+
     vectors = jnp.stack([ln_gain, ln_bias, out_bias]).astype(F32).reshape(1, 3 * third)
     table = jnp.where(jnp.arange(n_tensor)[:, None] == t_index, vectors, 0.0)
-    tables_small = flip_sums(table, "tensor", n_tensor)
-    packed = jnp.concatenate(
-        [tables_small[-1].reshape(-1), b_qkv.astype(F32).reshape(-1), b_fc1.astype(F32).reshape(-1)]
-    )[None, :]
-    packed = jnp.where(jnp.arange(n_dp)[:, None] == d_index, packed, 0.0)
-    packed_steps = flip_sums(packed, "dp", n_dp)
-    packed = packed_steps[-1]
+    table = flip_sum(table, "tensor", n_tensor)
+    small = jnp.concatenate([table.reshape(-1), b_qkv.astype(F32).reshape(-1), b_fc1.astype(F32).reshape(-1)])
+    g_placed, bias_part = order_columns(blocks, g, after=heads_own)
+    small, g_placed = ring_step(heads_own, heads_sib, [small, g_placed])
+    fc1_shard = stage(w_fc1, False, [small])
+    tables = rotary_rows(length)
+    small = flip_sum(
+        jnp.where(jnp.arange(n_dp)[:, None] == d_index, small[None, :], 0.0), "dp", n_dp
+    )
+    small, fc1_shard = ring_step(heads_own, heads_sib, [small, fc1_shard])
+    chosen = (blocks[:, None] == jnp.arange(n_dp)[None, :]).astype(F32)
     cut = n_tensor * 3 * third
-    vectors = packed[:, :cut].reshape(n_dp, n_tensor, 3, third)
-    vectors = jnp.transpose(vectors, (2, 0, 1, 3)).reshape(3, n_dp, n_tensor * third)
-    chosen = (blocks[:, None] == jnp.arange(n_dp)[None, :]).astype(F32)
-    vectors = jnp.einsum("pd,kdj->kpj", chosen, vectors, precision=lax.Precision.HIGHEST)
+    vectors = jnp.einsum("pd,dj->pj", chosen, small[:, :cut], precision=lax.Precision.HIGHEST)
+    vectors = jnp.transpose(vectors.reshape(n_dp, n_tensor, 3, third), (2, 0, 1, 3))
     gain, shift, bias_out = (vectors[i].reshape(1, width) for i in range(3))
+    b_width = HD // n_dp
     tail = cut + b_qkv.size
-    bias_qkv = jnp.transpose(packed[:, cut:tail].reshape(n_dp, 3, heads, -1), (1, 2, 0, 3))
+    bias_qkv = jnp.transpose(small[:, cut:tail].reshape(n_dp, 3, heads, b_width), (1, 2, 0, 3))
     bias_qkv = bias_qkv.reshape(1, 3 * inner)
-    bias_fc1 = jnp.transpose(packed[:, tail:].reshape(n_dp, units // HD, -1), (1, 0, 2))
+    bias_fc1 = jnp.transpose(small[:, tail:].reshape(n_dp, units // HD, b_width), (1, 0, 2))
     bias_fc1 = bias_fc1.reshape(1, units)
-    tables = rotary_rows(length)
-
-    x, _ = order_columns(blocks, layer_input[0])
-    shard = heads_shard(w_qkv.reshape(depth, 3 * inner), w_out, [x])
-    rows = min(256, local)
-    heads_own, heads_sib = [shard], []
+    gain, bias_qkv, bias_fc1, fc1_shard, *tables = ring_step(
+        heads_own, heads_sib, [gain, bias_qkv, bias_fc1, fc1_shard, *tables]
+    )
+    while len(heads_own) < chips:
+        ring_step(heads_own, heads_sib, [])
+    heads_sib.append(ring.swap(heads_own[-1]))
+    heads_weights = Weights(heads_own + heads_sib)
+    g_all = lax.all_gather(g_placed, "tensor", axis=0, tiled=True)
     if square:
-        cut = local // 2
-        lower = x[cut:]
-        beside, below = [flip(x[:cut], "tensor", 4, 1)], [flip(x[:cut], "tensor", 4, 2)]
-        heads_own.append(ring.send(shard))
-        heads_sib.append(ring.swap(shard))
-        lower, heads_own[1], beside[0], below[0] = tie(
-            [lower, heads_own[1], beside[0], below[0]], [tables_small[-1], heads_sib[0]]
-        )
-        beside.append(flip(lower, "tensor", 4, 1))
-        below.append(flip(lower, "tensor", 4, 2))
-        heads_own.append(ring.send(heads_own[1]))
-        heads_sib.append(ring.swap(heads_own[1]))
-        heads_own[2], beside[1], below[1] = tie(
-            [heads_own[2], beside[1], below[1]], [pick(packed_steps, 2), heads_sib[1], tables[0]]
-        )
-        across = [flip(beside[0], "tensor", 4, 2), flip(below[1], "tensor", 4, 1)]
-        for _ in range(chips - 3):
-            heads_own.append(ring.send(heads_own[-1]))
-            heads_sib.append(ring.swap(heads_own[-2]))
-        heads_own[-1], *across = tie([heads_own[-1], *across], [gain, heads_sib[-1]])
-        heads_sib.append(ring.swap(heads_own[-1]))
-        pieces = [x, *beside, *below, *across]
-        rows = min(rows, cut)
-        each = local // rows
-        relative = [r * each + i for r in (0, 1, 2, 3) for i in range(each)]
-        relative = jnp.array(relative, jnp.int32)
-        out_blocks = ((relative // each) ^ t_index) * each + relative % each
-        g, bias_part = order_columns(blocks, out_grad[0], after=across)
         order = (jnp.array([3, 1, 2, 0], jnp.int32) ^ t_index).astype(jnp.int32)
     else:
-        for _ in range(chips - 1):
-            heads_own.append(ring.send(heads_own[-1]))
-        heads_sib = [ring.swap(piece) for piece in heads_own]
-        pieces = [lax.all_gather(x, "tensor", axis=0, tiled=True)]
-        out_blocks = jnp.arange(length // rows, dtype=jnp.int32)
-        g, bias_part = order_columns(blocks, out_grad[0])
         order = jnp.arange(n_tensor, dtype=jnp.int32)
-    heads_weights = Weights(heads_own + heads_sib)
-    g_all = lax.all_gather(g, "tensor", axis=0, tiled=True)
 
     def split(kind):
         return kind if square else None
@@ -987,119 +1040,119 @@
             return [got]
         return [list(terms) for terms in zip(parts[1::2], got, last)]
 
-    fc1_pieces = [stage(w_fc1, False, [heads_own[-1]])]
+    fc1_own, fc1_sib = [fc1_shard], []
     normed, unit, qkv = norm_project(
-        blocks, out_blocks, pieces, rows, gain, shift, bias_qkv, tables, heads_weights, after=[fc1_pieces[0]]
-    )
-    ring.extend(fc1_pieces, 1, [qkv])
+        blocks, x_all, gain, shift, bias_qkv, tables, heads_weights, after=[fc1_shard]
+    )
+    (qkv,) = ring_step(fc1_own, fc1_sib, [qkv])
     first = pairs // 2
-    context, log_first = attend(qkv, 0, first, after=[fc1_pieces[-1]])
-    ring.extend(fc1_pieces, 2, [log_first])
-    context, log_second = attend(qkv, first, pairs - first, before=context, after=[fc1_pieces[-1]])
+    context, log_first = attend(qkv, 0, first, after=[fc1_own[-1]])
+    (log_first,) = ring_step(fc1_own, fc1_sib, [log_first])
+    context, log_second = attend(qkv, first, pairs - first, before=context, after=[fc1_own[-1]])
+    (log_second,) = ring_step(fc1_own, fc1_sib, [log_second])
+    while len(fc1_own) < chips:
+        ring_step(fc1_own, fc1_sib, [])
+    fc1_sib.append(ring.swap(fc1_own[-1]))
     log_total = jnp.concatenate([log_first, log_second], axis=0)
-    ring.extend(fc1_pieces, chips - 1, [log_second])
-    fc1_own = jnp.concatenate(fc1_pieces, axis=0)
-    fc1_weights = Weights([fc1_own, ring.swap(fc1_own)])
-    fc2_shard = stage(w_fc2, True, [fc1_own])
-    fc2_weights = Weights([lax.all_gather(fc2_shard, "dp", axis=0, tiled=True)], placed=True)
-    context_grad = context_back(blocks, g_all, heads_weights, after=[fc2_shard, log_second])
-    act, slope = expand(blocks, normed, fc1_weights, bias_fc1, after=[context_grad])
+    fc1_weights = Weights(fc1_own + fc1_sib)
+    fc2_shard = stage(w_fc2, True, [log_second])
+    fc2_weights = Weights([lax.all_gather(fc2_shard, "dp", axis=0, tiled=True)], depth, placed=True)
+    act, slope = expand(blocks, normed, fc1_weights, bias_fc1, after=[fc2_shard])
 
     def scatter(parts):
         return lax.psum_scatter(parts, "dp", scatter_dimension=0, tiled=True)
 
-    fc2_sums = scatter(weight_grad(blocks, g_all, [act, context], min(512, inner), "fc2_grad"))
-    backs = attend_back(qkv, context, context_grad, log_total, tables, after=[act])
-    heads_cols, fc2_cols = (heads_weights, 0, 3 * inner), (fc2_weights, 0, units)
-    out_cols, fc1_cols = (heads_weights, 3 * inner, inner), (fc1_weights, 0, units)
-    branch = []
-    for side, kind in enumerate(("first", "second")):
-        parts = rows_back(
-            blocks, order, split(kind), [act, context], [fc2_cols, out_cols], side, "branch_half",
-            after=[backs[0]] if side == 0 else branch[0],
-        )
-        branch.append(parts)
-    branch_got = [cross_once("first", branch[0]), cross_once("second", branch[1])]
-    hidden_grad, b_fc1_part = hidden_back(blocks, g_all, fc2_weights, slope, after=branch[1])
-    fc1_grad = weight_grad(blocks, normed, [hidden_grad], min(512, units), "fc1_grad")
-    fc1_grad, branch_got[0][0], branch_got[1][0] = tie([fc1_grad, branch_got[0][0], branch_got[1][0]], [])
-    fc1_sums = scatter(fc1_grad)
-    branch_sums = [cross_add(parts, got) for parts, got in zip(branch, branch_got)]
-    branch_last = [cross_twice(kind, sums) for kind, sums in zip(("first", "second"), branch_sums)]
-    heads_grads = weight_grad_halves(
-        normed, backs[:3], inner, "heads_grad", after=[fc1_grad, *branch_sums[0], *branch_sums[1]]
-    )
-    if square:
-        heads_sib_grad, heads_own_grad, branch_last[0][0], branch_last[1][0] = tie(
-            [*heads_grads, branch_last[0][0], branch_last[1][0]], []
-        )
-    else:
-        heads_sib_grad, heads_own_grad = heads_grads
-    branch_terms = [
-        part for parts in zip(branch, branch_got, branch_last) for part in cross_terms(*parts)
-    ]
-    heads_other = ring.swap(heads_sib_grad)
-    lefts = [*backs[:3], hidden_grad]
-    back_own = rows_back(
-        blocks, order, split("both"), lefts, [heads_cols, fc1_cols], 0, "normed_back_half", unit=unit,
-        after=[heads_own_grad],
-    )
-    *back_own, heads_other = tie([*back_own, heads_other], [])
-
-    def ring_add(k, moving):
+    fc2_grad, context_grad = weight_grad(
+        blocks, g_all, [act, context], min(512, inner), "fc2_grad", heads_weights
+    )
+    fc2_sums = scatter(fc2_grad)
+    *backs, b_qkv_part = attend_back(qkv, context, context_grad, log_total, tables)
+    heads_sib_grad, heads_own_grad = weight_grad_halves(normed, backs, inner, "heads_grad")
+
+    def ring_add(k, moving=None):
         cut = slice(k * depth, (k + 1) * depth)
         total = heads_own_grad[cut].astype(F32) + heads_other[cut].astype(F32)
         return total if moving is None else total + moving.astype(F32)
 
-    own_got = cross_once("both", back_own[:-1])
-    message = ring_add(1, None).astype(BF)
-    moving = ring.send(message)
+    heads_cols, fc2_cols = (heads_weights, 0, 3 * inner), (fc2_weights, 0, units)
+    out_cols, fc1_cols = (heads_weights, 3 * inner, inner), (fc1_weights, 0, units)
+    lefts = [act, context]
+    branch_own = rows_back(
+        blocks, order, split("first"), lefts, [fc2_cols, out_cols], 0, "branch_half", after=[heads_own_grad]
+    )
+    *branch_own, heads_other = tie([*branch_own, ring.swap(heads_sib_grad)], [])
+    message = ring_add(1).astype(BF)
+    branch_sib = rows_back(
+        blocks, order, split("second"), lefts, [fc2_cols, out_cols], 1, "branch_half", after=[message]
+    )
+    *branch_sib, moving = tie([*branch_sib, ring.send(message)], [])
+    message = ring_add(2, moving).astype(BF)
+    hidden_grad, b_fc1_part = hidden_back(blocks, g_all, fc2_weights, slope, after=[message])
+    hidden_grad, moving = tie([hidden_grad, ring.send(message)], [])
+    for k in range(3, chips):
+        message = ring_add(k, moving).astype(BF)
+        if k < chips - 1:
+            moving = ring.send(message)
+    (fc1_grad,) = weight_grad(blocks, normed, [hidden_grad], min(1024, units), "fc1_grad", after=[message])
+    branch_got = cross_once("first", branch_own) + cross_once("second", branch_sib)
+    n = len(branch_got)
+    fc1_grad, moving, *branch_got = tie([fc1_grad, ring.send(message), *branch_got], [])
+    fc1_sums = scatter(fc1_grad)
+    heads_sums = ring_add(0, moving)
+    branch_sums = cross_add(branch_own, branch_got[:1]) + cross_add(branch_sib, branch_got[1:])
+    branch_last = cross_twice("first", branch_sums[:1]) + cross_twice("second", branch_sums[1:])
+
+    lefts = [*backs, hidden_grad]
+    back_own = rows_back(
+        blocks, order, split("both"), lefts, [heads_cols, fc1_cols], 0, "normed_back_half",
+        after=[fc1_grad, *branch_sums],
+    )
+    n = len(back_own)
+    joined = tie([*back_own, *branch_last], [])
+    back_own, branch_last = joined[:n], joined[n:]
+    branch_terms = cross_terms(branch_own, branch_got[:1], branch_last[:1])
+    branch_terms += cross_terms(branch_sib, branch_got[1:], branch_last[1:])
+    own_got = cross_once("both", back_own)
     back_sib = rows_back(
-        blocks, order, split("both"), lefts, [heads_cols, fc1_cols], 1, "normed_back_half", unit=unit,
-        after=[message],
-    )
-    n = len(back_sib)
-    *joined, moving = tie([*back_sib, *own_got, moving], [])
+        blocks, order, split("both"), lefts, [heads_cols, fc1_cols], 1, "normed_back_half",
+        after=[back_own[0]],
+    )
+    joined = tie([*back_sib, *own_got], [])
     back_sib, own_got = joined[:n], joined[n:]
-    sib_got = cross_once("both", back_sib[:-1])
-    own_sums = cross_add(back_own[:-1], own_got)
-    own_last = cross_twice("both", own_sums)
-    message = ring_add(2, moving).astype(BF) if chips > 2 else None
-    for k in range(2, chips):
-        moving = ring.send(message if k == 2 else ring_add(k, moving).astype(BF))
-    layer_output = add_branch(blocks, x, branch_terms, bias_out, after=[back_sib[0], *own_sums])
-    layer_output, *sib_got = tie([layer_output, *sib_got], [])
-    sib_last = cross_twice("both", cross_add(back_sib[:-1], sib_got))
-    heads_sums = ring_add(0, moving)
-    back_terms = cross_terms(back_own[:-1], own_got, own_last) + cross_terms(back_sib[:-1], sib_got, sib_last)
-    input_grad = norm_back(blocks, x, g, back_terms, gain)
-
+
+    sib_got = cross_once("both", back_sib)
+    own_last = cross_twice("both", cross_add(back_own, own_got))
+    norm_sums = gain_sums(order, split("both"), (back_own, back_sib), unit).reshape(2, 8, n_dp, depth)
+    norm_sums = jnp.einsum("pd,kpj->dkj", chosen, jnp.sum(norm_sums, axis=1), precision=lax.Precision.HIGHEST)
+    b_qkv_part = jnp.sum(b_qkv_part.reshape(pairs, 3, 8, 128), axis=2)
+    b_qkv_part = jnp.transpose(b_qkv_part, (1, 0, 2)).reshape(3, heads, n_dp, b_width)
+    b_fc1_part = jnp.sum(b_fc1_part, axis=0).reshape(units // HD, n_dp, b_width)
+    by_owner = jnp.concatenate(
+        [
+            norm_sums.reshape(n_dp, 2 * depth),
+            bias_part[0].reshape(n_dp, depth),
+            jnp.transpose(b_qkv_part, (2, 0, 1, 3)).reshape(n_dp, -1),
+            jnp.transpose(b_fc1_part, (1, 0, 2)).reshape(n_dp, -1),
+        ],
+        axis=1,
+    )
+
+    sums = flip_sum(by_owner, "dp", n_dp)
+    sums = lax.dynamic_index_in_dim(sums, d_index, 0, keepdims=False)
+    w_fc2_grad, w_out_grad = turned_sums(fc2_sums, units)
+    layer_output = add_branch(
+        blocks, x, branch_terms, bias_out, after=[back_sib[0], w_fc2_grad, w_out_grad]
+    )
+    layer_output, sums, *sib_got = tie([layer_output, sums, *sib_got], [])
+    sib_last = cross_twice("both", cross_add(back_sib, sib_got))
+    mine = flip_sum(sums[: 3 * depth].reshape(3, depth), "tensor", n_tensor)
+    mine = lax.dynamic_slice_in_dim(mine, t_index * third, third, 1)
+    b_qkv_grad = sums[3 * depth : 3 * depth + b_qkv.size].reshape(b_qkv.shape)
+    b_fc1_grad = sums[3 * depth + b_qkv.size :].reshape(b_fc1.shape)
+    w_fc1_grad = fc1_sums.astype(F32)
     w_qkv_grad = heads_sums.reshape(depth, 3, inner)
-    w_out_grad = fc2_sums[:, units:].T.astype(F32)
-    w_fc1_grad = fc1_sums.astype(F32)
-    w_fc2_grad = fc2_sums[:, :units].T.astype(F32)
-
-    norm_sums = jnp.concatenate([back_own[-1][:2], back_sib[-1][:2]], axis=1).reshape(2, n_dp, depth)
-    norm_sums = jnp.einsum("pd,kpj->kdj", chosen, norm_sums, precision=lax.Precision.HIGHEST)
-    vector_sums = jnp.concatenate([norm_sums.reshape(2, width), bias_part[:1]], axis=0)
-    vector_sums = flip_sums(vector_sums, "tensor", n_tensor)[-1]
-    unit_sums = jnp.concatenate(
-        [
-            vector_sums.reshape(-1),
-            jnp.transpose(backs[3][:, :3, :], (1, 0, 2)).reshape(-1),
-            b_fc1_part[0],
-        ]
-    )
-    unit_sums = flip_sums(unit_sums, "dp", n_dp)[-1]
-    mine = unit_sums[: 3 * width].reshape(3, n_dp * n_tensor, third)
-    mine = lax.dynamic_index_in_dim(mine, d_index * n_tensor + t_index, 1, keepdims=False)
-    b_width = HD // n_dp
-    b_qkv_grad = lax.dynamic_slice_in_dim(
-        unit_sums[3 * width : 3 * width + 3 * inner].reshape(3, heads, HD), d_index * b_width, b_width, 2
-    )
-    b_fc1_grad = lax.dynamic_slice_in_dim(
-        unit_sums[3 * width + 3 * inner :].reshape(units // HD, HD), d_index * b_width, b_width, 1
-    )
+    back_terms = cross_terms(back_own, own_got, own_last) + cross_terms(back_sib, sib_got, sib_last)
+    input_grad = norm_back(blocks, x, g, back_terms, gain, after=[w_fc1_grad, w_qkv_grad])
     return (
         layer_output[None],
         input_grad[None],

time: 666 us -> 609 us (0.914)
  waiting for transfers between devices: 126 us -> 95.5 us
  Pallas kernels: 407 us -> 395 us
  starting transfers between devices: 36.7 us -> 29.9 us
    ppermute x34 -> x31, waiting for transfers between devices: 92.1 us -> 41 us  [flip(): return lax.ppermute(value, axis, [(i, i ^ bit) for i in range(size)])]
    ppermute x9, waiting for transfers between devices: 34.3 us -> 53.8 us  [send(): return lax.ppermute(value, 'dp', pairs)]
    pallas_call x21, Pallas kernels: 407 us -> 395 us  [call(): pl.pallas_call(body, name=name, grid_spec=pltpu.PrefetchScalarGridSpec(nu...]
    ppermute x34 -> x31, starting transfers between devices: 30.5 us -> 25.8 us  [flip(): return lax.ppermute(value, axis, [(i, i ^ bit) for i in range(size)])]
    unnamed x110 -> x111, local copies, waits for them, and re-layouts: 25.3 us -> 21.7 us
  transfers between devices with their start and end apart: 47 -> 45, of which waited for: 13 -> 16; matrix products, arithmetic and copies ran while one was open for 8% -> 8% of each run, Pallas kernels for 60% -> 64%
where the time goes in v3:
time: 609 us; the launch traced here: 602 us
  Pallas kernels  395 us (65%)
  waiting for transfers between devices  95.5 us (16%)
  local copies, waits for them, and re-layouts  35.8 us (6%)
  other arithmetic  30.4 us (5%)
  starting transfers between devices  29.9 us (5%)
  between operations  14.8 us (2%)
    pallas_call x21, Pallas kernels, call(): pl.pallas_call(body, name=name, grid_spec=pltpu.PrefetchScalarGridSpec(nu...  395 us
    ppermute x9, waiting for transfers between devices, send(): return lax.ppermute(value, 'dp', pairs)  53.8 us
    ppermute x31, waiting for transfers between devices, flip(): return lax.ppermute(value, axis, [(i, i ^ bit) for i in range(size)])  41 us
    ppermute x31, starting transfers between devices, flip(): return lax.ppermute(value, axis, [(i, i ^ bit) for i in range(size)])  25.8 us
    unnamed x111, local copies, waits for them, and re-layouts  21.7 us
  transfers between devices with their start and end apart: 45, of which 16 were waited for; matrix products, arithmetic and copies ran while one was open for 8% of the time, Pallas kernels for 64%

profile of v3, /device:TPU:0, one launch (start us, length us, event | category | flops | bytes accessed | tf_op | source)
XLA Modules:
  0.0 602.0 jit_solution(16434180364989449259)
XLA Ops:
  8.6 1.2 copy.95.refs_0_
  9.8 2.3 heads_shard.1.refs_2_.refs_8_.refs_4_.refs_5_.refs_6_
  12.5 2.6 collective-permute-start
  15.3 1.5 collective-permute-start.2
  16.8 2.1 collective-permute-done.2
  19.0 1.5 collective-permute-start.3
  21.4 3.6 order_columns.1
  25.9 15.3 %collective-permute-done.refs_0_ = bf16[256,2048]{1,0:T(8,128)(2,1)S(1)} collective-permute-done((bf16[256,2048]{1,0:T(8,128)(2,1)}, bf16[256,2048]{1,0:T(8,128)(2,1)S(1)}, u32[]{:S(2)}, u32[]{:S(2)}) %collective-permute-start) | collective-permute-done | bytes 1048608 | tf_op jit(solution)/shard_map/ppermute | solution.py:945
  41.2 1.0 copy-done.30
  45.7 25.4 %collective-permute-done.7 = f32[8,1216]{1,0:T(8,128)S(1)} collective-permute-done((f32[8,1216]{1,0:T(8,128)S(1)}, f32[8,1216]{1,0:T(8,128)S(1)}, u32[]{:S(2)}, u32[]{:S(2)}) %collective-permute-start.7) | collective-permute-done | bytes 38944 | tf_op jit(solution)/shard_map/ppermute | solution.py:925
  72.2 2.3 stage_weight.2.refs_3_
  74.5 1.6 collective-permute-done.8
  78.9 5.0 fusion.1
  87.4 19.0 %collective-permute-done.9.refs_0_ = bf16[256,2048]{1,0:T(8,128)(2,1)S(1)} collective-permute-done((bf16[256,2048]{1,0:T(8,128)(2,1)}, bf16[256,2048]{1,0:T(8,128)(2,1)S(1)}, u32[]{:S(2)}, u32[]{:S(2)}) %collective-permute-start.9) | collective-permute-done | bytes 1048608 | tf_op jit(solution)/shard_map/ppermute | solution.py:945
  108.5 1.7 collective-permute-done.11.refs_15_.refs_11_.refs_12_.refs_13_
  111.2 27.4 %norm_project.1 = (bf16[2048,2048]{1,0:T(8,128)(2,1)}, bf16[2048,2048]{1,0:T(8,128)(2,1)}, bf16[2048,1536]{1,0:T(8,128)(2,1)}) custom-call(s32[8]{0:T(128)} %pad_add_fusion.refs_0_, bf16[2048,2048]{1,0:T(8,128)(2,1)} %bitcast.55, f32[1,2048]{1,0:T(1,128)} %get-tuple-element.106.refs_2_.refs_15_, f32[1,2048]{1,0:T(1,128)} %reshape_squeeze.13.refs_3_, ...), custom_call_target="tpu_custom_call" | custom-call | flops 19327352832 | bytes 37748736 | tf_op jit(solution)/shard_map/norm_project/pallas_call | solution.py:40
  140.3 19.7 %attend.2 = (bf16[2048,512]{1,0:T(8,128)(2,1)}, f32[2,2,2048]{2,1,0:T(2,128)}) custom-call(bf16[2048,1536]{1,0:T(8,128)(2,1)} %get-tuple-element.119.refs_0_.refs_1_.refs_2_, bf16[2048,1536]{1,0:T(8,128)(2,1)} %get-tuple-element.119.refs_0_.refs_1_.refs_2_, bf16[2048,1536]{1,0:T(8,128)(2,1)} %get-tuple-element.119.refs_0_.refs_1_.refs_2_, ...), custom_call_target="tpu_custom_call" | custom-call | flops 42949672960 | bytes 4194304 | tf_op jit(solution)/shard_map/attend/pallas_call | solution.py:40
  160.1 7.6 %collective-permute-done.14.refs_0_ = bf16[256,2048]{1,0:T(8,128)(2,1)S(1)} collective-permute-done((bf16[256,2048]{1,0:T(8,128)(2,1)}, bf16[256,2048]{1,0:T(8,128)(2,1)S(1)}, u32[]{:S(2)}, u32[]{:S(2)}) %collective-permute-start.14) | collective-permute-done | bytes 1048608 | tf_op jit(solution)/shard_map/ppermute | solution.py:945
  168.9 19.8 %attend.3 = (bf16[2048,512]{1,0:T(8,128)(2,1)}, f32[2,2,2048]{2,1,0:T(2,128)}) custom-call(bf16[2048,1536]{1,0:T(8,128)(2,1)} %get-tuple-element.119.refs_0_.refs_1_.refs_2_, bf16[2048,1536]{1,0:T(8,128)(2,1)} %get-tuple-element.119.refs_0_.refs_1_.refs_2_, ...), custom_call_target="tpu_custom_call", output_to_operand_aliasing={{0}: (3, {})} | custom-call | flops 42949672960 | bytes 4194304 | tf_op jit(solution)/shard_map/attend/pallas_call | solution.py:40
  188.7 7.7 %collective-permute-done.16.refs_0_ = bf16[256,2048]{1,0:T(8,128)(2,1)S(1)} collective-permute-done((bf16[256,2048]{1,0:T(8,128)(2,1)}, bf16[256,2048]{1,0:T(8,128)(2,1)S(1)}, u32[]{:S(2)}, u32[]{:S(2)}) %collective-permute-start.16) | collective-permute-done | bytes 1048608 | tf_op jit(solution)/shard_map/ppermute | solution.py:945
  197.5 2.6 stage_weight.3.refs_11_
  201.4 2.0 collective-permute-done.18.refs_9_.refs_21_
  204.4 33.0 %expand.1 = (bf16[2048,2048]{1,0:T(8,128)(2,1)}, bf16[2048,2048]{1,0:T(8,128)(2,1)}) custom-call(s32[8]{0:T(128)} %pad_add_fusion.refs_0_, bf16[2048,2048]{1,0:T(8,128)(2,1)} %get-tuple-element.116.refs_1_.refs_0_, bf16[256,2048]{1,0:T(8,128)(2,1)} %get-tuple-element.115.refs_16_.refs_2_.refs_14_, bf16[256,2048]{1,0:T(8,128)(2,1)} %get-tuple-element.118.refs_3_.refs_15_, ...), custom_call_target="tpu_custom_call" | custom-call | flops 17179869184 | bytes 33554432 | tf_op jit(solution)/shard_map/expand/pallas_call | solution.py:40
  237.4 37.7 %fc2_grad.1 = (bf16[2048,2560]{1,0:T(8,128)(2,1)}, bf16[2048,512]{1,0:T(8,128)(2,1)}) custom-call(s32[8]{0:T(128)} %pad_add_fusion.refs_0_, bf16[2048,2048]{1,0:T(8,128)(2,1)} %all-gather.7.cloned.1.call-done.refs_1_, bf16[2048,2048]{1,0:T(8,128)(2,1)} %get-tuple-element.130.refs_2_, bf16[2048,512]{1,0:T(8,128)(2,1)} %get-tuple-element.131.refs_3_, ...), custom_call_target="tpu_custom_call" | custom-call | flops 21474836480 | bytes 39845888 | tf_op jit(solution)/shard_map/fc2_grad/pallas_call | solution.py:40
  275.1 65.4 %attend_back.1 = (bf16[2048,512]{1,0:T(8,128)(2,1)}, bf16[2048,512]{1,0:T(8,128)(2,1)}, bf16[2048,512]{1,0:T(8,128)(2,1)}, f32[4,24,128]{2,1,0:T(8,128)}) custom-call(bf16[2048,1536]{1,0:T(8,128)(2,1)} %get-tuple-element.119.refs_0_.refs_1_.refs_2_, bf16[2048,1536]{1,0:T(8,128)(2,1)} %get-tuple-element.119.refs_0_.refs_1_.refs_2_, ...), custom_call_target="tpu_custom_call" | custom-call | flops 128849018880 | bytes 16777216 | tf_op jit(solution)/shard_map/attend_back/pallas_call | solution.py:40
  340.6 20.7 %heads_grad.1 = (bf16[1024,1536]{1,0:T(8,128)(2,1)}, bf16[1024,1536]{1,0:T(8,128)(2,1)}) custom-call(bf16[2048,2048]{1,0:T(8,128)(2,1)} %get-tuple-element.116.refs_1_.refs_0_, bf16[2048,512]{1,0:T(8,128)(2,1)} %get-tuple-element.135.refs_1_.refs_2_, bf16[2048,512]{1,0:T(8,128)(2,1)} %get-tuple-element.136.refs_2_.refs_3_, ...), custom_call_target="tpu_custom_call" | custom-call | flops 12884901888 | bytes 27262976 | tf_op jit(solution)/shard_map/heads_grad/pallas_call | solution.py:40
  362.0 17.6 %branch_half.2 = (bf16[1024,1024]{1,0:T(8,128)(2,1)}, bf16[1024,1024]{1,0:T(8,128)(2,1)}) custom-call(s32[8]{0:T(128)} %pad_add_fusion.refs_0_, s32[4]{0:T(128)} %broadcast_xor_fusion.refs_1_.refs_0_, bf16[2048,2048]{1,0:T(8,128)(2,1)} %get-tuple-element.130.refs_2_, bf16[2048,512]{1,0:T(8,128)(2,1)} %get-tuple-element.131.refs_3_, ...), custom_call_target="tpu_custom_call" | custom-call | flops 10737418240 | bytes 19922944 | tf_op jit(solution)/shard_map/branch_half/pallas_call | solution.py:40
  379.6 1.7 copy-done.7
  381.2 1.6 add_convert_fusion.4.refs_13_
  382.9 1.7 collective-permute-start.23
  384.6 17.7 %branch_half.3 = (bf16[1024,1024]{1,0:T(8,128)(2,1)}, bf16[1024,1024]{1,0:T(8,128)(2,1)}) custom-call(s32[8]{0:T(128)} %pad_add_fusion.refs_0_, s32[4]{0:T(128)} %broadcast_xor_fusion.refs_1_.refs_0_, bf16[2048,2048]{1,0:T(8,128)(2,1)} %get-tuple-element.130.refs_2_, bf16[2048,512]{1,0:T(8,128)(2,1)} %get-tuple-element.131.refs_3_, ...), custom_call_target="tpu_custom_call" | custom-call | flops 10737418240 | bytes 19922944 | tf_op jit(solution)/shard_map/branch_half/pallas_call | solution.py:40
  402.2 4.2 collective-permute-done.20.refs_2_
  407.3 1.9 add_convert_fusion.3.refs_4_
  409.3 1.5 collective-permute-start.24
  410.8 26.0 %hidden_back.1 = (bf16[2048,2048]{1,0:T(8,128)(2,1)}, f32[8,2048]{1,0:T(8,128)}) custom-call(s32[8]{0:T(128)} %pad_add_fusion.refs_0_, bf16[2048,2048]{1,0:T(8,128)(2,1)} %all-gather.7.cloned.1.call-done.refs_1_, bf16[2048,2048]{1,0:T(8,128)(2,1)} %all-gather.5.cloned.1.call-done.refs_4_.refs_2_, bf16[2048,2048]{1,0:T(8,128)(2,1)} %get-tuple-element.143.refs_3_, ...), custom_call_target="tpu_custom_call" | custom-call | flops 17179869184 | bytes 33554432 | tf_op jit(solution)/shard_map/hidden_back/pallas_call | solution.py:40
  437.7 1.9 add_convert_fusion.2.refs_3_
  440.5 24.7 %fc1_grad.1.refs_0_ = bf16[2048,2048]{1,0:T(8,128)(2,1)} custom-call(s32[8]{0:T(128)} %pad_add_fusion.refs_0_, bf16[2048,2048]{1,0:T(8,128)(2,1)} %get-tuple-element.116.refs_1_.refs_0_, bf16[2048,2048]{1,0:T(8,128)(2,1)} %get-tuple-element.149.refs_2_.refs_5_, bf16[256,1536]{1,0:T(8,128)(2,1)} %copy-done.36), custom_call_target="tpu_custom_call" | custom-call | flops 17179869184 | bytes 33554432 | tf_op jit(solution)/shard_map/fc1_grad/pallas_call | solution.py:40
  465.3 1.3 copy-done
  466.9 2.1 add_convert_fusion.refs_24_
  469.0 1.5 collective-permute-start.26
  471.9 24.0 %normed_back_half.2 = (bf16[1024,512]{1,0:T(8,128)(2,1)}, bf16[1024,512]{1,0:T(8,128)(2,1)}, bf16[1024,512]{1,0:T(8,128)(2,1)}, bf16[1024,512]{1,0:T(8,128)(2,1)}) custom-call(s32[8]{0:T(128)} %pad_add_fusion.refs_0_, s32[4]{0:T(128)} %broadcast_xor_fusion.refs_1_.refs_0_, bf16[2048,512]{1,0:T(8,128)(2,1)} %get-tuple-element.135.refs_1_.refs_2_, ...), custom_call_target="tpu_custom_call" | custom-call | flops 15032385536 | bytes 26214400 | tf_op jit(solution)/shard_map/normed_back_half/pallas_call | solution.py:40
  497.3 1.3 collective-permute-start.28
  499.2 23.6 %normed_back_half.3 = (bf16[1024,512]{1,0:T(8,128)(2,1)}, bf16[1024,512]{1,0:T(8,128)(2,1)}, bf16[1024,512]{1,0:T(8,128)(2,1)}, bf16[1024,512]{1,0:T(8,128)(2,1)}) custom-call(s32[8]{0:T(128)} %pad_add_fusion.refs_0_, s32[4]{0:T(128)} %broadcast_xor_fusion.refs_1_.refs_0_, bf16[2048,512]{1,0:T(8,128)(2,1)} %get-tuple-element.135.refs_1_.refs_2_, ...), custom_call_target="tpu_custom_call" | custom-call | flops 15032385536 | bytes 26214400 | tf_op jit(solution)/shard_map/normed_back_half/pallas_call | solution.py:40
  525.0 1.2 collective-permute-start.32
  527.7 8.5 %gain_sums.1 = f32[16,2048]{1,0:T(8,128)} custom-call(s32[4]{0:T(128)} %broadcast_xor_fusion.refs_1_.refs_0_, bf16[2048,2048]{1,0:T(8,128)(2,1)} %get-tuple-element.173.refs_1_, bf16[1024,512]{1,0:T(8,128)(2,1)} %get-tuple-element.163.refs_22_.refs_2_, bf16[1024,512]{1,0:T(8,128)(2,1)} %get-tuple-element.174.refs_3_, ...), custom_call_target="tpu_custom_call" | custom-call | bytes 16777216 | tf_op jit(solution)/shard_map/gain_sums/pallas_call | solution.py:40
  536.2 1.0 reduce_sum.27
  539.7 2.0 add_convert_fusion.8
  541.7 2.8 collective-permute-done.30
  544.6 2.4 collective-permute-start.31
  547.9 1.1 collective-permute-start.35
  549.0 1.3 collective-permute-start.34
  550.3 1.5 collective-permute-done.31
  552.5 3.2 turned_sums.1
  555.6 6.9 %add_branch.1.refs_0_ = bf16[512,2048]{1,0:T(8,128)(2,1)} custom-call(s32[8]{0:T(128)} %pad_add_fusion.refs_0_, bf16[512,2048]{1,0:T(8,128)(2,1)} %bitcast.35, bf16[1024,1024]{1,0:T(8,128)(2,1)} %get-tuple-element.142.refs_2_, bf16[1024,1024]{1,0:T(8,128)(2,1)} %get-tuple-element.153.refs_3_, bf16[512,1024]{1,0:T(8,128)(2,1)} %get-tuple-element.161.refs_4_, ...), custom_call_target="tpu_custom_call" | custom-call | bytes 10485760 | tf_op jit(solution)/shard_map/add_branch/pallas_call | solution.py:40
  565.1 2.0 add_convert_fusion.6
  567.0 2.0 add_convert_fusion.5
  569.0 1.2 collective-permute-start.37
  570.2 1.4 collective-permute-start.36
  572.3 1.6 convert_add_fusion
  574.4 1.6 copy.104
  576.0 1.9 copy.103.refs_17_
  580.8 2.4 collective-permute-done.39
  583.8 2.8 convert_element_type.156.refs_16_
  586.7 8.6 %norm_back.1 = f32[512,2048]{1,0:T(8,128)} custom-call(s32[8]{0:T(128)} %pad_add_fusion.refs_0_, bf16[512,2048]{1,0:T(8,128)(2,1)} %bitcast.36, bf16[512,2048]{1,0:T(8,128)(2,1)} %bitcast.40, bf16[1024,512]{1,0:T(8,128)(2,1)} %get-tuple-element.174.refs_3_, bf16[1024,512]{1,0:T(8,128)(2,1)} %get-tuple-element.183.refs_4_, ...), custom_call_target="tpu_custom_call" | custom-call | bytes 10485760 | tf_op jit(solution)/shard_map/norm_back/pallas_call | solution.py:40
  (254 shorter events, 45.8 us)
Async XLA Ops:
  7.2 103.0 %all-gather.9.cloned.1.call-start = ((), (), s32[]{:S(2)}) async-start(), calls=%async_computation.6 | async-start | bytes 10485760 | tf_op jit(solution)/shard_map/all_gather | solution.py:974
  7.9 229.5 %all-gather.7.cloned.1.call-start = ((), (), s32[]{:S(2)}) async-start(), calls=%async_computation.3 | async-start | bytes 10485760 | tf_op jit(solution)/shard_map/all_gather | solution.py:1013
  8.6 6.5 %copy-start.48 = (bf16[64]{0:T(256)(128)(2,1)S(1)}, bf16[64]{0:T(256)(128)(2,1)}, u32[]{:S(2)}) copy-start(bf16[64]{0:T(256)(128)(2,1)} %param.15) | copy-start | bytes 388
  8.6 6.5 %copy-start.49 = (bf16[64]{0:T(256)(128)(2,1)S(1)}, bf16[64]{0:T(256)(128)(2,1)}, u32[]{:S(2)}) copy-start(bf16[64]{0:T(256)(128)(2,1)} %param.14) | copy-start | bytes 388
  8.6 6.5 %copy-start.50 = (bf16[64]{0:T(256)(128)(2,1)S(1)}, bf16[64]{0:T(256)(128)(2,1)}, u32[]{:S(2)}) copy-start(bf16[64]{0:T(256)(128)(2,1)} %param.13) | copy-start | bytes 388
  8.6 12.6 %copy-start.44 = (bf16[3,8,8]{2,1,0:T(8,128)(2,1)S(1)}, bf16[3,8,8]{2,1,0:T(8,128)(2,1)}, u32[]{:S(2)}) copy-start(bf16[3,8,8]{2,1,0:T(8,128)(2,1)} %param.17) | copy-start | bytes 1156
  8.6 12.6 %copy-start.47 = (bf16[32,8]{0,1:T(8,128)(2,1)S(1)}, bf16[32,8]{0,1:T(8,128)(2,1)}, u32[]{:S(2)}) copy-start(bf16[32,8]{0,1:T(8,128)(2,1)} %param.20) | copy-start | bytes 1540
  12.1 13.8 %collective-permute-start.1 = (bf16[256,2048]{1,0:T(8,128)(2,1)}, bf16[256,2048]{1,0:T(8,128)(2,1)S(1)}, u32[]{:S(2)}, u32[]{:S(2)}) collective-permute-start(bf16[256,2048]{1,0:T(8,128)(2,1)} %heads_shard.1.refs_2_.refs_8_.refs_4_.refs_5_.refs_6_), channel_id=1, source_target_pairs={{0,4},{4,0},{8,12},{12,8},{16,20},{20,16},{24,28},{28,24},{1,5},{5... | collective-permute-start | bytes 3145736 | tf_op jit(solution)/shard_map/ppermute | solution.py:925
  12.5 28.6 %collective-permute-start = (bf16[256,2048]{1,0:T(8,128)(2,1)}, bf16[256,2048]{1,0:T(8,128)(2,1)S(1)}, u32[]{:S(2)}, u32[]{:S(2)}) collective-permute-start(bf16[256,2048]{1,0:T(8,128)(2,1)} %heads_shard.1.refs_2_.refs_8_.refs_4_.refs_5_.refs_6_), channel_id=1, source_target_pairs={{0,8},{4,12},{8,16},{12,20},{16,24},{20,28},{24,0},{28,4},{1,9},{5... | collective-permute-start | bytes 3145736 | tf_op jit(solution)/shard_map/ppermute | solution.py:945
  15.3 3.6 collective-permute-start.2
  19.0 6.1 %collective-permute-start.3 = (f32[4,192]{1,0:T(4,128)S(1)}, f32[4,192]{1,0:T(4,128)S(1)}, u32[]{:S(2)}, u32[]{:S(2)}) collective-permute-start(f32[4,192]{1,0:T(4,128)S(1)} %fusion.15), channel_id=1, source_target_pairs={{0,2},{1,3},{2,0},{3,1},{4,6},{5,7},{6,4},{7,5},{8,10},{9,11},{10,... | collective-permute-start | bytes 9224 | tf_op jit(solution)/shard_map/ppermute | solution.py:925
  25.9 15.3 %copy-start.29 = (bf16[256,2048]{1,0:T(8,128)(2,1)}, bf16[256,2048]{1,0:T(8,128)(2,1)S(1)}, u32[]{:S(2)}) copy-start(bf16[256,2048]{1,0:T(8,128)(2,1)S(1)} %collective-permute-done.1.refs_1_) | copy-start | bytes 3145732
  42.2 28.9 %copy-start.38 = (f32[1216]{0:T(1024)S(1)}, f32[1216]{0:T(1024)}, u32[]{:S(2)}) copy-start(f32[1216]{0:T(1024)} %get-tuple-element.102.refs_1_) | copy-start | bytes 14596
  43.1 1.2 collective-permute-start.6
  43.1 33.7 %collective-permute-start.5 = (bf16[256,2048]{1,0:T(8,128)(2,1)}, bf16[256,2048]{1,0:T(8,128)(2,1)S(1)}, u32[]{:S(2)}, u32[]{:S(2)}) collective-permute-start(bf16[256,2048]{1,0:T(8,128)(2,1)} %get-tuple-element.101.refs_9_.refs_5_.refs_6_.refs_7_), channel_id=1, source_target_pairs={{0,4},{4,0},{8,12},{12,8},{16,20},{20,16},{24,28},{28,24},{1,5},{5... | collective-permute-start | bytes 3145736 | tf_op jit(solution)/shard_map/ppermute | solution.py:925
  43.6 33.2 %collective-permute-start.4 = (bf16[256,2048]{1,0:T(8,128)(2,1)}, bf16[256,2048]{1,0:T(8,128)(2,1)S(1)}, u32[]{:S(2)}, u32[]{:S(2)}) collective-permute-start(bf16[256,2048]{1,0:T(8,128)(2,1)} %get-tuple-element.101.refs_9_.refs_5_.refs_6_.refs_7_), channel_id=1, source_target_pairs={{0,8},{4,12},{8,16},{12,20},{16,24},{20,28},{24,0},{28,4},{1,9},{5... | collective-permute-start | bytes 3145736 | tf_op jit(solution)/shard_map/ppermute | solution.py:945
  45.1 26.1 %collective-permute-start.7 = (f32[8,1216]{1,0:T(8,128)S(1)}, f32[8,1216]{1,0:T(8,128)S(1)}, u32[]{:S(2)}, u32[]{:S(2)}) collective-permute-start(f32[8,1216]{1,0:T(8,128)S(1)} %fusion.4), channel_id=1, source_target_pairs={{0,8},{4,12},{8,0},{12,4},{16,24},{20,28},{24,16},{28,20},{1,9},{5... | collective-permute-start | bytes 116744 | tf_op jit(solution)/shard_map/ppermute | solution.py:925
  45.7 316.3 %all-gather.5.cloned.1.call-start = ((), (), s32[]{:S(2)}) async-start(), calls=%async_computation.2 | async-start | bytes 9437184 | tf_op jit(solution)/shard_map/all_gather | solution.py:1059
  71.2 4.9 collective-permute-start.8
  78.7 5.1 copy-start.39
  78.7 5.2 copy-start.45
  78.8 8.6 %collective-permute-start.10 = (bf16[256,2048]{1,0:T(8,128)(2,1)}, bf16[256,2048]{1,0:T(8,128)(2,1)S(1)}, u32[]{:S(2)}, u32[]{:S(2)}) collective-permute-start(bf16[256,2048]{1,0:T(8,128)(2,1)} %get-tuple-element.103.refs_10_.refs_6_.refs_7_.refs_8_), channel_id=1, source_target_pairs={{0,4},{4,0},{8,12},{12,8},{16,20},{20,16},{24,28},{28,24},{1,5},{5... | collective-permute-start | bytes 3145736 | tf_op jit(solution)/shard_map/ppermute | solution.py:925
  78.8 27.6 %collective-permute-start.9 = (bf16[256,2048]{1,0:T(8,128)(2,1)}, bf16[256,2048]{1,0:T(8,128)(2,1)S(1)}, u32[]{:S(2)}, u32[]{:S(2)}) collective-permute-start(bf16[256,2048]{1,0:T(8,128)(2,1)} %get-tuple-element.103.refs_10_.refs_6_.refs_7_.refs_8_), channel_id=1, source_target_pairs={{0,8},{4,12},{8,16},{12,20},{16,24},{20,28},{24,0},{28,4},{1,9},{5... | collective-permute-start | bytes 3145736 | tf_op jit(solution)/shard_map/ppermute | solution.py:945
  87.4 19.0 %copy-start.18 = (bf16[256,2048]{1,0:T(8,128)(2,1)}, bf16[256,2048]{1,0:T(8,128)(2,1)S(1)}, u32[]{:S(2)}) copy-start(bf16[256,2048]{1,0:T(8,128)(2,1)S(1)} %collective-permute-done.10.refs_1_) | copy-start | bytes 3145732
  107.3 2.9 collective-permute-start.11
  108.0 30.5 %collective-permute-start.13 = (bf16[256,2048]{1,0:T(8,128)(2,1)}, bf16[256,2048]{1,0:T(8,128)(2,1)S(1)}, u32[]{:S(2)}, u32[]{:S(2)}) collective-permute-start(bf16[256,2048]{1,0:T(8,128)(2,1)} %get-tuple-element.115.refs_16_.refs_2_.refs_14_), channel_id=1, source_target_pairs={{0,4},{4,0},{8,12},{12,8},{16,20},{20,16},{24,28},{28,24},{1,5},{5... | collective-permute-start | bytes 3145736 | tf_op jit(solution)/shard_map/ppermute | solution.py:925
  108.5 30.0 %collective-permute-start.12 = (bf16[256,2048]{1,0:T(8,128)(2,1)}, bf16[256,2048]{1,0:T(8,128)(2,1)S(1)}, u32[]{:S(2)}, u32[]{:S(2)}) collective-permute-start(bf16[256,2048]{1,0:T(8,128)(2,1)} %get-tuple-element.115.refs_16_.refs_2_.refs_14_), channel_id=1, source_target_pairs={{0,8},{4,12},{8,16},{12,20},{16,24},{20,28},{24,0},{28,4},{1,9},{5... | collective-permute-start | bytes 3145736 | tf_op jit(solution)/shard_map/ppermute | solution.py:945
  139.9 20.1 %collective-permute-start.15 = (bf16[256,2048]{1,0:T(8,128)(2,1)}, bf16[256,2048]{1,0:T(8,128)(2,1)S(1)}, u32[]{:S(2)}, u32[]{:S(2)}) collective-permute-start(bf16[256,2048]{1,0:T(8,128)(2,1)} %get-tuple-element.118.refs_3_.refs_15_), channel_id=1, source_target_pairs={{0,4},{4,0},{8,12},{12,8},{16,20},{20,16},{24,28},{28,24},{1,5},{5... | collective-permute-start | bytes 3145736 | tf_op jit(solution)/shard_map/ppermute | solution.py:925
  140.1 27.5 %collective-permute-start.14 = (bf16[256,2048]{1,0:T(8,128)(2,1)}, bf16[256,2048]{1,0:T(8,128)(2,1)S(1)}, u32[]{:S(2)}, u32[]{:S(2)}) collective-permute-start(bf16[256,2048]{1,0:T(8,128)(2,1)} %get-tuple-element.118.refs_3_.refs_15_), channel_id=1, source_target_pairs={{0,8},{4,12},{8,16},{12,20},{16,24},{20,28},{24,0},{28,4},{1,9},{5... | collective-permute-start | bytes 3145736 | tf_op jit(solution)/shard_map/ppermute | solution.py:945
  160.1 7.6 %copy-start.25 = (bf16[256,2048]{1,0:T(8,128)(2,1)}, bf16[256,2048]{1,0:T(8,128)(2,1)S(1)}, u32[]{:S(2)}) copy-start(bf16[256,2048]{1,0:T(8,128)(2,1)S(1)} %collective-permute-done.15.refs_1_) | copy-start | bytes 3145732
  168.7 20.1 %collective-permute-start.17 = (bf16[256,2048]{1,0:T(8,128)(2,1)}, bf16[256,2048]{1,0:T(8,128)(2,1)S(1)}, u32[]{:S(2)}, u32[]{:S(2)}) collective-permute-start(bf16[256,2048]{1,0:T(8,128)(2,1)} %get-tuple-element.121.refs_4_.refs_16_), channel_id=1, source_target_pairs={{0,4},{4,0},{8,12},{12,8},{16,20},{20,16},{24,28},{28,24},{1,5},{5... | collective-permute-start | bytes 3145736 | tf_op jit(solution)/shard_map/ppermute | solution.py:925
  168.7 27.8 %collective-permute-start.16 = (bf16[256,2048]{1,0:T(8,128)(2,1)}, bf16[256,2048]{1,0:T(8,128)(2,1)S(1)}, u32[]{:S(2)}, u32[]{:S(2)}) collective-permute-start(bf16[256,2048]{1,0:T(8,128)(2,1)} %get-tuple-element.121.refs_4_.refs_16_), channel_id=1, source_target_pairs={{0,8},{4,12},{8,16},{12,20},{16,24},{20,28},{24,0},{28,4},{1,9},{5... | collective-permute-start | bytes 3145736 | tf_op jit(solution)/shard_map/ppermute | solution.py:945
  188.7 7.7 %copy-start.24 = (bf16[256,2048]{1,0:T(8,128)(2,1)}, bf16[256,2048]{1,0:T(8,128)(2,1)S(1)}, u32[]{:S(2)}) copy-start(bf16[256,2048]{1,0:T(8,128)(2,1)S(1)} %collective-permute-done.17.refs_1_) | copy-start | bytes 3145732
  200.1 352.3 %reduce-scatter.3.cloned.1.call-start = ((), (), s32[]{:S(2)}) async-start(), calls=%async_computation.4 | async-start | bytes 11796480 | tf_op jit(solution)/shard_map/reduce_scatter | solution.py:1063
  200.7 2.7 collective-permute-start.18
  275.1 308.7 %reduce-scatter.5.cloned.1.call-start = ((), (), s32[]{:S(2)}) async-start(), calls=%async_computation.5 | async-start | bytes 9437184 | tf_op jit(solution)/shard_map/reduce_scatter | solution.py:1063
  340.6 20.9 %copy-start.53 = (s32[4]{0:T(128)S(1)}, s32[4]{0:T(128)}, u32[]{:S(2)}) copy-start(s32[4]{0:T(128)} %constant.99.clone) | copy-start | bytes 52
  361.3 18.2 %collective-permute-start.19 = (bf16[1024,1536]{1,0:T(8,128)(2,1)}, bf16[1024,1536]{1,0:T(8,128)(2,1)S(1)}, u32[]{:S(2)}, u32[]{:S(2)}) collective-permute-start(bf16[1024,1536]{1,0:T(8,128)(2,1)} %get-tuple-element.141), channel_id=1, source_target_pairs={{0,4},{4,0},{8,12},{12,8},{16,20},{20,16},{24,28},{28,24},{1,5},{5... | collective-permute-start | bytes 9437192 | tf_op jit(solution)/shard_map/ppermute | solution.py:925
  382.8 23.6 %collective-permute-start.20 = (bf16[256,1536]{1,0:T(8,128)(2,1)S(1)}, bf16[256,1536]{1,0:T(8,128)(2,1)S(1)}, u32[]{:S(2)}, u32[]{:S(2)}) collective-permute-start(bf16[256,1536]{1,0:T(8,128)(2,1)S(1)} %add_convert_fusion.4.refs_13_), channel_id=1, source_target_pairs={{0,8},{4,12},{8,16},{12,20},{16,24},{20,28},{24,0},{28,4},{1,9},{5... | collective-permute-start | bytes 2359304 | tf_op jit(solution)/shard_map/ppermute | solution.py:945
  382.9 82.4 %collective-permute-start.23 = (bf16[1024,1024]{1,0:T(8,128)(2,1)}, bf16[1024,1024]{1,0:T(8,128)(2,1)S(1)}, u32[]{:S(2)}, u32[]{:S(2)}) collective-permute-start(bf16[1024,1024]{1,0:T(8,128)(2,1)} %get-tuple-element.151), channel_id=1, source_target_pairs={{0,1},{1,0},{2,3},{3,2},{4,5},{5,4},{6,7},{7,6},{8,9},{9,8},{10,11... | collective-permute-start | bytes 6291464 | tf_op jit(solution)/shard_map/ppermute | solution.py:925
  409.2 27.7 %collective-permute-start.21 = (bf16[256,1536]{1,0:T(8,128)(2,1)S(1)}, bf16[256,1536]{1,0:T(8,128)(2,1)S(1)}, u32[]{:S(2)}, u32[]{:S(2)}) collective-permute-start(bf16[256,1536]{1,0:T(8,128)(2,1)S(1)} %add_convert_fusion.3.refs_4_), channel_id=1, source_target_pairs={{0,8},{4,12},{8,16},{12,20},{16,24},{20,28},{24,0},{28,4},{1,9},{5... | collective-permute-start | bytes 2359304 | tf_op jit(solution)/shard_map/ppermute | solution.py:945
  409.3 56.0 %collective-permute-start.24 = (bf16[1024,1024]{1,0:T(8,128)(2,1)}, bf16[1024,1024]{1,0:T(8,128)(2,1)}, u32[]{:S(2)}, u32[]{:S(2)}) collective-permute-start(bf16[1024,1024]{1,0:T(8,128)(2,1)} %get-tuple-element.152), channel_id=1, source_target_pairs={{0,2},{1,3},{2,0},{3,1},{4,6},{5,7},{6,4},{7,5},{8,10},{9,11},{10,... | collective-permute-start | bytes 6291464 | tf_op jit(solution)/shard_map/ppermute | solution.py:925
  439.7 25.6 %collective-permute-start.22 = (bf16[256,1536]{1,0:T(8,128)(2,1)S(1)}, bf16[256,1536]{1,0:T(8,128)(2,1)S(1)}, u32[]{:S(2)}, u32[]{:S(2)}) collective-permute-start(bf16[256,1536]{1,0:T(8,128)(2,1)S(1)} %add_convert_fusion.2.refs_3_), channel_id=1, source_target_pairs={{0,8},{4,12},{8,16},{12,20},{16,24},{20,28},{24,0},{28,4},{1,9},{5... | collective-permute-start | bytes 2359304 | tf_op jit(solution)/shard_map/ppermute | solution.py:945
  469.0 26.9 %collective-permute-start.26 = (bf16[512,1024]{1,0:T(8,128)(2,1)S(1)}, bf16[512,1024]{1,0:T(8,128)(2,1)S(1)}, u32[]{:S(2)}, u32[]{:S(2)}) collective-permute-start(bf16[512,1024]{1,0:T(8,128)(2,1)S(1)} %add_convert_fusion.refs_24_), channel_id=1, source_target_pairs={{0,1},{1,0},{2,3},{3,2},{4,5},{5,4},{6,7},{7,6},{8,9},{9,8},{10,11... | collective-permute-start | bytes 3145736 | tf_op jit(solution)/shard_map/ppermute | solution.py:925
  470.9 25.0 %collective-permute-start.25 = (bf16[512,1024]{1,0:T(8,128)(2,1)S(1)}, bf16[512,1024]{1,0:T(8,128)(2,1)S(1)}, u32[]{:S(2)}, u32[]{:S(2)}) collective-permute-start(bf16[512,1024]{1,0:T(8,128)(2,1)S(1)} %add_convert_fusion.1.refs_23_), channel_id=1, source_target_pairs={{0,2},{1,3},{2,0},{3,1},{4,6},{5,7},{6,4},{7,5},{8,10},{9,11},{10,... | collective-permute-start | bytes 3145736 | tf_op jit(solution)/shard_map/ppermute | solution.py:925
  497.3 25.5 %collective-permute-start.28 = (bf16[1024,512]{1,0:T(8,128)(2,1)}, bf16[1024,512]{1,0:T(8,128)(2,1)S(1)}, u32[]{:S(2)}, u32[]{:S(2)}) collective-permute-start(bf16[1024,512]{1,0:T(8,128)(2,1)} %get-tuple-element.168.refs_4_), channel_id=1, source_target_pairs={{0,2},{1,3},{2,0},{3,1},{4,6},{5,7},{6,4},{7,5},{8,10},{9,11},{10,... | collective-permute-start | bytes 3145736 | tf_op jit(solution)/shard_map/ppermute | solution.py:925
  498.6 24.3 %collective-permute-start.27 = (bf16[1024,512]{1,0:T(8,128)(2,1)}, bf16[1024,512]{1,0:T(8,128)(2,1)S(1)}, u32[]{:S(2)}, u32[]{:S(2)}) collective-permute-start(bf16[1024,512]{1,0:T(8,128)(2,1)} %get-tuple-element.163.refs_22_.refs_2_), channel_id=1, source_target_pairs={{0,1},{1,0},{2,3},{3,2},{4,5},{5,4},{6,7},{7,6},{8,9},{9,8},{10,11... | collective-permute-start | bytes 3145736 | tf_op jit(solution)/shard_map/ppermute | solution.py:925
  524.1 38.4 %collective-permute-start.33 = (bf16[1024,512]{1,0:T(8,128)(2,1)}, bf16[1024,512]{1,0:T(8,128)(2,1)S(1)}, u32[]{:S(2)}, u32[]{:S(2)}) collective-permute-start(bf16[1024,512]{1,0:T(8,128)(2,1)} %get-tuple-element.177.refs_8_), channel_id=1, source_target_pairs={{0,2},{1,3},{2,0},{3,1},{4,6},{5,7},{6,4},{7,5},{8,10},{9,11},{10,... | collective-permute-start | bytes 3145736 | tf_op jit(solution)/shard_map/ppermute | solution.py:925
  525.0 37.6 %collective-permute-start.32 = (bf16[1024,512]{1,0:T(8,128)(2,1)}, bf16[1024,512]{1,0:T(8,128)(2,1)}, u32[]{:S(2)}, u32[]{:S(2)}) collective-permute-start(bf16[1024,512]{1,0:T(8,128)(2,1)} %get-tuple-element.169.refs_9_.refs_6_), channel_id=1, source_target_pairs={{0,1},{1,0},{2,3},{3,2},{4,5},{5,4},{6,7},{7,6},{8,9},{9,8},{10,11... | collective-permute-start | bytes 3145736 | tf_op jit(solution)/shard_map/ppermute | solution.py:925
  527.6 9.6 %copy-start.46 = (s32[8]{0:T(128)S(1)}, s32[8]{0:T(128)}, u32[]{:S(2)}) copy-start(s32[8]{0:T(128)} %pad_add_fusion.refs_0_) | copy-start | bytes 100
  527.6 10.0 %copy-start.42 = (f32[8,4,64]{2,1,0:T(4,128)S(1)}, f32[8,4,64]{2,1,0:T(4,128)}, u32[]{:S(2)}) copy-start(f32[8,4,64]{2,1,0:T(4,128)} %get-tuple-element.222) | copy-start | bytes 24580
  527.6 12.1 %copy-start.5 = (bf16[1024,512]{1,0:T(8,128)(2,1)S(1)}, bf16[1024,512]{1,0:T(8,128)(2,1)}, u32[]{:S(2)}) copy-start(bf16[1024,512]{1,0:T(8,128)(2,1)} %get-tuple-element.174.refs_3_) | copy-start | bytes 3145732
  536.2 10.8 %copy-start.6 = (bf16[1024,512]{1,0:T(8,128)(2,1)S(1)}, bf16[1024,512]{1,0:T(8,128)(2,1)}, u32[]{:S(2)}) copy-start(bf16[1024,512]{1,0:T(8,128)(2,1)} %get-tuple-element.175.refs_5_.refs_6_) | copy-start | bytes 3145732
  537.6 1.2 collective-permute-start.29
  538.3 8.7 %copy-start.10 = (bf16[1024,512]{1,0:T(8,128)(2,1)S(1)}, bf16[1024,512]{1,0:T(8,128)(2,1)}, u32[]{:S(2)}) copy-start(bf16[1024,512]{1,0:T(8,128)(2,1)} %get-tuple-element.184.refs_7_) | copy-start | bytes 3145732
  538.8 5.8 collective-permute-start.30
  544.6 7.3 %collective-permute-start.31 = (f32[8,1216]{1,0:T(8,128)S(1)}, f32[8,1216]{1,0:T(8,128)S(1)}, u32[]{:S(2)}, u32[]{:S(2)}) collective-permute-start(f32[8,1216]{1,0:T(8,128)S(1)} %add.161), channel_id=1, source_target_pairs={{0,16},{4,20},{8,24},{12,28},{16,0},{20,4},{24,8},{28,12},{1,17},{... | collective-permute-start | bytes 116744 | tf_op jit(solution)/shard_map/ppermute | solution.py:925
  547.9 38.7 %collective-permute-start.35 = (bf16[512,512]{1,0:T(8,128)(2,1)}, bf16[512,512]{1,0:T(8,128)(2,1)}, u32[]{:S(2)}, u32[]{:S(2)}) collective-permute-start(bf16[512,512]{1,0:T(8,128)(2,1)} %add_convert_fusion.7), channel_id=1, source_target_pairs={{0,1},{1,0},{2,3},{3,2},{4,5},{5,4},{6,7},{7,6},{8,9},{9,8},{10,11... | collective-permute-start | bytes 1572872 | tf_op jit(solution)/shard_map/ppermute | solution.py:925
  549.0 37.6 %collective-permute-start.34 = (bf16[512,512]{1,0:T(8,128)(2,1)}, bf16[512,512]{1,0:T(8,128)(2,1)}, u32[]{:S(2)}, u32[]{:S(2)}) collective-permute-start(bf16[512,512]{1,0:T(8,128)(2,1)} %add_convert_fusion.8), channel_id=1, source_target_pairs={{0,2},{1,3},{2,0},{3,1},{4,6},{5,7},{6,4},{7,5},{8,10},{9,11},{10,... | collective-permute-start | bytes 1572872 | tf_op jit(solution)/shard_map/ppermute | solution.py:925
  564.2 8.0 %copy-start.17 = (bf16[256,1536]{1,0:T(8,128)(2,1)S(1)}, bf16[256,1536]{1,0:T(8,128)(2,1)}, u32[]{:S(2)}) copy-start(bf16[256,1536]{1,0:T(8,128)(2,1)} %get-tuple-element.187) | copy-start | bytes 2359300
  564.2 7.4 %collective-permute-start.38 = (f32[3,256]{1,0:T(4,128)S(1)}, f32[3,256]{1,0:T(4,128)S(1)}, u32[]{:S(2)}, u32[]{:S(2)}) collective-permute-start(f32[3,256]{1,0:T(4,128)S(1)} %reshape.191), channel_id=1, source_target_pairs={{0,1},{1,0},{2,3},{3,2},{4,5},{5,4},{6,7},{7,6},{8,9},{9,8},{10,11... | collective-permute-start | bytes 9224 | tf_op jit(solution)/shard_map/ppermute | solution.py:925
  569.0 17.6 %collective-permute-start.37 = (bf16[512,512]{1,0:T(8,128)(2,1)}, bf16[512,512]{1,0:T(8,128)(2,1)}, u32[]{:S(2)}, u32[]{:S(2)}) collective-permute-start(bf16[512,512]{1,0:T(8,128)(2,1)} %add_convert_fusion.5), channel_id=1, source_target_pairs={{0,1},{1,0},{2,3},{3,2},{4,5},{5,4},{6,7},{7,6},{8,9},{9,8},{10,11... | collective-permute-start | bytes 1572872 | tf_op jit(solution)/shard_map/ppermute | solution.py:925
  570.2 16.4 %collective-permute-start.36 = (bf16[512,512]{1,0:T(8,128)(2,1)}, bf16[512,512]{1,0:T(8,128)(2,1)}, u32[]{:S(2)}, u32[]{:S(2)}) collective-permute-start(bf16[512,512]{1,0:T(8,128)(2,1)} %add_convert_fusion.6), channel_id=1, source_target_pairs={{0,2},{1,3},{2,0},{3,1},{4,6},{5,7},{6,4},{7,5},{8,10},{9,11},{10,... | collective-permute-start | bytes 1572872 | tf_op jit(solution)/shard_map/ppermute | solution.py:925
  571.6 11.6 %collective-permute-start.39 = (f32[3,256]{1,0:T(4,128)S(1)}, f32[3,256]{1,0:T(4,128)S(1)}, u32[]{:S(2)}, u32[]{:S(2)}) collective-permute-start(f32[3,256]{1,0:T(4,128)S(1)} %add.170), channel_id=1, source_target_pairs={{0,2},{1,3},{2,0},{3,1},{4,6},{5,7},{6,4},{7,5},{8,10},{9,11},{10,... | collective-permute-start | bytes 9224 | tf_op jit(solution)/shard_map/ppermute | solution.py:925
  (35 other events, 61.7 us)
Sparse Core Ops, SparseCore 0:
  9.9 90.2 all-gather.8
  102.6 87.5 all-gather.6
  200.3 80.4 all-gather.4
  282.9 109.3 reduce-scatter.2
  467.0 91.7 reduce-scatter.4

commit v4 on v3

--- a/solution.py
+++ b/solution.py
@@ -100,7 +100,7 @@
 
 def tie(values, after):
     n = len(values)
-    anywhere = pl.BlockSpec(memory_space=pl.ANY)
+    anywhere = pl.BlockSpec(memory_space=pltpu.HBM)
 
     def kernel(*refs):
         del refs
@@ -149,23 +149,50 @@
 
 
 def heads_shard(w_qkv, w_out):
-    depth, wide = w_qkv.shape
-    inner = w_out.shape[0]
+    _, depth, inner = w_qkv.shape
 
     def kernel(q_ref, o_ref, out_ref):
-        out_ref[:, :wide] = q_ref[...]
-        out_ref[:, wide:] = o_ref[...].T
+        for part in range(3):
+            out_ref[:, part * inner : (part + 1) * inner] = q_ref[part]
+        out_ref[:, 3 * inner :] = o_ref[...].T
 
     return call(
         kernel,
         "heads_shard",
         0,
-        4 * depth * (wide + inner),
+        16 * depth * inner,
         (w_qkv, w_out),
         (1,),
-        [pl.BlockSpec(w.shape, lambda i: (0, 0)) for w in (w_qkv, w_out)],
-        pl.BlockSpec((depth, wide + inner), lambda i: (0, 0)),
-        struct((depth, wide + inner)),
+        [
+            pl.BlockSpec(w_qkv.shape, lambda i: (0, 0, 0)),
+            pl.BlockSpec(w_out.shape, lambda i: (0, 0)),
+        ],
+        pl.BlockSpec((depth, 4 * inner), lambda i: (0, 0)),
+        struct((depth, 4 * inner)),
+    )
+
+
+def heads_sum(own, other, moving):
+    depth, wide = moving.shape
+    inner = wide // 3
+    rows = min(64, depth)
+
+    def kernel(own_ref, other_ref, moving_ref, out_ref):
+        total = own_ref[...].astype(F32) + other_ref[...].astype(F32) + moving_ref[...].astype(F32)
+        for part in range(3):
+            out_ref[part] = total[:, part * inner : (part + 1) * inner]
+
+    block = pl.BlockSpec((rows, wide), lambda m: (m, 0))
+    return call(
+        kernel,
+        "heads_sum",
+        0,
+        10 * depth * wide,
+        (own, other, moving),
+        (depth // rows,),
+        [block] * 3,
+        pl.BlockSpec((3, rows, inner), lambda m: (0, m, 0)),
+        struct((3, depth, inner), F32),
     )
 
 
@@ -217,7 +244,7 @@
     length, width = x_all.shape
     wide = bias.shape[1]
     inner = wide // 3
-    rows = min(256, length)
+    rows = min(512, length)
     k, count = len(weights.arrays), blocks.shape[0]
 
     def kernel(blk, x_ref, gain_ref, shift_ref, bias_ref, keep_ref, ahead_ref, behind_ref, *refs):
@@ -243,15 +270,12 @@
             for copy in copies:
                 copy.wait()
 
-        for part in range(3):
-            cols = slice(part * inner, (part + 1) * inner)
-            merged = dot(normed_ref[...], w_ref[:, cols], NN) + bias_ref[:, cols]
-            for pair in range(inner // 128):
-                u = merged[:, pair * 128 : (pair + 1) * 128]
-                if part < 2:
-                    u = turn(u, keep_ref[...], ahead_ref[...], behind_ref[...])
-                start = part * inner + pair * 128
-                qkv_ref[:, start : start + 128] = u.astype(BF)
+        merged = dot(normed_ref[...], w_ref[...], NN) + bias_ref[...]
+        for start in range(0, wide, 128):
+            u = merged[:, start : start + 128]
+            if start < 2 * inner:
+                u = turn(u, keep_ref[...], ahead_ref[...], behind_ref[...])
+            qkv_ref[:, start : start + 128] = u.astype(BF)
 
     def whole(shape):
         return pl.BlockSpec(shape, lambda j, blk: (0, 0))
@@ -262,8 +286,8 @@
     return call(
         kernel,
         "norm_project",
-        3 * length * width * wide,
-        6 * length * width + 4 * width * wide,
+        0,
+        0,
         (x_all, gain, shift, bias, *tables, *weights.arrays),
         (length // rows,),
         [block(width), whole((1, width)), whole((1, width)), whole((1, wide))]
@@ -281,7 +305,7 @@
     length = qkv.shape[0]
     inner = qkv.shape[1] // 3
     pairs = inner // 128
-    block = min(512, length)
+    block = min(1024, length)
     count = length // block
     scale = LOG2E / math.sqrt(HD)
     n = 0 if before is None else 1
@@ -323,8 +347,8 @@
     return call(
         kernel,
         "attend",
-        40 * length * length * 128 * number,
-        8 * length * 128 * number,
+        0,
+        0,
         (qkv, qkv, qkv) + ((before,) if n else ()),
         (number, count),
         [
@@ -546,61 +570,65 @@
     return starts + [total]
 
 
-def weight_grad(blocks, rows_in, rights, cols, name, weights=None, after=()):
+def weight_grad(blocks, rows_in, right, name, more=None, weights=None, after=()):
     length, width = rows_in.shape
     half = width // 2
     count = blocks.shape[0]
     depth = width // count
-    starts = columns_of(rights, cols)
-    n, total = len(rights), starts[-1]
+    cols = min(1024, right.shape[1])
+    total = right.shape[1] // cols
     k = len(weights.arrays) if weights else 0
-    more = 1 if k else 0
-
-    def kernel(blk, a_ref, *refs):
-        w_refs, out_ref = refs[n : n + k], refs[n + k]
+    extra = 2 if k else 0
+
+    def kernel(blk, a_ref, right_ref, *refs):
         chunk, side = pl.program_id(0), pl.program_id(1)
-        if more:
-            back_ref, w_ref, sum_ref, sems = refs[n + k + 1 :]
-            inner = w_ref.shape[1]
-            copies = weights.copies(w_refs, blk, count, None, 3 * inner, inner, w_ref, sems)
-
-            @pl.when((chunk == 0) & (side == 0))
-            def _():
-                for copy in copies:
-                    copy.start()
-
-            @pl.when((chunk == total) & (side == 0))
-            def _():
-                for copy in copies:
-                    copy.wait()
-                sum_ref[...] = dot(a_ref[...], w_ref[:half, :], NN)
-
-            @pl.when((chunk == total) & (side == 1))
-            def _():
-                back_ref[...] = (sum_ref[...] + dot(a_ref[...], w_ref[half:, :], NN)).astype(BF)
-
-        for i in range(n):
-
-            @pl.when((chunk >= starts[i]) & (chunk < starts[i + 1]))
-            def _(i=i):
-                product = dot(a_ref[...], refs[i][...], TN).astype(BF)
-                for p in range(count // 2):
-                    place = pl.multiple_of(blk[side * (count // 2) + p] * depth, depth)
-                    out_ref[pl.ds(place, depth), :] = product[p * depth : (p + 1) * depth]
-
-    def right_spec(i):
-        number = starts[i + 1] - starts[i]
-        return pl.BlockSpec(
-            (length, cols), lambda n, s, blk: (0, jnp.clip(n - starts[i], 0, number - 1))
-        )
-
+
+        def product(ref, target):
+            low = dot(a_ref[...], ref[...], TN).astype(BF)
+            for p in range(count // 2):
+                place = pl.multiple_of(blk[side * (count // 2) + p] * depth, depth)
+                target[pl.ds(place, depth), :] = low[p * depth : (p + 1) * depth]
+
+        if not k:
+            product(right_ref, refs[0])
+            return
+        more_ref, w_refs, inner = refs[0], refs[1 : 1 + k], more.shape[1]
+        out_ref, more_out_ref, back_ref, w_ref, sum_ref, sems = refs[1 + k :]
+        copies = weights.copies(w_refs, blk, count, None, weights.cols - inner, inner, w_ref, sems)
+
+        @pl.when((chunk == 0) & (side == 0))
+        def _():
+            for copy in copies:
+                copy.start()
+
+        pl.when(chunk < total)(lambda: product(right_ref, out_ref))
+        pl.when(chunk == total)(lambda: product(more_ref, more_out_ref))
+
+        @pl.when((chunk == total + 1) & (side == 0))
+        def _():
+            for copy in copies:
+                copy.wait()
+            sum_ref[...] = dot(a_ref[...], w_ref[:half, :], NN)
+
+        @pl.when((chunk == total + 1) & (side == 1))
+        def _():
+            back_ref[...] = (sum_ref[...] + dot(a_ref[...], w_ref[half:, :], NN)).astype(BF)
+
+    def whole(shape):
+        return pl.BlockSpec(shape, lambda n, s, blk: (0, 0))
+
+    in_specs = [
+        pl.BlockSpec((length, half), lambda n, s, blk: (0, s)),
+        pl.BlockSpec((length, cols), lambda n, s, blk: (0, jnp.minimum(n, total - 1))),
+    ]
     out_specs = [pl.BlockSpec((width, cols), lambda n, s, blk: (0, jnp.minimum(n, total - 1)))]
-    out_shape = [struct((width, total * cols))]
+    out_shape = [struct((width, right.shape[1]))]
     scratch = []
-    if more:
-        inner = weights.cols // 4
-        out_specs.append(pl.BlockSpec((length, inner), lambda n, s, blk: (0, 0)))
-        out_shape.append(struct((length, inner)))
+    if k:
+        inner = more.shape[1]
+        in_specs += [whole((length, inner))] + [pl.BlockSpec(memory_space=pl.ANY)] * k
+        out_specs += [whole((width, inner)), whole((length, inner))]
+        out_shape += [struct((width, inner)), struct((length, inner))]
         scratch = [
             pltpu.VMEM((width, inner), BF),
             pltpu.VMEM((length, inner), F32),
@@ -609,13 +637,11 @@
     return call(
         kernel,
         name,
-        2 * length * width * total * cols,
-        2 * length * width + 4 * length * total * cols + 2 * width * total * cols,
-        (rows_in, *rights, *(weights.arrays if more else ())),
-        (total + more, 2),
-        [pl.BlockSpec((length, half), lambda n, s, blk: (0, s))]
-        + [right_spec(i) for i in range(n)]
-        + [pl.BlockSpec(memory_space=pl.ANY)] * k,
+        2 * length * width * right.shape[1],
+        2 * length * width + 4 * length * right.shape[1] + 2 * width * right.shape[1],
+        (rows_in, right, *((more, *weights.arrays) if k else ())),
+        (total + extra, 2),
+        in_specs,
         out_specs,
         out_shape,
         scratch=scratch,
@@ -688,7 +714,7 @@
     ]
 
 
-def rows_back(blocks, order, split, lefts, groups, side, name, after=()):
+def rows_back(blocks, order, splits, lefts, groups, name, after=()):
     length = lefts[0].shape[0]
     count, places = blocks.shape[0], order.shape[0]
     half = groups[0][0].rows // 2
@@ -698,8 +724,13 @@
     n = len(lefts)
     arrays = [array for weights, _, _ in groups for array in weights.arrays]
     k = len(arrays)
-    pieces = count // 2
-    plan = split_outputs(split, rows, half, places)
+    sides = sorted(splits)
+    side = sides[0] if len(sides) == 1 else None
+    plan = []
+    for i, one in enumerate(sides):
+        plan += [(i * half + col, *rest) for col, *rest in split_outputs(splits[one], rows, half, places)]
+    whole = len(sides) * half
+    pieces = max(weights.number(count, side) for weights, _, _ in groups)
 
     def kernel(blk, places_ref, *refs):
         left_refs, w_refs = refs[:n], refs[n : n + k]
@@ -769,8 +800,8 @@
     return call(
         kernel,
         name,
-        2 * length * half * depth,
-        2 * length * depth + 2 * half * depth + 2 * length * half,
+        2 * length * whole * depth,
+        2 * length * depth + 2 * whole * depth + 2 * length * whole,
         (*lefts, *arrays),
         (places,),
         [pl.BlockSpec(memory_space=pl.ANY)] * (n + k),
@@ -778,7 +809,7 @@
         [struct((len(steps) * rows, cols)) for _, cols, steps, _ in plan],
         scratch=[
             pltpu.VMEM((2, rows, depth), BF),
-            pltpu.VMEM((half, depth), BF),
+            pltpu.VMEM((whole, depth), BF),
             pltpu.SemaphoreType.DMA((2, n)),
             pltpu.SemaphoreType.DMA((len(groups), pieces)),
         ],
@@ -835,13 +866,12 @@
     )
 
 
-def turned_sums(sums, units):
-    depth, cols = sums.shape
-    inner = cols - units
-
-    def kernel(sums_ref, fc2_ref, out_ref):
-        fc2_ref[...] = sums_ref[:, :units].T.astype(F32)
-        out_ref[...] = sums_ref[:, units:].T.astype(F32)
+def turned_sums(sums):
+    n = len(sums)
+
+    def kernel(*refs):
+        for ref, out_ref in zip(refs[:n], refs[n:]):
+            out_ref[...] = ref[...].T.astype(F32)
 
     def whole(shape):
         return pl.BlockSpec(shape, lambda i: (0, 0))
@@ -850,18 +880,18 @@
         kernel,
         "turned_sums",
         0,
-        6 * depth * cols,
-        (sums,),
+        6 * sum(value.size for value in sums),
+        sums,
         (1,),
-        [whole((depth, cols))],
-        [whole((units, depth)), whole((inner, depth))],
-        [struct((units, depth), F32), struct((inner, depth), F32)],
+        [whole(value.shape) for value in sums],
+        [whole(value.shape[::-1]) for value in sums],
+        [struct(value.shape[::-1], F32) for value in sums],
     )
 
 
 def end_call(kernel, name, blocks, fulls, terms, vector, dtype, after):
     length, width = fulls[0].shape
-    rows = min(128, length)
+    rows = min(256, length)
     n = len(fulls)
     counts = [len(part) for part in terms]
 
@@ -938,9 +968,11 @@
         self.size = n_dp
         self.chips = n_dp // 2
 
-    def send(self, value):
+    def send(self, value, distance=1):
         pairs = [
-            (z * 2 + c, ((z + 1) % self.chips) * 2 + c) for z in range(self.chips) for c in range(2)
+            (z * 2 + c, ((z + distance) % self.chips) * 2 + c)
+            for z in range(self.chips)
+            for c in range(2)
         ]
         return lax.ppermute(value, "dp", pairs)
 
@@ -972,26 +1004,26 @@
     third = ln_gain.shape[0]
     x, g = layer_input[0], out_grad[0]
     x_all = lax.all_gather(x, "tensor", axis=0, tiled=True)
-    heads_own, heads_sib = [heads_shard(w_qkv.reshape(depth, 3 * inner), w_out)], []
-
-    def ring_step(own, sib, after):
-        own.append(ring.send(own[-1]))
-        sib.append(ring.swap(own[-2]))
-        own[-1], sib[-1], *rest = tie([own[-1], sib[-1], *after], [])
-        return rest
+    heads_own = [heads_shard(jnp.transpose(w_qkv, (1, 0, 2)), w_out)]
 
     vectors = jnp.stack([ln_gain, ln_bias, out_bias]).astype(F32).reshape(1, 3 * third)
     table = jnp.where(jnp.arange(n_tensor)[:, None] == t_index, vectors, 0.0)
-    table = flip_sum(table, "tensor", n_tensor)
+    table = table + sum(flip(table, "tensor", n_tensor, bit) for bit in range(1, n_tensor))
     small = jnp.concatenate([table.reshape(-1), b_qkv.astype(F32).reshape(-1), b_fc1.astype(F32).reshape(-1)])
+    fc1_shard, fc2_shard = stage(w_fc1, False, heads_own), stage(w_fc2, True, heads_own)
     g_placed, bias_part = order_columns(blocks, g, after=heads_own)
-    small, g_placed = ring_step(heads_own, heads_sib, [small, g_placed])
-    fc1_shard = stage(w_fc1, False, [small])
+    heads_own.append(ring.send(heads_own[0]))
+    heads_sib = [ring.swap(heads_own[0])]
+    small, g_placed = tie([small, g_placed], [heads_own[1], heads_sib[0]])
+    g_all = lax.all_gather(g_placed, "tensor", axis=0, tiled=True)
+
+    heads_own.append(ring.send(heads_own[1]))
+    heads_sib.append(ring.swap(heads_own[1]))
+    small = jnp.where(jnp.arange(n_dp)[:, None] == d_index, small[None, :], 0.0)
+    small = flip_sum(small, "dp", n_dp)
+    (small,) = tie([small], [heads_own[2], heads_sib[1]])
+
     tables = rotary_rows(length)
-    small = flip_sum(
-        jnp.where(jnp.arange(n_dp)[:, None] == d_index, small[None, :], 0.0), "dp", n_dp
-    )
-    small, fc1_shard = ring_step(heads_own, heads_sib, [small, fc1_shard])
     chosen = (blocks[:, None] == jnp.arange(n_dp)[None, :]).astype(F32)
     cut = n_tensor * 3 * third
     vectors = jnp.einsum("pd,dj->pj", chosen, small[:, :cut], precision=lax.Precision.HIGHEST)
@@ -1003,14 +1035,15 @@
     bias_qkv = bias_qkv.reshape(1, 3 * inner)
     bias_fc1 = jnp.transpose(small[:, tail:].reshape(n_dp, units // HD, b_width), (1, 0, 2))
     bias_fc1 = bias_fc1.reshape(1, units)
-    gain, bias_qkv, bias_fc1, fc1_shard, *tables = ring_step(
-        heads_own, heads_sib, [gain, bias_qkv, bias_fc1, fc1_shard, *tables]
-    )
     while len(heads_own) < chips:
-        ring_step(heads_own, heads_sib, [])
+        heads_own.append(ring.send(heads_own[-1]))
+        heads_sib.append(ring.swap(heads_own[-2]))
+    gain, bias_qkv, bias_fc1, fc1_shard, fc2_shard, *tables = tie(
+        [gain, bias_qkv, bias_fc1, fc1_shard, fc2_shard, *tables], [heads_own[-1], heads_sib[-1]]
+    )
     heads_sib.append(ring.swap(heads_own[-1]))
     heads_weights = Weights(heads_own + heads_sib)
-    g_all = lax.all_gather(g_placed, "tensor", axis=0, tiled=True)
+    fc2_weights = Weights([lax.all_gather(fc2_shard, "dp", axis=0, tiled=True)], depth, placed=True)
     if square:
         order = (jnp.array([3, 1, 2, 0], jnp.int32) ^ t_index).astype(jnp.int32)
     else:
@@ -1040,32 +1073,36 @@
             return [got]
         return [list(terms) for terms in zip(parts[1::2], got, last)]
 
-    fc1_own, fc1_sib = [fc1_shard], []
+    fc1_own = {k: ring.send(fc1_shard, k) for k in ((1, 3) if chips == 4 else range(1, chips))}
+    fc1_sib = {0: ring.swap(fc1_shard)}
     normed, unit, qkv = norm_project(
         blocks, x_all, gain, shift, bias_qkv, tables, heads_weights, after=[fc1_shard]
     )
-    (qkv,) = ring_step(fc1_own, fc1_sib, [qkv])
     first = pairs // 2
-    context, log_first = attend(qkv, 0, first, after=[fc1_own[-1]])
-    (log_first,) = ring_step(fc1_own, fc1_sib, [log_first])
-    context, log_second = attend(qkv, first, pairs - first, before=context, after=[fc1_own[-1]])
-    (log_second,) = ring_step(fc1_own, fc1_sib, [log_second])
-    while len(fc1_own) < chips:
-        ring_step(fc1_own, fc1_sib, [])
-    fc1_sib.append(ring.swap(fc1_own[-1]))
+    context, log_first = attend(qkv, 0, first, after=[fc1_shard])
+    near = [1, 3] if chips == 4 else []
+    log_first, *joined = tie([log_first, *(fc1_own[k] for k in near)], [fc1_sib[0]])
+    fc1_own.update(zip(near, joined))
+    if chips == 4:
+        fc1_own[2] = ring.send(fc1_own[1])
+    fc1_sib.update({k: ring.swap(fc1_own[k]) for k in near})
+    context, log_second = attend(qkv, first, pairs - first, before=context, after=[log_first])
+    far = [k for k in range(1, chips) if k not in near]
+    log_second, *joined = tie([log_second, *(fc1_own[k] for k in far)], [fc1_sib[k] for k in near])
+    fc1_own.update(zip(far, joined))
+    fc1_sib.update({k: ring.swap(fc1_own[k]) for k in far})
+    fc1_own[0] = fc1_shard
     log_total = jnp.concatenate([log_first, log_second], axis=0)
-    fc1_weights = Weights(fc1_own + fc1_sib)
-    fc2_shard = stage(w_fc2, True, [log_second])
-    fc2_weights = Weights([lax.all_gather(fc2_shard, "dp", axis=0, tiled=True)], depth, placed=True)
-    act, slope = expand(blocks, normed, fc1_weights, bias_fc1, after=[fc2_shard])
+    fc1_weights = Weights([fc1[k] for fc1 in (fc1_own, fc1_sib) for k in range(chips)])
+    act, slope = expand(blocks, normed, fc1_weights, bias_fc1, after=[log_second])
 
     def scatter(parts):
         return lax.psum_scatter(parts, "dp", scatter_dimension=0, tiled=True)
 
-    fc2_grad, context_grad = weight_grad(
-        blocks, g_all, [act, context], min(512, inner), "fc2_grad", heads_weights
-    )
-    fc2_sums = scatter(fc2_grad)
+    fc2_grad, out_grads, context_grad = weight_grad(
+        blocks, g_all, act, "fc2_grad", context, heads_weights
+    )
+    fc2_sums, out_sums = scatter(fc2_grad), scatter(out_grads)
     *backs, b_qkv_part = attend_back(qkv, context, context_grad, log_total, tables)
     heads_sib_grad, heads_own_grad = weight_grad_halves(normed, backs, inner, "heads_grad")
 
@@ -1077,51 +1114,51 @@
     heads_cols, fc2_cols = (heads_weights, 0, 3 * inner), (fc2_weights, 0, units)
     out_cols, fc1_cols = (heads_weights, 3 * inner, inner), (fc1_weights, 0, units)
     lefts = [act, context]
-    branch_own = rows_back(
-        blocks, order, split("first"), lefts, [fc2_cols, out_cols], 0, "branch_half", after=[heads_own_grad]
-    )
-    *branch_own, heads_other = tie([*branch_own, ring.swap(heads_sib_grad)], [])
+    branch = rows_back(
+        blocks, order, {0: split("first"), 1: split("second")}, lefts, [fc2_cols, out_cols], "branch",
+        after=[heads_own_grad],
+    )
+    *branch, heads_other = tie([*branch, ring.swap(heads_sib_grad)], [])
+    n = len(branch) // 2
+    branch_own, branch_sib = branch[:n], branch[n:]
     message = ring_add(1).astype(BF)
-    branch_sib = rows_back(
-        blocks, order, split("second"), lefts, [fc2_cols, out_cols], 1, "branch_half", after=[message]
-    )
-    *branch_sib, moving = tie([*branch_sib, ring.send(message)], [])
+    moving = ring.send(message)
+    hidden_grad, b_fc1_part = hidden_back(blocks, g_all, fc2_weights, slope, after=[message])
+    hidden_grad, moving = tie([hidden_grad, moving], [])
     message = ring_add(2, moving).astype(BF)
-    hidden_grad, b_fc1_part = hidden_back(blocks, g_all, fc2_weights, slope, after=[message])
-    hidden_grad, moving = tie([hidden_grad, ring.send(message)], [])
-    for k in range(3, chips):
-        message = ring_add(k, moving).astype(BF)
-        if k < chips - 1:
-            moving = ring.send(message)
-    (fc1_grad,) = weight_grad(blocks, normed, [hidden_grad], min(1024, units), "fc1_grad", after=[message])
+    (fc1_grad,) = weight_grad(blocks, normed, hidden_grad, "fc1_grad", after=[message])
     branch_got = cross_once("first", branch_own) + cross_once("second", branch_sib)
     n = len(branch_got)
     fc1_grad, moving, *branch_got = tie([fc1_grad, ring.send(message), *branch_got], [])
     fc1_sums = scatter(fc1_grad)
-    heads_sums = ring_add(0, moving)
+    for k in range(3, chips):
+        message = ring_add(k, moving).astype(BF)
+        moving = ring.send(message)
     branch_sums = cross_add(branch_own, branch_got[:1]) + cross_add(branch_sib, branch_got[1:])
     branch_last = cross_twice("first", branch_sums[:1]) + cross_twice("second", branch_sums[1:])
 
     lefts = [*backs, hidden_grad]
     back_own = rows_back(
-        blocks, order, split("both"), lefts, [heads_cols, fc1_cols], 0, "normed_back_half",
-        after=[fc1_grad, *branch_sums],
+        blocks, order, {0: split("both")}, lefts, [heads_cols, fc1_cols], "normed_back_half",
+        after=[fc1_grad, message, *branch_sums],
     )
     n = len(back_own)
-    joined = tie([*back_own, *branch_last], [])
-    back_own, branch_last = joined[:n], joined[n:]
+    joined = tie([*back_own, moving, *branch_last], [])
+    back_own, moving, branch_last = joined[:n], joined[n], joined[n + 1 :]
+    heads_sums = heads_sum(heads_own_grad, heads_other, moving)
     branch_terms = cross_terms(branch_own, branch_got[:1], branch_last[:1])
     branch_terms += cross_terms(branch_sib, branch_got[1:], branch_last[1:])
     own_got = cross_once("both", back_own)
     back_sib = rows_back(
-        blocks, order, split("both"), lefts, [heads_cols, fc1_cols], 1, "normed_back_half",
+        blocks, order, {1: split("both")}, lefts, [heads_cols, fc1_cols], "normed_back_half",
         after=[back_own[0]],
     )
     joined = tie([*back_sib, *own_got], [])
     back_sib, own_got = joined[:n], joined[n:]
 
     sib_got = cross_once("both", back_sib)
-    own_last = cross_twice("both", cross_add(back_own, own_got))
+    own_sums = cross_add(back_own, own_got)
+    own_last = cross_twice("both", own_sums)
     norm_sums = gain_sums(order, split("both"), (back_own, back_sib), unit).reshape(2, 8, n_dp, depth)
     norm_sums = jnp.einsum("pd,kpj->dkj", chosen, jnp.sum(norm_sums, axis=1), precision=lax.Precision.HIGHEST)
     b_qkv_part = jnp.sum(b_qkv_part.reshape(pairs, 3, 8, 128), axis=2)
@@ -1139,20 +1176,21 @@
 
     sums = flip_sum(by_owner, "dp", n_dp)
     sums = lax.dynamic_index_in_dim(sums, d_index, 0, keepdims=False)
-    w_fc2_grad, w_out_grad = turned_sums(fc2_sums, units)
-    layer_output = add_branch(
-        blocks, x, branch_terms, bias_out, after=[back_sib[0], w_fc2_grad, w_out_grad]
-    )
-    layer_output, sums, *sib_got = tie([layer_output, sums, *sib_got], [])
-    sib_last = cross_twice("both", cross_add(back_sib, sib_got))
-    mine = flip_sum(sums[: 3 * depth].reshape(3, depth), "tensor", n_tensor)
+    w_fc2_grad, w_out_grad = turned_sums((fc2_sums, out_sums))
+    sums, *sib_got = tie([sums, *sib_got], [w_fc2_grad, *own_sums])
+    sib_sums = cross_add(back_sib, sib_got)
+    sib_last = cross_twice("both", sib_sums)
+    layer_output = add_branch(blocks, x, branch_terms, bias_out, after=[*sib_sums, *back_sib[:1]])
+    w_fc1_grad = fc1_sums.astype(F32)
+    (sums,) = tie([sums], [layer_output, heads_sums, w_fc1_grad])
+    mine = sums[: 3 * depth].reshape(3, depth)
+    mine = mine + sum(flip(mine, "tensor", n_tensor, bit) for bit in range(1, n_tensor))
     mine = lax.dynamic_slice_in_dim(mine, t_index * third, third, 1)
     b_qkv_grad = sums[3 * depth : 3 * depth + b_qkv.size].reshape(b_qkv.shape)
     b_fc1_grad = sums[3 * depth + b_qkv.size :].reshape(b_fc1.shape)
-    w_fc1_grad = fc1_sums.astype(F32)
-    w_qkv_grad = heads_sums.reshape(depth, 3, inner)
+    w_qkv_grad = jnp.transpose(heads_sums, (1, 0, 2))
     back_terms = cross_terms(back_own, own_got, own_last) + cross_terms(back_sib, sib_got, sib_last)
-    input_grad = norm_back(blocks, x, g, back_terms, gain, after=[w_fc1_grad, w_qkv_grad])
+    input_grad = norm_back(blocks, x, g, back_terms, gain, after=[sums])
     return (
         layer_output[None],
         input_grad[None],

time: 609 us -> 594 us (0.975)
  waiting for transfers between devices: 95.5 us -> 87.9 us
    ppermute x31 -> x33, waiting for transfers between devices: 41 us -> 28.2 us  [flip(): return lax.ppermute(value, axis, [(i, i ^ bit) for i in range(size)])]
    ppermute x31 -> x33, starting transfers between devices: 25.8 us -> 28 us  [flip(): return lax.ppermute(value, axis, [(i, i ^ bit) for i in range(size)])]
    unnamed x111 -> x103, local copies, waits for them, and re-layouts: 21.7 us -> 20.9 us
  transfers between devices with their start and end apart: 45 -> 48, of which waited for: 16 -> 12; matrix products, arithmetic and copies ran while one was open for 8% -> 7% of each run, Pallas kernels for 64% -> 66%
where the time goes in v4:
time: 594 us; the launch traced here: 588 us
  Pallas kernels  391 us (66%)
  waiting for transfers between devices  87.9 us (15%)
  starting transfers between devices  34.1 us (6%)
  local copies, waits for them, and re-layouts  32.8 us (6%)
  other arithmetic  26.8 us (5%)
  between operations  15.1 us (3%)
    pallas_call x21, Pallas kernels, call(): pl.pallas_call(body, name=name, grid_spec=pltpu.PrefetchScalarGridSpec(nu...  391 us
    ppermute x9, waiting for transfers between devices, send(): return lax.ppermute(value, 'dp', pairs)  58.9 us
    ppermute x33, waiting for transfers between devices, flip(): return lax.ppermute(value, axis, [(i, i ^ bit) for i in range(size)])  28.2 us
    ppermute x33, starting transfers between devices, flip(): return lax.ppermute(value, axis, [(i, i ^ bit) for i in range(size)])  28 us
    unnamed x103, local copies, waits for them, and re-layouts  20.9 us
  transfers between devices with their start and end apart: 48, of which 12 were waited for; matrix products, arithmetic and copies ran while one was open for 7% of the time, Pallas kernels for 66%

profile of v4, /device:TPU:0, one launch (start us, length us, event | category | flops | bytes accessed | tf_op | source)
XLA Modules:
  0.0 588.4 jit_solution(9645210460404742881)
XLA Ops:
  8.0 2.3 heads_shard.1.refs_2_.refs_1_.refs_8_.refs_4_.refs_5_.refs_6_
  10.7 2.6 collective-permute-start.3
  13.5 2.4 collective-permute-start.2
  17.9 3.7 order_columns.1
  22.5 16.9 %collective-permute-done.3.refs_2_.refs_9_.refs_5_.refs_6_.refs_7_ = bf16[256,2048]{1,0:T(8,128)(2,1)S(1)} collective-permute-done((bf16[256,2048]{1,0:T(8,128)(2,1)}, bf16[256,2048]{1,0:T(8,128)(2,1)S(1)}, u32[]{:S(2)}, u32[]{:S(2)}) %collective-permute-start.3) | collective-permute-done | bytes 1048608 | tf_op jit(solution)/shard_map/ppermute | solution.py:977
  40.5 1.1 copy-done.18
  43.0 1.3 collective-permute-start.6
  44.3 24.6 %collective-permute-done.8.refs_1_.refs_10_.refs_6_.refs_7_.refs_8_ = bf16[256,2048]{1,0:T(8,128)(2,1)S(1)} collective-permute-done((bf16[256,2048]{1,0:T(8,128)(2,1)S(1)}, bf16[256,2048]{1,0:T(8,128)(2,1)S(1)}, u32[]{:S(2)}, u32[]{:S(2)}) %collective-permute-start.8) | collective-permute-done | bytes 1048608 | tf_op jit(solution)/shard_map/ppermute | solution.py:977
  69.9 5.0 fusion.1
  74.9 2.5 stage_weight.3.refs_4_
  77.5 2.3 stage_weight.2.refs_3_
  79.8 17.7 %collective-permute-done.7 = f32[8,1216]{1,0:T(8,128)S(1)} collective-permute-done((f32[8,1216]{1,0:T(8,128)S(1)}, f32[8,1216]{1,0:T(8,128)S(1)}, u32[]{:S(2)}, u32[]{:S(2)}) %collective-permute-start.7) | collective-permute-done | bytes 38944 | tf_op jit(solution)/shard_map/ppermute | solution.py:955
  98.0 1.0 copy-done.15
  105.3 2.2 collective-permute-start.13
  108.2 1.0 copy-done.23
  109.2 27.6 %norm_project.1 = (bf16[2048,2048]{1,0:T(8,128)(2,1)}, bf16[2048,2048]{1,0:T(8,128)(2,1)}, bf16[2048,1536]{1,0:T(8,128)(2,1)}) custom-call(s32[8]{0:T(128)} %pad_add_fusion.refs_0_, bf16[2048,2048]{1,0:T(8,128)(2,1)} %bitcast.39, f32[1,2048]{1,0:T(1,128)} %get-tuple-element.91.refs_2_.refs_15_, f32[1,2048]{1,0:T(1,128)} %reshape_squeeze.13.refs_3_, ...), custom_call_target="tpu_custom_call" | custom-call | tf_op jit(solution)/shard_map/norm_project/pallas_call | solution.py:40
  136.8 19.1 %attend.2 = (bf16[2048,512]{1,0:T(8,128)(2,1)}, f32[2,2,2048]{2,1,0:T(2,128)}) custom-call(bf16[2048,1536]{1,0:T(8,128)(2,1)} %get-tuple-element.98.refs_0_.refs_1_.refs_2_, bf16[2048,1536]{1,0:T(8,128)(2,1)} %get-tuple-element.98.refs_0_.refs_1_.refs_2_, bf16[2048,1536]{1,0:T(8,128)(2,1)} %get-tuple-element.98.refs_0_.refs_1_.refs_2_, ...), custom_call_target="tpu_custom_call" | custom-call | tf_op jit(solution)/shard_map/attend/pallas_call | solution.py:40
  158.7 19.1 %attend.3 = (bf16[2048,512]{1,0:T(8,128)(2,1)}, f32[2,2,2048]{2,1,0:T(2,128)}) custom-call(bf16[2048,1536]{1,0:T(8,128)(2,1)} %get-tuple-element.98.refs_0_.refs_1_.refs_2_, bf16[2048,1536]{1,0:T(8,128)(2,1)} %get-tuple-element.98.refs_0_.refs_1_.refs_2_, ...), custom_call_target="tpu_custom_call", output_to_operand_aliasing={{0}: (3, {})} | custom-call | tf_op jit(solution)/shard_map/attend/pallas_call | solution.py:40
  177.9 7.2 %collective-permute-done.16.refs_1_ = bf16[256,2048]{1,0:T(8,128)(2,1)S(1)} collective-permute-done((bf16[256,2048]{1,0:T(8,128)(2,1)}, bf16[256,2048]{1,0:T(8,128)(2,1)S(1)}, u32[]{:S(2)}, u32[]{:S(2)}) %collective-permute-start.16) | collective-permute-done | bytes 1048608 | tf_op jit(solution)/shard_map/ppermute | solution.py:977
  186.0 2.9 collective-permute-done.19.refs_8_.refs_20_
  189.9 32.1 %expand.1 = (bf16[2048,2048]{1,0:T(8,128)(2,1)}, bf16[2048,2048]{1,0:T(8,128)(2,1)}) custom-call(s32[8]{0:T(128)} %pad_add_fusion.refs_0_, bf16[2048,2048]{1,0:T(8,128)(2,1)} %get-tuple-element.97.refs_1_.refs_0_, bf16[256,2048]{1,0:T(8,128)(2,1)} %get-tuple-element.96.refs_16_.refs_3_.refs_2_.refs_14_, ...), custom_call_target="tpu_custom_call" | custom-call | flops 17179869184 | bytes 33554432 | tf_op jit(solution)/shard_map/expand/pallas_call | solution.py:40
  222.0 36.9 %fc2_grad.1 = (bf16[2048,2048]{1,0:T(8,128)(2,1)}, bf16[2048,512]{1,0:T(8,128)(2,1)}, bf16[2048,512]{1,0:T(8,128)(2,1)}) custom-call(s32[8]{0:T(128)} %pad_add_fusion.refs_0_, bf16[2048,2048]{1,0:T(8,128)(2,1)} %all-gather.7.cloned.1.call-done.refs_1_, bf16[2048,2048]{1,0:T(8,128)(2,1)} %get-tuple-element.108.refs_2_, ...), custom_call_target="tpu_custom_call" | custom-call | flops 17179869184 | bytes 33554432 | tf_op jit(solution)/shard_map/fc2_grad/pallas_call | solution.py:40
  260.4 65.5 %attend_back.1 = (bf16[2048,512]{1,0:T(8,128)(2,1)}, bf16[2048,512]{1,0:T(8,128)(2,1)}, bf16[2048,512]{1,0:T(8,128)(2,1)}, f32[4,24,128]{2,1,0:T(8,128)}) custom-call(bf16[2048,1536]{1,0:T(8,128)(2,1)} %get-tuple-element.98.refs_0_.refs_1_.refs_2_, bf16[2048,1536]{1,0:T(8,128)(2,1)} %get-tuple-element.98.refs_0_.refs_1_.refs_2_, ...), custom_call_target="tpu_custom_call" | custom-call | flops 128849018880 | bytes 16777216 | tf_op jit(solution)/shard_map/attend_back/pallas_call | solution.py:40
  325.9 20.8 %heads_grad.1 = (bf16[1024,1536]{1,0:T(8,128)(2,1)}, bf16[1024,1536]{1,0:T(8,128)(2,1)}) custom-call(bf16[2048,2048]{1,0:T(8,128)(2,1)} %get-tuple-element.97.refs_1_.refs_0_, bf16[2048,512]{1,0:T(8,128)(2,1)} %get-tuple-element.113.refs_1_.refs_2_, bf16[2048,512]{1,0:T(8,128)(2,1)} %get-tuple-element.114.refs_2_.refs_3_, ...), custom_call_target="tpu_custom_call" | custom-call | flops 12884901888 | bytes 27262976 | tf_op jit(solution)/shard_map/heads_grad/pallas_call | solution.py:40
  347.3 31.3 %branch.1 = (bf16[1024,1024]{1,0:T(8,128)(2,1)}, bf16[1024,1024]{1,0:T(8,128)(2,1)}, bf16[1024,1024]{1,0:T(8,128)(2,1)}, bf16[1024,1024]{1,0:T(8,128)(2,1)}) custom-call(s32[8]{0:T(128)} %pad_add_fusion.refs_0_, s32[4]{0:T(128)} %broadcast_xor_fusion.refs_1_.refs_0_, bf16[2048,2048]{1,0:T(8,128)(2,1)} %get-tuple-element.108.refs_2_, ...), custom_call_target="tpu_custom_call" | custom-call | flops 21474836480 | bytes 29360128 | tf_op jit(solution)/shard_map/branch/pallas_call | solution.py:40
  378.6 1.7 copy-done
  380.3 1.6 add_convert_fusion.4.refs_4_
  381.9 1.6 collective-permute-start.23
  383.6 1.5 collective-permute-start.24
  385.1 26.1 %hidden_back.1 = (bf16[2048,2048]{1,0:T(8,128)(2,1)}, f32[8,2048]{1,0:T(8,128)}) custom-call(s32[8]{0:T(128)} %pad_add_fusion.refs_0_, bf16[2048,2048]{1,0:T(8,128)(2,1)} %all-gather.7.cloned.1.call-done.refs_1_, bf16[2048,2048]{1,0:T(8,128)(2,1)} %all-gather.5.cloned.1.call-done.refs_4_.refs_2_, bf16[2048,2048]{1,0:T(8,128)(2,1)} %get-tuple-element.123.refs_3_, ...), custom_call_target="tpu_custom_call" | custom-call | flops 17179869184 | bytes 33554432 | tf_op jit(solution)/shard_map/hidden_back/pallas_call | solution.py:40
  411.2 6.1 %collective-permute-done.21.refs_1_ = bf16[256,1536]{1,0:T(8,128)(2,1)S(1)} collective-permute-done((bf16[256,1536]{1,0:T(8,128)(2,1)S(1)}, bf16[256,1536]{1,0:T(8,128)(2,1)S(1)}, u32[]{:S(2)}, u32[]{:S(2)}) %collective-permute-start.21) | collective-permute-done | bytes 786464 | tf_op jit(solution)/shard_map/ppermute | solution.py:977
  418.1 1.9 copy-done.1
  420.0 1.7 add_convert_fusion.3.refs_3_
  422.6 24.5 %fc1_grad.1.refs_0_ = bf16[2048,2048]{1,0:T(8,128)(2,1)} custom-call(s32[8]{0:T(128)} %pad_add_fusion.refs_0_, bf16[2048,2048]{1,0:T(8,128)(2,1)} %get-tuple-element.97.refs_1_.refs_0_, bf16[2048,2048]{1,0:T(8,128)(2,1)} %get-tuple-element.126.refs_2_.refs_5_, bf16[256,1536]{1,0:T(8,128)(2,1)} %copy-done.33), custom_call_target="tpu_custom_call" | custom-call | flops 17179869184 | bytes 33554432 | tf_op jit(solution)/shard_map/fc1_grad/pallas_call | solution.py:40
  447.2 1.8 add_convert_fusion.2.refs_23_
  449.2 2.0 add_convert_fusion.refs_25_
  451.3 1.5 collective-permute-start.27
  452.8 1.9 add_convert_fusion.1.refs_24_
  454.7 1.3 collective-permute-start.26
  456.0 23.6 %normed_back_half.2 = (bf16[1024,512]{1,0:T(8,128)(2,1)}, bf16[1024,512]{1,0:T(8,128)(2,1)}, bf16[1024,512]{1,0:T(8,128)(2,1)}, bf16[1024,512]{1,0:T(8,128)(2,1)}) custom-call(s32[8]{0:T(128)} %pad_add_fusion.refs_0_, s32[4]{0:T(128)} %broadcast_xor_fusion.refs_1_.refs_0_, bf16[2048,512]{1,0:T(8,128)(2,1)} %get-tuple-element.113.refs_1_.refs_2_, ...), custom_call_target="tpu_custom_call" | custom-call | flops 15032385536 | bytes 26214400 | tf_op jit(solution)/shard_map/normed_back_half/pallas_call | solution.py:40
  479.6 4.1 collective-permute-done.25.refs_4_
  485.3 1.5 collective-permute-start.29
  486.8 1.5 collective-permute-start.28
  488.2 23.4 %normed_back_half.3 = (bf16[1024,512]{1,0:T(8,128)(2,1)}, bf16[1024,512]{1,0:T(8,128)(2,1)}, bf16[1024,512]{1,0:T(8,128)(2,1)}, bf16[1024,512]{1,0:T(8,128)(2,1)}) custom-call(s32[8]{0:T(128)} %pad_add_fusion.refs_0_, s32[4]{0:T(128)} %broadcast_xor_fusion.refs_1_.refs_0_, bf16[2048,512]{1,0:T(8,128)(2,1)} %get-tuple-element.113.refs_1_.refs_2_, ...), custom_call_target="tpu_custom_call" | custom-call | flops 15032385536 | bytes 26214400 | tf_op jit(solution)/shard_map/normed_back_half/pallas_call | solution.py:40
  515.7 8.6 %gain_sums.1 = f32[16,2048]{1,0:T(8,128)} custom-call(s32[4]{0:T(128)} %broadcast_xor_fusion.refs_1_.refs_0_, bf16[2048,2048]{1,0:T(8,128)(2,1)} %get-tuple-element.148.refs_1_, bf16[1024,512]{1,0:T(8,128)(2,1)} %get-tuple-element.141.refs_22_.refs_2_, bf16[1024,512]{1,0:T(8,128)(2,1)} %get-tuple-element.149.refs_3_, ...), custom_call_target="tpu_custom_call" | custom-call | bytes 16777216 | tf_op jit(solution)/shard_map/gain_sums/pallas_call | solution.py:40
  524.2 1.0 reduce_sum.27
  525.7 1.2 collective-permute-done.30
  526.9 2.0 add_convert_fusion.8.refs_4_
  528.9 3.1 collective-permute-done.31
  533.9 1.4 collective-permute-start.36
  535.3 1.5 collective-permute-start.35
  536.8 2.4 collective-permute-done.32
  539.8 3.1 turned_sums.1
  543.8 1.2 copy-done.6
  545.1 1.2 add_convert_fusion.6.refs_9_
  546.3 1.4 add_convert_fusion.5.refs_10_
  547.6 1.5 collective-permute-start.38
  549.2 1.4 collective-permute-start.37
  551.3 3.9 heads_sum.1.refs_2_
  555.1 5.7 add_branch.1.refs_1_
  560.8 2.8 convert_element_type.147.refs_3_
  564.9 1.4 collective-permute-start.40
  566.3 1.5 collective-permute-start.39
  572.3 8.4 %norm_back.1 = f32[512,2048]{1,0:T(8,128)} custom-call(s32[8]{0:T(128)} %pad_add_fusion.refs_0_, bf16[512,2048]{1,0:T(8,128)(2,1)} %bitcast.36, bf16[512,2048]{1,0:T(8,128)(2,1)} %bitcast.38, bf16[1024,512]{1,0:T(8,128)(2,1)} %get-tuple-element.149.refs_3_, bf16[1024,512]{1,0:T(8,128)(2,1)} %get-tuple-element.160.refs_4_, ...), custom_call_target="tpu_custom_call" | custom-call | bytes 10485760 | tf_op jit(solution)/shard_map/norm_back/pallas_call | solution.py:40
  (246 shorter events, 40.4 us)
Async XLA Ops:
  7.2 6.1 %copy-start.46 = (bf16[64]{0:T(256)(128)(2,1)S(1)}, bf16[64]{0:T(256)(128)(2,1)}, u32[]{:S(2)}) copy-start(bf16[64]{0:T(256)(128)(2,1)} %param.15) | copy-start | bytes 388
  7.2 10.4 %copy-start.44 = (bf16[3,8,8]{2,1,0:T(8,128)(2,1)S(1)}, bf16[3,8,8]{2,1,0:T(8,128)(2,1)}, u32[]{:S(2)}) copy-start(bf16[3,8,8]{2,1,0:T(8,128)(2,1)} %param.17) | copy-start | bytes 1156
  7.2 10.5 %copy-start.45 = (bf16[32,8]{0,1:T(8,128)(2,1)S(1)}, bf16[32,8]{0,1:T(8,128)(2,1)}, u32[]{:S(2)}) copy-start(bf16[32,8]{0,1:T(8,128)(2,1)} %param.20) | copy-start | bytes 1540
  7.2 100.9 %all-gather.9.cloned.1.call-start = ((), (), s32[]{:S(2)}) async-start(), calls=%async_computation.8 | async-start | bytes 10485760 | tf_op jit(solution)/shard_map/all_gather | solution.py:1006
  8.0 214.0 %all-gather.7.cloned.1.call-start = ((), (), s32[]{:S(2)}) async-start(), calls=%async_computation.4 | async-start | bytes 10485760 | tf_op jit(solution)/shard_map/all_gather | solution.py:1018
  10.3 12.2 %collective-permute-start.4 = (bf16[256,2048]{1,0:T(8,128)(2,1)}, bf16[256,2048]{1,0:T(8,128)(2,1)S(1)}, u32[]{:S(2)}, u32[]{:S(2)}) collective-permute-start(bf16[256,2048]{1,0:T(8,128)(2,1)} %heads_shard.1.refs_2_.refs_1_.refs_8_.refs_4_.refs_5_.refs_6_), channel_id=1, source_target_pairs={{0,4},{4,0},{8,12},{12,8},{16,20},{20,16},{24,28},{28,24},{1,5},{5... | collective-permute-start | bytes 3145736 | tf_op jit(solution)/shard_map/ppermute | solution.py:955
  10.7 28.6 %collective-permute-start.3 = (bf16[256,2048]{1,0:T(8,128)(2,1)}, bf16[256,2048]{1,0:T(8,128)(2,1)S(1)}, u32[]{:S(2)}, u32[]{:S(2)}) collective-permute-start(bf16[256,2048]{1,0:T(8,128)(2,1)} %heads_shard.1.refs_2_.refs_1_.refs_8_.refs_4_.refs_5_.refs_6_), channel_id=1, source_target_pairs={{0,8},{4,12},{8,16},{12,20},{16,24},{20,28},{24,0},{28,4},{1,9},{5... | collective-permute-start | bytes 3145736 | tf_op jit(solution)/shard_map/ppermute | solution.py:977
  13.5 8.1 %collective-permute-start.2 = (f32[4,192]{1,0:T(4,128)S(1)}, f32[4,192]{1,0:T(4,128)S(1)}, u32[]{:S(2)}, u32[]{:S(2)}) collective-permute-start(f32[4,192]{1,0:T(4,128)S(1)} %broadcast_select_fusion.1), channel_id=1, source_target_pairs={{0,3},{1,2},{2,1},{3,0},{4,7},{5,6},{6,5},{7,4},{8,11},{9,10},{10,... | collective-permute-start | bytes 9224 | tf_op jit(solution)/shard_map/ppermute | solution.py:955
  16.0 5.7 collective-permute-start.1
  16.5 5.2 collective-permute-start
  22.5 16.9 %copy-start.16 = (bf16[256,2048]{1,0:T(8,128)(2,1)}, bf16[256,2048]{1,0:T(8,128)(2,1)S(1)}, u32[]{:S(2)}) copy-start(bf16[256,2048]{1,0:T(8,128)(2,1)S(1)} %collective-permute-done.4.refs_3_.refs_12_.refs_8_.refs_9_.refs_10_) | copy-start | bytes 3145732
  40.4 306.9 %all-gather.5.cloned.1.call-start = ((), (), s32[]{:S(2)}) async-start(), calls=%async_computation.3 | async-start | bytes 9437184 | tf_op jit(solution)/shard_map/all_gather | solution.py:1046
  41.6 27.3 %collective-permute-start.8 = (bf16[256,2048]{1,0:T(8,128)(2,1)S(1)}, bf16[256,2048]{1,0:T(8,128)(2,1)S(1)}, u32[]{:S(2)}, u32[]{:S(2)}) collective-permute-start(bf16[256,2048]{1,0:T(8,128)(2,1)S(1)} %copy-done.18), channel_id=1, source_target_pairs={{0,8},{4,12},{8,16},{12,20},{16,24},{20,28},{24,0},{28,4},{1,9},{5... | collective-permute-start | bytes 3145736 | tf_op jit(solution)/shard_map/ppermute | solution.py:977
  41.7 1.2 collective-permute-start.5
  41.7 56.3 %collective-permute-start.9 = (bf16[256,2048]{1,0:T(8,128)(2,1)S(1)}, bf16[256,2048]{1,0:T(8,128)(2,1)S(1)}, u32[]{:S(2)}, u32[]{:S(2)}) collective-permute-start(bf16[256,2048]{1,0:T(8,128)(2,1)S(1)} %copy-done.18), channel_id=1, source_target_pairs={{0,4},{4,0},{8,12},{12,8},{16,20},{20,16},{24,28},{28,24},{1,5},{5... | collective-permute-start | bytes 3145736 | tf_op jit(solution)/shard_map/ppermute | solution.py:955
  43.0 26.1 %collective-permute-start.6 = (f32[8,1216]{1,0:T(8,128)S(1)}, f32[8,1216]{1,0:T(8,128)S(1)}, u32[]{:S(2)}, u32[]{:S(2)}) collective-permute-start(f32[8,1216]{1,0:T(8,128)S(1)} %fusion.4), channel_id=1, source_target_pairs={{0,8},{4,12},{8,0},{12,4},{16,24},{20,28},{24,16},{28,20},{1,9},{5... | collective-permute-start | bytes 116744 | tf_op jit(solution)/shard_map/ppermute | solution.py:955
  68.9 8.6 %copy-start.14 = (bf16[256,2048]{1,0:T(8,128)(2,1)}, bf16[256,2048]{1,0:T(8,128)(2,1)S(1)}, u32[]{:S(2)}) copy-start(bf16[256,2048]{1,0:T(8,128)(2,1)S(1)} %collective-permute-done.8.refs_1_.refs_10_.refs_6_.refs_7_.refs_8_) | copy-start | bytes 3145732
  68.9 35.8 %collective-permute-start.11 = (bf16[256,2048]{1,0:T(8,128)(2,1)S(1)}, bf16[256,2048]{1,0:T(8,128)(2,1)}, u32[]{:S(2)}, u32[]{:S(2)}) collective-permute-start(bf16[256,2048]{1,0:T(8,128)(2,1)S(1)} %collective-permute-done.8.refs_1_.refs_10_.refs_6_.refs_7_.refs_8_), channel_id=1, source_target_pairs={{0,4},{4,0},{8,12},{12,8},{16,20},{20,16},{24,28},{28,24},{1,5},{5... | collective-permute-start | bytes 3145736 | tf_op jit(solution)/shard_map/ppermute | solution.py:955
  68.9 35.8 %collective-permute-start.10 = (bf16[256,2048]{1,0:T(8,128)(2,1)S(1)}, bf16[256,2048]{1,0:T(8,128)(2,1)}, u32[]{:S(2)}, u32[]{:S(2)}) collective-permute-start(bf16[256,2048]{1,0:T(8,128)(2,1)S(1)} %collective-permute-done.8.refs_1_.refs_10_.refs_6_.refs_7_.refs_8_), channel_id=1, source_target_pairs={{0,8},{4,12},{8,16},{12,20},{16,24},{20,28},{24,0},{28,4},{1,9},{5... | collective-permute-start | bytes 3145736 | tf_op jit(solution)/shard_map/ppermute | solution.py:977
  69.2 28.3 %collective-permute-start.7 = (f32[8,1216]{1,0:T(8,128)S(1)}, f32[8,1216]{1,0:T(8,128)S(1)}, u32[]{:S(2)}, u32[]{:S(2)}) collective-permute-start(f32[8,1216]{1,0:T(8,128)S(1)} %fusion.16), channel_id=1, source_target_pairs={{0,16},{4,20},{8,24},{12,28},{16,0},{20,4},{24,8},{28,12},{1,17},{... | collective-permute-start | bytes 116744 | tf_op jit(solution)/shard_map/ppermute | solution.py:955
  77.5 23.1 %copy-start.42 = (s32[8]{0:T(128)S(1)}, s32[8]{0:T(128)}, u32[]{:S(2)}) copy-start(s32[8]{0:T(128)} %pad_add_fusion.refs_0_) | copy-start | bytes 100
  104.7 435.1 %reduce-scatter.6.cloned.1.call-start = ((), (), s32[]{:S(2)}) async-start(), calls=%async_computation.6 | async-start | bytes 2359296 | tf_op jit(solution)/shard_map/reduce_scatter | solution.py:1100
  104.7 3.4 collective-permute-start.12
  104.8 51.1 %collective-permute-start.15 = (bf16[256,2048]{1,0:T(8,128)(2,1)}, bf16[256,2048]{1,0:T(8,128)(2,1)S(1)}, u32[]{:S(2)}, u32[]{:S(2)}) collective-permute-start(bf16[256,2048]{1,0:T(8,128)(2,1)} %get-tuple-element.96.refs_16_.refs_3_.refs_2_.refs_14_), channel_id=1, source_target_pairs={{0,4},{4,0},{8,12},{12,8},{16,20},{20,16},{24,28},{28,24},{1,5},{5... | collective-permute-start | bytes 3145736 | tf_op jit(solution)/shard_map/ppermute | solution.py:955
  105.3 50.6 %collective-permute-start.14 = (bf16[256,2048]{1,0:T(8,128)(2,1)}, bf16[256,2048]{1,0:T(8,128)(2,1)S(1)}, u32[]{:S(2)}, u32[]{:S(2)}) collective-permute-start(bf16[256,2048]{1,0:T(8,128)(2,1)} %get-tuple-element.96.refs_16_.refs_3_.refs_2_.refs_14_), channel_id=1, source_target_pairs={{0,24},{4,28},{8,0},{12,4},{16,8},{20,12},{24,16},{28,20},{1,25},{... | collective-permute-start | bytes 3145736 | tf_op jit(solution)/shard_map/ppermute | solution.py:977
  105.3 50.6 %collective-permute-start.13 = (bf16[256,2048]{1,0:T(8,128)(2,1)}, bf16[256,2048]{1,0:T(8,128)(2,1)}, u32[]{:S(2)}, u32[]{:S(2)}) collective-permute-start(bf16[256,2048]{1,0:T(8,128)(2,1)} %get-tuple-element.96.refs_16_.refs_3_.refs_2_.refs_14_), channel_id=1, source_target_pairs={{0,8},{4,12},{8,16},{12,20},{16,24},{20,28},{24,0},{28,4},{1,9},{5... | collective-permute-start | bytes 3145736 | tf_op jit(solution)/shard_map/ppermute | solution.py:977
  157.3 20.6 %collective-permute-start.18 = (bf16[256,2048]{1,0:T(8,128)(2,1)}, bf16[256,2048]{1,0:T(8,128)(2,1)S(1)}, u32[]{:S(2)}, u32[]{:S(2)}) collective-permute-start(bf16[256,2048]{1,0:T(8,128)(2,1)} %get-tuple-element.104.refs_5_.refs_17_), channel_id=1, source_target_pairs={{0,4},{4,0},{8,12},{12,8},{16,20},{20,16},{24,28},{28,24},{1,5},{5... | collective-permute-start | bytes 3145736 | tf_op jit(solution)/shard_map/ppermute | solution.py:955
  157.3 20.6 %collective-permute-start.17 = (bf16[256,2048]{1,0:T(8,128)(2,1)}, bf16[256,2048]{1,0:T(8,128)(2,1)S(1)}, u32[]{:S(2)}, u32[]{:S(2)}) collective-permute-start(bf16[256,2048]{1,0:T(8,128)(2,1)} %get-tuple-element.100.refs_3_.refs_15_), channel_id=1, source_target_pairs={{0,4},{4,0},{8,12},{12,8},{16,20},{20,16},{24,28},{28,24},{1,5},{5... | collective-permute-start | bytes 3145736 | tf_op jit(solution)/shard_map/ppermute | solution.py:955
  157.8 27.3 %collective-permute-start.16 = (bf16[256,2048]{1,0:T(8,128)(2,1)}, bf16[256,2048]{1,0:T(8,128)(2,1)S(1)}, u32[]{:S(2)}, u32[]{:S(2)}) collective-permute-start(bf16[256,2048]{1,0:T(8,128)(2,1)} %get-tuple-element.100.refs_3_.refs_15_), channel_id=1, source_target_pairs={{0,8},{4,12},{8,16},{12,20},{16,24},{20,28},{24,0},{28,4},{1,9},{5... | collective-permute-start | bytes 3145736 | tf_op jit(solution)/shard_map/ppermute | solution.py:977
  177.8 7.2 %copy-start.25 = (bf16[256,2048]{1,0:T(8,128)(2,1)}, bf16[256,2048]{1,0:T(8,128)(2,1)S(1)}, u32[]{:S(2)}) copy-start(bf16[256,2048]{1,0:T(8,128)(2,1)S(1)} %collective-permute-done.18.refs_3_.refs_9_.refs_21_) | copy-start | bytes 3145732
  177.9 7.2 %copy-start.26 = (bf16[256,2048]{1,0:T(8,128)(2,1)}, bf16[256,2048]{1,0:T(8,128)(2,1)S(1)}, u32[]{:S(2)}) copy-start(bf16[256,2048]{1,0:T(8,128)(2,1)S(1)} %collective-permute-done.17.refs_2_.refs_7_.refs_19_) | copy-start | bytes 3145732
  186.0 2.9 collective-permute-start.19
  258.9 280.9 %reduce-scatter.4.cloned.1.call-start = ((), (), s32[]{:S(2)}) async-start(), calls=%async_computation.5 | async-start | bytes 9437184 | tf_op jit(solution)/shard_map/reduce_scatter | solution.py:1100
  260.3 300.5 %reduce-scatter.8.cloned.1.call-start = ((), (), s32[]{:S(2)}) async-start(), calls=%async_computation.7 | async-start | bytes 9437184 | tf_op jit(solution)/shard_map/reduce_scatter | solution.py:1100
  325.9 20.9 %copy-start.50 = (s32[4]{0:T(128)S(1)}, s32[4]{0:T(128)}, u32[]{:S(2)}) copy-start(s32[4]{0:T(128)} %constant.99.clone) | copy-start | bytes 52
  346.7 31.9 %collective-permute-start.20 = (bf16[1024,1536]{1,0:T(8,128)(2,1)}, bf16[1024,1536]{1,0:T(8,128)(2,1)S(1)}, u32[]{:S(2)}, u32[]{:S(2)}) collective-permute-start(bf16[1024,1536]{1,0:T(8,128)(2,1)} %get-tuple-element.121), channel_id=1, source_target_pairs={{0,4},{4,0},{8,12},{12,8},{16,20},{20,16},{24,28},{28,24},{1,5},{5... | collective-permute-start | bytes 9437192 | tf_op jit(solution)/shard_map/ppermute | solution.py:955
  381.9 35.4 %collective-permute-start.21 = (bf16[256,1536]{1,0:T(8,128)(2,1)S(1)}, bf16[256,1536]{1,0:T(8,128)(2,1)S(1)}, u32[]{:S(2)}, u32[]{:S(2)}) collective-permute-start(bf16[256,1536]{1,0:T(8,128)(2,1)S(1)} %add_convert_fusion.4.refs_4_), channel_id=1, source_target_pairs={{0,8},{4,12},{8,16},{12,20},{16,24},{20,28},{24,0},{28,4},{1,9},{5... | collective-permute-start | bytes 2359304 | tf_op jit(solution)/shard_map/ppermute | solution.py:977
  381.9 65.2 %collective-permute-start.23 = (bf16[1024,1024]{1,0:T(8,128)(2,1)}, bf16[1024,1024]{1,0:T(8,128)(2,1)}, u32[]{:S(2)}, u32[]{:S(2)}) collective-permute-start(bf16[1024,1024]{1,0:T(8,128)(2,1)} %get-tuple-element.128), channel_id=1, source_target_pairs={{0,1},{1,0},{2,3},{3,2},{4,5},{5,4},{6,7},{7,6},{8,9},{9,8},{10,11... | collective-permute-start | bytes 6291464 | tf_op jit(solution)/shard_map/ppermute | solution.py:955
  383.6 63.5 %collective-permute-start.24 = (bf16[1024,1024]{1,0:T(8,128)(2,1)}, bf16[1024,1024]{1,0:T(8,128)(2,1)}, u32[]{:S(2)}, u32[]{:S(2)}) collective-permute-start(bf16[1024,1024]{1,0:T(8,128)(2,1)} %get-tuple-element.129), channel_id=1, source_target_pairs={{0,2},{1,3},{2,0},{3,1},{4,6},{5,7},{6,4},{7,5},{8,10},{9,11},{10,... | collective-permute-start | bytes 6291464 | tf_op jit(solution)/shard_map/ppermute | solution.py:955
  421.7 25.4 %collective-permute-start.22 = (bf16[256,1536]{1,0:T(8,128)(2,1)S(1)}, bf16[256,1536]{1,0:T(8,128)(2,1)}, u32[]{:S(2)}, u32[]{:S(2)}) collective-permute-start(bf16[256,1536]{1,0:T(8,128)(2,1)S(1)} %add_convert_fusion.3.refs_3_), channel_id=1, source_target_pairs={{0,8},{4,12},{8,16},{12,20},{16,24},{20,28},{24,0},{28,4},{1,9},{5... | collective-permute-start | bytes 2359304 | tf_op jit(solution)/shard_map/ppermute | solution.py:977
  449.0 34.7 %collective-permute-start.25 = (bf16[256,1536]{1,0:T(8,128)(2,1)S(1)}, bf16[256,1536]{1,0:T(8,128)(2,1)S(1)}, u32[]{:S(2)}, u32[]{:S(2)}) collective-permute-start(bf16[256,1536]{1,0:T(8,128)(2,1)S(1)} %add_convert_fusion.2.refs_23_), channel_id=1, source_target_pairs={{0,8},{4,12},{8,16},{12,20},{16,24},{20,28},{24,0},{28,4},{1,9},{5... | collective-permute-start | bytes 2359304 | tf_op jit(solution)/shard_map/ppermute | solution.py:977
  451.3 32.5 %collective-permute-start.27 = (bf16[512,1024]{1,0:T(8,128)(2,1)S(1)}, bf16[512,1024]{1,0:T(8,128)(2,1)S(1)}, u32[]{:S(2)}, u32[]{:S(2)}) collective-permute-start(bf16[512,1024]{1,0:T(8,128)(2,1)S(1)} %add_convert_fusion.refs_25_), channel_id=1, source_target_pairs={{0,1},{1,0},{2,3},{3,2},{4,5},{5,4},{6,7},{7,6},{8,9},{9,8},{10,11... | collective-permute-start | bytes 3145736 | tf_op jit(solution)/shard_map/ppermute | solution.py:955
  454.7 29.0 %collective-permute-start.26 = (bf16[512,1024]{1,0:T(8,128)(2,1)S(1)}, bf16[512,1024]{1,0:T(8,128)(2,1)S(1)}, u32[]{:S(2)}, u32[]{:S(2)}) collective-permute-start(bf16[512,1024]{1,0:T(8,128)(2,1)S(1)} %add_convert_fusion.1.refs_24_), channel_id=1, source_target_pairs={{0,2},{1,3},{2,0},{3,1},{4,6},{5,7},{6,4},{7,5},{8,10},{9,11},{10,... | collective-permute-start | bytes 3145736 | tf_op jit(solution)/shard_map/ppermute | solution.py:955
  485.3 26.4 %collective-permute-start.29 = (bf16[1024,512]{1,0:T(8,128)(2,1)}, bf16[1024,512]{1,0:T(8,128)(2,1)S(1)}, u32[]{:S(2)}, u32[]{:S(2)}) collective-permute-start(bf16[1024,512]{1,0:T(8,128)(2,1)} %get-tuple-element.146.refs_4_), channel_id=1, source_target_pairs={{0,2},{1,3},{2,0},{3,1},{4,6},{5,7},{6,4},{7,5},{8,10},{9,11},{10,... | collective-permute-start | bytes 3145736 | tf_op jit(solution)/shard_map/ppermute | solution.py:955
  486.8 24.9 %collective-permute-start.28 = (bf16[1024,512]{1,0:T(8,128)(2,1)}, bf16[1024,512]{1,0:T(8,128)(2,1)S(1)}, u32[]{:S(2)}, u32[]{:S(2)}) collective-permute-start(bf16[1024,512]{1,0:T(8,128)(2,1)} %get-tuple-element.141.refs_22_.refs_2_), channel_id=1, source_target_pairs={{0,1},{1,0},{2,3},{3,2},{4,5},{5,4},{6,7},{7,6},{8,9},{9,8},{10,11... | collective-permute-start | bytes 3145736 | tf_op jit(solution)/shard_map/ppermute | solution.py:955
  513.1 29.8 %collective-permute-start.34 = (bf16[1024,512]{1,0:T(8,128)(2,1)}, bf16[1024,512]{1,0:T(8,128)(2,1)S(1)}, u32[]{:S(2)}, u32[]{:S(2)}) collective-permute-start(bf16[1024,512]{1,0:T(8,128)(2,1)} %get-tuple-element.152.refs_8_), channel_id=1, source_target_pairs={{0,2},{1,3},{2,0},{3,1},{4,6},{5,7},{6,4},{7,5},{8,10},{9,11},{10,... | collective-permute-start | bytes 3145736 | tf_op jit(solution)/shard_map/ppermute | solution.py:955
  513.7 29.2 %collective-permute-start.33 = (bf16[1024,512]{1,0:T(8,128)(2,1)}, bf16[1024,512]{1,0:T(8,128)(2,1)}, u32[]{:S(2)}, u32[]{:S(2)}) collective-permute-start(bf16[1024,512]{1,0:T(8,128)(2,1)} %get-tuple-element.151.refs_6_.refs_11_), channel_id=1, source_target_pairs={{0,1},{1,0},{2,3},{3,2},{4,5},{5,4},{6,7},{7,6},{8,9},{9,8},{10,11... | collective-permute-start | bytes 3145736 | tf_op jit(solution)/shard_map/ppermute | solution.py:955
  515.7 9.6 %copy-start.43 = (s32[8]{0:T(128)S(1)}, s32[8]{0:T(128)}, u32[]{:S(2)}) copy-start(s32[8]{0:T(128)} %pad_add_fusion.refs_0_) | copy-start | bytes 100
  515.7 11.2 %copy-start.4 = (bf16[1024,512]{1,0:T(8,128)(2,1)S(1)}, bf16[1024,512]{1,0:T(8,128)(2,1)}, u32[]{:S(2)}) copy-start(bf16[1024,512]{1,0:T(8,128)(2,1)} %get-tuple-element.149.refs_3_) | copy-start | bytes 3145732
  524.2 8.8 %copy-start.5 = (bf16[1024,512]{1,0:T(8,128)(2,1)S(1)}, bf16[1024,512]{1,0:T(8,128)(2,1)}, u32[]{:S(2)}) copy-start(bf16[1024,512]{1,0:T(8,128)(2,1)} %get-tuple-element.150.refs_5_.refs_6_) | copy-start | bytes 3145732
  525.6 1.2 collective-permute-start.30
  525.7 7.4 %copy-start.10 = (bf16[1024,512]{1,0:T(8,128)(2,1)S(1)}, bf16[1024,512]{1,0:T(8,128)(2,1)}, u32[]{:S(2)}) copy-start(bf16[1024,512]{1,0:T(8,128)(2,1)} %get-tuple-element.161.refs_7_) | copy-start | bytes 3145732
  526.9 5.1 collective-permute-start.31
  532.0 7.1 %collective-permute-start.32 = (f32[8,1216]{1,0:T(8,128)S(1)}, f32[8,1216]{1,0:T(8,128)S(1)}, u32[]{:S(2)}, u32[]{:S(2)}) collective-permute-start(f32[8,1216]{1,0:T(8,128)S(1)} %add.164), channel_id=1, source_target_pairs={{0,16},{4,20},{8,24},{12,28},{16,0},{20,4},{24,8},{28,12},{1,17},{... | collective-permute-start | bytes 116744 | tf_op jit(solution)/shard_map/ppermute | solution.py:955
  533.9 30.9 %collective-permute-start.36 = (bf16[512,512]{1,0:T(8,128)(2,1)}, bf16[512,512]{1,0:T(8,128)(2,1)}, u32[]{:S(2)}, u32[]{:S(2)}) collective-permute-start(bf16[512,512]{1,0:T(8,128)(2,1)} %add_convert_fusion.7.refs_5_), channel_id=1, source_target_pairs={{0,1},{1,0},{2,3},{3,2},{4,5},{5,4},{6,7},{7,6},{8,9},{9,8},{10,11... | collective-permute-start | bytes 1572872 | tf_op jit(solution)/shard_map/ppermute | solution.py:955
  535.3 31.0 %collective-permute-start.35 = (bf16[512,512]{1,0:T(8,128)(2,1)}, bf16[512,512]{1,0:T(8,128)(2,1)}, u32[]{:S(2)}, u32[]{:S(2)}) collective-permute-start(bf16[512,512]{1,0:T(8,128)(2,1)} %add_convert_fusion.8.refs_4_), channel_id=1, source_target_pairs={{0,2},{1,3},{2,0},{3,1},{4,6},{5,7},{6,4},{7,5},{8,10},{9,11},{10,... | collective-permute-start | bytes 1572872 | tf_op jit(solution)/shard_map/ppermute | solution.py:955
  543.8 6.8 %copy-start.40 = (f32[8,4,64]{2,1,0:T(4,128)S(1)}, f32[8,4,64]{2,1,0:T(4,128)}, u32[]{:S(2)}) copy-start(f32[8,4,64]{2,1,0:T(4,128)} %get-tuple-element.189) | copy-start | bytes 24580
  546.2 8.9 %copy-start.21 = (bf16[512,512]{1,0:T(8,128)(2,1)}, bf16[512,512]{1,0:T(8,128)(2,1)S(1)}, u32[]{:S(2)}) copy-start(bf16[512,512]{1,0:T(8,128)(2,1)S(1)} %add_convert_fusion.6.refs_9_) | copy-start | bytes 1572868
  547.6 7.5 %copy-start.22 = (bf16[512,512]{1,0:T(8,128)(2,1)}, bf16[512,512]{1,0:T(8,128)(2,1)S(1)}, u32[]{:S(2)}) copy-start(bf16[512,512]{1,0:T(8,128)(2,1)S(1)} %add_convert_fusion.5.refs_10_) | copy-start | bytes 1572868
  547.6 23.0 %collective-permute-start.38 = (bf16[512,512]{1,0:T(8,128)(2,1)S(1)}, bf16[512,512]{1,0:T(8,128)(2,1)S(1)}, u32[]{:S(2)}, u32[]{:S(2)}) collective-permute-start(bf16[512,512]{1,0:T(8,128)(2,1)S(1)} %add_convert_fusion.5.refs_10_), channel_id=1, source_target_pairs={{0,1},{1,0},{2,3},{3,2},{4,5},{5,4},{6,7},{7,6},{8,9},{9,8},{10,11... | collective-permute-start | bytes 1572872 | tf_op jit(solution)/shard_map/ppermute | solution.py:955
  549.2 21.5 %collective-permute-start.37 = (bf16[512,512]{1,0:T(8,128)(2,1)S(1)}, bf16[512,512]{1,0:T(8,128)(2,1)S(1)}, u32[]{:S(2)}, u32[]{:S(2)}) collective-permute-start(bf16[512,512]{1,0:T(8,128)(2,1)S(1)} %add_convert_fusion.6.refs_9_), channel_id=1, source_target_pairs={{0,2},{1,3},{2,0},{3,1},{4,6},{5,7},{6,4},{7,5},{8,10},{9,11},{10,... | collective-permute-start | bytes 1572872 | tf_op jit(solution)/shard_map/ppermute | solution.py:955
  564.3 16.4 %collective-permute-start.41 = (f32[3,256]{1,0:T(4,128)S(1)}, f32[3,256]{1,0:T(4,128)S(1)}, u32[]{:S(2)}, u32[]{:S(2)}) collective-permute-start(f32[3,256]{1,0:T(4,128)S(1)} %reshape.183), channel_id=1, source_target_pairs={{0,3},{1,2},{2,1},{3,0},{4,7},{5,6},{6,5},{7,4},{8,11},{9,10},{10,... | collective-permute-start | bytes 9224 | tf_op jit(solution)/shard_map/ppermute | solution.py:955
  564.9 15.8 %collective-permute-start.40 = (f32[3,256]{1,0:T(4,128)S(1)}, f32[3,256]{1,0:T(4,128)S(1)}, u32[]{:S(2)}, u32[]{:S(2)}) collective-permute-start(f32[3,256]{1,0:T(4,128)S(1)} %reshape.183), channel_id=1, source_target_pairs={{0,2},{1,3},{2,0},{3,1},{4,6},{5,7},{6,4},{7,5},{8,10},{9,11},{10,... | collective-permute-start | bytes 9224 | tf_op jit(solution)/shard_map/ppermute | solution.py:955
  566.3 14.4 %collective-permute-start.39 = (f32[3,256]{1,0:T(4,128)S(1)}, f32[3,256]{1,0:T(4,128)S(1)}, u32[]{:S(2)}, u32[]{:S(2)}) collective-permute-start(f32[3,256]{1,0:T(4,128)S(1)} %reshape.183), channel_id=1, source_target_pairs={{0,1},{1,0},{2,3},{3,2},{4,5},{5,4},{6,7},{7,6},{8,9},{9,8},{10,11... | collective-permute-start | bytes 9224 | tf_op jit(solution)/shard_map/ppermute | solution.py:955
  (35 other events, 66.2 us)
Sparse Core Ops, SparseCore 0:
  9.9 90.3 all-gather.8
  102.7 87.5 all-gather.6
  191.9 82.0 all-gather.4
  276.7 34.3 reduce-scatter.5
  313.3 101.3 reduce-scatter.3
  447.3 104.7 reduce-scatter.7

commit v5 on v4

--- a/solution.py
+++ b/solution.py
@@ -818,7 +818,7 @@
     )
 
 
-def gain_sums(order, split, parts, unit, after=()):
+def gain_sums(order, split, parts, unit, side):
     length, width = unit.shape
     half, places = width // 2, order.shape[0]
     rows = length // places
@@ -826,26 +826,24 @@
     n = len(plan)
 
     def kernel(places_ref, unit_ref, *refs):
-        sum_ref = refs[2 * n]
+        sum_ref = refs[n]
         step = pl.program_id(0)
 
         @pl.when(step == 0)
         def _():
             sum_ref[...] = jnp.zeros_like(sum_ref)
 
-        for side in range(2):
-            for i, (col, cols, steps, _) in enumerate(plan):
-
-                def add(ref=refs[side * n + i], start=side * half + col, cols=cols):
-                    here = slice(start, start + cols)
-                    wide = ref[...].astype(F32)
-                    sum_ref[0:8, here] += eight_rows(wide * unit_ref[:, here].astype(F32))
-                    sum_ref[8:16, here] += eight_rows(wide)
-
-                if len(steps) > 2:
-                    add()
-                else:
-                    pl.when(functools.reduce(jnp.logical_or, [step == at for at in steps]))(add)
+        for (col, cols, steps, _), ref in zip(plan, refs):
+
+            def add(ref=ref, here=slice(col, col + cols)):
+                wide = ref[...].astype(F32)
+                sum_ref[0:8, here] += eight_rows(wide * unit_ref[:, here].astype(F32))
+                sum_ref[8:16, here] += eight_rows(wide)
+
+            if len(steps) > 2:
+                add()
+            else:
+                pl.when(functools.reduce(jnp.logical_or, [step == at for at in steps]))(add)
 
     def spec(cols, where):
         return pl.BlockSpec((rows, cols), lambda m, o: where(m, o))
@@ -854,15 +852,14 @@
         kernel,
         "gain_sums",
         0,
-        4 * length * width,
-        (unit, *parts[0], *parts[1]),
+        2 * length * width,
+        (unit, *parts),
         (places,),
-        [pl.BlockSpec((rows, width), lambda m, o: (o[m], 0))]
-        + [spec(cols, where) for _, cols, _, where in plan] * 2,
-        pl.BlockSpec((16, width), lambda m, o: (0, 0)),
-        struct((16, width), F32),
+        [pl.BlockSpec((rows, half), lambda m, o: (o[m], side))]
+        + [spec(cols, where) for _, cols, _, where in plan],
+        pl.BlockSpec((16, half), lambda m, o: (0, 0)),
+        struct((16, half), F32),
         prefetch=(order,),
-        after=after,
     )
 
 
@@ -1021,9 +1018,9 @@
     heads_sib.append(ring.swap(heads_own[1]))
     small = jnp.where(jnp.arange(n_dp)[:, None] == d_index, small[None, :], 0.0)
     small = flip_sum(small, "dp", n_dp)
-    (small,) = tie([small], [heads_own[2], heads_sib[1]])
-
     tables = rotary_rows(length)
+    (small,) = tie([small], [heads_own[2], heads_sib[1], *tables])
+
     chosen = (blocks[:, None] == jnp.arange(n_dp)[None, :]).astype(F32)
     cut = n_tensor * 3 * third
     vectors = jnp.einsum("pd,dj->pj", chosen, small[:, :cut], precision=lax.Precision.HIGHEST)
@@ -1038,8 +1035,8 @@
     while len(heads_own) < chips:
         heads_own.append(ring.send(heads_own[-1]))
         heads_sib.append(ring.swap(heads_own[-2]))
-    gain, bias_qkv, bias_fc1, fc1_shard, fc2_shard, *tables = tie(
-        [gain, bias_qkv, bias_fc1, fc1_shard, fc2_shard, *tables], [heads_own[-1], heads_sib[-1]]
+    fc1_shard, fc2_shard = tie(
+        [fc1_shard, fc2_shard], [heads_own[-1], heads_sib[-1], gain, bias_qkv, bias_fc1]
     )
     heads_sib.append(ring.swap(heads_own[-1]))
     heads_weights = Weights(heads_own + heads_sib)
@@ -1143,7 +1140,8 @@
         after=[fc1_grad, message, *branch_sums],
     )
     n = len(back_own)
-    joined = tie([*back_own, moving, *branch_last], [])
+    sums_own = gain_sums(order, split("both"), back_own, unit, 0)
+    joined = tie([*back_own, moving, *branch_last], [sums_own])
     back_own, moving, branch_last = joined[:n], joined[n], joined[n + 1 :]
     heads_sums = heads_sum(heads_own_grad, heads_other, moving)
     branch_terms = cross_terms(branch_own, branch_got[:1], branch_last[:1])
@@ -1159,7 +1157,8 @@
     sib_got = cross_once("both", back_sib)
     own_sums = cross_add(back_own, own_got)
     own_last = cross_twice("both", own_sums)
-    norm_sums = gain_sums(order, split("both"), (back_own, back_sib), unit).reshape(2, 8, n_dp, depth)
+    norm_sums = [sums_own, gain_sums(order, split("both"), back_sib, unit, 1)]
+    norm_sums = jnp.concatenate(norm_sums, axis=1).reshape(2, 8, n_dp, depth)
     norm_sums = jnp.einsum("pd,kpj->dkj", chosen, jnp.sum(norm_sums, axis=1), precision=lax.Precision.HIGHEST)
     b_qkv_part = jnp.sum(b_qkv_part.reshape(pairs, 3, 8, 128), axis=2)
     b_qkv_part = jnp.transpose(b_qkv_part, (1, 0, 2)).reshape(3, heads, n_dp, b_width)
@@ -1177,14 +1176,14 @@
     sums = flip_sum(by_owner, "dp", n_dp)
     sums = lax.dynamic_index_in_dim(sums, d_index, 0, keepdims=False)
     w_fc2_grad, w_out_grad = turned_sums((fc2_sums, out_sums))
-    sums, *sib_got = tie([sums, *sib_got], [w_fc2_grad, *own_sums])
+    sums, *sib_got = tie([sums, *sib_got], [heads_sums, *own_sums])
     sib_sums = cross_add(back_sib, sib_got)
     sib_last = cross_twice("both", sib_sums)
     layer_output = add_branch(blocks, x, branch_terms, bias_out, after=[*sib_sums, *back_sib[:1]])
     w_fc1_grad = fc1_sums.astype(F32)
-    (sums,) = tie([sums], [layer_output, heads_sums, w_fc1_grad])
+    (sums,) = tie([sums], [layer_output, w_fc2_grad, w_fc1_grad])
     mine = sums[: 3 * depth].reshape(3, depth)
-    mine = mine + sum(flip(mine, "tensor", n_tensor, bit) for bit in range(1, n_tensor))
+    mine = flip_sum(mine, "tensor", n_tensor)
     mine = lax.dynamic_slice_in_dim(mine, t_index * third, third, 1)
     b_qkv_grad = sums[3 * depth : 3 * depth + b_qkv.size].reshape(b_qkv.shape)
     b_fc1_grad = sums[3 * depth + b_qkv.size :].reshape(b_fc1.shape)

time: 594 us -> 593 us (level)
  waiting for transfers between devices: 87.9 us -> 81.6 us
    pallas_call x21 -> x22, Pallas kernels: 391 us -> 394 us  [call(): pl.pallas_call(body, name=name, grid_spec=pltpu.PrefetchScalarGridSpec(nu...]
    ppermute x33 -> x32, starting transfers between devices: 28 us -> 25.5 us  [flip(): return lax.ppermute(value, axis, [(i, i ^ bit) for i in range(size)])]
    unnamed x103 -> x109, local copies, waits for them, and re-layouts: 20.9 us -> 22.8 us
    ppermute x33 -> x32, waiting for transfers between devices: 28.2 us -> 27.4 us  [flip(): return lax.ppermute(value, axis, [(i, i ^ bit) for i in range(size)])]
  transfers between devices with their start and end apart: 48 -> 47, of which waited for: 12 -> 12; matrix products, arithmetic and copies ran while one was open for 7% -> 7% of each run, Pallas kernels for 66% -> 67%
where the time goes in v5:
time: 593 us; the launch traced here: 587 us
  Pallas kernels  394 us (66%)
  waiting for transfers between devices  81.6 us (14%)
  starting transfers between devices  35.6 us (6%)
  local copies, waits for them, and re-layouts  34.7 us (6%)
  other arithmetic  25.5 us (4%)
  between operations  15.1 us (3%)
    pallas_call x22, Pallas kernels, call(): pl.pallas_call(body, name=name, grid_spec=pltpu.PrefetchScalarGridSpec(nu...  394 us
    ppermute x9, waiting for transfers between devices, send(): return lax.ppermute(value, 'dp', pairs)  53.4 us
    ppermute x32, waiting for transfers between devices, flip(): return lax.ppermute(value, axis, [(i, i ^ bit) for i in range(size)])  27.4 us
    ppermute x32, starting transfers between devices, flip(): return lax.ppermute(value, axis, [(i, i ^ bit) for i in range(size)])  25.5 us
    unnamed x109, local copies, waits for them, and re-layouts  22.8 us
  transfers between devices with their start and end apart: 47, of which 12 were waited for; matrix products, arithmetic and copies ran while one was open for 7% of the time, Pallas kernels for 67%

profile of v5, /device:TPU:0, one launch (start us, length us, event | category | flops | bytes accessed | tf_op | source)
XLA Modules:
  0.0 587.5 jit_solution(6606600441113334838)
XLA Ops:
  8.0 2.3 heads_shard.1.refs_2_.refs_1_.refs_8_.refs_4_.refs_5_.refs_6_
  10.7 2.6 collective-permute-start.3
  13.5 2.4 collective-permute-start.2
  17.9 3.7 order_columns.1
  22.5 16.9 %collective-permute-done.3.refs_2_.refs_9_.refs_5_.refs_6_.refs_7_ = bf16[256,2048]{1,0:T(8,128)(2,1)S(1)} collective-permute-done((bf16[256,2048]{1,0:T(8,128)(2,1)}, bf16[256,2048]{1,0:T(8,128)(2,1)S(1)}, u32[]{:S(2)}, u32[]{:S(2)}) %collective-permute-start.3) | collective-permute-done | bytes 1048608 | tf_op jit(solution)/shard_map/ppermute | solution.py:974
  40.5 1.1 copy-done.19
  43.0 1.3 collective-permute-start.6
  44.3 24.7 %collective-permute-done.8.refs_1_.refs_10_.refs_6_.refs_7_.refs_8_ = bf16[256,2048]{1,0:T(8,128)(2,1)} collective-permute-done((bf16[256,2048]{1,0:T(8,128)(2,1)S(1)}, bf16[256,2048]{1,0:T(8,128)(2,1)}, u32[]{:S(2)}, u32[]{:S(2)}) %collective-permute-start.8) | collective-permute-done | bytes 1048608 | tf_op jit(solution)/shard_map/ppermute | solution.py:974
  69.9 5.0 fusion.1
  74.9 2.6 stage_weight.3.refs_1_
  77.5 2.3 stage_weight.2.refs_0_
  79.8 13.7 %collective-permute-done.7 = f32[8,1216]{1,0:T(8,128)S(1)} collective-permute-done((f32[8,1216]{1,0:T(8,128)S(1)}, f32[8,1216]{1,0:T(8,128)S(1)}, u32[]{:S(2)}, u32[]{:S(2)}) %collective-permute-start.7) | collective-permute-done | bytes 38944 | tf_op jit(solution)/shard_map/ppermute | solution.py:952
  94.1 1.0 copy-done.20
  101.7 1.0 copy-done.14
  103.3 3.5 collective-permute-start.14
  106.8 1.2 collective-permute-start.13
  108.7 1.0 copy-done.25
  109.7 27.5 %norm_project.1 = (bf16[2048,2048]{1,0:T(8,128)(2,1)}, bf16[2048,2048]{1,0:T(8,128)(2,1)}, bf16[2048,1536]{1,0:T(8,128)(2,1)}) custom-call(s32[8]{0:T(128)} %pad_add_fusion.refs_0_, bf16[2048,2048]{1,0:T(8,128)(2,1)} %bitcast.40, f32[1,2048]{1,0:T(1,128)} %reshape_squeeze.12.refs_4_.refs_2_.refs_15_, f32[1,2048]{1,0:T(1,128)} %reshape_squeeze.13.refs_3_, ...), custom_call_target="tpu_custom_call" | custom-call | tf_op jit(solution)/shard_map/norm_project/pallas_call | solution.py:40
  137.2 19.1 %attend.2 = (bf16[2048,512]{1,0:T(8,128)(2,1)}, f32[2,2,2048]{2,1,0:T(2,128)}) custom-call(bf16[2048,1536]{1,0:T(8,128)(2,1)} %get-tuple-element.87.refs_0_.refs_1_.refs_2_, bf16[2048,1536]{1,0:T(8,128)(2,1)} %get-tuple-element.87.refs_0_.refs_1_.refs_2_, bf16[2048,1536]{1,0:T(8,128)(2,1)} %get-tuple-element.87.refs_0_.refs_1_.refs_2_, ...), custom_call_target="tpu_custom_call" | custom-call | tf_op jit(solution)/shard_map/attend/pallas_call | solution.py:40
  158.2 2.1 collective-permute-start.16
  160.3 19.1 %attend.3 = (bf16[2048,512]{1,0:T(8,128)(2,1)}, f32[2,2,2048]{2,1,0:T(2,128)}) custom-call(bf16[2048,1536]{1,0:T(8,128)(2,1)} %get-tuple-element.87.refs_0_.refs_1_.refs_2_, bf16[2048,1536]{1,0:T(8,128)(2,1)} %get-tuple-element.87.refs_0_.refs_1_.refs_2_, ...), custom_call_target="tpu_custom_call", output_to_operand_aliasing={{0}: (3, {})} | custom-call | tf_op jit(solution)/shard_map/attend/pallas_call | solution.py:40
  179.5 6.0 %collective-permute-done.16.refs_1_ = bf16[256,2048]{1,0:T(8,128)(2,1)S(1)} collective-permute-done((bf16[256,2048]{1,0:T(8,128)(2,1)}, bf16[256,2048]{1,0:T(8,128)(2,1)S(1)}, u32[]{:S(2)}, u32[]{:S(2)}) %collective-permute-start.16) | collective-permute-done | bytes 1048608 | tf_op jit(solution)/shard_map/ppermute | solution.py:974
  185.5 1.0 copy-done.32
  186.4 2.9 collective-permute-done.19.refs_8_.refs_20_
  190.3 32.1 %expand.1 = (bf16[2048,2048]{1,0:T(8,128)(2,1)}, bf16[2048,2048]{1,0:T(8,128)(2,1)}) custom-call(s32[8]{0:T(128)} %pad_add_fusion.refs_0_, bf16[2048,2048]{1,0:T(8,128)(2,1)} %get-tuple-element.86.refs_1_.refs_0_, bf16[256,2048]{1,0:T(8,128)(2,1)} %get-tuple-element.85.refs_16_.refs_3_.refs_2_.refs_14_, ...), custom_call_target="tpu_custom_call" | custom-call | flops 17179869184 | bytes 33554432 | tf_op jit(solution)/shard_map/expand/pallas_call | solution.py:40
  222.4 36.9 %fc2_grad.1 = (bf16[2048,2048]{1,0:T(8,128)(2,1)}, bf16[2048,512]{1,0:T(8,128)(2,1)}, bf16[2048,512]{1,0:T(8,128)(2,1)}) custom-call(s32[8]{0:T(128)} %pad_add_fusion.refs_0_, bf16[2048,2048]{1,0:T(8,128)(2,1)} %all-gather.7.cloned.1.call-done.refs_1_, bf16[2048,2048]{1,0:T(8,128)(2,1)} %get-tuple-element.96.refs_2_, ...), custom_call_target="tpu_custom_call" | custom-call | flops 17179869184 | bytes 33554432 | tf_op jit(solution)/shard_map/fc2_grad/pallas_call | solution.py:40
  260.8 65.5 %attend_back.1 = (bf16[2048,512]{1,0:T(8,128)(2,1)}, bf16[2048,512]{1,0:T(8,128)(2,1)}, bf16[2048,512]{1,0:T(8,128)(2,1)}, f32[4,24,128]{2,1,0:T(8,128)}) custom-call(bf16[2048,1536]{1,0:T(8,128)(2,1)} %get-tuple-element.87.refs_0_.refs_1_.refs_2_, bf16[2048,1536]{1,0:T(8,128)(2,1)} %get-tuple-element.87.refs_0_.refs_1_.refs_2_, ...), custom_call_target="tpu_custom_call" | custom-call | flops 128849018880 | bytes 16777216 | tf_op jit(solution)/shard_map/attend_back/pallas_call | solution.py:40
  326.3 20.8 %heads_grad.1 = (bf16[1024,1536]{1,0:T(8,128)(2,1)}, bf16[1024,1536]{1,0:T(8,128)(2,1)}) custom-call(bf16[2048,2048]{1,0:T(8,128)(2,1)} %get-tuple-element.86.refs_1_.refs_0_, bf16[2048,512]{1,0:T(8,128)(2,1)} %get-tuple-element.101.refs_1_.refs_2_, bf16[2048,512]{1,0:T(8,128)(2,1)} %get-tuple-element.102.refs_2_.refs_3_, ...), custom_call_target="tpu_custom_call" | custom-call | flops 12884901888 | bytes 27262976 | tf_op jit(solution)/shard_map/heads_grad/pallas_call | solution.py:40
  347.7 31.3 %branch.1 = (bf16[1024,1024]{1,0:T(8,128)(2,1)}, bf16[1024,1024]{1,0:T(8,128)(2,1)}, bf16[1024,1024]{1,0:T(8,128)(2,1)}, bf16[1024,1024]{1,0:T(8,128)(2,1)}) custom-call(s32[8]{0:T(128)} %pad_add_fusion.refs_0_, s32[4]{0:T(128)} %broadcast_xor_fusion.refs_1_.refs_0_, bf16[2048,2048]{1,0:T(8,128)(2,1)} %get-tuple-element.96.refs_2_, ...), custom_call_target="tpu_custom_call" | custom-call | flops 21474836480 | bytes 29360128 | tf_op jit(solution)/shard_map/branch/pallas_call | solution.py:40
  379.0 1.7 copy-done
  380.7 1.6 add_convert_fusion.4.refs_4_
  382.6 1.5 collective-permute-start.23
  384.1 1.5 collective-permute-start.24
  385.5 26.1 %hidden_back.1 = (bf16[2048,2048]{1,0:T(8,128)(2,1)}, f32[8,2048]{1,0:T(8,128)}) custom-call(s32[8]{0:T(128)} %pad_add_fusion.refs_0_, bf16[2048,2048]{1,0:T(8,128)(2,1)} %all-gather.7.cloned.1.call-done.refs_1_, bf16[2048,2048]{1,0:T(8,128)(2,1)} %all-gather.5.cloned.1.call-done.refs_4_.refs_2_, bf16[2048,2048]{1,0:T(8,128)(2,1)} %get-tuple-element.111.refs_3_, ...), custom_call_target="tpu_custom_call" | custom-call | flops 17179869184 | bytes 33554432 | tf_op jit(solution)/shard_map/hidden_back/pallas_call | solution.py:40
  411.6 5.8 collective-permute-done.21.refs_1_
  418.3 1.9 copy-done.1
  420.1 1.7 add_convert_fusion.3.refs_3_
  422.7 24.5 %fc1_grad.1.refs_0_ = bf16[2048,2048]{1,0:T(8,128)(2,1)} custom-call(s32[8]{0:T(128)} %pad_add_fusion.refs_0_, bf16[2048,2048]{1,0:T(8,128)(2,1)} %get-tuple-element.86.refs_1_.refs_0_, bf16[2048,2048]{1,0:T(8,128)(2,1)} %get-tuple-element.114.refs_2_.refs_5_, bf16[256,1536]{1,0:T(8,128)(2,1)} %copy-done.35), custom_call_target="tpu_custom_call" | custom-call | flops 17179869184 | bytes 33554432 | tf_op jit(solution)/shard_map/fc1_grad/pallas_call | solution.py:40
  448.2 1.8 add_convert_fusion.2.refs_23_
  450.2 2.0 add_convert_fusion.refs_25_
  452.3 1.5 collective-permute-start.27
  453.8 1.8 add_convert_fusion.1.refs_24_
  455.6 1.6 collective-permute-start.26
  457.2 23.5 %normed_back_half.2 = (bf16[1024,512]{1,0:T(8,128)(2,1)}, bf16[1024,512]{1,0:T(8,128)(2,1)}, bf16[1024,512]{1,0:T(8,128)(2,1)}, bf16[1024,512]{1,0:T(8,128)(2,1)}) custom-call(s32[8]{0:T(128)} %pad_add_fusion.refs_0_, s32[4]{0:T(128)} %broadcast_xor_fusion.refs_1_.refs_0_, bf16[2048,512]{1,0:T(8,128)(2,1)} %get-tuple-element.101.refs_1_.refs_2_, ...), custom_call_target="tpu_custom_call" | custom-call | flops 15032385536 | bytes 26214400 | tf_op jit(solution)/shard_map/normed_back_half/pallas_call | solution.py:40
  480.7 5.8 gain_sums.2.refs_7_
  489.7 1.1 collective-permute-start.28
  490.8 23.5 %normed_back_half.3 = (bf16[1024,512]{1,0:T(8,128)(2,1)}, bf16[1024,512]{1,0:T(8,128)(2,1)}, bf16[1024,512]{1,0:T(8,128)(2,1)}, bf16[1024,512]{1,0:T(8,128)(2,1)}) custom-call(s32[8]{0:T(128)} %pad_add_fusion.refs_0_, s32[4]{0:T(128)} %broadcast_xor_fusion.refs_1_.refs_0_, bf16[2048,512]{1,0:T(8,128)(2,1)} %get-tuple-element.101.refs_1_.refs_2_, ...), custom_call_target="tpu_custom_call" | custom-call | flops 15032385536 | bytes 26214400 | tf_op jit(solution)/shard_map/normed_back_half/pallas_call | solution.py:40
  516.3 1.3 collective-permute-start.33
  518.2 5.9 %gain_sums.3 = f32[16,1024]{1,0:T(8,128)} custom-call(s32[4]{0:T(128)} %broadcast_xor_fusion.refs_1_.refs_0_, bf16[2048,2048]{1,0:T(8,128)(2,1)} %get-tuple-element.127.refs_1_, bf16[1024,512]{1,0:T(8,128)(2,1)} %get-tuple-element.137.refs_2_.refs_11_, bf16[1024,512]{1,0:T(8,128)(2,1)} %get-tuple-element.136.refs_3_.refs_9_, ...), custom_call_target="tpu_custom_call" | custom-call | bytes 8388608 | tf_op jit(solution)/shard_map/gain_sums/pallas_call | solution.py:40
  525.4 4.0 heads_sum.1.refs_3_
  531.1 4.4 collective-permute-done.31
  535.5 2.3 collective-permute-start.32
  539.6 3.3 collective-permute-done.32
  543.5 1.0 copy-done.8
  545.1 1.2 add_convert_fusion.6.refs_9_
  546.3 1.4 add_convert_fusion.5.refs_10_
  548.3 1.0 collective-permute-start.37
  550.0 5.7 add_branch.1.refs_1_
  555.8 3.1 turned_sums.1
  558.9 2.8 convert_element_type.159.refs_3_
  562.3 1.4 collective-permute-start.39
  563.7 2.2 collective-permute-done.39
  565.9 1.0 collective-permute-start.40
  571.4 8.4 %norm_back.1 = f32[512,2048]{1,0:T(8,128)} custom-call(s32[8]{0:T(128)} %pad_add_fusion.refs_0_, bf16[512,2048]{1,0:T(8,128)(2,1)} %bitcast.36, bf16[512,2048]{1,0:T(8,128)(2,1)} %bitcast.39, bf16[1024,512]{1,0:T(8,128)(2,1)} %get-tuple-element.144.refs_3_, bf16[1024,512]{1,0:T(8,128)(2,1)} %get-tuple-element.145.refs_4_, ...), custom_call_target="tpu_custom_call" | custom-call | bytes 10485760 | tf_op jit(solution)/shard_map/norm_back/pallas_call | solution.py:40
  (253 shorter events, 42.7 us)
Async XLA Ops:
  7.2 6.1 %copy-start.49 = (bf16[64]{0:T(256)(128)(2,1)S(1)}, bf16[64]{0:T(256)(128)(2,1)}, u32[]{:S(2)}) copy-start(bf16[64]{0:T(256)(128)(2,1)} %param.15) | copy-start | bytes 388
  7.2 6.1 %copy-start.50 = (bf16[64]{0:T(256)(128)(2,1)S(1)}, bf16[64]{0:T(256)(128)(2,1)}, u32[]{:S(2)}) copy-start(bf16[64]{0:T(256)(128)(2,1)} %param.14) | copy-start | bytes 388
  7.2 6.1 %copy-start.51 = (bf16[64]{0:T(256)(128)(2,1)S(1)}, bf16[64]{0:T(256)(128)(2,1)}, u32[]{:S(2)}) copy-start(bf16[64]{0:T(256)(128)(2,1)} %param.13) | copy-start | bytes 388
  7.2 10.4 %copy-start.47 = (bf16[3,8,8]{2,1,0:T(8,128)(2,1)S(1)}, bf16[3,8,8]{2,1,0:T(8,128)(2,1)}, u32[]{:S(2)}) copy-start(bf16[3,8,8]{2,1,0:T(8,128)(2,1)} %param.17) | copy-start | bytes 1156
  7.2 10.5 %copy-start.48 = (bf16[32,8]{0,1:T(8,128)(2,1)S(1)}, bf16[32,8]{0,1:T(8,128)(2,1)}, u32[]{:S(2)}) copy-start(bf16[32,8]{0,1:T(8,128)(2,1)} %param.20) | copy-start | bytes 1540
  7.2 101.5 %all-gather.9.cloned.1.call-start = ((), (), s32[]{:S(2)}) async-start(), calls=%async_computation.8 | async-start | bytes 10485760 | tf_op jit(solution)/shard_map/all_gather | solution.py:1003
  8.0 214.4 %all-gather.7.cloned.1.call-start = ((), (), s32[]{:S(2)}) async-start(), calls=%async_computation.4 | async-start | bytes 10485760 | tf_op jit(solution)/shard_map/all_gather | solution.py:1015
  10.3 12.2 %collective-permute-start.4 = (bf16[256,2048]{1,0:T(8,128)(2,1)}, bf16[256,2048]{1,0:T(8,128)(2,1)S(1)}, u32[]{:S(2)}, u32[]{:S(2)}) collective-permute-start(bf16[256,2048]{1,0:T(8,128)(2,1)} %heads_shard.1.refs_2_.refs_1_.refs_8_.refs_4_.refs_5_.refs_6_), channel_id=1, source_target_pairs={{0,4},{4,0},{8,12},{12,8},{16,20},{20,16},{24,28},{28,24},{1,5},{5... | collective-permute-start | bytes 3145736 | tf_op jit(solution)/shard_map/ppermute | solution.py:952
  10.7 28.6 %collective-permute-start.3 = (bf16[256,2048]{1,0:T(8,128)(2,1)}, bf16[256,2048]{1,0:T(8,128)(2,1)S(1)}, u32[]{:S(2)}, u32[]{:S(2)}) collective-permute-start(bf16[256,2048]{1,0:T(8,128)(2,1)} %heads_shard.1.refs_2_.refs_1_.refs_8_.refs_4_.refs_5_.refs_6_), channel_id=1, source_target_pairs={{0,8},{4,12},{8,16},{12,20},{16,24},{20,28},{24,0},{28,4},{1,9},{5... | collective-permute-start | bytes 3145736 | tf_op jit(solution)/shard_map/ppermute | solution.py:974
  13.5 8.1 %collective-permute-start.2 = (f32[4,192]{1,0:T(4,128)S(1)}, f32[4,192]{1,0:T(4,128)S(1)}, u32[]{:S(2)}, u32[]{:S(2)}) collective-permute-start(f32[4,192]{1,0:T(4,128)S(1)} %broadcast_select_fusion.1), channel_id=1, source_target_pairs={{0,3},{1,2},{2,1},{3,0},{4,7},{5,6},{6,5},{7,4},{8,11},{9,10},{10,... | collective-permute-start | bytes 9224 | tf_op jit(solution)/shard_map/ppermute | solution.py:952
  16.0 5.7 collective-permute-start.1
  16.5 5.2 collective-permute-start
  22.5 16.9 %copy-start.17 = (bf16[256,2048]{1,0:T(8,128)(2,1)}, bf16[256,2048]{1,0:T(8,128)(2,1)S(1)}, u32[]{:S(2)}) copy-start(bf16[256,2048]{1,0:T(8,128)(2,1)S(1)} %collective-permute-done.4.refs_3_.refs_12_.refs_8_.refs_9_.refs_10_) | copy-start | bytes 3145732
  40.4 307.3 %all-gather.5.cloned.1.call-start = ((), (), s32[]{:S(2)}) async-start(), calls=%async_computation.3 | async-start | bytes 9437184 | tf_op jit(solution)/shard_map/all_gather | solution.py:1043
  41.6 27.4 %collective-permute-start.8 = (bf16[256,2048]{1,0:T(8,128)(2,1)S(1)}, bf16[256,2048]{1,0:T(8,128)(2,1)}, u32[]{:S(2)}, u32[]{:S(2)}) collective-permute-start(bf16[256,2048]{1,0:T(8,128)(2,1)S(1)} %copy-done.19), channel_id=1, source_target_pairs={{0,8},{4,12},{8,16},{12,20},{16,24},{20,28},{24,0},{28,4},{1,9},{5... | collective-permute-start | bytes 3145736 | tf_op jit(solution)/shard_map/ppermute | solution.py:974
  41.7 1.2 collective-permute-start.5
  41.7 52.4 %collective-permute-start.9 = (bf16[256,2048]{1,0:T(8,128)(2,1)S(1)}, bf16[256,2048]{1,0:T(8,128)(2,1)S(1)}, u32[]{:S(2)}, u32[]{:S(2)}) collective-permute-start(bf16[256,2048]{1,0:T(8,128)(2,1)S(1)} %copy-done.19), channel_id=1, source_target_pairs={{0,4},{4,0},{8,12},{12,8},{16,20},{20,16},{24,28},{28,24},{1,5},{5... | collective-permute-start | bytes 3145736 | tf_op jit(solution)/shard_map/ppermute | solution.py:952
  43.0 26.1 %collective-permute-start.6 = (f32[8,1216]{1,0:T(8,128)S(1)}, f32[8,1216]{1,0:T(8,128)S(1)}, u32[]{:S(2)}, u32[]{:S(2)}) collective-permute-start(f32[8,1216]{1,0:T(8,128)S(1)} %fusion.4), channel_id=1, source_target_pairs={{0,8},{4,12},{8,0},{12,4},{16,24},{20,28},{24,16},{28,20},{1,9},{5... | collective-permute-start | bytes 116744 | tf_op jit(solution)/shard_map/ppermute | solution.py:952
  69.0 31.7 %collective-permute-start.11 = (bf16[256,2048]{1,0:T(8,128)(2,1)}, bf16[256,2048]{1,0:T(8,128)(2,1)S(1)}, u32[]{:S(2)}, u32[]{:S(2)}) collective-permute-start(bf16[256,2048]{1,0:T(8,128)(2,1)} %collective-permute-done.8.refs_1_.refs_10_.refs_6_.refs_7_.refs_8_), channel_id=1, source_target_pairs={{0,4},{4,0},{8,12},{12,8},{16,20},{20,16},{24,28},{28,24},{1,5},{5... | collective-permute-start | bytes 3145736 | tf_op jit(solution)/shard_map/ppermute | solution.py:952
  69.0 31.7 %collective-permute-start.10 = (bf16[256,2048]{1,0:T(8,128)(2,1)}, bf16[256,2048]{1,0:T(8,128)(2,1)S(1)}, u32[]{:S(2)}, u32[]{:S(2)}) collective-permute-start(bf16[256,2048]{1,0:T(8,128)(2,1)} %collective-permute-done.8.refs_1_.refs_10_.refs_6_.refs_7_.refs_8_), channel_id=1, source_target_pairs={{0,8},{4,12},{8,16},{12,20},{16,24},{20,28},{24,0},{28,4},{1,9},{5... | collective-permute-start | bytes 3145736 | tf_op jit(solution)/shard_map/ppermute | solution.py:974
  69.2 24.3 %collective-permute-start.7 = (f32[8,1216]{1,0:T(8,128)S(1)}, f32[8,1216]{1,0:T(8,128)S(1)}, u32[]{:S(2)}, u32[]{:S(2)}) collective-permute-start(f32[8,1216]{1,0:T(8,128)S(1)} %fusion.16), channel_id=1, source_target_pairs={{0,16},{4,20},{8,24},{12,28},{16,0},{20,4},{24,8},{28,12},{1,17},{... | collective-permute-start | bytes 116744 | tf_op jit(solution)/shard_map/ppermute | solution.py:952
  102.7 453.1 %reduce-scatter.6.cloned.1.call-start = ((), (), s32[]{:S(2)}) async-start(), calls=%async_computation.6 | async-start | bytes 2359296 | tf_op jit(solution)/shard_map/reduce_scatter | solution.py:1097
  102.7 6.0 %collective-permute-start.12 = (bf16[256,2048]{1,0:T(8,128)(2,1)}, bf16[256,2048]{1,0:T(8,128)(2,1)S(1)}, u32[]{:S(2)}, u32[]{:S(2)}) collective-permute-start(bf16[256,2048]{1,0:T(8,128)(2,1)} %copy-done.14), channel_id=1, source_target_pairs={{0,4},{4,0},{8,12},{12,8},{16,20},{20,16},{24,28},{28,24},{1,5},{5... | collective-permute-start | bytes 3145736 | tf_op jit(solution)/shard_map/ppermute | solution.py:952
  102.8 53.5 %collective-permute-start.15 = (bf16[256,2048]{1,0:T(8,128)(2,1)}, bf16[256,2048]{1,0:T(8,128)(2,1)S(1)}, u32[]{:S(2)}, u32[]{:S(2)}) collective-permute-start(bf16[256,2048]{1,0:T(8,128)(2,1)} %get-tuple-element.85.refs_16_.refs_3_.refs_2_.refs_14_), channel_id=1, source_target_pairs={{0,4},{4,0},{8,12},{12,8},{16,20},{20,16},{24,28},{28,24},{1,5},{5... | collective-permute-start | bytes 3145736 | tf_op jit(solution)/shard_map/ppermute | solution.py:952
  103.3 53.0 %collective-permute-start.14 = (bf16[256,2048]{1,0:T(8,128)(2,1)}, bf16[256,2048]{1,0:T(8,128)(2,1)S(1)}, u32[]{:S(2)}, u32[]{:S(2)}) collective-permute-start(bf16[256,2048]{1,0:T(8,128)(2,1)} %get-tuple-element.85.refs_16_.refs_3_.refs_2_.refs_14_), channel_id=1, source_target_pairs={{0,24},{4,28},{8,0},{12,4},{16,8},{20,12},{24,16},{28,20},{1,25},{... | collective-permute-start | bytes 3145736 | tf_op jit(solution)/shard_map/ppermute | solution.py:974
  106.8 49.5 %collective-permute-start.13 = (bf16[256,2048]{1,0:T(8,128)(2,1)}, bf16[256,2048]{1,0:T(8,128)(2,1)}, u32[]{:S(2)}, u32[]{:S(2)}) collective-permute-start(bf16[256,2048]{1,0:T(8,128)(2,1)} %get-tuple-element.85.refs_16_.refs_3_.refs_2_.refs_14_), channel_id=1, source_target_pairs={{0,8},{4,12},{8,16},{12,20},{16,24},{20,28},{24,0},{28,4},{1,9},{5... | collective-permute-start | bytes 3145736 | tf_op jit(solution)/shard_map/ppermute | solution.py:974
  157.7 21.7 %collective-permute-start.18 = (bf16[256,2048]{1,0:T(8,128)(2,1)}, bf16[256,2048]{1,0:T(8,128)(2,1)S(1)}, u32[]{:S(2)}, u32[]{:S(2)}) collective-permute-start(bf16[256,2048]{1,0:T(8,128)(2,1)} %get-tuple-element.93.refs_5_.refs_17_), channel_id=1, source_target_pairs={{0,4},{4,0},{8,12},{12,8},{16,20},{20,16},{24,28},{28,24},{1,5},{5... | collective-permute-start | bytes 3145736 | tf_op jit(solution)/shard_map/ppermute | solution.py:952
  157.7 21.8 %collective-permute-start.17 = (bf16[256,2048]{1,0:T(8,128)(2,1)}, bf16[256,2048]{1,0:T(8,128)(2,1)S(1)}, u32[]{:S(2)}, u32[]{:S(2)}) collective-permute-start(bf16[256,2048]{1,0:T(8,128)(2,1)} %get-tuple-element.89.refs_3_.refs_15_), channel_id=1, source_target_pairs={{0,4},{4,0},{8,12},{12,8},{16,20},{20,16},{24,28},{28,24},{1,5},{5... | collective-permute-start | bytes 3145736 | tf_op jit(solution)/shard_map/ppermute | solution.py:952
  158.2 27.3 %collective-permute-start.16 = (bf16[256,2048]{1,0:T(8,128)(2,1)}, bf16[256,2048]{1,0:T(8,128)(2,1)S(1)}, u32[]{:S(2)}, u32[]{:S(2)}) collective-permute-start(bf16[256,2048]{1,0:T(8,128)(2,1)} %get-tuple-element.89.refs_3_.refs_15_), channel_id=1, source_target_pairs={{0,8},{4,12},{8,16},{12,20},{16,24},{20,28},{24,0},{28,4},{1,9},{5... | collective-permute-start | bytes 3145736 | tf_op jit(solution)/shard_map/ppermute | solution.py:974
  179.4 6.0 %copy-start.27 = (bf16[256,2048]{1,0:T(8,128)(2,1)}, bf16[256,2048]{1,0:T(8,128)(2,1)S(1)}, u32[]{:S(2)}) copy-start(bf16[256,2048]{1,0:T(8,128)(2,1)S(1)} %collective-permute-done.18.refs_3_.refs_9_.refs_21_) | copy-start | bytes 3145732
  179.4 6.0 %copy-start.28 = (bf16[256,2048]{1,0:T(8,128)(2,1)}, bf16[256,2048]{1,0:T(8,128)(2,1)S(1)}, u32[]{:S(2)}) copy-start(bf16[256,2048]{1,0:T(8,128)(2,1)S(1)} %collective-permute-done.17.refs_2_.refs_7_.refs_19_) | copy-start | bytes 3145732
  186.4 2.9 collective-permute-start.19
  259.3 296.4 %reduce-scatter.4.cloned.1.call-start = ((), (), s32[]{:S(2)}) async-start(), calls=%async_computation.5 | async-start | bytes 9437184 | tf_op jit(solution)/shard_map/reduce_scatter | solution.py:1097
  260.7 298.1 %reduce-scatter.8.cloned.1.call-start = ((), (), s32[]{:S(2)}) async-start(), calls=%async_computation.7 | async-start | bytes 9437184 | tf_op jit(solution)/shard_map/reduce_scatter | solution.py:1097
  326.3 20.8 %copy-start.53 = (s32[4]{0:T(128)S(1)}, s32[4]{0:T(128)}, u32[]{:S(2)}) copy-start(s32[4]{0:T(128)} %constant.99.clone) | copy-start | bytes 52
  347.1 31.9 %collective-permute-start.20 = (bf16[1024,1536]{1,0:T(8,128)(2,1)}, bf16[1024,1536]{1,0:T(8,128)(2,1)S(1)}, u32[]{:S(2)}, u32[]{:S(2)}) collective-permute-start(bf16[1024,1536]{1,0:T(8,128)(2,1)} %get-tuple-element.109), channel_id=1, source_target_pairs={{0,4},{4,0},{8,12},{12,8},{16,20},{20,16},{24,28},{28,24},{1,5},{5... | collective-permute-start | bytes 9437192 | tf_op jit(solution)/shard_map/ppermute | solution.py:952
  382.2 35.1 %collective-permute-start.21 = (bf16[256,1536]{1,0:T(8,128)(2,1)S(1)}, bf16[256,1536]{1,0:T(8,128)(2,1)S(1)}, u32[]{:S(2)}, u32[]{:S(2)}) collective-permute-start(bf16[256,1536]{1,0:T(8,128)(2,1)S(1)} %add_convert_fusion.4.refs_4_), channel_id=1, source_target_pairs={{0,8},{4,12},{8,16},{12,20},{16,24},{20,28},{24,0},{28,4},{1,9},{5... | collective-permute-start | bytes 2359304 | tf_op jit(solution)/shard_map/ppermute | solution.py:974
  382.6 64.6 %collective-permute-start.23 = (bf16[1024,1024]{1,0:T(8,128)(2,1)}, bf16[1024,1024]{1,0:T(8,128)(2,1)}, u32[]{:S(2)}, u32[]{:S(2)}) collective-permute-start(bf16[1024,1024]{1,0:T(8,128)(2,1)} %get-tuple-element.116), channel_id=1, source_target_pairs={{0,1},{1,0},{2,3},{3,2},{4,5},{5,4},{6,7},{7,6},{8,9},{9,8},{10,11... | collective-permute-start | bytes 6291464 | tf_op jit(solution)/shard_map/ppermute | solution.py:952
  384.1 63.2 %collective-permute-start.24 = (bf16[1024,1024]{1,0:T(8,128)(2,1)}, bf16[1024,1024]{1,0:T(8,128)(2,1)}, u32[]{:S(2)}, u32[]{:S(2)}) collective-permute-start(bf16[1024,1024]{1,0:T(8,128)(2,1)} %get-tuple-element.117), channel_id=1, source_target_pairs={{0,2},{1,3},{2,0},{3,1},{4,6},{5,7},{6,4},{7,5},{8,10},{9,11},{10,... | collective-permute-start | bytes 6291464 | tf_op jit(solution)/shard_map/ppermute | solution.py:952
  421.8 25.4 %collective-permute-start.22 = (bf16[256,1536]{1,0:T(8,128)(2,1)S(1)}, bf16[256,1536]{1,0:T(8,128)(2,1)}, u32[]{:S(2)}, u32[]{:S(2)}) collective-permute-start(bf16[256,1536]{1,0:T(8,128)(2,1)S(1)} %add_convert_fusion.3.refs_3_), channel_id=1, source_target_pairs={{0,8},{4,12},{8,16},{12,20},{16,24},{20,28},{24,0},{28,4},{1,9},{5... | collective-permute-start | bytes 2359304 | tf_op jit(solution)/shard_map/ppermute | solution.py:974
  450.0 5.6 copy-start.33
  450.0 36.5 %collective-permute-start.25 = (bf16[256,1536]{1,0:T(8,128)(2,1)S(1)}, bf16[256,1536]{1,0:T(8,128)(2,1)S(1)}, u32[]{:S(2)}, u32[]{:S(2)}) collective-permute-start(bf16[256,1536]{1,0:T(8,128)(2,1)S(1)} %add_convert_fusion.2.refs_23_), channel_id=1, source_target_pairs={{0,8},{4,12},{8,16},{12,20},{16,24},{20,28},{24,0},{28,4},{1,9},{5... | collective-permute-start | bytes 2359304 | tf_op jit(solution)/shard_map/ppermute | solution.py:974
  452.2 5.0 copy-start.30
  452.3 34.3 %collective-permute-start.27 = (bf16[512,1024]{1,0:T(8,128)(2,1)S(1)}, bf16[512,1024]{1,0:T(8,128)(2,1)S(1)}, u32[]{:S(2)}, u32[]{:S(2)}) collective-permute-start(bf16[512,1024]{1,0:T(8,128)(2,1)S(1)} %add_convert_fusion.refs_25_), channel_id=1, source_target_pairs={{0,1},{1,0},{2,3},{3,2},{4,5},{5,4},{6,7},{7,6},{8,9},{9,8},{10,11... | collective-permute-start | bytes 3145736 | tf_op jit(solution)/shard_map/ppermute | solution.py:952
  455.6 30.9 %collective-permute-start.26 = (bf16[512,1024]{1,0:T(8,128)(2,1)S(1)}, bf16[512,1024]{1,0:T(8,128)(2,1)S(1)}, u32[]{:S(2)}, u32[]{:S(2)}) collective-permute-start(bf16[512,1024]{1,0:T(8,128)(2,1)S(1)} %add_convert_fusion.1.refs_24_), channel_id=1, source_target_pairs={{0,2},{1,3},{2,0},{3,1},{4,6},{5,7},{6,4},{7,5},{8,10},{9,11},{10,... | collective-permute-start | bytes 3145736 | tf_op jit(solution)/shard_map/ppermute | solution.py:952
  488.7 25.6 %collective-permute-start.29 = (bf16[1024,512]{1,0:T(8,128)(2,1)}, bf16[1024,512]{1,0:T(8,128)(2,1)S(1)}, u32[]{:S(2)}, u32[]{:S(2)}) collective-permute-start(bf16[1024,512]{1,0:T(8,128)(2,1)} %get-tuple-element.135), channel_id=1, source_target_pairs={{0,2},{1,3},{2,0},{3,1},{4,6},{5,7},{6,4},{7,5},{8,10},{9,11},{10,... | collective-permute-start | bytes 3145736 | tf_op jit(solution)/shard_map/ppermute | solution.py:952
  489.7 24.7 %collective-permute-start.28 = (bf16[1024,512]{1,0:T(8,128)(2,1)}, bf16[1024,512]{1,0:T(8,128)(2,1)S(1)}, u32[]{:S(2)}, u32[]{:S(2)}) collective-permute-start(bf16[1024,512]{1,0:T(8,128)(2,1)} %get-tuple-element.130.refs_22_), channel_id=1, source_target_pairs={{0,1},{1,0},{2,3},{3,2},{4,5},{5,4},{6,7},{7,6},{8,9},{9,8},{10,11... | collective-permute-start | bytes 3145736 | tf_op jit(solution)/shard_map/ppermute | solution.py:952
  515.6 27.9 %collective-permute-start.34 = (bf16[1024,512]{1,0:T(8,128)(2,1)}, bf16[1024,512]{1,0:T(8,128)(2,1)S(1)}, u32[]{:S(2)}, u32[]{:S(2)}) collective-permute-start(bf16[1024,512]{1,0:T(8,128)(2,1)} %get-tuple-element.138.refs_4_), channel_id=1, source_target_pairs={{0,2},{1,3},{2,0},{3,1},{4,6},{5,7},{6,4},{7,5},{8,10},{9,11},{10,... | collective-permute-start | bytes 3145736 | tf_op jit(solution)/shard_map/ppermute | solution.py:952
  516.3 27.3 %collective-permute-start.33 = (bf16[1024,512]{1,0:T(8,128)(2,1)}, bf16[1024,512]{1,0:T(8,128)(2,1)}, u32[]{:S(2)}, u32[]{:S(2)}) collective-permute-start(bf16[1024,512]{1,0:T(8,128)(2,1)} %get-tuple-element.137.refs_2_.refs_11_), channel_id=1, source_target_pairs={{0,1},{1,0},{2,3},{3,2},{4,5},{5,4},{6,7},{7,6},{8,9},{9,8},{10,11... | collective-permute-start | bytes 3145736 | tf_op jit(solution)/shard_map/ppermute | solution.py:952
  518.2 6.0 %copy-start.36 = (f32[16,1024]{1,0:T(8,128)S(1)}, f32[16,1024]{1,0:T(8,128)}, u32[]{:S(2)}) copy-start(f32[16,1024]{1,0:T(8,128)} %gain_sums.2.refs_7_) | copy-start | bytes 196612
  518.2 6.8 %copy-start.46 = (s32[8]{0:T(128)S(1)}, s32[8]{0:T(128)}, u32[]{:S(2)}) copy-start(s32[8]{0:T(128)} %pad_add_fusion.refs_0_) | copy-start | bytes 100
  525.4 4.1 collective-permute-start.30
  525.4 4.2 copy-start.5
  525.4 12.3 %copy-start.12 = (bf16[1024,512]{1,0:T(8,128)(2,1)S(1)}, bf16[1024,512]{1,0:T(8,128)(2,1)}, u32[]{:S(2)}) copy-start(bf16[1024,512]{1,0:T(8,128)(2,1)} %get-tuple-element.145.refs_4_) | copy-start | bytes 3145732
  529.4 8.3 %copy-start.4 = (bf16[1024,512]{1,0:T(8,128)(2,1)S(1)}, bf16[1024,512]{1,0:T(8,128)(2,1)}, u32[]{:S(2)}) copy-start(bf16[1024,512]{1,0:T(8,128)(2,1)} %get-tuple-element.144.refs_3_) | copy-start | bytes 3145732
  529.5 6.0 %collective-permute-start.31 = (f32[8,1216]{1,0:T(8,128)S(1)}, f32[8,1216]{1,0:T(8,128)S(1)}, u32[]{:S(2)}, u32[]{:S(2)}) collective-permute-start(f32[8,1216]{1,0:T(8,128)S(1)} %add.184), channel_id=1, source_target_pairs={{0,8},{4,12},{8,0},{12,4},{16,24},{20,28},{24,16},{28,20},{1,9},{5... | collective-permute-start | bytes 116744 | tf_op jit(solution)/shard_map/ppermute | solution.py:952
  530.5 39.3 %collective-permute-start.36 = (bf16[512,512]{1,0:T(8,128)(2,1)}, bf16[512,512]{1,0:T(8,128)(2,1)}, u32[]{:S(2)}, u32[]{:S(2)}) collective-permute-start(bf16[512,512]{1,0:T(8,128)(2,1)} %add_convert_fusion.7.refs_5_), channel_id=1, source_target_pairs={{0,1},{1,0},{2,3},{3,2},{4,5},{5,4},{6,7},{7,6},{8,9},{9,8},{10,11... | collective-permute-start | bytes 1572872 | tf_op jit(solution)/shard_map/ppermute | solution.py:952
  535.5 7.4 %collective-permute-start.32 = (f32[8,1216]{1,0:T(8,128)S(1)}, f32[8,1216]{1,0:T(8,128)S(1)}, u32[]{:S(2)}, u32[]{:S(2)}) collective-permute-start(f32[8,1216]{1,0:T(8,128)S(1)} %add.185), channel_id=1, source_target_pairs={{0,16},{4,20},{8,24},{12,28},{16,0},{20,4},{24,8},{28,12},{1,17},{... | collective-permute-start | bytes 116744 | tf_op jit(solution)/shard_map/ppermute | solution.py:952
  538.7 31.2 %collective-permute-start.35 = (bf16[512,512]{1,0:T(8,128)(2,1)}, bf16[512,512]{1,0:T(8,128)(2,1)}, u32[]{:S(2)}, u32[]{:S(2)}) collective-permute-start(bf16[512,512]{1,0:T(8,128)(2,1)} %add_convert_fusion.8.refs_4_), channel_id=1, source_target_pairs={{0,2},{1,3},{2,0},{3,1},{4,6},{5,7},{6,4},{7,5},{8,10},{9,11},{10,... | collective-permute-start | bytes 1572872 | tf_op jit(solution)/shard_map/ppermute | solution.py:952
  544.5 4.8 copy-start.43
  547.7 22.1 %collective-permute-start.38 = (bf16[512,512]{1,0:T(8,128)(2,1)S(1)}, bf16[512,512]{1,0:T(8,128)(2,1)S(1)}, u32[]{:S(2)}, u32[]{:S(2)}) collective-permute-start(bf16[512,512]{1,0:T(8,128)(2,1)S(1)} %add_convert_fusion.5.refs_10_), channel_id=1, source_target_pairs={{0,1},{1,0},{2,3},{3,2},{4,5},{5,4},{6,7},{7,6},{8,9},{9,8},{10,11... | collective-permute-start | bytes 1572872 | tf_op jit(solution)/shard_map/ppermute | solution.py:952
  548.3 21.5 %collective-permute-start.37 = (bf16[512,512]{1,0:T(8,128)(2,1)S(1)}, bf16[512,512]{1,0:T(8,128)(2,1)S(1)}, u32[]{:S(2)}, u32[]{:S(2)}) collective-permute-start(bf16[512,512]{1,0:T(8,128)(2,1)S(1)} %add_convert_fusion.6.refs_9_), channel_id=1, source_target_pairs={{0,2},{1,3},{2,0},{3,1},{4,6},{5,7},{6,4},{7,5},{8,10},{9,11},{10,... | collective-permute-start | bytes 1572872 | tf_op jit(solution)/shard_map/ppermute | solution.py:952
  562.3 3.6 collective-permute-start.39
  565.9 13.9 %collective-permute-start.40 = (f32[3,256]{1,0:T(4,128)S(1)}, f32[3,256]{1,0:T(4,128)S(1)}, u32[]{:S(2)}, u32[]{:S(2)}) collective-permute-start(f32[3,256]{1,0:T(4,128)S(1)} %add.192), channel_id=1, source_target_pairs={{0,2},{1,3},{2,0},{3,1},{4,6},{5,7},{6,4},{7,5},{8,10},{9,11},{10,... | collective-permute-start | bytes 9224 | tf_op jit(solution)/shard_map/ppermute | solution.py:952
  (37 other events, 57.5 us)
Sparse Core Ops, SparseCore 0:
  9.9 90.3 all-gather.8
  102.7 87.6 all-gather.6
  192.0 82.0 all-gather.4
  276.8 34.3 reduce-scatter.5
  313.3 101.1 reduce-scatter.3
  447.4 105.6 reduce-scatter.7

commit v6 on v5

--- a/solution.py
+++ b/solution.py
@@ -172,26 +172,23 @@
     )
 
 
-def heads_sum(own, other, moving):
-    depth, wide = moving.shape
+def heads_sum(sums):
+    depth, wide = sums.shape
     inner = wide // 3
-    rows = min(64, depth)
-
-    def kernel(own_ref, other_ref, moving_ref, out_ref):
-        total = own_ref[...].astype(F32) + other_ref[...].astype(F32) + moving_ref[...].astype(F32)
+
+    def kernel(sums_ref, out_ref):
         for part in range(3):
-            out_ref[part] = total[:, part * inner : (part + 1) * inner]
-
-    block = pl.BlockSpec((rows, wide), lambda m: (m, 0))
+            out_ref[part] = sums_ref[:, part * inner : (part + 1) * inner].astype(F32)
+
     return call(
         kernel,
         "heads_sum",
         0,
-        10 * depth * wide,
-        (own, other, moving),
-        (depth // rows,),
-        [block] * 3,
-        pl.BlockSpec((3, rows, inner), lambda m: (0, m, 0)),
+        6 * depth * wide,
+        (sums,),
+        (1,),
+        [pl.BlockSpec((depth, wide), lambda m: (0, 0))],
+        pl.BlockSpec((3, depth, inner), lambda m: (0, 0, 0)),
         struct((3, depth, inner), F32),
     )
 
@@ -570,65 +567,69 @@
     return starts + [total]
 
 
-def weight_grad(blocks, rows_in, right, name, more=None, weights=None, after=()):
+def columns_of(rights, cols):
+    starts, total = [], 0
+    for right in rights:
+        starts.append(total)
+        total += right.shape[1] // cols
+    return starts + [total]
+
+
+def weight_grad(blocks, rows_in, rights, cols, name, weights=None, after=()):
     length, width = rows_in.shape
     half = width // 2
     count = blocks.shape[0]
     depth = width // count
-    cols = min(1024, right.shape[1])
-    total = right.shape[1] // cols
+    starts = columns_of(rights, cols)
+    n, total = len(rights), starts[-1]
     k = len(weights.arrays) if weights else 0
-    extra = 2 if k else 0
-
-    def kernel(blk, a_ref, right_ref, *refs):
+    more = 1 if k else 0
+
+    def kernel(blk, a_ref, *refs):
+        w_refs, out_ref = refs[n : n + k], refs[n + k]
         chunk, side = pl.program_id(0), pl.program_id(1)
-
-        def product(ref, target):
-            low = dot(a_ref[...], ref[...], TN).astype(BF)
-            for p in range(count // 2):
-                place = pl.multiple_of(blk[side * (count // 2) + p] * depth, depth)
-                target[pl.ds(place, depth), :] = low[p * depth : (p + 1) * depth]
-
-        if not k:
-            product(right_ref, refs[0])
-            return
-        more_ref, w_refs, inner = refs[0], refs[1 : 1 + k], more.shape[1]
-        out_ref, more_out_ref, back_ref, w_ref, sum_ref, sems = refs[1 + k :]
-        copies = weights.copies(w_refs, blk, count, None, weights.cols - inner, inner, w_ref, sems)
-
-        @pl.when((chunk == 0) & (side == 0))
-        def _():
-            for copy in copies:
-                copy.start()
-
-        pl.when(chunk < total)(lambda: product(right_ref, out_ref))
-        pl.when(chunk == total)(lambda: product(more_ref, more_out_ref))
-
-        @pl.when((chunk == total + 1) & (side == 0))
-        def _():
-            for copy in copies:
-                copy.wait()
-            sum_ref[...] = dot(a_ref[...], w_ref[:half, :], NN)
-
-        @pl.when((chunk == total + 1) & (side == 1))
-        def _():
-            back_ref[...] = (sum_ref[...] + dot(a_ref[...], w_ref[half:, :], NN)).astype(BF)
-
-    def whole(shape):
-        return pl.BlockSpec(shape, lambda n, s, blk: (0, 0))
-
-    in_specs = [
-        pl.BlockSpec((length, half), lambda n, s, blk: (0, s)),
-        pl.BlockSpec((length, cols), lambda n, s, blk: (0, jnp.minimum(n, total - 1))),
-    ]
+        if more:
+            back_ref, w_ref, sum_ref, sems = refs[n + k + 1 :]
+            inner = w_ref.shape[1]
+            copies = weights.copies(w_refs, blk, count, None, 3 * inner, inner, w_ref, sems)
+
+            @pl.when((chunk == 0) & (side == 0))
+            def _():
+                for copy in copies:
+                    copy.start()
+
+            @pl.when((chunk == total) & (side == 0))
+            def _():
+                for copy in copies:
+                    copy.wait()
+                sum_ref[...] = dot(a_ref[...], w_ref[:half, :], NN)
+
+            @pl.when((chunk == total) & (side == 1))
+            def _():
+                back_ref[...] = (sum_ref[...] + dot(a_ref[...], w_ref[half:, :], NN)).astype(BF)
+
+        for i in range(n):
+
+            @pl.when((chunk >= starts[i]) & (chunk < starts[i + 1]))
+            def _(i=i):
+                product = dot(a_ref[...], refs[i][...], TN).astype(BF)
+                for p in range(count // 2):
+                    place = pl.multiple_of(blk[side * (count // 2) + p] * depth, depth)
+                    out_ref[pl.ds(place, depth), :] = product[p * depth : (p + 1) * depth]
+
+    def right_spec(i):
+        number = starts[i + 1] - starts[i]
+        return pl.BlockSpec(
+            (length, cols), lambda n, s, blk: (0, jnp.clip(n - starts[i], 0, number - 1))
+        )
+
     out_specs = [pl.BlockSpec((width, cols), lambda n, s, blk: (0, jnp.minimum(n, total - 1)))]
-    out_shape = [struct((width, right.shape[1]))]
+    out_shape = [struct((width, total * cols))]
     scratch = []
-    if k:
-        inner = more.shape[1]
-        in_specs += [whole((length, inner))] + [pl.BlockSpec(memory_space=pl.ANY)] * k
-        out_specs += [whole((width, inner)), whole((length, inner))]
-        out_shape += [struct((width, inner)), struct((length, inner))]
+    if more:
+        inner = weights.cols // 4
+        out_specs.append(pl.BlockSpec((length, inner), lambda n, s, blk: (0, 0)))
+        out_shape.append(struct((length, inner)))
         scratch = [
             pltpu.VMEM((width, inner), BF),
             pltpu.VMEM((length, inner), F32),
@@ -637,59 +638,17 @@
     return call(
         kernel,
         name,
-        2 * length * width * right.shape[1],
-        2 * length * width + 4 * length * right.shape[1] + 2 * width * right.shape[1],
-        (rows_in, right, *((more, *weights.arrays) if k else ())),
-        (total + extra, 2),
-        in_specs,
+        2 * length * width * total * cols,
+        2 * length * width + 4 * length * total * cols + 2 * width * total * cols,
+        (rows_in, *rights, *(weights.arrays if more else ())),
+        (total + more, 2),
+        [pl.BlockSpec((length, half), lambda n, s, blk: (0, s))]
+        + [right_spec(i) for i in range(n)]
+        + [pl.BlockSpec(memory_space=pl.ANY)] * k,
         out_specs,
         out_shape,
         scratch=scratch,
         prefetch=(blocks,),
-        after=after,
-    )
-
-
-def weight_grad_halves(rows_in, rights, cols, name, after=()):
-    length, width = rows_in.shape
-    half = width // 2
-    starts = columns_of(rights, cols)
-    n, total = len(rights), starts[-1]
-
-    def kernel(a_ref, *refs):
-        sib_ref, own_ref = refs[n:]
-        side, chunk = pl.program_id(0), pl.program_id(1)
-        for i in range(n):
-
-            @pl.when((chunk >= starts[i]) & (chunk < starts[i + 1]))
-            def _(i=i):
-                product = dot(a_ref[...], refs[i][...], TN).astype(BF)
-
-                @pl.when(side == 0)
-                def _():
-                    sib_ref[...] = product
-
-                @pl.when(side == 1)
-                def _():
-                    own_ref[...] = product
-
-    def right_spec(i):
-        number = starts[i + 1] - starts[i]
-        return pl.BlockSpec((length, cols), lambda s, n: (0, jnp.clip(n - starts[i], 0, number - 1)))
-
-    return call(
-        kernel,
-        name,
-        2 * length * width * total * cols,
-        2 * length * width + 4 * length * total * cols + 2 * width * total * cols,
-        (rows_in, *rights),
-        (2, total),
-        [pl.BlockSpec((length, half), lambda s, n: (0, 1 - s))] + [right_spec(i) for i in range(n)],
-        [
-            pl.BlockSpec((half, cols), lambda s, n: (0, jnp.where(s == 0, n, total - 1))),
-            pl.BlockSpec((half, cols), lambda s, n: (0, jnp.where(s == 0, 0, n))),
-        ],
-        [struct((half, total * cols))] * 2,
         after=after,
     )
 
@@ -863,12 +822,13 @@
     )
 
 
-def turned_sums(sums):
-    n = len(sums)
-
-    def kernel(*refs):
-        for ref, out_ref in zip(refs[:n], refs[n:]):
-            out_ref[...] = ref[...].T.astype(F32)
+def turned_sums(sums, units):
+    depth, cols = sums.shape
+    inner = cols - units
+
+    def kernel(sums_ref, fc2_ref, out_ref):
+        fc2_ref[...] = sums_ref[:, :units].T.astype(F32)
+        out_ref[...] = sums_ref[:, units:].T.astype(F32)
 
     def whole(shape):
         return pl.BlockSpec(shape, lambda i: (0, 0))
@@ -877,12 +837,12 @@
         kernel,
         "turned_sums",
         0,
-        6 * sum(value.size for value in sums),
-        sums,
+        6 * depth * cols,
+        (sums,),
         (1,),
-        [whole(value.shape) for value in sums],
-        [whole(value.shape[::-1]) for value in sums],
-        [struct(value.shape[::-1], F32) for value in sums],
+        [whole((depth, cols))],
+        [whole((units, depth)), whole((inner, depth))],
+        [struct((units, depth), F32), struct((inner, depth), F32)],
     )
 
 
@@ -1096,54 +1056,42 @@
     def scatter(parts):
         return lax.psum_scatter(parts, "dp", scatter_dimension=0, tiled=True)
 
-    fc2_grad, out_grads, context_grad = weight_grad(
-        blocks, g_all, act, "fc2_grad", context, heads_weights
-    )
-    fc2_sums, out_sums = scatter(fc2_grad), scatter(out_grads)
+    fc2_grad, context_grad = weight_grad(
+        blocks, g_all, [act, context], min(512, inner), "fc2_grad", heads_weights
+    )
+    fc2_sums = scatter(fc2_grad)
     *backs, b_qkv_part = attend_back(qkv, context, context_grad, log_total, tables)
-    heads_sib_grad, heads_own_grad = weight_grad_halves(normed, backs, inner, "heads_grad")
-
-    def ring_add(k, moving=None):
-        cut = slice(k * depth, (k + 1) * depth)
-        total = heads_own_grad[cut].astype(F32) + heads_other[cut].astype(F32)
-        return total if moving is None else total + moving.astype(F32)
+    (heads_grad,) = weight_grad(blocks, normed, backs, inner, "heads_grad")
+    heads_scattered = scatter(heads_grad)
 
     heads_cols, fc2_cols = (heads_weights, 0, 3 * inner), (fc2_weights, 0, units)
     out_cols, fc1_cols = (heads_weights, 3 * inner, inner), (fc1_weights, 0, units)
     lefts = [act, context]
     branch = rows_back(
         blocks, order, {0: split("first"), 1: split("second")}, lefts, [fc2_cols, out_cols], "branch",
-        after=[heads_own_grad],
-    )
-    *branch, heads_other = tie([*branch, ring.swap(heads_sib_grad)], [])
+        after=[heads_grad],
+    )
     n = len(branch) // 2
     branch_own, branch_sib = branch[:n], branch[n:]
-    message = ring_add(1).astype(BF)
-    moving = ring.send(message)
-    hidden_grad, b_fc1_part = hidden_back(blocks, g_all, fc2_weights, slope, after=[message])
-    hidden_grad, moving = tie([hidden_grad, moving], [])
-    message = ring_add(2, moving).astype(BF)
-    (fc1_grad,) = weight_grad(blocks, normed, hidden_grad, "fc1_grad", after=[message])
+    hidden_grad, b_fc1_part = hidden_back(blocks, g_all, fc2_weights, slope, after=branch)
+    (fc1_grad,) = weight_grad(blocks, normed, [hidden_grad], min(1024, units), "fc1_grad")
     branch_got = cross_once("first", branch_own) + cross_once("second", branch_sib)
     n = len(branch_got)
-    fc1_grad, moving, *branch_got = tie([fc1_grad, ring.send(message), *branch_got], [])
+    fc1_grad, *branch_got = tie([fc1_grad, *branch_got], [])
     fc1_sums = scatter(fc1_grad)
-    for k in range(3, chips):
-        message = ring_add(k, moving).astype(BF)
-        moving = ring.send(message)
     branch_sums = cross_add(branch_own, branch_got[:1]) + cross_add(branch_sib, branch_got[1:])
     branch_last = cross_twice("first", branch_sums[:1]) + cross_twice("second", branch_sums[1:])
 
     lefts = [*backs, hidden_grad]
     back_own = rows_back(
         blocks, order, {0: split("both")}, lefts, [heads_cols, fc1_cols], "normed_back_half",
-        after=[fc1_grad, message, *branch_sums],
+        after=[fc1_grad, *branch_sums],
     )
     n = len(back_own)
     sums_own = gain_sums(order, split("both"), back_own, unit, 0)
-    joined = tie([*back_own, moving, *branch_last], [sums_own])
-    back_own, moving, branch_last = joined[:n], joined[n], joined[n + 1 :]
-    heads_sums = heads_sum(heads_own_grad, heads_other, moving)
+    joined = tie([*back_own, *branch_last], [sums_own])
+    back_own, branch_last = joined[:n], joined[n:]
+    heads_sums = heads_sum(heads_scattered)
     branch_terms = cross_terms(branch_own, branch_got[:1], branch_last[:1])
     branch_terms += cross_terms(branch_sib, branch_got[1:], branch_last[1:])
     own_got = cross_once("both", back_own)
@@ -1175,7 +1123,7 @@
 
     sums = flip_sum(by_owner, "dp", n_dp)
     sums = lax.dynamic_index_in_dim(sums, d_index, 0, keepdims=False)
-    w_fc2_grad, w_out_grad = turned_sums((fc2_sums, out_sums))
+    w_fc2_grad, w_out_grad = turned_sums(fc2_sums, units)
     sums, *sib_got = tie([sums, *sib_got], [heads_sums, *own_sums])
     sib_sums = cross_add(back_sib, sib_got)
     sib_last = cross_twice("both", sib_sums)

time: 593 us -> 651 us (1.098)
  waiting for transfers between devices: 81.6 us -> 151 us
    reduce_scatter x3, waiting for transfers between devices: 0.02 us -> 74.9 us  [scatter(): return lax.psum_scatter(parts, 'dp', scatter_dimension=0, tiled=True)]
    unnamed x109 -> x89, local copies, waits for them, and re-layouts: 22.8 us -> 16.1 us
    ppermute x9 -> x6, waiting for transfers between devices: 53.4 us -> 47.6 us  [send(): return lax.ppermute(value, 'dp', pairs)]
    ppermute x32 -> x31, starting transfers between devices: 25.5 us -> 23.8 us  [flip(): return lax.ppermute(value, axis, [(i, i ^ bit) for i in range(size)])]
    ppermute x32 -> x31, waiting for transfers between devices: 27.4 us -> 26.8 us  [flip(): return lax.ppermute(value, axis, [(i, i ^ bit) for i in range(size)])]
  transfers between devices with their start and end apart: 47 -> 43, of which waited for: 12 -> 14; matrix products, arithmetic and copies ran while one was open for 7% -> 6% of each run, Pallas kernels for 67% -> 61%
where the time goes in v6:
time: 651 us; the launch traced here: 646 us
  Pallas kernels  395 us (61%)
  waiting for transfers between devices  151 us (23%)
  starting transfers between devices  33.9 us (5%)
  local copies, waits for them, and re-layouts  28.3 us (4%)
  other arithmetic  22.1 us (3%)
  between operations  15 us (2%)
    pallas_call x22, Pallas kernels, call(): pl.pallas_call(body, name=name, grid_spec=pltpu.PrefetchScalarGridSpec(nu...  395 us
    reduce_scatter x3, waiting for transfers between devices, scatter(): return lax.psum_scatter(parts, 'dp', scatter_dimension=0, tiled=True)  74.9 us
    ppermute x6, waiting for transfers between devices, send(): return lax.ppermute(value, 'dp', pairs)  47.6 us
    ppermute x31, waiting for transfers between devices, flip(): return lax.ppermute(value, axis, [(i, i ^ bit) for i in range(size)])  26.8 us
    ppermute x31, starting transfers between devices, flip(): return lax.ppermute(value, axis, [(i, i ^ bit) for i in range(size)])  23.8 us
    unnamed x89, local copies, waits for them, and re-layouts  16.1 us
  transfers between devices with their start and end apart: 43, of which 14 were waited for; matrix products, arithmetic and copies ran while one was open for 6% of the time, Pallas kernels for 61%

profile of v6, /device:TPU:0, one launch (start us, length us, event | category | flops | bytes accessed | tf_op | source)
XLA Modules:
  0.0 645.7 jit_solution(3116278487095047946)
XLA Ops:
  8.0 2.3 heads_shard.1.refs_2_.refs_1_.refs_8_.refs_4_.refs_5_.refs_6_
  10.7 2.6 collective-permute-start.3
  13.5 2.4 collective-permute-start.2
  17.9 3.7 order_columns.1
  22.5 16.9 %collective-permute-done.3.refs_2_.refs_9_.refs_5_.refs_6_.refs_7_ = bf16[256,2048]{1,0:T(8,128)(2,1)S(1)} collective-permute-done((bf16[256,2048]{1,0:T(8,128)(2,1)}, bf16[256,2048]{1,0:T(8,128)(2,1)S(1)}, u32[]{:S(2)}, u32[]{:S(2)}) %collective-permute-start.3) | collective-permute-done | bytes 1048608 | tf_op jit(solution)/shard_map/ppermute | solution.py:934
  40.5 1.1 copy-done.16
  43.0 1.3 collective-permute-start.6
  44.3 24.7 %collective-permute-done.8.refs_1_.refs_10_.refs_6_.refs_7_.refs_8_ = bf16[256,2048]{1,0:T(8,128)(2,1)} collective-permute-done((bf16[256,2048]{1,0:T(8,128)(2,1)S(1)}, bf16[256,2048]{1,0:T(8,128)(2,1)}, u32[]{:S(2)}, u32[]{:S(2)}) %collective-permute-start.8) | collective-permute-done | bytes 1048608 | tf_op jit(solution)/shard_map/ppermute | solution.py:934
  69.9 5.0 fusion.1
  74.9 2.6 stage_weight.3.refs_1_
  77.5 2.3 stage_weight.2.refs_0_
  79.8 13.6 %collective-permute-done.7 = f32[8,1216]{1,0:T(8,128)S(1)} collective-permute-done((f32[8,1216]{1,0:T(8,128)S(1)}, f32[8,1216]{1,0:T(8,128)S(1)}, u32[]{:S(2)}, u32[]{:S(2)}) %collective-permute-start.7) | collective-permute-done | bytes 38944 | tf_op jit(solution)/shard_map/ppermute | solution.py:912
  94.1 1.0 copy-done.17
  100.9 1.0 copy-done.10
  102.3 3.5 collective-permute-start.14
  105.8 1.2 collective-permute-start.13
  107.7 1.0 copy-done.20
  108.7 27.8 %norm_project.1 = (bf16[2048,2048]{1,0:T(8,128)(2,1)}, bf16[2048,2048]{1,0:T(8,128)(2,1)}, bf16[2048,1536]{1,0:T(8,128)(2,1)}) custom-call(s32[8]{0:T(128)} %pad_add_fusion.refs_0_, bf16[2048,2048]{1,0:T(8,128)(2,1)} %bitcast.40, f32[1,2048]{1,0:T(1,128)} %reshape_squeeze.12.refs_4_.refs_2_.refs_15_, f32[1,2048]{1,0:T(1,128)} %reshape_squeeze.13.refs_3_, ...), custom_call_target="tpu_custom_call" | custom-call | tf_op jit(solution)/shard_map/norm_project/pallas_call | solution.py:40
  136.5 19.1 %attend.2 = (bf16[2048,512]{1,0:T(8,128)(2,1)}, f32[2,2,2048]{2,1,0:T(2,128)}) custom-call(bf16[2048,1536]{1,0:T(8,128)(2,1)} %get-tuple-element.75.refs_0_.refs_1_.refs_2_, bf16[2048,1536]{1,0:T(8,128)(2,1)} %get-tuple-element.75.refs_0_.refs_1_.refs_2_, bf16[2048,1536]{1,0:T(8,128)(2,1)} %get-tuple-element.75.refs_0_.refs_1_.refs_2_, ...), custom_call_target="tpu_custom_call" | custom-call | tf_op jit(solution)/shard_map/attend/pallas_call | solution.py:40
  157.1 2.2 collective-permute-start.16
  159.3 19.1 %attend.3 = (bf16[2048,512]{1,0:T(8,128)(2,1)}, f32[2,2,2048]{2,1,0:T(2,128)}) custom-call(bf16[2048,1536]{1,0:T(8,128)(2,1)} %get-tuple-element.75.refs_0_.refs_1_.refs_2_, bf16[2048,1536]{1,0:T(8,128)(2,1)} %get-tuple-element.75.refs_0_.refs_1_.refs_2_, ...), custom_call_target="tpu_custom_call", output_to_operand_aliasing={{0}: (3, {})} | custom-call | tf_op jit(solution)/shard_map/attend/pallas_call | solution.py:40
  178.4 6.0 collective-permute-done.16.refs_1_
  184.4 1.0 copy-done.24
  186.1 1.4 pad_maximum_fusion.1.refs_5_
  188.2 1.0 copy-done.42
  189.2 32.0 %expand.1 = (bf16[2048,2048]{1,0:T(8,128)(2,1)}, bf16[2048,2048]{1,0:T(8,128)(2,1)}) custom-call(s32[8]{0:T(128)} %pad_add_fusion.refs_0_, bf16[2048,2048]{1,0:T(8,128)(2,1)} %get-tuple-element.74.refs_1_, bf16[256,2048]{1,0:T(8,128)(2,1)} %get-tuple-element.73.refs_16_.refs_3_.refs_2_.refs_14_, bf16[256,2048]{1,0:T(8,128)(2,1)} %get-tuple-element.77.refs_3_.refs_15_, ...), custom_call_target="tpu_custom_call" | custom-call | flops 17179869184 | bytes 33554432 | tf_op jit(solution)/shard_map/expand/pallas_call | solution.py:40
  221.3 37.8 %fc2_grad.1 = (bf16[2048,2560]{1,0:T(8,128)(2,1)}, bf16[2048,512]{1,0:T(8,128)(2,1)}) custom-call(s32[8]{0:T(128)} %pad_add_fusion.refs_0_, bf16[2048,2048]{1,0:T(8,128)(2,1)} %all-gather.7.cloned.1.call-done.refs_1_, bf16[2048,2048]{1,0:T(8,128)(2,1)} %get-tuple-element.84.refs_2_, bf16[2048,512]{1,0:T(8,128)(2,1)} %get-tuple-element.85.refs_3_, ...), custom_call_target="tpu_custom_call" | custom-call | flops 21474836480 | bytes 39845888 | tf_op jit(solution)/shard_map/fc2_grad/pallas_call | solution.py:40
  259.1 65.5 %attend_back.1 = (bf16[2048,512]{1,0:T(8,128)(2,1)}, bf16[2048,512]{1,0:T(8,128)(2,1)}, bf16[2048,512]{1,0:T(8,128)(2,1)}, f32[4,24,128]{2,1,0:T(8,128)}) custom-call(bf16[2048,1536]{1,0:T(8,128)(2,1)} %get-tuple-element.75.refs_0_.refs_1_.refs_2_, bf16[2048,1536]{1,0:T(8,128)(2,1)} %get-tuple-element.75.refs_0_.refs_1_.refs_2_, ...), custom_call_target="tpu_custom_call" | custom-call | flops 128849018880 | bytes 16777216 | tf_op jit(solution)/shard_map/attend_back/pallas_call | solution.py:40
  324.6 21.5 %heads_grad.1.refs_13_ = bf16[2048,1536]{1,0:T(8,128)(2,1)} custom-call(s32[8]{0:T(128)} %pad_add_fusion.refs_0_, bf16[2048,2048]{1,0:T(8,128)(2,1)} %get-tuple-element.74.refs_1_, bf16[2048,512]{1,0:T(8,128)(2,1)} %get-tuple-element.89.refs_2_, bf16[2048,512]{1,0:T(8,128)(2,1)} %get-tuple-element.90.refs_3_, bf16[2048,512]{1,0:T(8,128)(2,1)} %get-tuple-element.91.refs_4_), custom_call_target="tpu_custom_call" | custom-call | flops 12884901888 | bytes 27262976 | tf_op jit(solution)/shard_map/heads_grad/pallas_call | solution.py:40
  347.3 31.8 %branch.1 = (bf16[1024,1024]{1,0:T(8,128)(2,1)}, bf16[1024,1024]{1,0:T(8,128)(2,1)}, bf16[1024,1024]{1,0:T(8,128)(2,1)}, bf16[1024,1024]{1,0:T(8,128)(2,1)}) custom-call(s32[8]{0:T(128)} %pad_add_fusion.refs_0_, s32[4]{0:T(128)} %broadcast_xor_fusion.refs_1_.refs_0_, bf16[2048,2048]{1,0:T(8,128)(2,1)} %get-tuple-element.84.refs_2_, ...), custom_call_target="tpu_custom_call" | custom-call | flops 21474836480 | bytes 29360128 | tf_op jit(solution)/shard_map/branch/pallas_call | solution.py:40
  379.1 1.6 collective-permute-start.20
  380.7 1.5 collective-permute-start.21
  382.2 26.1 %hidden_back.1 = (bf16[2048,2048]{1,0:T(8,128)(2,1)}, f32[8,2048]{1,0:T(8,128)}) custom-call(s32[8]{0:T(128)} %pad_add_fusion.refs_0_, bf16[2048,2048]{1,0:T(8,128)(2,1)} %all-gather.7.cloned.1.call-done.refs_1_, bf16[2048,2048]{1,0:T(8,128)(2,1)} %all-gather.5.cloned.1.call-done.refs_4_.refs_2_, bf16[2048,2048]{1,0:T(8,128)(2,1)} %get-tuple-element.93.refs_3_, ...), custom_call_target="tpu_custom_call" | custom-call | flops 17179869184 | bytes 33554432 | tf_op jit(solution)/shard_map/hidden_back/pallas_call | solution.py:40
  408.3 24.6 %fc1_grad.1.refs_0_ = bf16[2048,2048]{1,0:T(8,128)(2,1)} custom-call(s32[8]{0:T(128)} %pad_add_fusion.refs_0_, bf16[2048,2048]{1,0:T(8,128)(2,1)} %get-tuple-element.74.refs_1_, bf16[2048,2048]{1,0:T(8,128)(2,1)} %get-tuple-element.97.refs_2_.refs_5_), custom_call_target="tpu_custom_call" | custom-call | flops 17179869184 | bytes 33554432 | tf_op jit(solution)/shard_map/fc1_grad/pallas_call | solution.py:40
  433.0 1.3 copy-done
  434.3 1.0 slice_reduce_fusion.3
  435.3 1.9 add_convert_fusion.refs_24_
  437.9 1.6 add_convert_fusion.1.refs_23_
  440.5 23.6 %normed_back_half.2 = (bf16[1024,512]{1,0:T(8,128)(2,1)}, bf16[1024,512]{1,0:T(8,128)(2,1)}, bf16[1024,512]{1,0:T(8,128)(2,1)}, bf16[1024,512]{1,0:T(8,128)(2,1)}) custom-call(s32[8]{0:T(128)} %pad_add_fusion.refs_0_, s32[4]{0:T(128)} %broadcast_xor_fusion.refs_1_.refs_0_, bf16[2048,512]{1,0:T(8,128)(2,1)} %get-tuple-element.89.refs_2_, ...), custom_call_target="tpu_custom_call" | custom-call | flops 15032385536 | bytes 26214400 | tf_op jit(solution)/shard_map/normed_back_half/pallas_call | solution.py:40
  464.2 5.8 gain_sums.2.refs_6_
  471.9 1.1 collective-permute-start.25
  473.0 1.5 collective-permute-start.24
  474.5 23.5 %normed_back_half.3 = (bf16[1024,512]{1,0:T(8,128)(2,1)}, bf16[1024,512]{1,0:T(8,128)(2,1)}, bf16[1024,512]{1,0:T(8,128)(2,1)}, bf16[1024,512]{1,0:T(8,128)(2,1)}) custom-call(s32[8]{0:T(128)} %pad_add_fusion.refs_0_, s32[4]{0:T(128)} %broadcast_xor_fusion.refs_1_.refs_0_, bf16[2048,512]{1,0:T(8,128)(2,1)} %get-tuple-element.89.refs_2_, ...), custom_call_target="tpu_custom_call" | custom-call | flops 15032385536 | bytes 26214400 | tf_op jit(solution)/shard_map/normed_back_half/pallas_call | solution.py:40
  501.3 6.0 gain_sums.3
  508.7 1.2 collective-permute-done.26
  509.9 2.0 add_convert_fusion.4.refs_5_
  511.9 1.5 collective-permute-start.32
  513.3 2.2 collective-permute-done.27
  516.5 1.1 collective-permute-start.31
  517.6 4.8 collective-permute-done.28
  523.0 2.4 heads_sum.1.refs_3_
  525.6 1.0 collective-permute-done.29.refs_1_
  527.0 1.2 add_convert_fusion.3.refs_9_
  528.2 1.4 add_convert_fusion.2.refs_10_
  529.6 1.5 collective-permute-start.34
  531.1 1.1 collective-permute-start.33
  532.9 5.7 add_branch.1.refs_1_
  538.6 3.1 turned_sums.1
  541.7 74.9 %reduce-scatter.8.cloned.1.call-done = bf16[256,2048]{1,0:T(8,128)(2,1)} async-done(((bf16[2048,2048]{1,0:T(8,128)(2,1)}), bf16[256,2048]{1,0:T(8,128)(2,1)}) %reduce-scatter.8.cloned.1.call-update) | async-done | bytes 1048592 | tf_op jit(solution)/shard_map/reduce_scatter | solution.py:1057
  616.6 2.8 convert_element_type.115.refs_3_
  620.1 1.4 collective-permute-start.35
  621.5 2.2 collective-permute-done.35
  623.7 1.5 collective-permute-start.36
  629.7 8.4 %norm_back.1 = f32[512,2048]{1,0:T(8,128)} custom-call(s32[8]{0:T(128)} %pad_add_fusion.refs_0_, bf16[512,2048]{1,0:T(8,128)(2,1)} %bitcast.36, bf16[512,2048]{1,0:T(8,128)(2,1)} %bitcast.39, bf16[1024,512]{1,0:T(8,128)(2,1)} %get-tuple-element.121.refs_3_, bf16[1024,512]{1,0:T(8,128)(2,1)} %get-tuple-element.122.refs_4_, ...), custom_call_target="tpu_custom_call" | custom-call | bytes 10485760 | tf_op jit(solution)/shard_map/norm_back/pallas_call | solution.py:40
  (220 shorter events, 35.9 us)
Async XLA Ops:
  7.2 6.1 copy-start.39
  7.2 6.1 copy-start.40
  7.2 6.1 copy-start.41
  7.2 10.4 %copy-start.37 = (bf16[3,8,8]{2,1,0:T(8,128)(2,1)S(1)}, bf16[3,8,8]{2,1,0:T(8,128)(2,1)}, u32[]{:S(2)}) copy-start(bf16[3,8,8]{2,1,0:T(8,128)(2,1)} %param.17) | copy-start | bytes 1156
  7.2 10.5 %copy-start.38 = (bf16[32,8]{0,1:T(8,128)(2,1)S(1)}, bf16[32,8]{0,1:T(8,128)(2,1)}, u32[]{:S(2)}) copy-start(bf16[32,8]{0,1:T(8,128)(2,1)} %param.20) | copy-start | bytes 1540
  7.2 100.5 %all-gather.9.cloned.1.call-start = ((), (), s32[]{:S(2)}) async-start(), calls=%async_computation.8 | async-start | bytes 10485760 | tf_op jit(solution)/shard_map/all_gather | solution.py:963
  8.0 213.3 %all-gather.7.cloned.1.call-start = ((), (), s32[]{:S(2)}) async-start(), calls=%async_computation.4 | async-start | bytes 10485760 | tf_op jit(solution)/shard_map/all_gather | solution.py:975
  10.3 12.2 %collective-permute-start.4 = (bf16[256,2048]{1,0:T(8,128)(2,1)}, bf16[256,2048]{1,0:T(8,128)(2,1)S(1)}, u32[]{:S(2)}, u32[]{:S(2)}) collective-permute-start(bf16[256,2048]{1,0:T(8,128)(2,1)} %heads_shard.1.refs_2_.refs_1_.refs_8_.refs_4_.refs_5_.refs_6_), channel_id=1, source_target_pairs={{0,4},{4,0},{8,12},{12,8},{16,20},{20,16},{24,28},{28,24},{1,5},{5... | collective-permute-start | bytes 3145736 | tf_op jit(solution)/shard_map/ppermute | solution.py:912
  10.7 28.6 %collective-permute-start.3 = (bf16[256,2048]{1,0:T(8,128)(2,1)}, bf16[256,2048]{1,0:T(8,128)(2,1)S(1)}, u32[]{:S(2)}, u32[]{:S(2)}) collective-permute-start(bf16[256,2048]{1,0:T(8,128)(2,1)} %heads_shard.1.refs_2_.refs_1_.refs_8_.refs_4_.refs_5_.refs_6_), channel_id=1, source_target_pairs={{0,8},{4,12},{8,16},{12,20},{16,24},{20,28},{24,0},{28,4},{1,9},{5... | collective-permute-start | bytes 3145736 | tf_op jit(solution)/shard_map/ppermute | solution.py:934
  13.5 8.1 %collective-permute-start.2 = (f32[4,192]{1,0:T(4,128)S(1)}, f32[4,192]{1,0:T(4,128)S(1)}, u32[]{:S(2)}, u32[]{:S(2)}) collective-permute-start(f32[4,192]{1,0:T(4,128)S(1)} %broadcast_select_fusion.1), channel_id=1, source_target_pairs={{0,3},{1,2},{2,1},{3,0},{4,7},{5,6},{6,5},{7,4},{8,11},{9,10},{10,... | collective-permute-start | bytes 9224 | tf_op jit(solution)/shard_map/ppermute | solution.py:912
  16.0 5.7 collective-permute-start.1
  16.5 5.2 collective-permute-start
  22.5 16.9 %copy-start.14 = (bf16[256,2048]{1,0:T(8,128)(2,1)}, bf16[256,2048]{1,0:T(8,128)(2,1)S(1)}, u32[]{:S(2)}) copy-start(bf16[256,2048]{1,0:T(8,128)(2,1)S(1)} %collective-permute-done.4.refs_3_.refs_12_.refs_8_.refs_9_.refs_10_) | copy-start | bytes 3145732
  40.4 306.9 %all-gather.5.cloned.1.call-start = ((), (), s32[]{:S(2)}) async-start(), calls=%async_computation.3 | async-start | bytes 9437184 | tf_op jit(solution)/shard_map/all_gather | solution.py:1003
  41.6 27.4 %collective-permute-start.8 = (bf16[256,2048]{1,0:T(8,128)(2,1)S(1)}, bf16[256,2048]{1,0:T(8,128)(2,1)}, u32[]{:S(2)}, u32[]{:S(2)}) collective-permute-start(bf16[256,2048]{1,0:T(8,128)(2,1)S(1)} %copy-done.16), channel_id=1, source_target_pairs={{0,8},{4,12},{8,16},{12,20},{16,24},{20,28},{24,0},{28,4},{1,9},{5... | collective-permute-start | bytes 3145736 | tf_op jit(solution)/shard_map/ppermute | solution.py:934
  41.7 1.2 collective-permute-start.5
  41.7 52.4 %collective-permute-start.9 = (bf16[256,2048]{1,0:T(8,128)(2,1)S(1)}, bf16[256,2048]{1,0:T(8,128)(2,1)S(1)}, u32[]{:S(2)}, u32[]{:S(2)}) collective-permute-start(bf16[256,2048]{1,0:T(8,128)(2,1)S(1)} %copy-done.16), channel_id=1, source_target_pairs={{0,4},{4,0},{8,12},{12,8},{16,20},{20,16},{24,28},{28,24},{1,5},{5... | collective-permute-start | bytes 3145736 | tf_op jit(solution)/shard_map/ppermute | solution.py:912
  43.0 26.1 %collective-permute-start.6 = (f32[8,1216]{1,0:T(8,128)S(1)}, f32[8,1216]{1,0:T(8,128)S(1)}, u32[]{:S(2)}, u32[]{:S(2)}) collective-permute-start(f32[8,1216]{1,0:T(8,128)S(1)} %fusion.4), channel_id=1, source_target_pairs={{0,8},{4,12},{8,0},{12,4},{16,24},{20,28},{24,16},{28,20},{1,9},{5... | collective-permute-start | bytes 116744 | tf_op jit(solution)/shard_map/ppermute | solution.py:912
  69.0 31.9 %collective-permute-start.11 = (bf16[256,2048]{1,0:T(8,128)(2,1)}, bf16[256,2048]{1,0:T(8,128)(2,1)S(1)}, u32[]{:S(2)}, u32[]{:S(2)}) collective-permute-start(bf16[256,2048]{1,0:T(8,128)(2,1)} %collective-permute-done.8.refs_1_.refs_10_.refs_6_.refs_7_.refs_8_), channel_id=1, source_target_pairs={{0,4},{4,0},{8,12},{12,8},{16,20},{20,16},{24,28},{28,24},{1,5},{5... | collective-permute-start | bytes 3145736 | tf_op jit(solution)/shard_map/ppermute | solution.py:912
  69.0 30.9 %collective-permute-start.10 = (bf16[256,2048]{1,0:T(8,128)(2,1)}, bf16[256,2048]{1,0:T(8,128)(2,1)S(1)}, u32[]{:S(2)}, u32[]{:S(2)}) collective-permute-start(bf16[256,2048]{1,0:T(8,128)(2,1)} %collective-permute-done.8.refs_1_.refs_10_.refs_6_.refs_7_.refs_8_), channel_id=1, source_target_pairs={{0,8},{4,12},{8,16},{12,20},{16,24},{20,28},{24,0},{28,4},{1,9},{5... | collective-permute-start | bytes 3145736 | tf_op jit(solution)/shard_map/ppermute | solution.py:934
  69.1 24.3 %collective-permute-start.7 = (f32[8,1216]{1,0:T(8,128)S(1)}, f32[8,1216]{1,0:T(8,128)S(1)}, u32[]{:S(2)}, u32[]{:S(2)}) collective-permute-start(f32[8,1216]{1,0:T(8,128)S(1)} %fusion.16), channel_id=1, source_target_pairs={{0,16},{4,20},{8,24},{12,28},{16,0},{20,4},{24,8},{28,12},{1,17},{... | collective-permute-start | bytes 116744 | tf_op jit(solution)/shard_map/ppermute | solution.py:912
  99.9 7.8 %collective-permute-start.12 = (bf16[256,2048]{1,0:T(8,128)(2,1)S(1)}, bf16[256,2048]{1,0:T(8,128)(2,1)S(1)}, u32[]{:S(2)}, u32[]{:S(2)}) collective-permute-start(bf16[256,2048]{1,0:T(8,128)(2,1)S(1)} %collective-permute-done.10.refs_2_.refs_11_.refs_7_.refs_8_.refs_9_), channel_id=1, source_target_pairs={{0,4},{4,0},{8,12},{12,8},{16,20},{20,16},{24,28},{28,24},{1,5},{5... | collective-permute-start | bytes 3145736 | tf_op jit(solution)/shard_map/ppermute | solution.py:912
  101.9 53.7 %collective-permute-start.15 = (bf16[256,2048]{1,0:T(8,128)(2,1)}, bf16[256,2048]{1,0:T(8,128)(2,1)S(1)}, u32[]{:S(2)}, u32[]{:S(2)}) collective-permute-start(bf16[256,2048]{1,0:T(8,128)(2,1)} %get-tuple-element.73.refs_16_.refs_3_.refs_2_.refs_14_), channel_id=1, source_target_pairs={{0,4},{4,0},{8,12},{12,8},{16,20},{20,16},{24,28},{28,24},{1,5},{5... | collective-permute-start | bytes 3145736 | tf_op jit(solution)/shard_map/ppermute | solution.py:912
  102.3 53.3 %collective-permute-start.14 = (bf16[256,2048]{1,0:T(8,128)(2,1)}, bf16[256,2048]{1,0:T(8,128)(2,1)}, u32[]{:S(2)}, u32[]{:S(2)}) collective-permute-start(bf16[256,2048]{1,0:T(8,128)(2,1)} %get-tuple-element.73.refs_16_.refs_3_.refs_2_.refs_14_), channel_id=1, source_target_pairs={{0,24},{4,28},{8,0},{12,4},{16,8},{20,12},{24,16},{28,20},{1,25},{... | collective-permute-start | bytes 3145736 | tf_op jit(solution)/shard_map/ppermute | solution.py:934
  105.8 49.8 %collective-permute-start.13 = (bf16[256,2048]{1,0:T(8,128)(2,1)}, bf16[256,2048]{1,0:T(8,128)(2,1)}, u32[]{:S(2)}, u32[]{:S(2)}) collective-permute-start(bf16[256,2048]{1,0:T(8,128)(2,1)} %get-tuple-element.73.refs_16_.refs_3_.refs_2_.refs_14_), channel_id=1, source_target_pairs={{0,8},{4,12},{8,16},{12,20},{16,24},{20,28},{24,0},{28,4},{1,9},{5... | collective-permute-start | bytes 3145736 | tf_op jit(solution)/shard_map/ppermute | solution.py:934
  156.6 21.8 %collective-permute-start.18 = (bf16[256,2048]{1,0:T(8,128)(2,1)}, bf16[256,2048]{1,0:T(8,128)(2,1)S(1)}, u32[]{:S(2)}, u32[]{:S(2)}) collective-permute-start(bf16[256,2048]{1,0:T(8,128)(2,1)} %get-tuple-element.81.refs_5_.refs_17_), channel_id=1, source_target_pairs={{0,4},{4,0},{8,12},{12,8},{16,20},{20,16},{24,28},{28,24},{1,5},{5... | collective-permute-start | bytes 3145736 | tf_op jit(solution)/shard_map/ppermute | solution.py:912
  156.6 21.8 %collective-permute-start.17 = (bf16[256,2048]{1,0:T(8,128)(2,1)}, bf16[256,2048]{1,0:T(8,128)(2,1)S(1)}, u32[]{:S(2)}, u32[]{:S(2)}) collective-permute-start(bf16[256,2048]{1,0:T(8,128)(2,1)} %get-tuple-element.77.refs_3_.refs_15_), channel_id=1, source_target_pairs={{0,4},{4,0},{8,12},{12,8},{16,20},{20,16},{24,28},{28,24},{1,5},{5... | collective-permute-start | bytes 3145736 | tf_op jit(solution)/shard_map/ppermute | solution.py:912
  157.1 27.3 %collective-permute-start.16 = (bf16[256,2048]{1,0:T(8,128)(2,1)}, bf16[256,2048]{1,0:T(8,128)(2,1)S(1)}, u32[]{:S(2)}, u32[]{:S(2)}) collective-permute-start(bf16[256,2048]{1,0:T(8,128)(2,1)} %get-tuple-element.77.refs_3_.refs_15_), channel_id=1, source_target_pairs={{0,8},{4,12},{8,16},{12,20},{16,24},{20,28},{24,0},{28,4},{1,9},{5... | collective-permute-start | bytes 3145736 | tf_op jit(solution)/shard_map/ppermute | solution.py:934
  178.4 6.0 copy-start.22
  178.4 6.0 copy-start.23
  185.4 2.9 collective-permute-start.19
  185.4 337.6 %reduce-scatter.4.cloned.1.call-start = ((), (), s32[]{:S(2)}) async-start(), calls=%async_computation.5 | async-start | bytes 7077888 | tf_op jit(solution)/shard_map/reduce_scatter | solution.py:1057
  346.1 192.5 %reduce-scatter.6.cloned.1.call-start = ((), (), s32[]{:S(2)}) async-start(), calls=%async_computation.6 | async-start | bytes 11796480 | tf_op jit(solution)/shard_map/reduce_scatter | solution.py:1057
  346.7 269.9 %reduce-scatter.8.cloned.1.call-start = ((), (), s32[]{:S(2)}) async-start(), calls=%async_computation.7 | async-start | bytes 9437184 | tf_op jit(solution)/shard_map/reduce_scatter | solution.py:1057
  379.1 53.9 %collective-permute-start.20 = (bf16[1024,1024]{1,0:T(8,128)(2,1)}, bf16[1024,1024]{1,0:T(8,128)(2,1)S(1)}, u32[]{:S(2)}, u32[]{:S(2)}) collective-permute-start(bf16[1024,1024]{1,0:T(8,128)(2,1)} %get-tuple-element.94.refs_4_), channel_id=1, source_target_pairs={{0,1},{1,0},{2,3},{3,2},{4,5},{5,4},{6,7},{7,6},{8,9},{9,8},{10,11... | collective-permute-start | bytes 6291464 | tf_op jit(solution)/shard_map/ppermute | solution.py:912
  380.7 52.3 %collective-permute-start.21 = (bf16[1024,1024]{1,0:T(8,128)(2,1)}, bf16[1024,1024]{1,0:T(8,128)(2,1)}, u32[]{:S(2)}, u32[]{:S(2)}) collective-permute-start(bf16[1024,1024]{1,0:T(8,128)(2,1)} %get-tuple-element.95.refs_6_), channel_id=1, source_target_pairs={{0,2},{1,3},{2,0},{3,1},{4,6},{5,7},{6,4},{7,5},{8,10},{9,11},{10,... | collective-permute-start | bytes 6291464 | tf_op jit(solution)/shard_map/ppermute | solution.py:912
  434.3 3.6 copy-start.1
  437.3 2.8 copy-start.25
  437.3 32.7 %collective-permute-start.23 = (bf16[512,1024]{1,0:T(8,128)(2,1)S(1)}, bf16[512,1024]{1,0:T(8,128)(2,1)S(1)}, u32[]{:S(2)}, u32[]{:S(2)}) collective-permute-start(bf16[512,1024]{1,0:T(8,128)(2,1)S(1)} %add_convert_fusion.refs_24_), channel_id=1, source_target_pairs={{0,1},{1,0},{2,3},{3,2},{4,5},{5,4},{6,7},{7,6},{8,9},{9,8},{10,11... | collective-permute-start | bytes 3145736 | tf_op jit(solution)/shard_map/ppermute | solution.py:912
  439.6 30.4 %collective-permute-start.22 = (bf16[512,1024]{1,0:T(8,128)(2,1)S(1)}, bf16[512,1024]{1,0:T(8,128)(2,1)S(1)}, u32[]{:S(2)}, u32[]{:S(2)}) collective-permute-start(bf16[512,1024]{1,0:T(8,128)(2,1)S(1)} %add_convert_fusion.1.refs_23_), channel_id=1, source_target_pairs={{0,2},{1,3},{2,0},{3,1},{4,6},{5,7},{6,4},{7,5},{8,10},{9,11},{10,... | collective-permute-start | bytes 3145736 | tf_op jit(solution)/shard_map/ppermute | solution.py:912
  471.9 26.1 %collective-permute-start.25 = (bf16[1024,512]{1,0:T(8,128)(2,1)}, bf16[1024,512]{1,0:T(8,128)(2,1)S(1)}, u32[]{:S(2)}, u32[]{:S(2)}) collective-permute-start(bf16[1024,512]{1,0:T(8,128)(2,1)} %get-tuple-element.113), channel_id=1, source_target_pairs={{0,2},{1,3},{2,0},{3,1},{4,6},{5,7},{6,4},{7,5},{8,10},{9,11},{10,... | collective-permute-start | bytes 3145736 | tf_op jit(solution)/shard_map/ppermute | solution.py:912
  473.0 25.0 %collective-permute-start.24 = (bf16[1024,512]{1,0:T(8,128)(2,1)}, bf16[1024,512]{1,0:T(8,128)(2,1)S(1)}, u32[]{:S(2)}, u32[]{:S(2)}) collective-permute-start(bf16[1024,512]{1,0:T(8,128)(2,1)} %get-tuple-element.108.refs_22_), channel_id=1, source_target_pairs={{0,1},{1,0},{2,3},{3,2},{4,5},{5,4},{6,7},{7,6},{8,9},{9,8},{10,11... | collective-permute-start | bytes 3145736 | tf_op jit(solution)/shard_map/ppermute | solution.py:912
  499.3 1.7 copy-start.32
  499.3 26.3 %collective-permute-start.30 = (bf16[1024,512]{1,0:T(8,128)(2,1)}, bf16[1024,512]{1,0:T(8,128)(2,1)S(1)}, u32[]{:S(2)}, u32[]{:S(2)}) collective-permute-start(bf16[1024,512]{1,0:T(8,128)(2,1)} %get-tuple-element.116.refs_4_), channel_id=1, source_target_pairs={{0,2},{1,3},{2,0},{3,1},{4,6},{5,7},{6,4},{7,5},{8,10},{9,11},{10,... | collective-permute-start | bytes 3145736 | tf_op jit(solution)/shard_map/ppermute | solution.py:912
  500.2 26.4 %collective-permute-start.29 = (bf16[1024,512]{1,0:T(8,128)(2,1)}, bf16[1024,512]{1,0:T(8,128)(2,1)}, u32[]{:S(2)}, u32[]{:S(2)}) collective-permute-start(bf16[1024,512]{1,0:T(8,128)(2,1)} %get-tuple-element.115.refs_2_.refs_11_), channel_id=1, source_target_pairs={{0,1},{1,0},{2,3},{3,2},{4,5},{5,4},{6,7},{7,6},{8,9},{9,8},{10,11... | collective-permute-start | bytes 3145736 | tf_op jit(solution)/shard_map/ppermute | solution.py:912
  501.3 6.0 copy-start.27
  501.3 7.0 %copy-start.36 = (s32[8]{0:T(128)S(1)}, s32[8]{0:T(128)}, u32[]{:S(2)}) copy-start(s32[8]{0:T(128)} %pad_add_fusion.refs_0_) | copy-start | bytes 100
  501.3 8.5 %copy-start.3 = (bf16[1024,512]{1,0:T(8,128)(2,1)S(1)}, bf16[1024,512]{1,0:T(8,128)(2,1)}, u32[]{:S(2)}) copy-start(bf16[1024,512]{1,0:T(8,128)(2,1)} %get-tuple-element.123.refs_6_) | copy-start | bytes 3145732
  507.3 8.3 %copy-start.2 = (bf16[1024,512]{1,0:T(8,128)(2,1)S(1)}, bf16[1024,512]{1,0:T(8,128)(2,1)}, u32[]{:S(2)}) copy-start(bf16[1024,512]{1,0:T(8,128)(2,1)} %get-tuple-element.121.refs_3_) | copy-start | bytes 3145732
  508.6 1.2 collective-permute-start.26
  508.7 6.9 %copy-start.9 = (bf16[1024,512]{1,0:T(8,128)(2,1)S(1)}, bf16[1024,512]{1,0:T(8,128)(2,1)}, u32[]{:S(2)}) copy-start(bf16[1024,512]{1,0:T(8,128)(2,1)} %get-tuple-element.122.refs_4_) | copy-start | bytes 3145732
  509.9 5.7 collective-permute-start.27
  511.9 116.2 %collective-permute-start.32 = (bf16[512,512]{1,0:T(8,128)(2,1)}, bf16[512,512]{1,0:T(8,128)(2,1)}, u32[]{:S(2)}, u32[]{:S(2)}) collective-permute-start(bf16[512,512]{1,0:T(8,128)(2,1)} %add_convert_fusion.4.refs_5_), channel_id=1, source_target_pairs={{0,1},{1,0},{2,3},{3,2},{4,5},{5,4},{6,7},{7,6},{8,9},{9,8},{10,11... | collective-permute-start | bytes 1572872 | tf_op jit(solution)/shard_map/ppermute | solution.py:912
  515.6 6.9 %collective-permute-start.28 = (f32[8,1216]{1,0:T(8,128)S(1)}, f32[8,1216]{1,0:T(8,128)S(1)}, u32[]{:S(2)}, u32[]{:S(2)}) collective-permute-start(f32[8,1216]{1,0:T(8,128)S(1)} %add.165), channel_id=1, source_target_pairs={{0,16},{4,20},{8,24},{12,28},{16,0},{20,4},{24,8},{28,12},{1,17},{... | collective-permute-start | bytes 116744 | tf_op jit(solution)/shard_map/ppermute | solution.py:912
  516.5 111.6 %collective-permute-start.31 = (bf16[512,512]{1,0:T(8,128)(2,1)}, bf16[512,512]{1,0:T(8,128)(2,1)}, u32[]{:S(2)}, u32[]{:S(2)}) collective-permute-start(bf16[512,512]{1,0:T(8,128)(2,1)} %add_convert_fusion.5.refs_4_), channel_id=1, source_target_pairs={{0,2},{1,3},{2,0},{3,1},{4,6},{5,7},{6,4},{7,5},{8,10},{9,11},{10,... | collective-permute-start | bytes 1572872 | tf_op jit(solution)/shard_map/ppermute | solution.py:912
  525.4 1.6 copy-start.4
  525.4 2.8 copy-start.5
  526.6 5.6 copy-start.33
  528.2 4.7 copy-start.18
  529.6 3.3 copy-start.19
  529.6 98.5 %collective-permute-start.34 = (bf16[512,512]{1,0:T(8,128)(2,1)S(1)}, bf16[512,512]{1,0:T(8,128)(2,1)S(1)}, u32[]{:S(2)}, u32[]{:S(2)}) collective-permute-start(bf16[512,512]{1,0:T(8,128)(2,1)S(1)} %add_convert_fusion.2.refs_10_), channel_id=1, source_target_pairs={{0,1},{1,0},{2,3},{3,2},{4,5},{5,4},{6,7},{7,6},{8,9},{9,8},{10,11... | collective-permute-start | bytes 1572872 | tf_op jit(solution)/shard_map/ppermute | solution.py:912
  531.1 97.0 %collective-permute-start.33 = (bf16[512,512]{1,0:T(8,128)(2,1)S(1)}, bf16[512,512]{1,0:T(8,128)(2,1)S(1)}, u32[]{:S(2)}, u32[]{:S(2)}) collective-permute-start(bf16[512,512]{1,0:T(8,128)(2,1)S(1)} %add_convert_fusion.3.refs_9_), channel_id=1, source_target_pairs={{0,2},{1,3},{2,0},{3,1},{4,6},{5,7},{6,4},{7,5},{8,10},{9,11},{10,... | collective-permute-start | bytes 1572872 | tf_op jit(solution)/shard_map/ppermute | solution.py:912
  620.1 3.6 collective-permute-start.35
  623.7 14.4 %collective-permute-start.36 = (f32[3,256]{1,0:T(4,128)S(1)}, f32[3,256]{1,0:T(4,128)S(1)}, u32[]{:S(2)}, u32[]{:S(2)}) collective-permute-start(f32[3,256]{1,0:T(4,128)S(1)} %add.172), channel_id=1, source_target_pairs={{0,2},{1,3},{2,0},{3,1},{4,6},{5,7},{6,4},{7,5},{8,10},{9,11},{10,... | collective-permute-start | bytes 9224 | tf_op jit(solution)/shard_map/ppermute | solution.py:912
  (23 other events, 23.9 us)
Sparse Core Ops, SparseCore 0:
  9.9 90.3 all-gather.8
  102.7 87.6 all-gather.6
  191.9 82.0 all-gather.4
  346.2 68.4 reduce-scatter.3
  416.9 109.5 reduce-scatter.5
  528.6 87.9 reduce-scatter.7
